TPU v7x, 512 devices: a whole 4x8x8 slice. The times are simulated.
512 devices in a mesh: pop: 16 (over z, y_hi), row: 4 (over y_lo), col: 8 (over x, core).
Axes of the slice: x: 4, y: 8 (y_hi: 2, y_lo: 4; y = y_hi * 4 + y_lo), z: 8, core: 2. Of those that a mesh axis runs over, the one named last changes fastest.
Arguments:
- inputs: bfloat16 [8192, 4096], P(('pop', 'row'), 'col'), may hold values from -6 to 6
- mix: float32 [4096], P('col'), may hold values from 0.05 to 0.95
- key_weight: bfloat16 [4096, 16384], P('col', ('row', 'pop')), may hold values from -0.09375 to 0.09375
- value_weight: bfloat16 [16384, 4096], P(('row', 'pop'), 'col'), may hold values from -0.046875 to 0.046875
- dim_bank: float32 [64, 4096], P(None, 'col'), may hold values from -6 to 6
- hidden_bank: float32 [64, 16384], P(None, 'row'), may hold values from -6 to 6
- member_picks: int32 [128, 4], P(('pop', 'row')), may hold values from 0 to 63
- ranks: int32 [128], P(('pop', 'row')), may hold values from 0 to 127, each once
Outputs:
- outputs: bfloat16 [8192, 4096], P(('pop', 'row'), 'col')
- key_step: float32 [4096, 16384], P('col', ('row', 'pop'))
- value_step: float32 [16384, 4096], P(('row', 'pop'), 'col')
Inputs may be any that keep to these rules, and one draw needn't show every extreme that they name: `member_picks`: factor indices into the banks. `ranks`: each rank appears once.
All inputs are finite; a program needn't handle non-finite values.
Results may differ from a plain program's by a relative error of at most 0.022.
Values may be sent and summed in bfloat16 or wider, within the bound.
No kernel may reach another device: no remote copies, remote signals or barrier semaphores. Data moves between devices by JAX's collectives and lax.ppermute only.
A program may use at most 64 MiB of HBM per device.

v0:
```python
import jax
import jax.numpy as jnp
from jax import lax
from jax.sharding import PartitionSpec as P

D = 4096
FF = 16384
BATCH = 64


def shards(inputs, mix, key_weight, value_weight, dim_bank, hidden_bank, member_picks, ranks):
    sigma_k = 0.5 / D**0.5
    sigma_v = 0.5 / FF**0.5
    feat = inputs.shape[1]
    local_tok = inputs.shape[0]
    hidden_cols = hidden_bank.shape[1]
    slice_cols = key_weight.shape[1]
    values = inputs.astype(jnp.float32).reshape(local_tok // BATCH, BATCH, feat)
    previous = jnp.concatenate(
        [jnp.zeros((local_tok // BATCH, 1, feat), jnp.float32), values[:, :-1, :]], axis=1
    )
    shifted = (values + (previous - values) * mix).reshape(local_tok, feat).astype(jnp.bfloat16)
    group = lax.all_gather(shifted, "row", axis=0, tiled=True)
    picks, order = (
        lax.all_gather(member_picks, ("pop", "row"), axis=0, tiled=True),
        lax.all_gather(ranks, ("pop", "row"), axis=0, tiled=True),
    )
    group_tok = group.shape[0]
    group_mem = group_tok // BATCH
    members = picks.shape[0]
    first = lax.axis_index("pop") * group_mem
    own = lax.dynamic_slice_in_dim(picks, first, group_mem, 0)
    fac_a = jnp.take(dim_bank, own[:, 0], axis=0)
    fac_b = jnp.take(hidden_bank, own[:, 1], axis=0)
    fac_c = jnp.take(hidden_bank, own[:, 2], axis=0)
    fac_d = jnp.take(dim_bank, own[:, 3], axis=0)
    offset = lax.axis_index("pop") * slice_cols
    all_a = jnp.take(dim_bank, picks[:, 0], axis=0)
    all_b = lax.dynamic_slice_in_dim(
        jnp.take(hidden_bank, picks[:, 1], axis=0), offset, slice_cols, 1
    )
    inner = jnp.sum(
        group.astype(jnp.float32).reshape(group_mem, BATCH, feat) * fac_a[:, None, :], axis=-1
    )
    product = jnp.dot(
        group,
        lax.all_gather(key_weight, "pop", axis=1, tiled=True),
        preferred_element_type=jnp.float32,
    )
    term = product.reshape(group_mem, BATCH, -1) + sigma_k * inner[:, :, None] * fac_b[:, None, :]
    partial_keys = term.reshape(group_tok, -1)
    key_pre = lax.psum(partial_keys.astype(jnp.bfloat16), "col").astype(jnp.float32)
    keys = (jnp.maximum(key_pre, 0.0) ** 2).astype(jnp.bfloat16)
    inner_c = jnp.sum(
        keys.astype(jnp.float32).reshape(group_mem, BATCH, hidden_cols) * fac_c[:, None, :], axis=-1
    )
    base = jnp.dot(
        keys,
        lax.all_gather(value_weight, "pop", axis=0, tiled=True),
        preferred_element_type=jnp.float32,
    )
    result = (
        base.reshape(group_mem, BATCH, feat) + sigma_v * inner_c[:, :, None] * fac_d[:, None, :]
    )
    outputs = lax.psum_scatter(
        result.reshape(group_tok, feat).astype(jnp.bfloat16), "row", scatter_dimension=0, tiled=True
    )
    fitness = 2.0 * order.astype(jnp.float32) / (members - 1) - 1.0
    scale = 1.0 / members**0.5
    all_c = lax.dynamic_slice_in_dim(
        jnp.take(hidden_bank, picks[:, 2], axis=0), offset, slice_cols, 1
    )
    all_d = jnp.take(dim_bank, picks[:, 3], axis=0)
    key_step = (
        jnp.dot(jnp.transpose(fitness[:, None] * all_a), all_b, precision=lax.Precision.HIGHEST)
        * scale
    )
    value_step = (
        jnp.dot(jnp.transpose(fitness[:, None] * all_c), all_d, precision=lax.Precision.HIGHEST)
        * scale
    )
    return (outputs, key_step, value_step)


def solution(mesh):
    in_specs = (
        P(("pop", "row"), "col"),
        P("col"),
        P("col", ("row", "pop")),
        P(("row", "pop"), "col"),
        P(None, "col"),
        P(None, "row"),
        P(("pop", "row"), None),
        P(("pop", "row")),
    )
    out_specs = (P(("pop", "row"), "col"), P("col", ("row", "pop")), P(("row", "pop"), "col"))
    return jax.shard_map(shards, mesh=mesh, in_specs=in_specs, out_specs=out_specs, check_vma=False)
```

profile of v0, /device:TPU:1, one launch (start us, length us, event | category | flops | bytes accessed | tf_op | source)
XLA Modules:
  0.0 411.1 jit_solution(10954718185610189302)
XLA Ops:
  7.2 0.0 copy-start
  7.2 0.0 all-gather.4.cloned.1.call-start
  7.2 0.7 all-gather.4.cloned.1.call-update
  7.9 0.0 all-reduce.4.cloned.1.call-start
  8.0 45.9 %all-gather = s32[64,2,4]{2,1,0:T(2,128)S(1)} all-gather(s32[1,2,4]{2,1,0:T(2,128)} %bitcast.62), channel_id=1, replica_groups=mesh['pop'=16,'row'=4,'col'=8] {'pop','row'}, dimensions={0}, use_global_device_ids=true | all-gather | bytes 2080 | tf_op jit(solution)/shard_map/all_gather | solution.py:25
  53.8 0.1 fusion.26
  53.9 0.1 copy.22
  54.0 0.1 copy.23
  54.1 0.9 slice.52
  55.0 1.5 gather_fusion
  56.5 1.0 add_convert_fusion
  57.5 12.3 %all_gather.15 = bf16[512,512]{1,0:T(8,128)(2,1)S(1)} all-gather(bf16[128,512]{1,0:T(8,128)(2,1)S(1)} %bitcast.61), channel_id=1, replica_groups=mesh['pop'=16,'row'=4,'col'=8] {'row'}, dimensions={0}, use_global_device_ids=true | all-gather | bytes 655360 | tf_op jit(solution)/shard_map/all_gather | solution.py:23
  69.9 0.1 broadcast_select_fusion.3
  69.9 0.2 fusion.6
  70.1 0.0 copy-done
  70.1 0.6 gather_fusion.1
  70.8 0.1 broadcast_select_fusion.1
  70.8 79.1 %all-gather.4.cloned.1.call-done = bf16[512,4096]{1,0:T(8,128)(2,1)} async-done(((bf16[512,256]{1,0:T(8,128)(2,1)}), bf16[512,4096]{1,0:T(8,128)(2,1)}) %all-gather.4.cloned.1.call-update) | async-done | bytes 4194320 | tf_op jit(solution)/shard_map/all_gather | solution.py:47
  150.0 6.5 %fusion.2 = bf16[512,4096]{1,0:T(8,128)(2,1)} fusion(bf16[512,512]{1,0:T(8,128)(2,1)S(1)} %all_gather.15, bf16[512,4096]{1,0:T(8,128)(2,1)} %all-gather.4.cloned.1.call-done, f32[8,4096]{1,0:T(8,128)S(1)} %broadcast_select_fusion.1, f32[512]{0:T(512)S(1)} %broadcast_multiply_fusion.1), kind=kOutput, calls=%fused_computation.12 | convolution fusion | flops 2153775104 | bytes 9046016 | tf_op jit(solution)/shard_map/dot_general | solution.py:45
  156.5 0.0 copy-start.1
  156.5 0.0 all-reduce.4.cloned.1.call-update
  156.5 0.0 all-gather.6.cloned.1.call-start
  156.6 0.7 all-gather.6.cloned.1.call-update
  157.3 0.0 reduce-scatter.2.cloned.1.call-start
  157.3 0.1 copy.24
  157.4 0.1 copy.25
  157.5 1.2 gather_fusion.2
  158.7 0.0 copy-done.1
  158.7 1.2 gather_fusion.3
  159.9 0.7 fusion.25
  160.6 0.1 copy.28
  160.7 0.1 copy.29
  160.8 0.5 copy-done.2
  161.3 0.0 copy-done.4
  161.3 1.3 gather_fusion.6
  162.6 0.8 gather_fusion.7
  163.4 0.9 copy.26
  164.3 0.9 copy.27
  165.2 0.5 compare_select_fusion.2
  165.8 0.0 copy-done.6
  165.8 2.6 gather_fusion.5
  168.3 0.0 copy-done.8
  168.3 0.7 pad_clamp_fusion.3
  169.0 1.5 gather_fusion.4
  170.5 1.3 dynamic-slice
  172.4 0.9 dynamic-update-slice
  173.3 20.5 %all-reduce.1 = s32[128]{0:T(128)} all-reduce(s32[128]{0:T(128)S(1)} %dynamic-update-slice), channel_id=1, replica_groups=mesh['pop'=16,'row'=4,'col'=8] {'pop','row'}, use_global_device_ids=true, to_apply=%add.1 | all-reduce | flops 128 | bytes 1024
  193.8 0.8 broadcast_select_fusion.2
  194.6 1.0 broadcast_select_fusion
  195.6 42.5 %all-reduce.4.cloned.1.call-done = bf16[512,4096]{1,0:T(8,128)(2,1)} async-done(((bf16[512,4096]{1,0:T(8,128)(2,1)}), bf16[512,4096]{1,0:T(8,128)(2,1)}) %all-reduce.4.cloned.1.call-update) | async-done | bytes 4194320 | tf_op jit(solution)/shard_map/psum | solution.py:52
  238.1 3.6 fusion
  241.7 1.2 bitcast_multiply_fusion.2
  242.9 0.0 copy-start.9
  242.9 127.5 %all-gather.6.cloned.1.call-done = bf16[4096,512]{1,0:T(8,128)(2,1)} async-done(((bf16[256,512]{1,0:T(8,128)(2,1)}), bf16[4096,512]{1,0:T(8,128)(2,1)}) %all-gather.6.cloned.1.call-update) | async-done | bytes 4194320 | tf_op jit(solution)/shard_map/all_gather | solution.py:59
  370.4 6.8 %fusion.5 = bf16[512,512]{1,0:T(8,128)(2,1)} fusion(f32[512,512]{1,0:T(8,128)} %bitcast_multiply_fusion.2, bf16[4096,512]{1,0:T(8,128)(2,1)} %all-gather.6.cloned.1.call-done, bf16[512,4096]{1,0:T(8,128)(2,1)} %all-reduce.4.cloned.1.call-done), kind=kOutput, calls=%fused_computation.16 | convolution fusion | flops 2156396544 | bytes 9961472 | tf_op jit(solution)/shard_map/dot_general | solution.py:57
  377.2 0.0 reduce-scatter.2.cloned.1.call-update
  377.3 0.0 copy-done.10
  377.3 0.0 copy-done.3
  377.3 0.0 copy-done.5
  377.3 0.0 copy-done.7
  377.3 0.0 copy-done.9
  377.4 1.5 convolution_multiply_fusion
  378.9 2.5 convolution_multiply_fusion.1
  381.3 23.2 %reduce-scatter.2.cloned.1.call-done = bf16[128,512]{1,0:T(8,128)(2,1)} async-done(((bf16[512,512]{1,0:T(8,128)(2,1)}), bf16[128,512]{1,0:T(8,128)(2,1)}) %reduce-scatter.2.cloned.1.call-update) | async-done | bytes 131088 | tf_op jit(solution)/shard_map/reduce_scatter | solution.py:65
  (29 shorter events, 0.1 us)
Async XLA Ops:
  7.2 63.0 %copy-start = (f32[64,4096]{1,0:T(8,128)S(1)}, f32[64,4096]{1,0:T(8,128)}, u32[]{:S(2)}) copy-start(f32[64,4096]{1,0:T(8,128)} %param.21) | copy-start | bytes 3145732
  7.2 142.8 %all-gather.4.cloned.1.call-start = ((), (), s32[]{:S(2)}) async-start(), calls=%async_computation.1 | async-start | bytes 4456448 | tf_op jit(solution)/shard_map/all_gather | solution.py:47
  7.9 230.2 %all-reduce.4.cloned.1.call-start = ((), (), s32[]{:S(2)}) async-start(), calls=%async_computation.2 | async-start | bytes 8388608 | tf_op jit(solution)/shard_map/psum | solution.py:52
  156.5 2.2 copy-start.1
  156.5 213.9 %all-gather.6.cloned.1.call-start = ((), (), s32[]{:S(2)}) async-start(), calls=%async_computation.3 | async-start | bytes 4456448 | tf_op jit(solution)/shard_map/all_gather | solution.py:59
  157.3 247.3 %reduce-scatter.2.cloned.1.call-start = ((), (), s32[]{:S(2)}) async-start(), calls=%async_computation.4 | async-start | bytes 655360 | tf_op jit(solution)/shard_map/reduce_scatter | solution.py:65
  160.7 0.6 copy-start.2
  160.8 0.5 copy-start.4
  164.3 1.5 copy-start.6
  165.2 3.1 copy-start.8
  242.9 134.3 %copy-start.10 = (s32[128]{0:T(128)S(1)}, s32[128]{0:T(128)}, u32[]{:S(2)}) copy-start(s32[128]{0:T(128)} %all-reduce.1) | copy-start | bytes 1540
  242.9 134.4 %copy-start.3 = (s32[128,1]{0,1:T(1,128)S(1)}, s32[128,1]{0,1:T(1,128)}, u32[]{:S(2)}) copy-start(s32[128,1]{0,1:T(1,128)} %copy-done.2) | copy-start | bytes 1540
  242.9 134.4 %copy-start.5 = (s32[128,1]{0,1:T(1,128)S(1)}, s32[128,1]{0,1:T(1,128)}, u32[]{:S(2)}) copy-start(s32[128,1]{0,1:T(1,128)} %copy-done.4) | copy-start | bytes 1540
  242.9 134.4 %copy-start.7 = (s32[128,1]{0,1:T(1,128)S(1)}, s32[128,1]{0,1:T(1,128)}, u32[]{:S(2)}) copy-start(s32[128,1]{0,1:T(1,128)} %copy-done.6) | copy-start | bytes 1540
  242.9 134.4 %copy-start.9 = (s32[128,1]{0,1:T(1,128)S(1)}, s32[128,1]{0,1:T(1,128)}, u32[]{:S(2)}) copy-start(s32[128,1]{0,1:T(1,128)} %copy-done.8) | copy-start | bytes 1540
Sparse Core Ops, SparseCore 0:
  11.1 138.8 all-gather.3
  156.6 81.3 all-reduce.3
  241.3 129.1 all-gather.5
  377.4 27.1 reduce-scatter.1
where the time goes:
time: 412 us; the launch traced here: 411 us
  waiting for transfers between devices  274 us (67%)
  blocking collectives  78.7 us (19%)
  local copies, waits for them, and re-layouts  17.3 us (4%)
  matrix products  17.3 us (4%)
  between operations  14.7 us (4%)
  other arithmetic  9.24 us (2%)
    all_gather x1, waiting for transfers between devices, shards(): lax.all_gather(value_weight, 'pop', axis=0, tiled=True)  127 us
    all_gather x1, waiting for transfers between devices, shards(): lax.all_gather(key_weight, 'pop', axis=1, tiled=True)  79.1 us
    all_gather x1, blocking collectives, shards(): lax.all_gather(member_picks, ('pop', 'row'), axis=0, tiled=True)  45.9 us
    psum x1, waiting for transfers between devices, shards(): lax.psum(partial_keys.astype(jnp.bfloat16), 'col').astype(jnp.float32)  42.5 us
    reduce_scatter x1, waiting for transfers between devices, shards(): lax.psum_scatter(result.reshape(group_tok, feat).astype(jnp.bfloat16), 'r...  23.2 us
    unnamed x1, blocking collectives  20.5 us
    all_gather x1, blocking collectives, shards(): group = lax.all_gather(shifted, 'row', axis=0, tiled=True)  12.3 us
  transfers between devices with their start and end apart: 4, of which 4 were waited for; matrix products, arithmetic and copies ran while one was open for 7% of the time, Pallas kernels for 0%

commit v1 on v0

v1 whole, which is shorter than its diff:
```python
import jax
import jax.numpy as jnp
from jax import lax
from jax.sharding import Mesh
from jax.sharding import PartitionSpec as P

D = 4096
FF = 16384
BATCH = 64
MEMBERS = 128
Y = ("y_hi", "y_lo")
HIGH = lax.Precision.HIGHEST


def swap(x):
    return lax.ppermute(x, "core", [(0, 1), (1, 0)])


def to_all(x, axis, n):
    return lax.all_to_all(jnp.broadcast_to(x[None], (n, *x.shape)), axis, 0, 0)


def one_hot(index, n):
    return (index[:, None] == lax.iota(jnp.int32, n)[None, :]).astype(jnp.float32)


def shards(inputs, mix, key_weight, value_weight, dim_bank, hidden_bank, member_picks, ranks):
    sigma_k = 0.5 / D**0.5
    sigma_v = 0.5 / FF**0.5
    bank = dim_bank.shape[0]
    tok, feat = inputs.shape
    hid = key_weight.shape[1]
    half = hid // 2
    own = tok // BATCH
    core = lax.axis_index("core")
    y_hi = lax.axis_index("y_hi")
    z = lax.axis_index("z")

    key_rows = key_weight.T
    key_mine = lax.dynamic_slice_in_dim(key_rows, core * half, half, 0)
    key_else = lax.dynamic_slice_in_dim(key_rows, (1 - core) * half, half, 0)
    value_mine = lax.dynamic_slice_in_dim(value_weight, core * half, half, 0)
    value_else = lax.dynamic_slice_in_dim(value_weight, (1 - core) * half, half, 0)
    got = swap(jnp.concatenate([key_else, value_else], axis=1))
    packed = jnp.concatenate([key_mine, got[:, :feat], value_mine, got[:, feat:]], axis=1)
    weights = lax.all_gather(packed, "z", axis=0, tiled=True)

    values = inputs.astype(jnp.float32).reshape(own, BATCH, feat)
    previous = jnp.concatenate([jnp.zeros((own, 1, feat), jnp.float32), values[:, :-1, :]], axis=1)
    shifted = (values + (previous - values) * mix).reshape(tok, feat).astype(jnp.bfloat16)
    info = jnp.concatenate([member_picks, ranks[:, None]], axis=1).astype(jnp.bfloat16)
    info = jnp.pad(info, ((0, 16 - own), (0, feat - info.shape[1])))
    group = to_all(jnp.concatenate([shifted, info], axis=0), Y, 8)
    mine = group[:, :tok].reshape(8 * tok, feat)
    tokens = jnp.concatenate([mine, swap(mine)], axis=1)
    members = 8 * own
    info = group[:, tok : tok + own, :128].reshape(members, 128)
    everyone = to_all(info, "z", 8).reshape(8 * members, 128)[:, :5].astype(jnp.int32)
    info = info[:, :4].astype(jnp.int32)

    banks = jnp.concatenate([dim_bank, swap(dim_bank)], axis=1)
    hidden = hidden_bank.reshape(bank, 8, 2, 2, half)
    hidden = lax.dynamic_index_in_dim(hidden, y_hi, 2, keepdims=False)
    hidden_own = lax.dynamic_index_in_dim(hidden, z, 1, keepdims=False).reshape(bank, hid)
    hidden = lax.dynamic_index_in_dim(hidden, core, 2, keepdims=False).reshape(bank, 8 * half)
    fac_a = jnp.dot(one_hot(info[:, 0], bank), banks, precision=HIGH)
    fac_b = jnp.dot(one_hot(info[:, 1], bank), hidden, precision=HIGH)
    fac_c = jnp.dot(one_hot(info[:, 2], bank), hidden, precision=HIGH)
    fac_d = jnp.dot(one_hot(info[:, 3], bank), banks, precision=HIGH)

    inner = jnp.sum(
        tokens.astype(jnp.float32).reshape(members, BATCH, -1) * fac_a[:, None, :], axis=-1
    )
    key_all = weights[:, : 2 * feat]
    product = lax.dot_general(
        tokens, key_all, (((1,), (1,)), ((), ())), preferred_element_type=jnp.float32
    )
    part = product.reshape(members, BATCH, -1) + sigma_k * inner[:, :, None] * fac_b[:, None, :]
    part = part.reshape(4, 2 * tok, -1).astype(jnp.bfloat16)
    parts = lax.all_to_all(part, "x", 0, 0)
    key_pre = jnp.sum(parts.astype(jnp.float32), axis=0)
    keys = (jnp.maximum(key_pre, 0.0) ** 2).astype(jnp.bfloat16)
    keys = to_all(keys, "x", 4).reshape(8 * tok, -1)

    inner_c = jnp.sum(
        keys.astype(jnp.float32).reshape(members, BATCH, -1) * fac_c[:, None, :], axis=-1
    )
    base = jnp.dot(keys, weights[:, 2 * feat :], preferred_element_type=jnp.float32)
    result = base.reshape(members, BATCH, -1) + sigma_v * inner_c[:, :, None] * fac_d[:, None, :]
    result = result.reshape(8 * tok, -1)
    rest = swap(result[:, feat:].astype(jnp.bfloat16))
    result = (result[:, :feat] + rest.astype(jnp.float32)).astype(jnp.bfloat16)
    pieces = lax.all_to_all(result.reshape(8, tok, feat), Y, 0, 0)
    outputs = jnp.sum(pieces.astype(jnp.float32), axis=0).astype(jnp.bfloat16)

    fitness = 2.0 * everyone[:, 4].astype(jnp.float32) / (MEMBERS - 1) - 1.0
    fitness = fitness * (1.0 / MEMBERS**0.5)
    pick = [one_hot(everyone[:, i], bank) for i in range(4)]
    pair_k = jnp.dot((fitness[:, None] * pick[0]).T, pick[1], precision=HIGH)
    pair_v = jnp.dot((fitness[:, None] * pick[2]).T, pick[3], precision=HIGH)
    key_step = jnp.dot(dim_bank.T, jnp.dot(pair_k, hidden_own, precision=HIGH), precision=HIGH)
    value_step = jnp.dot(hidden_own.T, jnp.dot(pair_v, dim_bank, precision=HIGH), precision=HIGH)
    return outputs, key_step, value_step


def solution(mesh):
    fine = Mesh(mesh.devices.reshape(8, 2, 4, 4, 2), ("z", "y_hi", "y_lo", "x", "core"))
    pop, row, col = ("z", "y_hi"), ("y_lo",), ("x", "core")
    in_specs = (
        P(pop + row, col),
        P(col),
        P(col, row + pop),
        P(row + pop, col),
        P(None, col),
        P(None, row),
        P(pop + row, None),
        P(pop + row),
    )
    out_specs = (P(pop + row, col), P(col, row + pop), P(row + pop, col))
    return jax.shard_map(shards, mesh=fine, in_specs=in_specs, out_specs=out_specs, check_vma=False)
```

time: 412 us -> 213 us (0.52)
  waiting for transfers between devices: 274 us -> 93.6 us
  blocking collectives: 78.7 us -> 29.2 us
  starting transfers between devices: 0.16 us -> 38.1 us
    all_gather x2 -> x1, waiting for transfers between devices: 207 us -> 13 us  [shards(): weights = lax.all_gather(packed, 'z', axis=0, tiled=True)]
    all_to_all x0 -> x4, waiting for transfers between devices: none -> 79.6 us  [the longest x3 56.3 us: to_all(): return lax.all_to_all(jnp.broadcast_to(x[None], (n, *x.shape)), axis, 0, 0)]
    all_gather x2 -> x0, blocking collectives: 58.2 us -> none  [the longest x1 45.9 us: shards(): lax.all_gather(member_picks, ('pop', 'row'), axis=0, tiled=True)]
    psum x1 -> x0, waiting for transfers between devices: 42.5 us -> none  [shards(): lax.psum(partial_keys.astype(jnp.bfloat16), 'col').astype(jnp.float32)]
    all_to_all x0 -> x1, blocking collectives: none -> 29.2 us  [shards(): parts = lax.all_to_all(part, 'x', 0, 0)]
    reduce_scatter x1 -> x0, waiting for transfers between devices: 23.2 us -> none  [shards(): lax.psum_scatter(result.reshape(group_tok, feat).astype(jnp.bfloat16), 'r...]
    ppermute x0 -> x4, starting transfers between devices: none -> 20.6 us  [swap(): return lax.ppermute(x, 'core', [(0, 1), (1, 0)])]
    unnamed x1 -> x0, blocking collectives: 20.5 us -> none
  transfers between devices with their start and end apart: 4 -> 9, of which waited for: 4 -> 6; matrix products, arithmetic and copies ran while one was open for 7% -> 7% of each run, Pallas kernels for 0% -> 0%
where the time goes in v1:
time: 213 us; the launch traced here: 212 us
  waiting for transfers between devices  93.6 us (44%)
  starting transfers between devices  38.1 us (18%)
  blocking collectives  29.2 us (14%)
  matrix products  15 us (7%)
  local copies, waits for them, and re-layouts  14.8 us (7%)
  between operations  14.5 us (7%)
  other arithmetic  6.8 us (3%)
    all_to_all x3, waiting for transfers between devices, to_all(): return lax.all_to_all(jnp.broadcast_to(x[None], (n, *x.shape)), axis, 0, 0)  56.3 us
    all_to_all x1, blocking collectives, shards(): parts = lax.all_to_all(part, 'x', 0, 0)  29.2 us
    all_to_all x1, waiting for transfers between devices, shards(): pieces = lax.all_to_all(result.reshape(8, tok, feat), Y, 0, 0)  23.2 us
    ppermute x4, starting transfers between devices, swap(): return lax.ppermute(x, 'core', [(0, 1), (1, 0)])  20.6 us
    all_gather x1, waiting for transfers between devices, shards(): weights = lax.all_gather(packed, 'z', axis=0, tiled=True)  13 us
    all_to_all x3, starting transfers between devices, to_all(): return lax.all_to_all(jnp.broadcast_to(x[None], (n, *x.shape)), axis, 0, 0)  11 us
    all_to_all x1, starting transfers between devices, shards(): pieces = lax.all_to_all(result.reshape(8, tok, feat), Y, 0, 0)  6.46 us
    unnamed x21, local copies, waits for them, and re-layouts  5.12 us
  transfers between devices with their start and end apart: 9, of which 6 were waited for; matrix products, arithmetic and copies ran while one was open for 7% of the time, Pallas kernels for 0%

profile of v1, /device:TPU:1, one launch (start us, length us, event | category | flops | bytes accessed | tf_op | source)
XLA Modules:
  0.0 212.0 jit_solution(10541598071829957)
XLA Ops:
  7.2 0.0 all-gather.2.cloned.1.call-start
  7.3 1.0 constant_dynamic-slice_fusion.1
  8.3 1.0 constant_dynamic-slice_fusion.4
  9.3 0.0 copy-start.3
  9.3 0.1 copy.31
  9.4 8.9 %collective-permute-start.1 = (bf16[128,1024]{1,0:T(8,128)(2,1)S(1)}, bf16[128,1024]{1,0:T(8,128)(2,1)S(1)}, u32[]{:S(2)}, u32[]{:S(2)}) collective-permute-start(bf16[128,1024]{1,0:T(8,128)(2,1)S(1)} %pad_maximum_fusion.1), channel_id=1, source_target_pairs={{0,1},{1,0},{2,3},{3,2},{4,5},{5,4},{6,7},{7,6},{8,9},{9,8},{10,11... | collective-permute-start | bytes 786440 | tf_op jit(solution)/shard_map/ppermute | solution.py:16
  18.3 0.1 copy.30
  18.5 1.0 collective-permute-done.1
  19.5 0.9 pad_maximum_fusion
  20.4 0.0 all-gather.2.cloned.1.call-update
  20.4 0.1 copy.25
  20.6 0.1 fusion.39
  20.6 0.1 add_convert_fusion
  20.7 1.1 broadcast_in_dim.10
  21.8 3.6 %all-to-all-start = ((bf16[8,144,512]{2,1,0:T(8,128)(2,1)}), bf16[8,144,512]{2,1,0:T(8,128)(2,1)S(1)}, u32[]{:S(2)}, u32[]{:S(2)}) async-start(bf16[8,144,512]{2,1,0:T(8,128)(2,1)} %broadcast_in_dim.10), calls=%async_computation | async-start | bytes 2359296 | tf_op jit(solution)/shard_map/all_to_all | solution.py:20
  25.4 2.3 %collective-permute-start.2 = (f32[64,512]{1,0:T(8,128)}, f32[64,512]{1,0:T(8,128)}, u32[]{:S(2)}, u32[]{:S(2)}) collective-permute-start(f32[64,512]{1,0:T(8,128)} %param.12), channel_id=1, source_target_pairs={{0,1},{1,0},{2,3},{3,2},{4,5},{5,4},{6,7},{7,6},{8,9},{9,8},{10,11... | collective-permute-start | bytes 393224 | tf_op jit(solution)/shard_map/ppermute | solution.py:16
  27.7 0.9 reshape.97
  28.6 26.4 %all-to-all-done = bf16[8,144,512]{2,1,0:T(8,128)(2,1)S(1)} async-done(((bf16[8,144,512]{2,1,0:T(8,128)(2,1)}), bf16[8,144,512]{2,1,0:T(8,128)(2,1)S(1)}, u32[]{:S(2)}, u32[]{:S(2)}) %all-to-all-start) | async-done | bytes 1179680 | tf_op jit(solution)/shard_map/all_to_all | solution.py:20
  55.0 0.1 slice.82
  55.1 4.7 %collective-permute-start = (bf16[1024,512]{1,0:T(8,128)(2,1)S(1)}, bf16[1024,512]{1,0:T(8,128)(2,1)S(1)}, u32[]{:S(2)}, u32[]{:S(2)}) collective-permute-start(bf16[1024,512]{1,0:T(8,128)(2,1)S(1)} %bitcast.72), channel_id=1, source_target_pairs={{0,1},{1,0},{2,3},{3,2},{4,5},{5,4},{6,7},{7,6},{8,9},{9,8},{10,11... | collective-permute-start | bytes 3145736 | tf_op jit(solution)/shard_map/ppermute | solution.py:16
  59.9 0.7 dynamic-slice_reduce_fusion
  60.6 0.9 constant_dynamic-update-slice_fusion.1
  61.5 0.9 constant_dynamic-update-slice_fusion
  62.5 0.2 slice_reduce_fusion.3
  62.7 0.2 fusion.40
  62.9 0.2 fusion.12
  63.2 1.0 copy-done.4
  64.2 0.5 multiply_reduce_fusion
  64.7 0.1 mul.126
  64.7 13.0 %all-gather.2.cloned.1.call-done = bf16[1024,2048]{1,0:T(8,128)(2,1)} async-done(((bf16[128,2048]{1,0:T(8,128)(2,1)}), bf16[1024,2048]{1,0:T(8,128)(2,1)}) %all-gather.2.cloned.1.call-update) | async-done | bytes 4194320 | tf_op jit(solution)/shard_map/all_gather | solution.py:46
  77.8 4.3 %fusion.5 = f32[1024,1024]{1,0:T(8,128)S(1)} fusion(bf16[1024,2048]{1,0:T(8,128)(2,1)} %all-gather.2.cloned.1.call-done, bf16[1024,512]{1,0:T(8,128)(2,1)} %copy-done.4, bf16[1024,512]{1,0:T(8,128)(2,1)S(1)} %bitcast.74), kind=kOutput, calls=%fused_computation.13 | convolution fusion | flops 2151677952 | bytes 8388608 | tf_op jit(solution)/shard_map/dot_general | solution.py:75
  82.1 0.5 mul.128
  82.6 0.4 fusion.2
  83.0 29.2 %all_to_all.25 = bf16[4,256,1024]{2,1,0:T(8,128)(2,1)S(1)} all-to-all(bf16[4,256,1024]{2,1,0:T(8,128)(2,1)S(1)} %fusion.2), channel_id=1, replica_groups=mesh['z'=8,'y_hi'=2,'y_lo'=4,'x'=4,'core'=2] {'x'}, dimensions={0} | all-to-all | bytes 4194304 | tf_op jit(solution)/shard_map/all_to_all | solution.py:80
  112.2 0.4 convert_reduce_fusion
  112.6 0.1 multiply_convert_fusion
  112.7 1.6 broadcast_in_dim.11
  114.3 3.6 %all-to-all-start.2 = ((bf16[4,256,1024]{2,1,0:T(8,128)(2,1)}), bf16[4,256,1024]{2,1,0:T(8,128)(2,1)S(1)}, u32[]{:S(2)}, u32[]{:S(2)}) async-start(bf16[4,256,1024]{2,1,0:T(8,128)(2,1)} %broadcast_in_dim.11), calls=%async_computation.2 | async-start | bytes 4194304 | tf_op jit(solution)/shard_map/all_to_all | solution.py:20
  117.9 1.2 fusion.41
  119.1 0.2 fusion.10
  119.4 23.0 %all-to-all-done.2 = bf16[4,256,1024]{2,1,0:T(8,128)(2,1)S(1)} async-done(((bf16[4,256,1024]{2,1,0:T(8,128)(2,1)}), bf16[4,256,1024]{2,1,0:T(8,128)(2,1)S(1)}, u32[]{:S(2)}, u32[]{:S(2)}) %all-to-all-start.2) | async-done | bytes 2097184 | tf_op jit(solution)/shard_map/all_to_all | solution.py:20
  142.4 0.5 mul.131
  142.9 0.6 fusion
  143.5 0.1 mul.136
  143.6 3.9 %multiply_add_fusion = f32[16,64,1024]{2,1,0:T(8,128)S(1)} fusion(f32[16,1024]{1,0:T(8,128)S(1)} %fusion.41, f32[16,64]{1,0:T(8,128)S(1)} %mul.136, bf16[16,64,1024]{2,1,0:T(8,128)(2,1)S(1)} %bitcast.70, bf16[1024,2048]{1,0:T(8,128)(2,1)} %all-gather.2.cloned.1.call-done), kind=kOutput, calls=%fused_computation.5 | convolution fusion | flops 2149580800 | bytes 8458240 | tf_op jit(solution)/shard_map/dot_general | solution.py:88
  147.6 1.9 copy-done
  149.5 0.2 slice.116
  149.6 4.7 %collective-permute-start.3 = (bf16[1024,512]{1,0:T(8,128)(2,1)S(1)}, bf16[1024,512]{1,0:T(8,128)(2,1)S(1)}, u32[]{:S(2)}, u32[]{:S(2)}) collective-permute-start(bf16[1024,512]{1,0:T(8,128)(2,1)S(1)} %slice.116), channel_id=1, source_target_pairs={{0,1},{1,0},{2,3},{3,2},{4,5},{5,4},{6,7},{7,6},{8,9},{9,8},{10,11... | collective-permute-start | bytes 3145736 | tf_op jit(solution)/shard_map/ppermute | solution.py:16
  154.4 0.6 broadcast_in_dim.12
  155.0 3.8 %all-to-all-start.4 = ((bf16[8,16,128]{2,1,0:T(8,128)(2,1)}), bf16[8,16,128]{2,1,0:T(8,128)(2,1)S(1)}, u32[]{:S(2)}, u32[]{:S(2)}) async-start(bf16[8,16,128]{2,1,0:T(8,128)(2,1)} %broadcast_in_dim.12), calls=%async_computation.4 | async-start | bytes 65536 | tf_op jit(solution)/shard_map/all_to_all | solution.py:20
  158.9 6.8 %all-to-all-done.4 = bf16[8,16,128]{2,1,0:T(8,128)(2,1)S(1)} async-done(((bf16[8,16,128]{2,1,0:T(8,128)(2,1)}), bf16[8,16,128]{2,1,0:T(8,128)(2,1)S(1)}, u32[]{:S(2)}, u32[]{:S(2)}) %all-to-all-start.4) | async-done | bytes 32800 | tf_op jit(solution)/shard_map/all_to_all | solution.py:20
  165.7 0.1 copy.32
  165.8 0.0 collective-permute-done.3
  165.8 2.9 %fusion.3 = bf16[1024,512]{1,0:T(8,128)(2,1)} fusion(f32[1024,1024]{1,0:T(8,128)} %bitcast.78, bf16[1024,512]{1,0:T(8,128)(2,1)S(1)} %collective-permute-done.3), kind=kLoop, calls=%fused_computation.10 | loop fusion | flops 1572864 | bytes 4194304 | tf_op jit(solution)/shard_map/convert_element_type | solution.py:92
  168.7 6.5 %all-to-all-start.3 = ((bf16[8,128,512]{2,1,0:T(8,128)(2,1)}), bf16[8,128,512]{2,1,0:T(8,128)(2,1)S(1)}, u32[]{:S(2)}, u32[]{:S(2)}) async-start(bf16[8,128,512]{2,1,0:T(8,128)(2,1)} %bitcast.16), calls=%async_computation.3 | async-start | bytes 2097152 | tf_op jit(solution)/shard_map/all_to_all | solution.py:93
  175.2 0.3 fusion.22
  175.5 0.2 fusion.18
  175.7 1.5 convolution_bitcast_fusion
  177.2 1.0 copy.29
  178.2 0.3 fusion.20
  178.5 1.2 fusion.50
  179.7 1.4 fusion.16
  181.1 23.2 %all-to-all-done.3 = bf16[8,128,512]{2,1,0:T(8,128)(2,1)S(1)} async-done(((bf16[8,128,512]{2,1,0:T(8,128)(2,1)}), bf16[8,128,512]{2,1,0:T(8,128)(2,1)S(1)}, u32[]{:S(2)}, u32[]{:S(2)}) %all-to-all-start.3) | async-done | bytes 1048608 | tf_op jit(solution)/shard_map/all_to_all | solution.py:93
  204.4 0.8 reduce_sum.42
  (29 shorter events, 0.2 us)
Async XLA Ops:
  7.2 13.2 %copy-start.7 = (s32[2]{0:T(128)S(1)}, s32[2]{0:T(128)}, u32[]{:S(2)}) copy-start(s32[2]{0:T(128)} %param.15) | copy-start | bytes 28
  7.2 13.3 %copy-start.6 = (s32[2,4]{1,0:T(2,128)S(1)}, s32[2,4]{1,0:T(2,128)}, u32[]{:S(2)}) copy-start(s32[2,4]{1,0:T(2,128)} %param.14) | copy-start | bytes 100
  7.2 13.3 %copy-start.2 = (bf16[128,512]{1,0:T(8,128)(2,1)S(1)}, bf16[128,512]{1,0:T(8,128)(2,1)}, u32[]{:S(2)}) copy-start(bf16[128,512]{1,0:T(8,128)(2,1)} %param.8) | copy-start | bytes 393220
  7.2 13.4 %copy-start.5 = (f32[512]{0:T(512)S(1)}, f32[512]{0:T(512)}, u32[]{:S(2)}) copy-start(f32[512]{0:T(512)} %param.9) | copy-start | bytes 6148
  7.2 70.6 %all-gather.2.cloned.1.call-start = ((), (), s32[]{:S(2)}) async-start(), calls=%async_computation.5 | async-start | bytes 4718592 | tf_op jit(solution)/shard_map/all_gather | solution.py:46
  9.3 18.4 %copy-start.3 = (f32[64,4096]{1,0:T(8,128)S(1)}, f32[64,4096]{1,0:T(8,128)}, u32[]{:S(2)}) copy-start(f32[64,4096]{1,0:T(8,128)} %param.13) | copy-start | bytes 3145732
  9.4 10.1 %collective-permute-start.1 = (bf16[128,1024]{1,0:T(8,128)(2,1)S(1)}, bf16[128,1024]{1,0:T(8,128)(2,1)S(1)}, u32[]{:S(2)}, u32[]{:S(2)}) collective-permute-start(bf16[128,1024]{1,0:T(8,128)(2,1)S(1)} %pad_maximum_fusion.1), channel_id=1, source_target_pairs={{0,1},{1,0},{2,3},{3,2},{4,5},{5,4},{6,7},{7,6},{8,9},{9,8},{10,11... | collective-permute-start | bytes 786440 | tf_op jit(solution)/shard_map/ppermute | solution.py:16
  21.8 33.2 %all-to-all-start = ((bf16[8,144,512]{2,1,0:T(8,128)(2,1)}), bf16[8,144,512]{2,1,0:T(8,128)(2,1)S(1)}, u32[]{:S(2)}, u32[]{:S(2)}) async-start(bf16[8,144,512]{2,1,0:T(8,128)(2,1)} %broadcast_in_dim.10), calls=%async_computation | async-start | bytes 2359296 | tf_op jit(solution)/shard_map/all_to_all | solution.py:20
  25.4 36.1 %collective-permute-start.2 = (f32[64,512]{1,0:T(8,128)}, f32[64,512]{1,0:T(8,128)}, u32[]{:S(2)}, u32[]{:S(2)}) collective-permute-start(f32[64,512]{1,0:T(8,128)} %param.12), channel_id=1, source_target_pairs={{0,1},{1,0},{2,3},{3,2},{4,5},{5,4},{6,7},{7,6},{8,9},{9,8},{10,11... | collective-permute-start | bytes 393224 | tf_op jit(solution)/shard_map/ppermute | solution.py:16
  55.1 8.0 %collective-permute-start = (bf16[1024,512]{1,0:T(8,128)(2,1)S(1)}, bf16[1024,512]{1,0:T(8,128)(2,1)S(1)}, u32[]{:S(2)}, u32[]{:S(2)}) collective-permute-start(bf16[1024,512]{1,0:T(8,128)(2,1)S(1)} %bitcast.72), channel_id=1, source_target_pairs={{0,1},{1,0},{2,3},{3,2},{4,5},{5,4},{6,7},{7,6},{8,9},{9,8},{10,11... | collective-permute-start | bytes 3145736 | tf_op jit(solution)/shard_map/ppermute | solution.py:16
  62.4 0.7 copy-start.1
  63.2 1.0 copy-start.4
  114.3 28.1 %all-to-all-start.2 = ((bf16[4,256,1024]{2,1,0:T(8,128)(2,1)}), bf16[4,256,1024]{2,1,0:T(8,128)(2,1)S(1)}, u32[]{:S(2)}, u32[]{:S(2)}) async-start(bf16[4,256,1024]{2,1,0:T(8,128)(2,1)} %broadcast_in_dim.11), calls=%async_computation.2 | async-start | bytes 4194304 | tf_op jit(solution)/shard_map/all_to_all | solution.py:20
  147.5 1.9 copy-start
  149.6 16.1 %collective-permute-start.3 = (bf16[1024,512]{1,0:T(8,128)(2,1)S(1)}, bf16[1024,512]{1,0:T(8,128)(2,1)S(1)}, u32[]{:S(2)}, u32[]{:S(2)}) collective-permute-start(bf16[1024,512]{1,0:T(8,128)(2,1)S(1)} %slice.116), channel_id=1, source_target_pairs={{0,1},{1,0},{2,3},{3,2},{4,5},{5,4},{6,7},{7,6},{8,9},{9,8},{10,11... | collective-permute-start | bytes 3145736 | tf_op jit(solution)/shard_map/ppermute | solution.py:16
  155.0 10.7 %all-to-all-start.4 = ((bf16[8,16,128]{2,1,0:T(8,128)(2,1)}), bf16[8,16,128]{2,1,0:T(8,128)(2,1)S(1)}, u32[]{:S(2)}, u32[]{:S(2)}) async-start(bf16[8,16,128]{2,1,0:T(8,128)(2,1)} %broadcast_in_dim.12), calls=%async_computation.4 | async-start | bytes 65536 | tf_op jit(solution)/shard_map/all_to_all | solution.py:20
  168.7 35.7 %all-to-all-start.3 = ((bf16[8,128,512]{2,1,0:T(8,128)(2,1)}), bf16[8,128,512]{2,1,0:T(8,128)(2,1)S(1)}, u32[]{:S(2)}, u32[]{:S(2)}) async-start(bf16[8,128,512]{2,1,0:T(8,128)(2,1)} %bitcast.16), calls=%async_computation.3 | async-start | bytes 2097152 | tf_op jit(solution)/shard_map/all_to_all | solution.py:93
Sparse Core Ops, SparseCore 0:
  20.5 57.2 all-gather.1

commit v2 on v1

v2 whole, which is shorter than its diff:
```python
import functools

import jax
import jax.numpy as jnp
from jax import lax
from jax.experimental import pallas as pl
from jax.experimental.pallas import tpu as pltpu
from jax.sharding import Mesh
from jax.sharding import PartitionSpec as P

D = 4096
FF = 16384
BATCH = 64
MEMBERS = 128
NY = 8
NX = 4
Y = ("y_hi", "y_lo")
HIGH = lax.Precision.HIGHEST
SIGMA_K = 0.5 / D**0.5
SIGMA_V = 0.5 / FF**0.5
VMEM = pl.BlockSpec(memory_space=pltpu.VMEM)
SMEM = pl.BlockSpec(memory_space=pltpu.SMEM)


def swap(x):
    return lax.ppermute(x, "core", [(0, 1), (1, 0)])


def turn(x, by):
    return lax.ppermute(x, "x", [(i, (i + by) % NX) for i in range(NX)])


def to_all(x, axis, n):
    return lax.all_to_all(jnp.broadcast_to(x[None], (n, *x.shape)), axis, 0, 0)


def one_hot(index, n):
    return (index[:, None] == lax.iota(jnp.int32, n)[None, :]).astype(jnp.float32)


def key_kernel(chunk, x_ref, info_ref, mine_ref, got_ref, w_ref, bank_ref, hid_ref, *rest):
    outs, rows_ref = rest[:NX], rest[NX]
    feat = mine_ref.shape[2]
    inner, picks = [], []
    for s in range(NX):
        for k in range(NY // NX):
            y = lax.rem(x_ref[0] + s, NX) * (NY // NX) + k
            at = (s * (NY // NX) + k) * BATCH
            rows_ref[at : at + BATCH, :feat] = mine_ref[y, chunk * BATCH : (chunk + 1) * BATCH, :]
            rows_ref[at : at + BATCH, feat:] = got_ref[y, chunk * BATCH : (chunk + 1) * BATCH, :]
            member = y * 2 + chunk
            fac_a = bank_ref[pl.ds(info_ref[member, 0], 1), :]
            rows = rows_ref[at : at + BATCH, :].astype(jnp.float32)
            inner.append(SIGMA_K * jnp.sum(rows * fac_a, axis=1, keepdims=True))
            picks.append(info_ref[member, 1])
    rows = rows_ref[...]
    wide = 2 * w_ref.shape[2]
    for n in range(w_ref.shape[0] // 2):
        cols = slice(n * wide, (n + 1) * wide)
        w = jnp.concatenate([w_ref[2 * n], w_ref[2 * n + 1]], axis=1)
        acc = jnp.dot(rows, w, preferred_element_type=jnp.float32)
        for j in range(NY):
            fac_b = hid_ref[pl.ds(picks[j], 1), cols]
            term = acc[j * BATCH : (j + 1) * BATCH] + inner[j] * fac_b
            s, k = divmod(j, NY // NX)
            outs[s][k * BATCH : (k + 1) * BATCH, cols] = term.astype(jnp.bfloat16)


def out_kernel(chunk, half, x_ref, info_ref, *rest):
    keys, (v_ref, bank_ref, hid_ref, out_ref) = rest[:NX], rest[NX:]
    feat = out_ref.shape[2]
    cols = slice(half * feat, (half + 1) * feat)
    rows = jnp.concatenate([k[...] for k in keys], axis=0)
    v = v_ref[:, cols]
    acc = jnp.dot(rows, v, preferred_element_type=jnp.float32)
    for s in range(NX):
        for k in range(NY // NX):
            y = lax.rem(x_ref[0] + (NX - s), NX) * (NY // NX) + k
            member = y * 2 + chunk
            at = (s * (NY // NX) + k) * BATCH
            fac_c = hid_ref[pl.ds(info_ref[member, 2], 1), :]
            fac_d = bank_ref[pl.ds(info_ref[member, 3], 1), cols]
            own = keys[s][k * BATCH : (k + 1) * BATCH, :].astype(jnp.float32)
            inner = SIGMA_V * jnp.sum(own * fac_c, axis=1, keepdims=True)
            out_ref[y] = (acc[at : at + BATCH] + inner * fac_d).astype(out_ref.dtype)


def cost(rows, depth, cols):
    return pl.CostEstimate(
        flops=2 * rows * depth * cols,
        bytes_accessed=2 * (rows * depth + depth * cols + rows * cols),
        transcendentals=0,
    )


def key_part(chunk, x, info, mine, got, w, banks, hidden):
    rows, deep, wide = NY * BATCH, 2 * mine.shape[2], w.shape[0] * w.shape[2]
    out = jax.ShapeDtypeStruct((rows // NX, wide), jnp.bfloat16)
    return pl.pallas_call(
        functools.partial(key_kernel, chunk),
        out_shape=[out] * NX,
        in_specs=[SMEM, SMEM] + [VMEM] * 5,
        out_specs=[VMEM] * NX,
        scratch_shapes=[pltpu.VMEM((rows, deep), jnp.bfloat16)],
        compiler_params=pltpu.CompilerParams(vmem_limit_bytes=24 << 20),
        cost_estimate=cost(rows, deep, wide),
        name="key_part",
    )(x, info, mine, got, w, banks, hidden)


def out_part(chunk, half, dtype, x, info, keys, v, banks, hidden):
    rows, deep, feat = NY * BATCH, v.shape[0], v.shape[1] // 2
    return pl.pallas_call(
        functools.partial(out_kernel, chunk, half),
        out_shape=jax.ShapeDtypeStruct((NY, BATCH, feat), dtype),
        in_specs=[SMEM, SMEM] + [VMEM] * (NX + 3),
        out_specs=VMEM,
        compiler_params=pltpu.CompilerParams(vmem_limit_bytes=24 << 20),
        cost_estimate=cost(rows, deep, feat),
        name="out_part",
    )(x, info, *keys, v, banks, hidden)


def shards(inputs, mix, key_weight, value_weight, dim_bank, hidden_bank, member_picks, ranks):
    bank = dim_bank.shape[0]
    tok, feat = inputs.shape
    hid = key_weight.shape[1]
    half = hid // 2
    own = tok // BATCH
    core = lax.axis_index("core")
    y_hi = lax.axis_index("y_hi")
    z = lax.axis_index("z")
    x = lax.axis_index("x").reshape(1)

    def hidden_half(array, axis):
        return lax.dynamic_slice_in_dim(array, core * half, half, axis)

    key_pack = jnp.concatenate(
        [hidden_half(key_weight, 1), hidden_half(swap(key_weight), 1)], axis=0
    )
    key_all = lax.all_gather(key_pack, "z", axis=0)
    value_pack = jnp.concatenate(
        [hidden_half(value_weight, 0), hidden_half(swap(value_weight), 0)], axis=1
    )
    value_all = lax.all_gather(value_pack, "z", axis=0, tiled=True)

    values = inputs.astype(jnp.float32).reshape(own, BATCH, feat)
    previous = jnp.concatenate([jnp.zeros((own, 1, feat), jnp.float32), values[:, :-1, :]], axis=1)
    shifted = (values + (previous - values) * mix).reshape(tok, feat).astype(jnp.bfloat16)
    info = jnp.concatenate([member_picks, ranks[:, None]], axis=1).astype(jnp.bfloat16)
    info = jnp.pad(info, ((0, 16 - own), (0, feat - info.shape[1])))
    mine = to_all(jnp.concatenate([shifted, info], axis=0), Y, NY)
    got = swap(mine)
    members = NY * own
    info = mine[:, tok : tok + own, :128].reshape(members, 128)
    everyone = to_all(info, "z", 8).reshape(8 * members, 128)[:, :5].astype(jnp.int32)
    info = info[:, :4].astype(jnp.int32)

    banks = jnp.concatenate([dim_bank, swap(dim_bank)], axis=1)
    hidden = hidden_bank.reshape(bank, 8, 2, 2, half)
    hidden = lax.dynamic_index_in_dim(hidden, y_hi, 2, keepdims=False)
    hidden_own = lax.dynamic_index_in_dim(hidden, z, 1, keepdims=False).reshape(bank, hid)
    hidden = lax.dynamic_index_in_dim(hidden, core, 2, keepdims=False).reshape(bank, 8 * half)
    got, everyone = lax.optimization_barrier((got, everyone))

    parts = [key_part(c, x, info, mine, got, key_all, banks, hidden) for c in range(own)]
    sums = [[p[0]] + [turn(p[s], s) for s in (1, 3, 2)] for p in parts]
    keys = []
    for terms in sums:
        key_pre = sum(t.astype(jnp.float32) for t in terms)
        keys.append((jnp.maximum(key_pre, 0.0) ** 2).astype(jnp.bfloat16))
    keys = [[k] + [turn(k, s) for s in (1, 2, 3)] for k in keys]

    outputs = []
    for c in range(own):
        rest = out_part(c, 1, jnp.bfloat16, x, info, keys[c], value_all, banks, hidden)
        base = out_part(c, 0, jnp.float32, x, info, keys[c], value_all, banks, hidden)
        result = (base + swap(rest).astype(jnp.float32)).astype(jnp.bfloat16)
        pieces = lax.all_to_all(result, Y, 0, 0)
        outputs.append(jnp.sum(pieces.astype(jnp.float32), axis=0).astype(jnp.bfloat16))
    outputs = jnp.concatenate(outputs, axis=0)

    fitness = 2.0 * everyone[:, 4].astype(jnp.float32) / (MEMBERS - 1) - 1.0
    fitness = fitness * (1.0 / MEMBERS**0.5)
    pick = [one_hot(everyone[:, i], bank) for i in range(4)]
    pair_k = jnp.dot((fitness[:, None] * pick[0]).T, pick[1], precision=HIGH)
    pair_v = jnp.dot((fitness[:, None] * pick[2]).T, pick[3], precision=HIGH)
    key_step = jnp.dot(dim_bank.T, jnp.dot(pair_k, hidden_own, precision=HIGH), precision=HIGH)
    value_step = jnp.dot(hidden_own.T, jnp.dot(pair_v, dim_bank, precision=HIGH), precision=HIGH)
    return outputs, key_step, value_step


def solution(mesh):
    fine = Mesh(mesh.devices.reshape(8, 2, 4, 4, 2), ("z", "y_hi", "y_lo", "x", "core"))
    pop, row, col = ("z", "y_hi"), ("y_lo",), ("x", "core")
    in_specs = (
        P(pop + row, col),
        P(col),
        P(col, row + pop),
        P(row + pop, col),
        P(None, col),
        P(None, row),
        P(pop + row, None),
        P(pop + row),
    )
    out_specs = (P(pop + row, col), P(col, row + pop), P(row + pop, col))
    return jax.shard_map(shards, mesh=fine, in_specs=in_specs, out_specs=out_specs, check_vma=False)
```

time: 213 us -> 215 us (level)
  starting transfers between devices: 38.1 us -> 85 us
  blocking collectives: 29.2 us -> 0 us
  waiting for transfers between devices: 93.6 us -> 73.3 us
  Pallas kernels: 0 us -> 12.6 us
  matrix products: 15 us -> 5.18 us
    ppermute x0 -> x12, starting transfers between devices: none -> 38.9 us  [turn(): return lax.ppermute(x, 'x', [(i, (i + by) % NX) for i in range(NX)])]
    all_to_all x1 -> x0, blocking collectives: 29.2 us -> none  [shards(): parts = lax.all_to_all(part, 'x', 0, 0)]
    all_to_all x3 -> x2, waiting for transfers between devices: 56.3 us -> 32.1 us  [to_all(): return lax.all_to_all(jnp.broadcast_to(x[None], (n, *x.shape)), axis, 0, 0)]
    ppermute x0 -> x12, waiting for transfers between devices: none -> 15.5 us  [turn(): return lax.ppermute(x, 'x', [(i, (i + by) % NX) for i in range(NX)])]
    all_gather x1 -> x2, waiting for transfers between devices: 13 us -> 0.04 us  [the longest x1 0.02 us: shards(): key_all = lax.all_gather(key_pack, 'z', axis=0)]
    pallas_call x0 -> x6, Pallas kernels: none -> 12.6 us  [the longest x4 6.52 us: out_part(): pl.pallas_call(functools.partial(out_kernel, chunk, half), out_shape=jax....]
    dot_general x6 -> x0, matrix products: 10.1 us -> none  [the longest x1 4.3 us: shards(): lax.dot_general(tokens, key_all, (((1,), (1,)), ((), ())), preferred_elem...]
    ppermute x4 -> x6, starting transfers between devices: 20.6 us -> 26.6 us  [swap(): return lax.ppermute(x, 'core', [(0, 1), (1, 0)])]
  transfers between devices with their start and end apart: 9 -> 24, of which waited for: 6 -> 10; matrix products, arithmetic and copies ran while one was open for 7% -> 9% of each run, Pallas kernels for 0% -> 6%
where the time goes in v2:
time: 215 us; the launch traced here: 213 us
  starting transfers between devices  85 us (40%)
  waiting for transfers between devices  73.3 us (34%)
  between operations  14.7 us (7%)
  local copies, waits for them, and re-layouts  14.5 us (7%)
  Pallas kernels  12.6 us (6%)
  other arithmetic  8.02 us (4%)
  matrix products  5.18 us (2%)
    ppermute x12, starting transfers between devices, turn(): return lax.ppermute(x, 'x', [(i, (i + by) % NX) for i in range(NX)])  38.9 us
    all_to_all x2, waiting for transfers between devices, to_all(): return lax.all_to_all(jnp.broadcast_to(x[None], (n, *x.shape)), axis, 0, 0)  32.1 us
    ppermute x6, starting transfers between devices, swap(): return lax.ppermute(x, 'core', [(0, 1), (1, 0)])  26.6 us
    all_to_all x2, waiting for transfers between devices, shards(): pieces = lax.all_to_all(result, Y, 0, 0)  24 us
    ppermute x12, waiting for transfers between devices, turn(): return lax.ppermute(x, 'x', [(i, (i + by) % NX) for i in range(NX)])  15.5 us
    all_to_all x2, starting transfers between devices, to_all(): return lax.all_to_all(jnp.broadcast_to(x[None], (n, *x.shape)), axis, 0, 0)  11.7 us
    unnamed x60, local copies, waits for them, and re-layouts  8.42 us
    all_to_all x2, starting transfers between devices, shards(): pieces = lax.all_to_all(result, Y, 0, 0)  7.78 us
  transfers between devices with their start and end apart: 24, of which 10 were waited for; matrix products, arithmetic and copies ran while one was open for 9% of the time, Pallas kernels for 6%

profile of v2, /device:TPU:1, one launch (start us, length us, event | category | flops | bytes accessed | tf_op | source)
XLA Modules:
  0.0 213.4 jit_solution(6244000663994492768)
XLA Ops:
  7.3 8.9 %collective-permute-start.1 = (bf16[512,256]{1,0:T(8,128)(2,1)}, bf16[512,256]{1,0:T(8,128)(2,1)S(1)}, u32[]{:S(2)}, u32[]{:S(2)}) collective-permute-start(bf16[512,256]{1,0:T(8,128)(2,1)} %param.10), channel_id=1, source_target_pairs={{0,1},{1,0},{2,3},{3,2},{4,5},{5,4},{6,7},{7,6},{8,9},{9,8},{10,11... | collective-permute-start | bytes 786440 | tf_op jit(solution)/shard_map/ppermute | solution.py:26
  16.2 0.9 constant_dynamic-slice_fusion.5
  17.1 0.4 collective-permute-done.1
  17.5 0.7 pad_maximum_fusion
  18.6 1.1 broadcast_in_dim.8
  19.8 3.7 %all-to-all-start = ((bf16[8,144,512]{2,1,0:T(8,128)(2,1)}), bf16[8,144,512]{2,1,0:T(8,128)(2,1)S(1)}, u32[]{:S(2)}, u32[]{:S(2)}) async-start(bf16[8,144,512]{2,1,0:T(8,128)(2,1)} %broadcast_in_dim.8), calls=%async_computation | async-start | bytes 2359296 | tf_op jit(solution)/shard_map/all_to_all | solution.py:34
  23.6 2.4 %collective-permute-start.9 = (bf16[256,512]{1,0:T(8,128)(2,1)S(1)}, bf16[256,512]{1,0:T(8,128)(2,1)S(1)}, u32[]{:S(2)}, u32[]{:S(2)}) collective-permute-start(bf16[256,512]{1,0:T(8,128)(2,1)S(1)} %copy-done.21), channel_id=1, source_target_pairs={{0,1},{1,0},{2,3},{3,2},{4,5},{5,4},{6,7},{7,6},{8,9},{9,8},{10,11... | collective-permute-start | bytes 786440 | tf_op jit(solution)/shard_map/ppermute | solution.py:26
  26.0 1.1 collective-permute-done.9
  27.1 0.7 pad_maximum_fusion.1
  27.9 25.2 %all-to-all-done.mine_ref = bf16[8,144,512]{2,1,0:T(8,128)(2,1)S(1)} async-done(((bf16[8,144,512]{2,1,0:T(8,128)(2,1)}), bf16[8,144,512]{2,1,0:T(8,128)(2,1)S(1)}, u32[]{:S(2)}, u32[]{:S(2)}) %all-to-all-start) | async-done | bytes 1179680 | tf_op jit(solution)/shard_map/all_to_all | solution.py:34
  53.1 4.7 %collective-permute-start = (bf16[8,144,512]{2,1,0:T(8,128)(2,1)S(1)}, bf16[8,144,512]{2,1,0:T(8,128)(2,1)}, u32[]{:S(2)}, u32[]{:S(2)}) collective-permute-start(bf16[8,144,512]{2,1,0:T(8,128)(2,1)S(1)} %all-to-all-done.mine_ref), channel_id=1, source_target_pairs={{0,1},{1,0},{2,3},{3,2},{4,5},{5,4},{6,7},{7,6},{8,9},{9,8},{10,11... | collective-permute-start | bytes 3538952 | tf_op jit(solution)/shard_map/ppermute | solution.py:26
  57.9 1.9 collective-permute-start.2
  59.8 0.9 reshape.46
  61.0 0.7 copy-done.15
  61.8 0.6 broadcast_in_dim.9
  62.4 8.0 %all-to-all-start.1 = ((bf16[8,16,128]{2,1,0:T(8,128)(2,1)}), bf16[8,16,128]{2,1,0:T(8,128)(2,1)S(1)}, u32[]{:S(2)}, u32[]{:S(2)}) async-start(bf16[8,16,128]{2,1,0:T(8,128)(2,1)} %broadcast_in_dim.9), calls=%async_computation.1 | async-start | bytes 65536 | tf_op jit(solution)/shard_map/all_to_all | solution.py:34
  70.5 6.9 %all-to-all-done.1 = bf16[8,16,128]{2,1,0:T(8,128)(2,1)S(1)} async-done(((bf16[8,16,128]{2,1,0:T(8,128)(2,1)}), bf16[8,16,128]{2,1,0:T(8,128)(2,1)S(1)}, u32[]{:S(2)}, u32[]{:S(2)}) %all-to-all-start.1) | async-done | bytes 32800 | tf_op jit(solution)/shard_map/all_to_all | solution.py:34
  77.5 1.6 copy-done.2
  79.1 2.6 %key_part.3 = (bf16[128,1024]{1,0:T(8,128)(2,1)S(1)}, bf16[128,1024]{1,0:T(8,128)(2,1)S(1)}, bf16[128,1024]{1,0:T(8,128)(2,1)S(1)}, bf16[128,1024]{1,0:T(8,128)(2,1)S(1)}) custom-call(s32[1]{0:T(128)} %bitcast.x_ref, s32[16,4]{1,0:T(8,128)S(1)} %slice_convert_fusion.info_ref, bf16[8,144,512]{2,1,0:T(8,128)(2,1)S(1)} %all-to-all-done.mine_ref, ...), custom_call_target="tpu_custom_call" | custom-call | flops 1073741824 | bytes 4194304 | tf_op jit(solution)/shard_map/key_part/pallas_call | solution.py:99
  81.7 3.1 %collective-permute-start.11 = (bf16[128,1024]{1,0:T(8,128)(2,1)S(1)}, bf16[128,1024]{1,0:T(8,128)(2,1)S(1)}, u32[]{:S(2)}, u32[]{:S(2)}) collective-permute-start(bf16[128,1024]{1,0:T(8,128)(2,1)S(1)} %get-tuple-element.19), channel_id=1, source_target_pairs={{0,2},{2,4},{4,6},{6,0},{1,3},{3,5},{5,7},{7,1},{8,10},{10,12},{12... | collective-permute-start | bytes 786440 | tf_op jit(solution)/shard_map/ppermute | solution.py:30
  84.8 3.4 %collective-permute-start.12 = (bf16[128,1024]{1,0:T(8,128)(2,1)S(1)}, bf16[128,1024]{1,0:T(8,128)(2,1)S(1)}, u32[]{:S(2)}, u32[]{:S(2)}) collective-permute-start(bf16[128,1024]{1,0:T(8,128)(2,1)S(1)} %get-tuple-element.20), channel_id=1, source_target_pairs={{0,6},{2,0},{4,2},{6,4},{1,7},{3,1},{5,3},{7,5},{8,14},{10,8},{12,... | collective-permute-start | bytes 786440 | tf_op jit(solution)/shard_map/ppermute | solution.py:30
  88.2 3.4 %collective-permute-start.13 = (bf16[128,1024]{1,0:T(8,128)(2,1)S(1)}, bf16[128,1024]{1,0:T(8,128)(2,1)S(1)}, u32[]{:S(2)}, u32[]{:S(2)}) collective-permute-start(bf16[128,1024]{1,0:T(8,128)(2,1)S(1)} %get-tuple-element.21), channel_id=1, source_target_pairs={{0,4},{2,6},{4,0},{6,2},{1,5},{3,7},{5,1},{7,3},{8,12},{10,14},{12... | collective-permute-start | bytes 786440 | tf_op jit(solution)/shard_map/ppermute | solution.py:30
  91.7 0.6 collective-permute-done.12
  92.3 4.6 %collective-permute-done.13 = bf16[128,1024]{1,0:T(8,128)(2,1)S(1)} collective-permute-done((bf16[128,1024]{1,0:T(8,128)(2,1)S(1)}, bf16[128,1024]{1,0:T(8,128)(2,1)S(1)}, u32[]{:S(2)}, u32[]{:S(2)}) %collective-permute-start.13) | collective-permute-done | bytes 262176 | tf_op jit(solution)/shard_map/ppermute | solution.py:30
  97.0 6.3 %collective-permute-start.16 = (bf16[128,1024]{1,0:T(8,128)(2,1)S(1)}, bf16[128,1024]{1,0:T(8,128)(2,1)S(1)}, u32[]{:S(2)}, u32[]{:S(2)}) collective-permute-start(bf16[128,1024]{1,0:T(8,128)(2,1)S(1)} %multiply_convert_fusion.rest_0_), channel_id=1, source_target_pairs={{0,6},{2,0},{4,2},{6,4},{1,7},{3,1},{5,3},{7,5},{8,14},{10,8},{12,... | collective-permute-start | bytes 786440 | tf_op jit(solution)/shard_map/ppermute | solution.py:30
  103.3 2.5 %collective-permute-start.15 = (bf16[128,1024]{1,0:T(8,128)(2,1)S(1)}, bf16[128,1024]{1,0:T(8,128)(2,1)S(1)}, u32[]{:S(2)}, u32[]{:S(2)}) collective-permute-start(bf16[128,1024]{1,0:T(8,128)(2,1)S(1)} %multiply_convert_fusion.rest_0_), channel_id=1, source_target_pairs={{0,4},{2,6},{4,0},{6,2},{1,5},{3,7},{5,1},{7,3},{8,12},{10,14},{12... | collective-permute-start | bytes 786440 | tf_op jit(solution)/shard_map/ppermute | solution.py:30
  105.8 1.9 collective-permute-start.14
  107.8 3.4 %key_part.2 = (bf16[128,1024]{1,0:T(8,128)(2,1)S(1)}, bf16[128,1024]{1,0:T(8,128)(2,1)}, bf16[128,1024]{1,0:T(8,128)(2,1)}, bf16[128,1024]{1,0:T(8,128)(2,1)}) custom-call(s32[1]{0:T(128)} %bitcast.x_ref, s32[16,4]{1,0:T(8,128)S(1)} %slice_convert_fusion.info_ref, bf16[8,144,512]{2,1,0:T(8,128)(2,1)S(1)} %all-to-all-done.mine_ref, ...), custom_call_target="tpu_custom_call" | custom-call | flops 1073741824 | bytes 4194304 | tf_op jit(solution)/shard_map/key_part/pallas_call | solution.py:99
  111.2 0.7 copy-done.13
  111.9 4.0 %collective-permute-start.3 = (bf16[128,1024]{1,0:T(8,128)(2,1)}, bf16[128,1024]{1,0:T(8,128)(2,1)}, u32[]{:S(2)}, u32[]{:S(2)}) collective-permute-start(bf16[128,1024]{1,0:T(8,128)(2,1)} %get-tuple-element.15), channel_id=1, source_target_pairs={{0,2},{2,4},{4,6},{6,0},{1,3},{3,5},{5,7},{7,1},{8,10},{10,12},{12... | collective-permute-start | bytes 786440 | tf_op jit(solution)/shard_map/ppermute | solution.py:30
  115.9 2.5 %collective-permute-start.4 = (bf16[128,1024]{1,0:T(8,128)(2,1)}, bf16[128,1024]{1,0:T(8,128)(2,1)}, u32[]{:S(2)}, u32[]{:S(2)}) collective-permute-start(bf16[128,1024]{1,0:T(8,128)(2,1)} %get-tuple-element.16), channel_id=1, source_target_pairs={{0,6},{2,0},{4,2},{6,4},{1,7},{3,1},{5,3},{7,5},{8,14},{10,8},{12,... | collective-permute-start | bytes 786440 | tf_op jit(solution)/shard_map/ppermute | solution.py:30
  118.4 3.1 %collective-permute-start.5 = (bf16[128,1024]{1,0:T(8,128)(2,1)}, bf16[128,1024]{1,0:T(8,128)(2,1)}, u32[]{:S(2)}, u32[]{:S(2)}) collective-permute-start(bf16[128,1024]{1,0:T(8,128)(2,1)} %get-tuple-element.17), channel_id=1, source_target_pairs={{0,4},{2,6},{4,0},{6,2},{1,5},{3,7},{5,1},{7,3},{8,12},{10,14},{12... | collective-permute-start | bytes 786440 | tf_op jit(solution)/shard_map/ppermute | solution.py:30
  121.6 0.7 copy-done.5
  122.3 1.6 copy-done
  123.9 0.9 copy-done.6
  124.9 1.4 out_part.7
  126.3 6.2 %collective-permute-start.17 = (bf16[8,64,512]{2,1,0:T(8,128)(2,1)S(1)}, bf16[8,64,512]{2,1,0:T(8,128)(2,1)S(1)}, u32[]{:S(2)}, u32[]{:S(2)}) collective-permute-start(bf16[8,64,512]{2,1,0:T(8,128)(2,1)S(1)} %out_part.7), channel_id=1, source_target_pairs={{0,1},{1,0},{2,3},{3,2},{4,5},{5,4},{6,7},{7,6},{8,9},{9,8},{10,11... | collective-permute-start | bytes 1572872 | tf_op jit(solution)/shard_map/ppermute | solution.py:26
  132.5 1.3 multiply_convert_fusion.1.rest_0_
  133.8 3.9 %collective-permute-start.8 = (bf16[128,1024]{1,0:T(8,128)(2,1)S(1)}, bf16[128,1024]{1,0:T(8,128)(2,1)S(1)}, u32[]{:S(2)}, u32[]{:S(2)}) collective-permute-start(bf16[128,1024]{1,0:T(8,128)(2,1)S(1)} %multiply_convert_fusion.1.rest_0_), channel_id=1, source_target_pairs={{0,6},{2,0},{4,2},{6,4},{1,7},{3,1},{5,3},{7,5},{8,14},{10,8},{12,... | collective-permute-start | bytes 786440 | tf_op jit(solution)/shard_map/ppermute | solution.py:30
  137.7 2.9 %collective-permute-start.7 = (bf16[128,1024]{1,0:T(8,128)(2,1)S(1)}, bf16[128,1024]{1,0:T(8,128)(2,1)S(1)}, u32[]{:S(2)}, u32[]{:S(2)}) collective-permute-start(bf16[128,1024]{1,0:T(8,128)(2,1)S(1)} %multiply_convert_fusion.1.rest_0_), channel_id=1, source_target_pairs={{0,4},{2,6},{4,0},{6,2},{1,5},{3,7},{5,1},{7,3},{8,12},{10,14},{12... | collective-permute-start | bytes 786440 | tf_op jit(solution)/shard_map/ppermute | solution.py:30
  140.6 1.9 collective-permute-start.6
  142.5 1.5 constant_dynamic-slice_fusion
  144.0 0.6 slice_bitcast_fusion.1
  144.6 3.4 %collective-permute-done.7.rest_2_ = bf16[128,1024]{1,0:T(8,128)(2,1)S(1)} collective-permute-done((bf16[128,1024]{1,0:T(8,128)(2,1)S(1)}, bf16[128,1024]{1,0:T(8,128)(2,1)S(1)}, u32[]{:S(2)}, u32[]{:S(2)}) %collective-permute-start.7) | collective-permute-done | bytes 262176 | tf_op jit(solution)/shard_map/ppermute | solution.py:30
  148.0 6.9 %collective-permute-done.6.rest_1_ = bf16[128,1024]{1,0:T(8,128)(2,1)S(1)} collective-permute-done((bf16[128,1024]{1,0:T(8,128)(2,1)S(1)}, bf16[128,1024]{1,0:T(8,128)(2,1)S(1)}, u32[]{:S(2)}, u32[]{:S(2)}) %collective-permute-start.6) | collective-permute-done | bytes 262176 | tf_op jit(solution)/shard_map/ppermute | solution.py:30
  154.9 2.2 %out_part.5 = bf16[8,64,512]{2,1,0:T(8,128)(2,1)} custom-call(s32[1]{0:T(128)} %bitcast.x_ref, s32[16,4]{1,0:T(8,128)S(1)} %slice_convert_fusion.info_ref, bf16[128,1024]{1,0:T(8,128)(2,1)S(1)} %multiply_convert_fusion.1.rest_0_, bf16[128,1024]{1,0:T(8,128)(2,1)S(1)} %collective-permute-done.6.rest_1_, bf16[128,1024]{1,0:T(8,128)(2,1)S(1)} %collective-permute-done.7.rest_2_, ...), custom_call_target="tpu_custom_call" | custom-call | flops 536870912 | bytes 2621440 | tf_op jit(solution)/shard_map/out_part/pallas_call | solution.py:113
  157.2 2.4 %collective-permute-start.10 = (bf16[8,64,512]{2,1,0:T(8,128)(2,1)}, bf16[8,64,512]{2,1,0:T(8,128)(2,1)}, u32[]{:S(2)}, u32[]{:S(2)}) collective-permute-start(bf16[8,64,512]{2,1,0:T(8,128)(2,1)} %out_part.5), channel_id=1, source_target_pairs={{0,1},{1,0},{2,3},{3,2},{4,5},{5,4},{6,7},{7,6},{8,9},{9,8},{10,11... | collective-permute-start | bytes 1572872 | tf_op jit(solution)/shard_map/ppermute | solution.py:26
  159.6 1.4 out_part.6
  161.1 1.0 add_convert_fusion
  162.0 4.3 %all-to-all-start.3 = ((bf16[8,64,512]{2,1,0:T(8,128)(2,1)}), bf16[8,64,512]{2,1,0:T(8,128)(2,1)}, u32[]{:S(2)}, u32[]{:S(2)}) async-start(bf16[8,64,512]{2,1,0:T(8,128)(2,1)} %add_convert_fusion), calls=%async_computation.3 | async-start | bytes 1048576 | tf_op jit(solution)/shard_map/all_to_all | solution.py:179
  166.4 0.9 fusion.6
  167.3 1.7 fusion.2
  169.0 0.9 copy-done.12
  169.9 1.4 out_part.4
  171.4 2.1 add_convert_fusion.1
  173.5 10.9 %all-to-all-done.3 = bf16[8,64,512]{2,1,0:T(8,128)(2,1)} async-done(((bf16[8,64,512]{2,1,0:T(8,128)(2,1)}), bf16[8,64,512]{2,1,0:T(8,128)(2,1)}, u32[]{:S(2)}, u32[]{:S(2)}) %all-to-all-start.3) | async-done | bytes 524320 | tf_op jit(solution)/shard_map/all_to_all | solution.py:179
  184.4 3.5 %all-to-all-start.2 = ((bf16[8,64,512]{2,1,0:T(8,128)(2,1)}), bf16[8,64,512]{2,1,0:T(8,128)(2,1)S(1)}, u32[]{:S(2)}, u32[]{:S(2)}) async-start(bf16[8,64,512]{2,1,0:T(8,128)(2,1)} %add_convert_fusion.1), calls=%async_computation.2 | async-start | bytes 1048576 | tf_op jit(solution)/shard_map/all_to_all | solution.py:179
  187.9 0.6 convolution_bitcast_fusion
  188.5 1.0 copy.24
  189.5 0.3 fusion.4
  190.1 1.4 fusion
  191.5 1.1 reduce_sum.25
  192.7 13.1 %all-to-all-done.2 = bf16[8,64,512]{2,1,0:T(8,128)(2,1)S(1)} async-done(((bf16[8,64,512]{2,1,0:T(8,128)(2,1)}), bf16[8,64,512]{2,1,0:T(8,128)(2,1)S(1)}, u32[]{:S(2)}, u32[]{:S(2)}) %all-to-all-start.2) | async-done | bytes 524320 | tf_op jit(solution)/shard_map/all_to_all | solution.py:179
  205.8 0.7 pad_maximum_fusion.3
  (89 shorter events, 1.6 us)
Async XLA Ops:
  7.2 11.1 %copy-start.24 = (s32[2,4]{1,0:T(2,128)S(1)}, s32[2,4]{1,0:T(2,128)}, u32[]{:S(2)}) copy-start(s32[2,4]{1,0:T(2,128)} %param.14) | copy-start | bytes 100
  7.2 11.1 %copy-start.25 = (s32[2]{0:T(128)S(1)}, s32[2]{0:T(128)}, u32[]{:S(2)}) copy-start(s32[2]{0:T(128)} %param.15) | copy-start | bytes 28
  7.2 11.3 %copy-start.16 = (bf16[128,512]{1,0:T(8,128)(2,1)S(1)}, bf16[128,512]{1,0:T(8,128)(2,1)}, u32[]{:S(2)}) copy-start(bf16[128,512]{1,0:T(8,128)(2,1)} %param.8) | copy-start | bytes 393220
  7.2 11.3 %copy-start.22 = (f32[512]{0:T(512)S(1)}, f32[512]{0:T(512)}, u32[]{:S(2)}) copy-start(f32[512]{0:T(512)} %param.9) | copy-start | bytes 6148
  7.2 70.3 %all-gather.6.cloned.1.call-start = ((), (), s32[]{:S(2)}) async-start(), calls=%async_computation.5 | async-start | bytes 2359296 | tf_op jit(solution)/shard_map/all_gather | solution.py:141
  7.3 10.3 %collective-permute-start.1 = (bf16[512,256]{1,0:T(8,128)(2,1)}, bf16[512,256]{1,0:T(8,128)(2,1)S(1)}, u32[]{:S(2)}, u32[]{:S(2)}) collective-permute-start(bf16[512,256]{1,0:T(8,128)(2,1)} %param.10), channel_id=1, source_target_pairs={{0,1},{1,0},{2,3},{3,2},{4,5},{5,4},{6,7},{7,6},{8,9},{9,8},{10,11... | collective-permute-start | bytes 786440 | tf_op jit(solution)/shard_map/ppermute | solution.py:26
  19.8 3.8 %copy-start.21 = (bf16[256,512]{1,0:T(8,128)(2,1)S(1)}, bf16[256,512]{1,0:T(8,128)(2,1)}, u32[]{:S(2)}) copy-start(bf16[256,512]{1,0:T(8,128)(2,1)} %param.11) | copy-start | bytes 786436
  19.8 33.4 %all-to-all-start = ((bf16[8,144,512]{2,1,0:T(8,128)(2,1)}), bf16[8,144,512]{2,1,0:T(8,128)(2,1)S(1)}, u32[]{:S(2)}, u32[]{:S(2)}) async-start(bf16[8,144,512]{2,1,0:T(8,128)(2,1)} %broadcast_in_dim.8), calls=%async_computation | async-start | bytes 2359296 | tf_op jit(solution)/shard_map/all_to_all | solution.py:34
  23.5 34.4 %copy-start.17 = (f32[64,512]{1,0:T(8,128)S(1)}, f32[64,512]{1,0:T(8,128)}, u32[]{:S(2)}) copy-start(f32[64,512]{1,0:T(8,128)} %param.12) | copy-start | bytes 393220
  23.5 36.3 %copy-start.18 = (f32[64,4096]{1,0:T(8,128)S(1)}, f32[64,4096]{1,0:T(8,128)}, u32[]{:S(2)}) copy-start(f32[64,4096]{1,0:T(8,128)} %param.13) | copy-start | bytes 3145732
  23.5 98.0 %all-gather.4.cloned.1.call-start = ((), (), s32[]{:S(2)}) async-start(), calls=%async_computation.4 | async-start | bytes 2359296 | tf_op jit(solution)/shard_map/all_gather | solution.py:145
  23.6 3.6 %collective-permute-start.9 = (bf16[256,512]{1,0:T(8,128)(2,1)S(1)}, bf16[256,512]{1,0:T(8,128)(2,1)S(1)}, u32[]{:S(2)}, u32[]{:S(2)}) collective-permute-start(bf16[256,512]{1,0:T(8,128)(2,1)S(1)} %copy-done.21), channel_id=1, source_target_pairs={{0,1},{1,0},{2,3},{3,2},{4,5},{5,4},{6,7},{7,6},{8,9},{9,8},{10,11... | collective-permute-start | bytes 786440 | tf_op jit(solution)/shard_map/ppermute | solution.py:26
  53.1 24.3 %collective-permute-start = (bf16[8,144,512]{2,1,0:T(8,128)(2,1)S(1)}, bf16[8,144,512]{2,1,0:T(8,128)(2,1)}, u32[]{:S(2)}, u32[]{:S(2)}) collective-permute-start(bf16[8,144,512]{2,1,0:T(8,128)(2,1)S(1)} %all-to-all-done.mine_ref), channel_id=1, source_target_pairs={{0,1},{1,0},{2,3},{3,2},{4,5},{5,4},{6,7},{7,6},{8,9},{9,8},{10,11... | collective-permute-start | bytes 3538952 | tf_op jit(solution)/shard_map/ppermute | solution.py:26
  57.9 3.9 %collective-permute-start.2 = (f32[64,512]{1,0:T(8,128)S(1)}, f32[64,512]{1,0:T(8,128)S(1)}, u32[]{:S(2)}, u32[]{:S(2)}) collective-permute-start(f32[64,512]{1,0:T(8,128)S(1)} %copy-done.17), channel_id=1, source_target_pairs={{0,1},{1,0},{2,3},{3,2},{4,5},{5,4},{6,7},{7,6},{8,9},{9,8},{10,11... | collective-permute-start | bytes 393224 | tf_op jit(solution)/shard_map/ppermute | solution.py:26
  60.7 1.0 copy-start.15
  62.4 14.9 %all-to-all-start.1 = ((bf16[8,16,128]{2,1,0:T(8,128)(2,1)}), bf16[8,16,128]{2,1,0:T(8,128)(2,1)S(1)}, u32[]{:S(2)}, u32[]{:S(2)}) async-start(bf16[8,16,128]{2,1,0:T(8,128)(2,1)} %broadcast_in_dim.9), calls=%async_computation.1 | async-start | bytes 65536 | tf_op jit(solution)/shard_map/all_to_all | solution.py:34
  77.5 1.6 copy-start.2
  81.7 10.0 %collective-permute-start.11 = (bf16[128,1024]{1,0:T(8,128)(2,1)S(1)}, bf16[128,1024]{1,0:T(8,128)(2,1)S(1)}, u32[]{:S(2)}, u32[]{:S(2)}) collective-permute-start(bf16[128,1024]{1,0:T(8,128)(2,1)S(1)} %get-tuple-element.19), channel_id=1, source_target_pairs={{0,2},{2,4},{4,6},{6,0},{1,3},{3,5},{5,7},{7,1},{8,10},{10,12},{12... | collective-permute-start | bytes 786440 | tf_op jit(solution)/shard_map/ppermute | solution.py:30
  84.8 7.5 %collective-permute-start.12 = (bf16[128,1024]{1,0:T(8,128)(2,1)S(1)}, bf16[128,1024]{1,0:T(8,128)(2,1)S(1)}, u32[]{:S(2)}, u32[]{:S(2)}) collective-permute-start(bf16[128,1024]{1,0:T(8,128)(2,1)S(1)} %get-tuple-element.20), channel_id=1, source_target_pairs={{0,6},{2,0},{4,2},{6,4},{1,7},{3,1},{5,3},{7,5},{8,14},{10,8},{12,... | collective-permute-start | bytes 786440 | tf_op jit(solution)/shard_map/ppermute | solution.py:30
  88.2 8.7 %collective-permute-start.13 = (bf16[128,1024]{1,0:T(8,128)(2,1)S(1)}, bf16[128,1024]{1,0:T(8,128)(2,1)S(1)}, u32[]{:S(2)}, u32[]{:S(2)}) collective-permute-start(bf16[128,1024]{1,0:T(8,128)(2,1)S(1)} %get-tuple-element.21), channel_id=1, source_target_pairs={{0,4},{2,6},{4,0},{6,2},{1,5},{3,7},{5,1},{7,3},{8,12},{10,14},{12... | collective-permute-start | bytes 786440 | tf_op jit(solution)/shard_map/ppermute | solution.py:30
  97.0 21.4 %collective-permute-start.16 = (bf16[128,1024]{1,0:T(8,128)(2,1)S(1)}, bf16[128,1024]{1,0:T(8,128)(2,1)S(1)}, u32[]{:S(2)}, u32[]{:S(2)}) collective-permute-start(bf16[128,1024]{1,0:T(8,128)(2,1)S(1)} %multiply_convert_fusion.rest_0_), channel_id=1, source_target_pairs={{0,6},{2,0},{4,2},{6,4},{1,7},{3,1},{5,3},{7,5},{8,14},{10,8},{12,... | collective-permute-start | bytes 786440 | tf_op jit(solution)/shard_map/ppermute | solution.py:30
  103.3 18.2 %collective-permute-start.15 = (bf16[128,1024]{1,0:T(8,128)(2,1)S(1)}, bf16[128,1024]{1,0:T(8,128)(2,1)S(1)}, u32[]{:S(2)}, u32[]{:S(2)}) collective-permute-start(bf16[128,1024]{1,0:T(8,128)(2,1)S(1)} %multiply_convert_fusion.rest_0_), channel_id=1, source_target_pairs={{0,4},{2,6},{4,0},{6,2},{1,5},{3,7},{5,1},{7,3},{8,12},{10,14},{12... | collective-permute-start | bytes 786440 | tf_op jit(solution)/shard_map/ppermute | solution.py:30
  105.8 15.7 %collective-permute-start.14 = (bf16[128,1024]{1,0:T(8,128)(2,1)S(1)}, bf16[128,1024]{1,0:T(8,128)(2,1)S(1)}, u32[]{:S(2)}, u32[]{:S(2)}) collective-permute-start(bf16[128,1024]{1,0:T(8,128)(2,1)S(1)} %multiply_convert_fusion.rest_0_), channel_id=1, source_target_pairs={{0,2},{2,4},{4,6},{6,0},{1,3},{3,5},{5,7},{7,1},{8,10},{10,12},{12... | collective-permute-start | bytes 786440 | tf_op jit(solution)/shard_map/ppermute | solution.py:30
  111.2 0.7 copy-start.13
  111.9 20.6 %collective-permute-start.3 = (bf16[128,1024]{1,0:T(8,128)(2,1)}, bf16[128,1024]{1,0:T(8,128)(2,1)}, u32[]{:S(2)}, u32[]{:S(2)}) collective-permute-start(bf16[128,1024]{1,0:T(8,128)(2,1)} %get-tuple-element.15), channel_id=1, source_target_pairs={{0,2},{2,4},{4,6},{6,0},{1,3},{3,5},{5,7},{7,1},{8,10},{10,12},{12... | collective-permute-start | bytes 786440 | tf_op jit(solution)/shard_map/ppermute | solution.py:30
  115.9 16.6 %collective-permute-start.4 = (bf16[128,1024]{1,0:T(8,128)(2,1)}, bf16[128,1024]{1,0:T(8,128)(2,1)}, u32[]{:S(2)}, u32[]{:S(2)}) collective-permute-start(bf16[128,1024]{1,0:T(8,128)(2,1)} %get-tuple-element.16), channel_id=1, source_target_pairs={{0,6},{2,0},{4,2},{6,4},{1,7},{3,1},{5,3},{7,5},{8,14},{10,8},{12,... | collective-permute-start | bytes 786440 | tf_op jit(solution)/shard_map/ppermute | solution.py:30
  118.4 14.1 %collective-permute-start.5 = (bf16[128,1024]{1,0:T(8,128)(2,1)}, bf16[128,1024]{1,0:T(8,128)(2,1)}, u32[]{:S(2)}, u32[]{:S(2)}) collective-permute-start(bf16[128,1024]{1,0:T(8,128)(2,1)} %get-tuple-element.17), channel_id=1, source_target_pairs={{0,4},{2,6},{4,0},{6,2},{1,5},{3,7},{5,1},{7,3},{8,12},{10,14},{12... | collective-permute-start | bytes 786440 | tf_op jit(solution)/shard_map/ppermute | solution.py:30
  121.6 4.7 %copy-start.3 = (bf16[128,1024]{1,0:T(8,128)(2,1)}, bf16[128,1024]{1,0:T(8,128)(2,1)S(1)}, u32[]{:S(2)}) copy-start(bf16[128,1024]{1,0:T(8,128)(2,1)S(1)} %collective-permute-done.15.rest_2_) | copy-start | bytes 786436
  121.6 0.7 copy-start.5
  122.3 1.6 copy-start
  123.9 0.9 copy-start.6
  124.9 7.7 %copy-start.14 = (bf16[128,1024]{1,0:T(8,128)(2,1)S(1)}, bf16[128,1024]{1,0:T(8,128)(2,1)}, u32[]{:S(2)}) copy-start(bf16[128,1024]{1,0:T(8,128)(2,1)} %copy-done.13) | copy-start | bytes 786436
  124.9 30.1 %copy-start.1 = (bf16[1024,1024]{1,0:T(8,128)(2,1)S(1)}, bf16[1024,1024]{1,0:T(8,128)(2,1)}, u32[]{:S(2)}) copy-start(bf16[1024,1024]{1,0:T(8,128)(2,1)} %all-gather.4.cloned.1.call-done.rest_4_) | copy-start | bytes 6291460
  126.3 34.7 %collective-permute-start.17 = (bf16[8,64,512]{2,1,0:T(8,128)(2,1)S(1)}, bf16[8,64,512]{2,1,0:T(8,128)(2,1)S(1)}, u32[]{:S(2)}, u32[]{:S(2)}) collective-permute-start(bf16[8,64,512]{2,1,0:T(8,128)(2,1)S(1)} %out_part.7), channel_id=1, source_target_pairs={{0,1},{1,0},{2,3},{3,2},{4,5},{5,4},{6,7},{7,6},{8,9},{9,8},{10,11... | collective-permute-start | bytes 1572872 | tf_op jit(solution)/shard_map/ppermute | solution.py:26
  133.8 10.8 %collective-permute-start.8 = (bf16[128,1024]{1,0:T(8,128)(2,1)S(1)}, bf16[128,1024]{1,0:T(8,128)(2,1)S(1)}, u32[]{:S(2)}, u32[]{:S(2)}) collective-permute-start(bf16[128,1024]{1,0:T(8,128)(2,1)S(1)} %multiply_convert_fusion.1.rest_0_), channel_id=1, source_target_pairs={{0,6},{2,0},{4,2},{6,4},{1,7},{3,1},{5,3},{7,5},{8,14},{10,8},{12,... | collective-permute-start | bytes 786440 | tf_op jit(solution)/shard_map/ppermute | solution.py:30
  137.7 10.3 %collective-permute-start.7 = (bf16[128,1024]{1,0:T(8,128)(2,1)S(1)}, bf16[128,1024]{1,0:T(8,128)(2,1)S(1)}, u32[]{:S(2)}, u32[]{:S(2)}) collective-permute-start(bf16[128,1024]{1,0:T(8,128)(2,1)S(1)} %multiply_convert_fusion.1.rest_0_), channel_id=1, source_target_pairs={{0,4},{2,6},{4,0},{6,2},{1,5},{3,7},{5,1},{7,3},{8,12},{10,14},{12... | collective-permute-start | bytes 786440 | tf_op jit(solution)/shard_map/ppermute | solution.py:30
  140.6 14.3 %collective-permute-start.6 = (bf16[128,1024]{1,0:T(8,128)(2,1)S(1)}, bf16[128,1024]{1,0:T(8,128)(2,1)S(1)}, u32[]{:S(2)}, u32[]{:S(2)}) collective-permute-start(bf16[128,1024]{1,0:T(8,128)(2,1)S(1)} %multiply_convert_fusion.1.rest_0_), channel_id=1, source_target_pairs={{0,2},{2,4},{4,6},{6,0},{1,3},{3,5},{5,7},{7,1},{8,10},{10,12},{12... | collective-permute-start | bytes 786440 | tf_op jit(solution)/shard_map/ppermute | solution.py:30
  144.6 15.0 %copy-start.4 = (bf16[128,1024]{1,0:T(8,128)(2,1)S(1)}, bf16[128,1024]{1,0:T(8,128)(2,1)}, u32[]{:S(2)}) copy-start(bf16[128,1024]{1,0:T(8,128)(2,1)} %copy-done.3) | copy-start | bytes 786436
  144.6 12.6 %copy-start.7 = (bf16[128,1024]{1,0:T(8,128)(2,1)}, bf16[128,1024]{1,0:T(8,128)(2,1)S(1)}, u32[]{:S(2)}) copy-start(bf16[128,1024]{1,0:T(8,128)(2,1)S(1)} %collective-permute-done.8.rest_3_) | copy-start | bytes 786436
  148.0 9.1 %copy-start.9 = (bf16[128,1024]{1,0:T(8,128)(2,1)}, bf16[128,1024]{1,0:T(8,128)(2,1)S(1)}, u32[]{:S(2)}) copy-start(bf16[128,1024]{1,0:T(8,128)(2,1)S(1)} %collective-permute-done.7.rest_2_) | copy-start | bytes 786436
  154.9 2.2 %copy-start.11 = (bf16[128,1024]{1,0:T(8,128)(2,1)}, bf16[128,1024]{1,0:T(8,128)(2,1)S(1)}, u32[]{:S(2)}) copy-start(bf16[128,1024]{1,0:T(8,128)(2,1)S(1)} %collective-permute-done.6.rest_1_) | copy-start | bytes 786436
  157.2 14.2 %collective-permute-start.10 = (bf16[8,64,512]{2,1,0:T(8,128)(2,1)}, bf16[8,64,512]{2,1,0:T(8,128)(2,1)}, u32[]{:S(2)}, u32[]{:S(2)}) collective-permute-start(bf16[8,64,512]{2,1,0:T(8,128)(2,1)} %out_part.5), channel_id=1, source_target_pairs={{0,1},{1,0},{2,3},{3,2},{4,5},{5,4},{6,7},{7,6},{8,9},{9,8},{10,11... | collective-permute-start | bytes 1572872 | tf_op jit(solution)/shard_map/ppermute | solution.py:26
  162.0 6.9 %copy-start.8 = (bf16[128,1024]{1,0:T(8,128)(2,1)S(1)}, bf16[128,1024]{1,0:T(8,128)(2,1)}, u32[]{:S(2)}) copy-start(bf16[128,1024]{1,0:T(8,128)(2,1)} %copy-done.7) | copy-start | bytes 786436
  162.0 6.9 %copy-start.10 = (bf16[128,1024]{1,0:T(8,128)(2,1)S(1)}, bf16[128,1024]{1,0:T(8,128)(2,1)}, u32[]{:S(2)}) copy-start(bf16[128,1024]{1,0:T(8,128)(2,1)} %copy-done.9) | copy-start | bytes 786436
  162.0 22.3 %all-to-all-start.3 = ((bf16[8,64,512]{2,1,0:T(8,128)(2,1)}), bf16[8,64,512]{2,1,0:T(8,128)(2,1)}, u32[]{:S(2)}, u32[]{:S(2)}) async-start(bf16[8,64,512]{2,1,0:T(8,128)(2,1)} %add_convert_fusion), calls=%async_computation.3 | async-start | bytes 1048576 | tf_op jit(solution)/shard_map/all_to_all | solution.py:179
  166.4 0.9 copy-start.26
  169.0 1.0 copy-start.12
  171.4 16.5 %copy-start.20 = (f32[64,256]{1,0:T(8,128)S(1)}, f32[64,256]{1,0:T(8,128)}, u32[]{:S(2)}) copy-start(f32[64,256]{1,0:T(8,128)} %fusion.2) | copy-start | bytes 196612
  173.4 16.1 %copy-start.23 = (s32[128]{0:T(128)S(1)}, s32[128]{0:T(128)}, u32[]{:S(2)}) copy-start(s32[128]{0:T(128)} %get-tuple-element.36) | copy-start | bytes 1540
  173.4 16.1 %copy-start.27 = (f32[128]{0:T(128)S(1)}, f32[128]{0:T(128)}, u32[]{:S(2)}) copy-start(f32[128]{0:T(128)} %copy-done.26) | copy-start | bytes 1540
  184.4 21.4 %all-to-all-start.2 = ((bf16[8,64,512]{2,1,0:T(8,128)(2,1)}), bf16[8,64,512]{2,1,0:T(8,128)(2,1)S(1)}, u32[]{:S(2)}, u32[]{:S(2)}) async-start(bf16[8,64,512]{2,1,0:T(8,128)(2,1)} %add_convert_fusion.1), calls=%async_computation.2 | async-start | bytes 1048576 | tf_op jit(solution)/shard_map/all_to_all | solution.py:179
  187.9 2.2 %copy-start.19 = (f32[64,1,1,2,128]{4,3,2,1,0:T(2,128)S(1)}, f32[64,1,1,2,128]{4,3,2,1,0:T(2,128)}, u32[]{:S(2)}) copy-start(f32[64,1,1,2,128]{4,3,2,1,0:T(2,128)} %constant_dynamic-slice_fusion) | copy-start | bytes 196612
Sparse Core Ops, SparseCore 0:
  18.4 39.5 all-gather.5
  60.7 42.7 all-gather.3

commit v3 on v1

v3 whole, which is shorter than its diff:
```python
import functools

import jax
import jax.numpy as jnp
from jax import lax
from jax.experimental import pallas as pl
from jax.experimental.pallas import tpu as pltpu
from jax.sharding import Mesh
from jax.sharding import PartitionSpec as P

D = 4096
FF = 16384
BATCH = 64
MEMBERS = 128
NY = 8
NX = 4
INFO = 16
Y = ("y_hi", "y_lo")
HIGH = lax.Precision.HIGHEST
SIGMA_K = 0.5 / D**0.5
SIGMA_V = 0.5 / FF**0.5
VMEM = pl.BlockSpec(memory_space=pltpu.VMEM)
SMEM = pl.BlockSpec(memory_space=pltpu.SMEM)


def swap(x):
    return lax.ppermute(x, "core", [(0, 1), (1, 0)])


def one_hot(index, n):
    return (index[:, None] == lax.iota(jnp.int32, n)[None, :]).astype(jnp.float32)


def shift_kernel(copies, x_ref, mix_ref, info_ref, out_ref):
    tok = x_ref.shape[0]
    values = x_ref[...].astype(jnp.float32)
    first = lax.broadcasted_iota(jnp.int32, values.shape, 0) % BATCH == 0
    previous = jnp.where(first, 0.0, pltpu.roll(values, 1, 0))
    shifted = (values + (previous - values) * mix_ref[...]).astype(jnp.bfloat16)
    for i in range(copies):
        out_ref[i, :tok, :] = shifted
        out_ref[i, tok:, :] = info_ref[...]


def key_kernel(own, info_ref, mine_ref, got_ref, w_ref, bank_ref, hid_ref, out_ref, rows_ref):
    feat, tok = mine_ref.shape[2], own * BATCH
    inner = []
    for y in range(NY):
        rows_ref[y * tok : (y + 1) * tok, :feat] = mine_ref[y, :tok, :]
        rows_ref[y * tok : (y + 1) * tok, feat:] = got_ref[y, :tok, :]
    for m in range(NY * own):
        fac_a = bank_ref[pl.ds(info_ref[m, 0], 1), :]
        rows = rows_ref[m * BATCH : (m + 1) * BATCH, :].astype(jnp.float32)
        inner.append(SIGMA_K * jnp.sum(rows * fac_a, axis=1, keepdims=True))
    wide = 2 * w_ref.shape[2]
    block = out_ref.shape[1]
    for n in range(w_ref.shape[0] // 2):
        cols = slice(n * wide, (n + 1) * wide)
        w = jnp.concatenate([w_ref[2 * n], w_ref[2 * n + 1]], axis=1)
        acc = jnp.dot(rows_ref[...], w, preferred_element_type=jnp.float32)
        for m in range(NY * own):
            fac_b = hid_ref[pl.ds(info_ref[m, 1], 1), cols]
            term = acc[m * BATCH : (m + 1) * BATCH] + inner[m] * fac_b
            i, at = divmod(m * BATCH, block)
            out_ref[i, at : at + BATCH, cols] = term.astype(jnp.bfloat16)


def square_kernel(parts_ref, out_ref):
    block = 64
    for r in range(0, parts_ref.shape[1], block):
        total = sum(parts_ref[i, r : r + block, :].astype(jnp.float32) for i in range(NX))
        keys = (jnp.maximum(total, 0.0) ** 2).astype(jnp.bfloat16)
        for i in range(NX):
            out_ref[i, r : r + block, :] = keys


def out_kernel(half, info_ref, keys_ref, v_ref, bank_ref, hid_ref, out_ref):
    feat, half_hid = out_ref.shape[2], hid_ref.shape[1] // v_ref.shape[0]
    tok, block = out_ref.shape[1], keys_ref.shape[1]
    cols = slice(half * feat, (half + 1) * feat)
    v = jnp.concatenate([v_ref[i, :half_hid, cols] for i in range(v_ref.shape[0])], axis=0)
    for i in range(NX):
        acc = jnp.dot(keys_ref[i], v, preferred_element_type=jnp.float32)
        for j in range(block // BATCH):
            m = i * (block // BATCH) + j
            at = slice(j * BATCH, (j + 1) * BATCH)
            fac_c = hid_ref[pl.ds(info_ref[m, 2], 1), :]
            fac_d = bank_ref[pl.ds(info_ref[m, 3], 1), cols]
            inner = SIGMA_V * jnp.sum(
                keys_ref[i, at, :].astype(jnp.float32) * fac_c, axis=1, keepdims=True
            )
            y, row = divmod(m * BATCH, tok)
            out_ref[y, row : row + BATCH, :] = (acc[at] + inner * fac_d).astype(out_ref.dtype)


def cost(rows, depth, cols):
    return pl.CostEstimate(
        flops=2 * rows * depth * cols,
        bytes_accessed=2 * (rows * depth + depth * cols + rows * cols),
        transcendentals=0,
    )


def call(kernel, name, out, scratch, n_smem, estimate, *args):
    return pl.pallas_call(
        kernel,
        out_shape=jax.ShapeDtypeStruct(*out),
        in_specs=[SMEM] * n_smem + [VMEM] * (len(args) - n_smem),
        out_specs=VMEM,
        scratch_shapes=scratch,
        compiler_params=pltpu.CompilerParams(vmem_limit_bytes=24 << 20),
        cost_estimate=estimate,
        name=name,
    )(*args)


def out_part(half, dtype, info, keys, v, banks, hidden):
    rows, deep, feat = keys.shape[0] * keys.shape[1], keys.shape[2], v.shape[2] // 2
    out = (NY, rows // NY, feat), dtype
    kernel = functools.partial(out_kernel, half)
    return call(kernel, "out_part", out, [], 1, cost(rows, deep, feat), info, keys, v, banks, hidden)


def shards(inputs, mix, key_weight, value_weight, dim_bank, hidden_bank, member_picks, ranks):
    bank = dim_bank.shape[0]
    tok, feat = inputs.shape
    hid = key_weight.shape[1]
    half = hid // 2
    own = tok // BATCH
    core = lax.axis_index("core")
    y_hi = lax.axis_index("y_hi")
    z = lax.axis_index("z")

    info = jnp.concatenate([member_picks, ranks[:, None]], axis=1).astype(jnp.bfloat16)
    info = jnp.pad(info, ((0, INFO - own), (0, feat - info.shape[1])))
    shape = NY, tok + INFO, feat
    shifted = call(
        functools.partial(shift_kernel, NY), "shift", (shape, jnp.bfloat16), [], 0,
        cost(tok, 16, feat), inputs, mix[None], info,
    )
    mine = lax.all_to_all(shifted, Y, 0, 0)
    got = swap(mine)
    members = NY * own
    info = mine[:, tok : tok + own, :128].reshape(members, 128)
    ids = info[:, :4].astype(jnp.int32)

    def hidden_half(array, axis):
        return lax.dynamic_slice_in_dim(array, core * half, half, axis)

    key_pack = jnp.concatenate(
        [hidden_half(key_weight, 1), hidden_half(swap(key_weight), 1)], axis=0
    )
    key_all = lax.all_gather(key_pack, "z", axis=0)
    value_pack = jnp.concatenate(
        [hidden_half(value_weight, 0), hidden_half(swap(value_weight), 0)], axis=1
    )
    info = jnp.pad(info, ((0, INFO - members), (0, 2 * feat - 128)))
    value_all = lax.all_gather(jnp.concatenate([value_pack, info], axis=0), "z", axis=0)
    everyone = value_all[:, half : half + members, :5].reshape(8 * members, 5).astype(jnp.int32)

    banks = jnp.concatenate([dim_bank, swap(dim_bank)], axis=1)
    hidden = hidden_bank.reshape(bank, 8, 2, 2, half)
    hidden = lax.dynamic_index_in_dim(hidden, y_hi, 2, keepdims=False)
    hidden_own = lax.dynamic_index_in_dim(hidden, z, 1, keepdims=False).reshape(bank, hid)
    hidden = lax.dynamic_index_in_dim(hidden, core, 2, keepdims=False).reshape(bank, 8 * half)

    rows, deep, wide = NY * tok, 2 * feat, 8 * half
    blocks = (NX, rows // NX, wide), jnp.bfloat16
    part = call(
        functools.partial(key_kernel, own), "key_part", blocks,
        [pltpu.VMEM((rows, deep), jnp.bfloat16)], 1, cost(rows, deep, wide),
        ids, mine, got, key_all, banks, hidden,
    )
    parts = lax.all_to_all(part, "x", 0, 0)
    keys = call(square_kernel, "square", blocks, [], 0, cost(rows, 1, wide), parts)
    keys = lax.all_to_all(keys, "x", 0, 0)

    rest = out_part(1, jnp.bfloat16, ids, keys, value_all, banks, hidden)
    base = out_part(0, jnp.float32, ids, keys, value_all, banks, hidden)
    result = (base + swap(rest).astype(jnp.float32)).astype(jnp.bfloat16)
    pieces = lax.all_to_all(result, Y, 0, 0)
    outputs = jnp.sum(pieces.astype(jnp.float32), axis=0).astype(jnp.bfloat16)

    fitness = 2.0 * everyone[:, 4].astype(jnp.float32) / (MEMBERS - 1) - 1.0
    fitness = fitness * (1.0 / MEMBERS**0.5)
    pick = [one_hot(everyone[:, i], bank) for i in range(4)]
    pair_k = jnp.dot((fitness[:, None] * pick[0]).T, pick[1], precision=HIGH)
    pair_v = jnp.dot((fitness[:, None] * pick[2]).T, pick[3], precision=HIGH)
    key_step = jnp.dot(dim_bank.T, jnp.dot(pair_k, hidden_own, precision=HIGH), precision=HIGH)
    value_step = jnp.dot(hidden_own.T, jnp.dot(pair_v, dim_bank, precision=HIGH), precision=HIGH)
    return outputs, key_step, value_step


def solution(mesh):
    fine = Mesh(mesh.devices.reshape(8, 2, 4, 4, 2), ("z", "y_hi", "y_lo", "x", "core"))
    pop, row, col = ("z", "y_hi"), ("y_lo",), ("x", "core")
    in_specs = (
        P(pop + row, col),
        P(col),
        P(col, row + pop),
        P(row + pop, col),
        P(None, col),
        P(None, row),
        P(pop + row, None),
        P(pop + row),
    )
    out_specs = (P(pop + row, col), P(col, row + pop), P(row + pop, col))
    return jax.shard_map(shards, mesh=fine, in_specs=in_specs, out_specs=out_specs, check_vma=False)
```

time: 213 us -> 189 us (0.89)
  waiting for transfers between devices: 93.6 us -> 77.2 us
  matrix products: 15 us -> 3.13 us
  Pallas kernels: 0 us -> 10.1 us
  starting transfers between devices: 38.1 us -> 32.8 us
    all_gather x1 -> x2, waiting for transfers between devices: 13 us -> 0.04 us  [the longest x1 0.02 us: shards(): key_all = lax.all_gather(key_pack, 'z', axis=0)]
    pallas_call x0 -> x5, Pallas kernels: none -> 10.1 us  [call(): pl.pallas_call(kernel, out_shape=jax.ShapeDtypeStruct(*out), in_specs=[SM...]
    dot_general x6 -> x0, matrix products: 10.1 us -> none  [the longest x1 4.3 us: shards(): lax.dot_general(tokens, key_all, (((1,), (1,)), ((), ())), preferred_elem...]
    all_to_all x4 -> x3, starting transfers between devices: 17.5 us -> 10.9 us  [the longest x1 3.69 us: shards(): mine = lax.all_to_all(shifted, Y, 0, 0)]
    unnamed x21 -> x26, local copies, waits for them, and re-layouts: 5.12 us -> 9.23 us
    broadcast_in_dim x3 -> x0, local copies, waits for them, and re-layouts: 3.31 us -> none  [to_all(): return lax.all_to_all(jnp.broadcast_to(x[None], (n, *x.shape)), axis, 0, 0)]
    all_to_all x4 -> x3, waiting for transfers between devices: 79.6 us -> 76.7 us  [the longest x1 27.3 us: shards(): mine = lax.all_to_all(shifted, Y, 0, 0)]
    ppermute x4 -> x5, starting transfers between devices: 20.6 us -> 21.9 us  [swap(): return lax.ppermute(x, 'core', [(0, 1), (1, 0)])]
  transfers between devices with their start and end apart: 9 -> 10, of which waited for: 6 -> 4; matrix products, arithmetic and copies ran while one was open for 7% -> 7% of each run, Pallas kernels for 0% -> 4%
where the time goes in v3:
time: 189 us; the launch traced here: 188 us
  waiting for transfers between devices  77.2 us (41%)
  starting transfers between devices  32.8 us (17%)
  blocking collectives  28.4 us (15%)
  local copies, waits for them, and re-layouts  15.2 us (8%)
  between operations  14.4 us (8%)
  Pallas kernels  10.1 us (5%)
  other arithmetic  6.44 us (3%)
  matrix products  3.13 us (2%)
    all_to_all x1, blocking collectives, shards(): parts = lax.all_to_all(part, 'x', 0, 0)  28.4 us
    all_to_all x1, waiting for transfers between devices, shards(): mine = lax.all_to_all(shifted, Y, 0, 0)  27.3 us
    all_to_all x1, waiting for transfers between devices, shards(): keys = lax.all_to_all(keys, 'x', 0, 0)  24.9 us
    all_to_all x1, waiting for transfers between devices, shards(): pieces = lax.all_to_all(result, Y, 0, 0)  24.5 us
    ppermute x5, starting transfers between devices, swap(): return lax.ppermute(x, 'core', [(0, 1), (1, 0)])  21.9 us
    pallas_call x5, Pallas kernels, call(): pl.pallas_call(kernel, out_shape=jax.ShapeDtypeStruct(*out), in_specs=[SM...  10.1 us
    unnamed x26, local copies, waits for them, and re-layouts  9.23 us
  transfers between devices with their start and end apart: 10, of which 4 were waited for; matrix products, arithmetic and copies ran while one was open for 7% of the time, Pallas kernels for 4%

profile of v3, /device:TPU:1, one launch (start us, length us, event | category | flops | bytes accessed | tf_op | source)
XLA Modules:
  0.0 187.6 jit_solution(14574530808186739902)
XLA Ops:
  7.2 0.0 all-gather.5.cloned.1.call-start
  7.2 8.8 %collective-permute-start.1 = (bf16[512,256]{1,0:T(8,128)(2,1)}, bf16[512,256]{1,0:T(8,128)(2,1)S(1)}, u32[]{:S(2)}, u32[]{:S(2)}) collective-permute-start(bf16[512,256]{1,0:T(8,128)(2,1)} %param.10), channel_id=1, source_target_pairs={{0,1},{1,0},{2,3},{3,2},{4,5},{5,4},{6,7},{7,6},{8,9},{9,8},{10,11... | collective-permute-start | bytes 786440 | tf_op jit(solution)/shard_map/ppermute | solution.py:27
  16.0 0.9 constant_dynamic-slice_fusion.5
  16.9 0.4 collective-permute-done.1
  17.4 0.7 pad_maximum_fusion
  18.1 0.0 all-gather.5.cloned.1.call-update
  18.1 0.7 convert_bitcast_fusion
  18.8 0.1 copy.11
  18.9 0.7 convert.9
  19.6 0.1 fusion.25.info_ref
  19.7 0.9 copy-done.3
  20.6 0.7 copy-done.4
  21.3 1.1 shift.1
  22.4 3.7 %all-to-all-start = ((bf16[8,144,512]{2,1,0:T(8,128)(2,1)}), bf16[8,144,512]{2,1,0:T(8,128)(2,1)S(1)}, u32[]{:S(2)}, u32[]{:S(2)}) async-start(bf16[8,144,512]{2,1,0:T(8,128)(2,1)} %shift.1), calls=%async_computation | async-start | bytes 2359296 | tf_op jit(solution)/shard_map/all_to_all | solution.py:141
  26.1 0.0 all-gather.7.cloned.1.call-start
  26.2 0.0 copy-done.8
  26.2 2.3 %collective-permute-start.3 = (bf16[256,512]{1,0:T(8,128)(2,1)S(1)}, bf16[256,512]{1,0:T(8,128)(2,1)S(1)}, u32[]{:S(2)}, u32[]{:S(2)}) collective-permute-start(bf16[256,512]{1,0:T(8,128)(2,1)S(1)} %copy-done.8), channel_id=1, source_target_pairs={{0,1},{1,0},{2,3},{3,2},{4,5},{5,4},{6,7},{7,6},{8,9},{9,8},{10,11... | collective-permute-start | bytes 786440 | tf_op jit(solution)/shard_map/ppermute | solution.py:27
  28.5 27.3 %all-to-all-done.mine_ref = bf16[8,144,512]{2,1,0:T(8,128)(2,1)S(1)} async-done(((bf16[8,144,512]{2,1,0:T(8,128)(2,1)}), bf16[8,144,512]{2,1,0:T(8,128)(2,1)S(1)}, u32[]{:S(2)}, u32[]{:S(2)}) %all-to-all-start) | async-done | bytes 1179680 | tf_op jit(solution)/shard_map/all_to_all | solution.py:141
  55.8 4.7 %collective-permute-start = (bf16[8,144,512]{2,1,0:T(8,128)(2,1)S(1)}, bf16[8,144,512]{2,1,0:T(8,128)(2,1)}, u32[]{:S(2)}, u32[]{:S(2)}) collective-permute-start(bf16[8,144,512]{2,1,0:T(8,128)(2,1)S(1)} %all-to-all-done.mine_ref), channel_id=1, source_target_pairs={{0,1},{1,0},{2,3},{3,2},{4,5},{5,4},{6,7},{7,6},{8,9},{9,8},{10,11... | collective-permute-start | bytes 3538952 | tf_op jit(solution)/shard_map/ppermute | solution.py:27
  60.5 0.0 collective-permute-done.3
  60.5 0.7 fusion.1
  61.3 0.0 all-gather.7.cloned.1.call-update
  61.3 0.0 copy-done.6
  61.3 1.9 %collective-permute-start.2 = (f32[64,512]{1,0:T(8,128)S(1)}, f32[64,512]{1,0:T(8,128)S(1)}, u32[]{:S(2)}, u32[]{:S(2)}) collective-permute-start(f32[64,512]{1,0:T(8,128)S(1)} %copy-done.6), channel_id=1, source_target_pairs={{0,1},{1,0},{2,3},{3,2},{4,5},{5,4},{6,7},{7,6},{8,9},{9,8},{10,11... | collective-permute-start | bytes 393224 | tf_op jit(solution)/shard_map/ppermute | solution.py:27
  63.3 1.9 reshape.28
  65.1 1.3 constant_dynamic-slice_fusion.3
  66.5 0.0 collective-permute-done.2
  66.5 0.0 collective-permute-done.got_ref
  66.5 0.0 all-gather.5.cloned.1.call-done
  66.6 0.0 copy-start.5
  66.6 1.6 copy-done.5
  68.1 3.8 %key_part.1 = bf16[4,256,1024]{2,1,0:T(8,128)(2,1)S(1)} custom-call(s32[16,4]{1,0:T(8,128)S(1)} %slice_convert_fusion.info_ref, bf16[8,144,512]{2,1,0:T(8,128)(2,1)S(1)} %all-to-all-done.mine_ref, bf16[8,144,512]{2,1,0:T(8,128)(2,1)} %collective-permute-done.got_ref, bf16[8,1024,128]{2,1,0:T(8,128)(2,1)S(1)} %bitcast.43, ...), custom_call_target="tpu_custom_call" | custom-call | flops 2147483648 | bytes 6291456 | tf_op jit(solution)/shard_map/key_part/pallas_call | solution.py:105
  72.0 28.4 %all_to_all.20.parts_ref = bf16[4,256,1024]{2,1,0:T(8,128)(2,1)S(1)} all-to-all(bf16[4,256,1024]{2,1,0:T(8,128)(2,1)S(1)} %key_part.1), channel_id=1, replica_groups=mesh['z'=8,'y_hi'=2,'y_lo'=4,'x'=4,'core'=2] {'x'}, dimensions={0} | all-to-all | bytes 4194304 | tf_op jit(solution)/shard_map/all_to_all | solution.py:174
  100.4 0.3 square.1
  100.7 1.3 copy-done.2
  102.1 3.6 %all-to-all-start.2 = ((bf16[4,256,1024]{2,1,0:T(8,128)(2,1)}), bf16[4,256,1024]{2,1,0:T(8,128)(2,1)S(1)}, u32[]{:S(2)}, u32[]{:S(2)}) async-start(bf16[4,256,1024]{2,1,0:T(8,128)(2,1)} %copy-done.2), calls=%async_computation.2 | async-start | bytes 4194304 | tf_op jit(solution)/shard_map/all_to_all | solution.py:176
  105.7 0.0 all-gather.7.cloned.1.call-done
  105.7 24.9 %all-to-all-done.2.keys_ref = bf16[4,256,1024]{2,1,0:T(8,128)(2,1)S(1)} async-done(((bf16[4,256,1024]{2,1,0:T(8,128)(2,1)}), bf16[4,256,1024]{2,1,0:T(8,128)(2,1)S(1)}, u32[]{:S(2)}, u32[]{:S(2)}) %all-to-all-start.2) | async-done | bytes 2097184 | tf_op jit(solution)/shard_map/all_to_all | solution.py:176
  130.6 1.7 copy-done
  132.3 2.9 %out_part.3 = bf16[8,128,512]{2,1,0:T(8,128)(2,1)} custom-call(s32[16,4]{1,0:T(8,128)S(1)} %slice_convert_fusion.info_ref, bf16[4,256,1024]{2,1,0:T(8,128)(2,1)S(1)} %all-to-all-done.2.keys_ref, bf16[8,144,1024]{2,1,0:T(8,128)(2,1)S(1)} %bitcast.37, f32[64,1024]{1,0:T(8,128)S(1)} %constant_dynamic-update-slice_fusion.bank_ref, f32[64,1024]{1,0:T(8,128)S(1)} %bitcast.40), custom_call_target="tpu_custom_call" | custom-call | flops 1073741824 | bytes 4194304 | tf_op jit(solution)/shard_map/out_part/pallas_call | solution.py:105
  135.2 4.2 %collective-permute-start.4 = (bf16[8,128,512]{2,1,0:T(8,128)(2,1)}, bf16[8,128,512]{2,1,0:T(8,128)(2,1)}, u32[]{:S(2)}, u32[]{:S(2)}) collective-permute-start(bf16[8,128,512]{2,1,0:T(8,128)(2,1)} %out_part.3), channel_id=1, source_target_pairs={{0,1},{1,0},{2,3},{3,2},{4,5},{5,4},{6,7},{7,6},{8,9},{9,8},{10,11... | collective-permute-start | bytes 3145736 | tf_op jit(solution)/shard_map/ppermute | solution.py:27
  139.4 0.9 constant_dynamic-slice_fusion
  140.3 0.8 slice.34
  141.1 1.7 copy-done.1
  142.7 1.9 %out_part.2 = f32[8,128,512]{2,1,0:T(8,128)S(1)} custom-call(s32[16,4]{1,0:T(8,128)S(1)} %slice_convert_fusion.info_ref, bf16[4,256,1024]{2,1,0:T(8,128)(2,1)S(1)} %all-to-all-done.2.keys_ref, bf16[8,144,1024]{2,1,0:T(8,128)(2,1)S(1)} %bitcast.38, f32[64,1024]{1,0:T(8,128)S(1)} %constant_dynamic-update-slice_fusion.bank_ref, f32[64,1024]{1,0:T(8,128)S(1)} %bitcast.41), custom_call_target="tpu_custom_call" | custom-call | flops 1073741824 | bytes 4194304 | tf_op jit(solution)/shard_map/out_part/pallas_call | solution.py:105
  144.7 0.0 collective-permute-done.4
  144.7 2.6 %add_convert_fusion = bf16[8,128,512]{2,1,0:T(8,128)(2,1)} fusion(f32[8,128,512]{2,1,0:T(8,128)S(1)} %out_part.2, bf16[8,128,512]{2,1,0:T(8,128)(2,1)} %collective-permute-done.4), kind=kLoop, calls=%fused_computation | loop fusion | flops 1572864 | bytes 4194304 | tf_op jit(solution)/shard_map/convert_element_type | solution.py:180
  147.2 3.6 %all-to-all-start.3 = ((bf16[8,128,512]{2,1,0:T(8,128)(2,1)}), bf16[8,128,512]{2,1,0:T(8,128)(2,1)S(1)}, u32[]{:S(2)}, u32[]{:S(2)}) async-start(bf16[8,128,512]{2,1,0:T(8,128)(2,1)} %add_convert_fusion), calls=%async_computation.3 | async-start | bytes 2097152 | tf_op jit(solution)/shard_map/all_to_all | solution.py:181
  150.8 0.1 fusion.28
  150.9 0.1 copy.20
  151.0 0.1 copy.22
  151.0 0.1 add_multiply_fusion
  151.2 0.1 copy.27
  151.2 0.3 fusion.8
  151.6 0.2 fusion.4
  151.8 0.6 convolution_bitcast_fusion
  152.4 1.0 copy.18
  153.4 0.1 copy.23
  153.4 0.1 copy.24
  153.5 0.3 fusion.6
  153.8 0.3 fusion.29
  154.1 1.4 fusion.2
  155.5 24.5 %all-to-all-done.3 = bf16[8,128,512]{2,1,0:T(8,128)(2,1)S(1)} async-done(((bf16[8,128,512]{2,1,0:T(8,128)(2,1)}), bf16[8,128,512]{2,1,0:T(8,128)(2,1)S(1)}, u32[]{:S(2)}, u32[]{:S(2)}) %all-to-all-start.3) | async-done | bytes 1048608 | tf_op jit(solution)/shard_map/all_to_all | solution.py:181
  180.0 0.8 reduce_sum.12
  (18 shorter events, 0.2 us)
Async XLA Ops:
  7.2 59.4 %all-gather.5.cloned.1.call-start = ((), (), s32[]{:S(2)}) async-start(), calls=%async_computation.4 | async-start | bytes 2359296 | tf_op jit(solution)/shard_map/all_gather | solution.py:153
  7.2 10.1 %collective-permute-start.1 = (bf16[512,256]{1,0:T(8,128)(2,1)}, bf16[512,256]{1,0:T(8,128)(2,1)S(1)}, u32[]{:S(2)}, u32[]{:S(2)}) collective-permute-start(bf16[512,256]{1,0:T(8,128)(2,1)} %param.10), channel_id=1, source_target_pairs={{0,1},{1,0},{2,3},{3,2},{4,5},{5,4},{6,7},{7,6},{8,9},{9,8},{10,11... | collective-permute-start | bytes 786440 | tf_op jit(solution)/shard_map/ppermute | solution.py:27
  18.1 8.1 %copy-start.8 = (bf16[256,512]{1,0:T(8,128)(2,1)S(1)}, bf16[256,512]{1,0:T(8,128)(2,1)}, u32[]{:S(2)}) copy-start(bf16[256,512]{1,0:T(8,128)(2,1)} %param.11) | copy-start | bytes 786436
  19.7 0.9 copy-start.3
  20.6 0.7 copy-start.4
  22.4 38.9 %copy-start.6 = (f32[64,512]{1,0:T(8,128)S(1)}, f32[64,512]{1,0:T(8,128)}, u32[]{:S(2)}) copy-start(f32[64,512]{1,0:T(8,128)} %param.12) | copy-start | bytes 393220
  22.4 40.9 %copy-start.7 = (f32[64,4096]{1,0:T(8,128)S(1)}, f32[64,4096]{1,0:T(8,128)}, u32[]{:S(2)}) copy-start(f32[64,4096]{1,0:T(8,128)} %param.13) | copy-start | bytes 3145732
  22.4 33.4 %all-to-all-start = ((bf16[8,144,512]{2,1,0:T(8,128)(2,1)}), bf16[8,144,512]{2,1,0:T(8,128)(2,1)S(1)}, u32[]{:S(2)}, u32[]{:S(2)}) async-start(bf16[8,144,512]{2,1,0:T(8,128)(2,1)} %shift.1), calls=%async_computation | async-start | bytes 2359296 | tf_op jit(solution)/shard_map/all_to_all | solution.py:141
  26.1 79.6 %all-gather.7.cloned.1.call-start = ((), (), s32[]{:S(2)}) async-start(), calls=%async_computation.5 | async-start | bytes 2654208 | tf_op jit(solution)/shard_map/all_gather | solution.py:158
  26.2 34.3 %collective-permute-start.3 = (bf16[256,512]{1,0:T(8,128)(2,1)S(1)}, bf16[256,512]{1,0:T(8,128)(2,1)S(1)}, u32[]{:S(2)}, u32[]{:S(2)}) collective-permute-start(bf16[256,512]{1,0:T(8,128)(2,1)S(1)} %copy-done.8), channel_id=1, source_target_pairs={{0,1},{1,0},{2,3},{3,2},{4,5},{5,4},{6,7},{7,6},{8,9},{9,8},{10,11... | collective-permute-start | bytes 786440 | tf_op jit(solution)/shard_map/ppermute | solution.py:27
  55.8 10.8 %collective-permute-start = (bf16[8,144,512]{2,1,0:T(8,128)(2,1)S(1)}, bf16[8,144,512]{2,1,0:T(8,128)(2,1)}, u32[]{:S(2)}, u32[]{:S(2)}) collective-permute-start(bf16[8,144,512]{2,1,0:T(8,128)(2,1)S(1)} %all-to-all-done.mine_ref), channel_id=1, source_target_pairs={{0,1},{1,0},{2,3},{3,2},{4,5},{5,4},{6,7},{7,6},{8,9},{9,8},{10,11... | collective-permute-start | bytes 3538952 | tf_op jit(solution)/shard_map/ppermute | solution.py:27
  61.3 5.2 %collective-permute-start.2 = (f32[64,512]{1,0:T(8,128)S(1)}, f32[64,512]{1,0:T(8,128)S(1)}, u32[]{:S(2)}, u32[]{:S(2)}) collective-permute-start(f32[64,512]{1,0:T(8,128)S(1)} %copy-done.6), channel_id=1, source_target_pairs={{0,1},{1,0},{2,3},{3,2},{4,5},{5,4},{6,7},{7,6},{8,9},{9,8},{10,11... | collective-permute-start | bytes 393224 | tf_op jit(solution)/shard_map/ppermute | solution.py:27
  66.6 1.6 copy-start.5
  100.7 1.3 copy-start.2
  102.1 28.6 %all-to-all-start.2 = ((bf16[4,256,1024]{2,1,0:T(8,128)(2,1)}), bf16[4,256,1024]{2,1,0:T(8,128)(2,1)S(1)}, u32[]{:S(2)}, u32[]{:S(2)}) async-start(bf16[4,256,1024]{2,1,0:T(8,128)(2,1)} %copy-done.2), calls=%async_computation.2 | async-start | bytes 4194304 | tf_op jit(solution)/shard_map/all_to_all | solution.py:176
  130.6 1.7 copy-start
  135.2 9.4 %collective-permute-start.4 = (bf16[8,128,512]{2,1,0:T(8,128)(2,1)}, bf16[8,128,512]{2,1,0:T(8,128)(2,1)}, u32[]{:S(2)}, u32[]{:S(2)}) collective-permute-start(bf16[8,128,512]{2,1,0:T(8,128)(2,1)} %out_part.3), channel_id=1, source_target_pairs={{0,1},{1,0},{2,3},{3,2},{4,5},{5,4},{6,7},{7,6},{8,9},{9,8},{10,11... | collective-permute-start | bytes 3145736 | tf_op jit(solution)/shard_map/ppermute | solution.py:27
  141.1 1.7 copy-start.1
  147.2 32.8 %all-to-all-start.3 = ((bf16[8,128,512]{2,1,0:T(8,128)(2,1)}), bf16[8,128,512]{2,1,0:T(8,128)(2,1)S(1)}, u32[]{:S(2)}, u32[]{:S(2)}) async-start(bf16[8,128,512]{2,1,0:T(8,128)(2,1)} %add_convert_fusion), calls=%async_computation.3 | async-start | bytes 2097152 | tf_op jit(solution)/shard_map/all_to_all | solution.py:181
Sparse Core Ops, SparseCore 0:
  18.2 39.5 all-gather.4
  61.4 42.9 all-gather.6

commit v4 on v1

v4 whole, which is shorter than its diff:
```python
import functools

import jax
import jax.numpy as jnp
from jax import lax
from jax.experimental import pallas as pl
from jax.experimental.pallas import tpu as pltpu
from jax.sharding import Mesh
from jax.sharding import PartitionSpec as P

D = 4096
FF = 16384
BATCH = 64
MEMBERS = 128
NY, NQ = 8, 4
NX, NZ = 4, 8
INFO = 16
YQ = ("y_hi", "y_mid")
HIGH = lax.Precision.HIGHEST
SIGMA_K = 0.5 / D**0.5
SIGMA_V = 0.5 / FF**0.5
VMEM = pl.BlockSpec(memory_space=pltpu.VMEM)
HBM = pl.BlockSpec(memory_space=pltpu.HBM)
SMEM = pl.BlockSpec(memory_space=pltpu.SMEM)


def swap(x):
    return lax.ppermute(x, "core", [(0, 1), (1, 0)])


def exchange(x, second):
    pairs = []
    for i in range(NX):
        for core in range(2):
            to = i ^ 1 if core == second else NX - 1 - i
            pairs.append((2 * i + core, 2 * to + core))
    return lax.ppermute(x, ("x", "core"), pairs)


def beside(x):
    pairs = []
    for y in range(NY):
        for core in range(2):
            to = y ^ 1 if core == 0 else (y + 2 * (y % 2) - 1) % NY
            pairs.append((2 * y + core, 2 * to + core))
    return lax.ppermute(x, YQ + ("y_low", "core"), pairs)


def shift_kernel(copies, picks_hbm, ranks_hbm, x_hbm, mix_hbm, out_ref, picks_ref, ranks_ref, x_ref, mix_ref, sems):
    pairs = (x_hbm, x_ref), (mix_hbm, mix_ref), (picks_hbm, picks_ref), (ranks_hbm, ranks_ref)
    fetches = [pltpu.make_async_copy(src, dst, sems.at[i]) for i, (src, dst) in enumerate(pairs)]
    for fetch in fetches:
        fetch.start()
    for fetch in fetches:
        fetch.wait()
    tok, feat = x_ref.shape
    values = x_ref[...].astype(jnp.float32)
    first = lax.broadcasted_iota(jnp.int32, values.shape, 0) % BATCH == 0
    previous = jnp.where(first, 0.0, pltpu.roll(values, 1, 0))
    shifted = (values + (previous - values) * mix_ref[...]).astype(jnp.bfloat16)
    row = lax.broadcasted_iota(jnp.int32, (INFO, feat), 0)
    lane = lax.broadcasted_iota(jnp.int32, (INFO, feat), 1)
    info = jnp.zeros((INFO, feat), jnp.float32)
    for i in range(tok // BATCH):
        entries = [picks_ref[i, j] for j in range(4)] + [ranks_ref[i]]
        for j, entry in enumerate(entries):
            info = jnp.where((row == i) & (lane == j), entry.astype(jnp.float32), info)
    info = info.astype(jnp.bfloat16)
    for i in range(copies):
        out_ref[i, :tok, :] = shifted
        out_ref[i, tok:, :] = info


def hidden_kernel(at_ref, hid_hbm, out_ref, sems):
    apart, width = hid_hbm.shape[1] // NZ, out_ref.shape[1] // NZ
    fetches = []
    for i in range(NZ):
        start = pl.multiple_of(at_ref[0] + i * apart, width)
        src, dst = hid_hbm.at[:, pl.ds(start, width)], out_ref.at[:, pl.ds(i * width, width)]
        fetches.append(pltpu.make_async_copy(src, dst, sems.at[i]))
        fetches[-1].start()
    for fetch in fetches:
        fetch.wait()


def key_kernel(order, order_ref, ids_ref, *refs):
    tokens, (w_ref, bank_ref, other_ref, hid_ref, *out_refs) = refs[:4], refs[4:]
    tok = tokens[0].shape[1] - INFO
    own = tok // BATCH
    blocks, inner, picks = [], [], []
    for i in order:
        u = order_ref[i]
        for s in range(2):
            for j in range(own):
                rows = [r[u, j * BATCH : (j + 1) * BATCH, :] for r in (tokens[s], tokens[2 + s])]
                m = (s * NX + u) * own + j
                fac_a = [r[pl.ds(ids_ref[m, 0], 1), :] for r in (bank_ref, other_ref)]
                dots = sum(r.astype(jnp.float32) * a for r, a in zip(rows, fac_a))
                inner.append(SIGMA_K * jnp.sum(dots, axis=1, keepdims=True))
                picks.append(ids_ref[m, 1])
                blocks.append(jnp.concatenate(rows, axis=1))
    rows = jnp.concatenate(blocks, axis=0)
    width, per = w_ref.shape[2], 2 * own
    for n in range(0, NZ, 2):
        cols = slice(n * width, (n + 2) * width)
        w = jnp.concatenate([w_ref[n], w_ref[n + 1]], axis=1)
        acc = jnp.dot(rows, w, preferred_element_type=jnp.float32)
        for k, (part, pick) in enumerate(zip(inner, picks)):
            term = acc[k * BATCH : (k + 1) * BATCH] + part * hid_ref[pl.ds(pick, 1), cols]
            i, at = divmod(k, per)
            out_refs[i][at * BATCH : (at + 1) * BATCH, cols] = term.astype(out_refs[i].dtype)


def add_kernel(kept_ref, came_ref, out_ref):
    out_ref[...] = (kept_ref[...] + came_ref[...].astype(jnp.float32)).astype(jnp.bfloat16)


def square_kernel(kept_ref, first_ref, second_ref, out_ref):
    total = kept_ref[...] + first_ref[...].astype(jnp.float32) + second_ref[...].astype(jnp.float32)
    out_ref[...] = (jnp.maximum(total, 0.0) ** 2).astype(jnp.bfloat16)


def out_kernel(half, order_ref, ids_ref, *refs):
    keys, (v_ref, bank_ref, hid_ref), rest = refs[:NX], refs[NX : NX + 3], refs[NX + 3 :]
    came, out_refs = rest[:-2], rest[-2:]
    feat, width = out_refs[0].shape[2], hid_ref.shape[1] // NZ
    tok = out_refs[0].shape[1]
    own, wide = tok // BATCH, 256
    inner, picks, places = [], [], []
    for i in range(NX):
        for s in range(2):
            for j in range(own):
                m = (s * NX + order_ref[i]) * own + j
                fac_c = hid_ref[pl.ds(ids_ref[m, 2], 1), :]
                at = s * tok + j * BATCH
                part = keys[i][at : at + BATCH, :].astype(jnp.float32)
                inner.append(SIGMA_V * jnp.sum(part * fac_c, axis=1, keepdims=True))
                picks.append(ids_ref[m, 3])
                places.append((s, order_ref[i], slice(j * BATCH, (j + 1) * BATCH)))
    rows = jnp.concatenate([k[...] for k in keys], axis=0)
    for n in range(feat // wide):
        cols = slice(n * wide, (n + 1) * wide)
        from_v = slice(half * feat + n * wide, half * feat + (n + 1) * wide)
        v = jnp.concatenate([v_ref[i, :width, from_v] for i in range(NZ)], axis=0)
        acc = jnp.dot(rows, v, preferred_element_type=jnp.float32)
        for k, (s, u, at) in enumerate(places):
            part = acc[k * BATCH : (k + 1) * BATCH] + inner[k] * bank_ref[pl.ds(picks[k], 1), cols]
            if came:
                part = part + came[s][u, at, cols].astype(jnp.float32)
            out_refs[s][u, at, cols] = part.astype(out_refs[s].dtype)


def step_kernel(at_ref, info_ref, bank_ref, hid_ref, key_ref, value_ref):
    info = info_ref[...].astype(jnp.float32)
    fitness = 2.0 * info[:, 4:5] / (MEMBERS - 1) - 1.0
    fitness = fitness * (1.0 / MEMBERS**0.5)
    lane = lax.broadcasted_iota(jnp.int32, (info.shape[0], bank_ref.shape[0]), 1).astype(jnp.float32)
    pick = [(info[:, i : i + 1] == lane).astype(jnp.float32) for i in range(4)]
    hid = key_ref.shape[1]
    hidden = hid_ref[:, pl.ds(pl.multiple_of(at_ref[1], hid), hid)]

    def product(a, b, contract):
        dims = ((contract,), (0,)), ((), ())
        return lax.dot_general(a, b, dims, precision=HIGH, preferred_element_type=jnp.float32)

    pair_k = product(fitness * pick[0], pick[1], 0)
    pair_v = product(fitness * pick[2], pick[3], 0)
    key_ref[...] = product(bank_ref[...], product(pair_k, hidden, 1), 0)
    value_ref[...] = product(hidden, product(pair_v, bank_ref[...], 1), 0)


def cost(rows, depth, cols):
    return pl.CostEstimate(
        flops=2 * rows * depth * cols,
        bytes_accessed=2 * (rows * depth + depth * cols + rows * cols),
        transcendentals=0,
    )


def call(kernel, name, outs, specs, estimate, args, scratch=()):
    args = [pltpu.with_memory_space_constraint(a, pltpu.HBM) if s is HBM else a for a, s in zip(args, specs)]
    return pl.pallas_call(
        kernel,
        out_shape=[jax.ShapeDtypeStruct(*out) for out in outs],
        in_specs=specs,
        out_specs=[VMEM] * len(outs),
        scratch_shapes=scratch,
        compiler_params=pltpu.CompilerParams(vmem_limit_bytes=16 << 20),
        cost_estimate=estimate,
        name=name,
    )(*args)


def shards(inputs, mix, key_weight, value_weight, dim_bank, hidden_bank, member_picks, ranks):
    tok, feat = inputs.shape
    hid = key_weight.shape[1]
    half = hid // 2
    own = tok // BATCH
    core, x, z = lax.axis_index("core"), lax.axis_index("x"), lax.axis_index("z")
    block = (z * 2 + lax.axis_index("y_hi")) * hid
    at = jnp.stack([lax.axis_index("y_hi") * hid + core * half, block]).astype(jnp.int32)

    key_other, value_other, bank_other = swap(key_weight), swap(value_weight), swap(dim_bank)
    scratch = [
        pltpu.SMEM(member_picks.shape, jnp.int32), pltpu.SMEM(ranks.shape, jnp.int32),
        pltpu.VMEM(inputs.shape, jnp.bfloat16), pltpu.VMEM((1, feat), jnp.float32),
        pltpu.SemaphoreType.DMA((4,)),
    ]
    shifted = call(
        functools.partial(shift_kernel, NQ), "shift", [((NQ, tok + INFO, feat), jnp.bfloat16)],
        [HBM] * 4, cost(tok, 16, feat), (member_picks, ranks, inputs, mix[None]), scratch,
    )[0]
    same = lax.all_to_all(shifted, YQ, 0, 0)
    other = beside(same)
    tokens = same, other, swap(same), swap(other)
    members = NY * own
    info = jnp.stack([t[:, tok : tok + own, :128] for t in (same, other)]).reshape(members, 128)
    ids = info[:, :4].astype(jnp.int32)

    def hidden_half(array, axis):
        return lax.dynamic_slice_in_dim(array, core * half, half, axis)

    key_pack = jnp.concatenate([hidden_half(key_weight, 1), hidden_half(key_other, 1)], axis=0)
    key_all = lax.all_gather(key_pack, "z", axis=0)
    value_other, bank_other = lax.optimization_barrier((value_other, bank_other))
    value_pack = jnp.concatenate([hidden_half(value_weight, 0), hidden_half(value_other, 0)], axis=1)
    info = jnp.pad(info, ((0, INFO - members), (0, 2 * feat - 128)))
    value_all = lax.all_gather(jnp.concatenate([value_pack, info], axis=0), "z", axis=0)
    everyone = value_all[:, half : half + members, :128].reshape(NZ * members, 128)

    lo, hi = lax.rem(x, 2), x // 2
    f, g = jnp.where(core == 0, lax.rem(lo + hi, 2), hi), jnp.where(core == 0, hi, lo)
    turned = jnp.where(core == 0, 1 - g, g)
    order = [2 * f + g, 2 * f + 1 - g, 2 * (1 - f) + turned, 2 * (1 - f) + 1 - turned]
    order = jnp.stack(order).astype(jnp.int32)
    deep, wide, quarter = 2 * feat, NZ * half, NY * tok // NX
    low, high = ((quarter, wide), jnp.bfloat16), ((quarter, wide), jnp.float32)
    hidden = call(
        hidden_kernel, "hidden", [((hidden_bank.shape[0], wide), jnp.float32)], [SMEM, HBM],
        cost(hidden_bank.shape[0], 1, wide), (at, hidden_bank), [pltpu.SemaphoreType.DMA((NZ,))],
    )[0]

    def key_part(which, outs):
        return call(
            functools.partial(key_kernel, which), "key_part", outs,
            [SMEM] * 2 + [VMEM] * 8, cost(len(which) * quarter, deep, wide),
            (order, ids, *tokens, key_all, dim_bank, bank_other, hidden),
        )

    def local(kernel, name, *args):
        return call(kernel, name, [low], [VMEM] * len(args), cost(quarter, 4, wide), args)[0]

    came_first = exchange(key_part((2,), [low])[0], 0)
    came_second = exchange(key_part((3,), [low])[0], 0)
    following, kept = key_part((1, 0), [high, high])
    came_next = exchange(local(add_kernel, "add", following, came_first), 1)
    key_own = local(square_kernel, "square", kept, came_second, came_next)

    key_next = exchange(key_own, 1)
    key_own, key_next = lax.optimization_barrier((key_own, key_next))
    key_second = exchange(key_own, 0)
    key_first = exchange(key_next, 0)
    keys = key_own, key_next, key_first, key_second

    def out_part(half, bank, kept, *came):
        out = NQ, tok, feat
        return call(
            functools.partial(out_kernel, half), "out_part", [(out, kept), (out, jnp.bfloat16)],
            [SMEM] * 2 + [VMEM] * (NX + 3 + len(came)), cost(NY * tok, wide, feat),
            (order, ids, *keys, value_all, bank, hidden, *came),
        )

    came = [swap(rest) for rest in out_part(1, bank_other, jnp.bfloat16)]
    same, other = out_part(0, dim_bank, jnp.float32, *came)
    pieces = (same + beside(other).astype(jnp.float32)).astype(jnp.bfloat16)
    pieces, everyone = lax.optimization_barrier((pieces, everyone))
    pieces = lax.all_to_all(pieces, YQ, 0, 0)
    outputs = jnp.sum(pieces.astype(jnp.float32), axis=0).astype(jnp.bfloat16)
    key_step, value_step = call(
        step_kernel, "steps", [(key_weight.shape, jnp.float32), (value_weight.shape, jnp.float32)],
        [SMEM] + [VMEM] * 3, cost(hid, 512, feat), (at, everyone, dim_bank, hidden_bank),
    )
    return outputs, key_step, value_step


def solution(mesh):
    axes = ("z", "y_hi", "y_mid", "y_low", "x", "core")
    fine = Mesh(mesh.devices.reshape(8, 2, 2, 2, 4, 2), axes)
    pop, row, col = ("z", "y_hi"), ("y_mid", "y_low"), ("x", "core")
    in_specs = (
        P(pop + row, col),
        P(col),
        P(col, row + pop),
        P(row + pop, col),
        P(None, col),
        P(None, row),
        P(pop + row, None),
        P(pop + row),
    )
    out_specs = (P(pop + row, col), P(col, row + pop), P(row + pop, col))
    return jax.shard_map(shards, mesh=fine, in_specs=in_specs, out_specs=out_specs, check_vma=False)
```

time: 213 us -> 172 us (0.81)
  blocking collectives: 29.2 us -> 0 us
  starting transfers between devices: 38.1 us -> 60.4 us
  waiting for transfers between devices: 93.6 us -> 72.7 us
  Pallas kernels: 0 us -> 15.9 us
  matrix products: 15 us -> 0 us
  local copies, waits for them, and re-layouts: 14.8 us -> 4.25 us
  other arithmetic: 6.8 us -> 3.36 us
    all_to_all x4 -> x2, waiting for transfers between devices: 79.6 us -> 25.2 us  [the longest x1 13.7 us: shards(): same = lax.all_to_all(shifted, YQ, 0, 0)]
    ppermute x0 -> x8, waiting for transfers between devices: none -> 43.9 us  [the longest x6 31.3 us: exchange(): return lax.ppermute(x, ('x', 'core'), pairs)]
    all_to_all x1 -> x0, blocking collectives: 29.2 us -> none  [shards(): parts = lax.all_to_all(part, 'x', 0, 0)]
    ppermute x0 -> x8, starting transfers between devices: none -> 24.5 us  [the longest x6 18 us: exchange(): return lax.ppermute(x, ('x', 'core'), pairs)]
    pallas_call x0 -> x10, Pallas kernels: none -> 15.9 us  [call(): pl.pallas_call(kernel, out_shape=[jax.ShapeDtypeStruct(*out) for out in o...]
    dot_general x12 -> x0, matrix products: 15 us -> none  [the longest x1 4.3 us: shards(): lax.dot_general(tokens, key_all, (((1,), (1,)), ((), ())), preferred_elem...]
    all_gather x1 -> x2, waiting for transfers between devices: 13 us -> 0.02 us  [the longest x1 0.02 us: shards(): lax.all_gather(jnp.concatenate([value_pack, info], axis=0), 'z', axis=0)]
    all_to_all x4 -> x2, starting transfers between devices: 17.5 us -> 9.94 us  [the longest x1 6.45 us: shards(): pieces = lax.all_to_all(pieces, YQ, 0, 0)]
  transfers between devices with their start and end apart: 9 -> 19, of which waited for: 6 -> 14; matrix products, arithmetic and copies ran while one was open for 7% -> 1% of each run, Pallas kernels for 0% -> 7%
where the time goes in v4:
time: 172 us; the launch traced here: 171 us
  waiting for transfers between devices  72.7 us (42%)
  starting transfers between devices  60.4 us (35%)
  Pallas kernels  15.9 us (9%)
  between operations  14.4 us (8%)
  local copies, waits for them, and re-layouts  4.25 us (2%)
  other arithmetic  3.36 us (2%)
    ppermute x6, waiting for transfers between devices, exchange(): return lax.ppermute(x, ('x', 'core'), pairs)  31.3 us
    ppermute x7, starting transfers between devices, swap(): return lax.ppermute(x, 'core', [(0, 1), (1, 0)])  25.9 us
    ppermute x6, starting transfers between devices, exchange(): return lax.ppermute(x, ('x', 'core'), pairs)  18 us
    pallas_call x10, Pallas kernels, call(): pl.pallas_call(kernel, out_shape=[jax.ShapeDtypeStruct(*out) for out in o...  15.9 us
    all_to_all x1, waiting for transfers between devices, shards(): same = lax.all_to_all(shifted, YQ, 0, 0)  13.7 us
    ppermute x2, waiting for transfers between devices, beside(): return lax.ppermute(x, YQ + ('y_low', 'core'), pairs)  12.7 us
    all_to_all x1, waiting for transfers between devices, shards(): pieces = lax.all_to_all(pieces, YQ, 0, 0)  11.4 us
    ppermute x2, starting transfers between devices, beside(): return lax.ppermute(x, YQ + ('y_low', 'core'), pairs)  6.5 us
  transfers between devices with their start and end apart: 19, of which 14 were waited for; matrix products, arithmetic and copies ran while one was open for 1% of the time, Pallas kernels for 7%

profile of v4, /device:TPU:1, one launch (start us, length us, event | category | flops | bytes accessed | tf_op | source)
XLA Modules:
  0.0 171.0 jit_solution(8494885036028956231)
XLA Ops:
  7.2 0.0 copy-start.4
  7.2 0.0 copy-start.3
  7.2 0.0 all-gather.5.cloned.1.call-start
  7.2 8.9 %collective-permute-start.3 = (bf16[512,256]{1,0:T(8,128)(2,1)}, bf16[512,256]{1,0:T(8,128)(2,1)S(1)}, u32[]{:S(2)}, u32[]{:S(2)}) collective-permute-start(bf16[512,256]{1,0:T(8,128)(2,1)} %param.10), channel_id=1, source_target_pairs={{0,1},{1,0},{2,3},{3,2},{4,5},{5,4},{6,7},{7,6},{8,9},{9,8},{10,11... | collective-permute-start | bytes 786440 | tf_op jit(solution)/shard_map/ppermute | solution.py:28
  16.2 0.9 constant_dynamic-slice_fusion.3
  17.1 0.4 collective-permute-done.3
  17.5 0.7 pad_maximum_fusion
  18.2 0.0 all-gather.5.cloned.1.call-update
  18.3 1.8 %shift.1 = bf16[4,144,512]{2,1,0:T(8,128)(2,1)} custom-call(s32[2,4]{1,0:T(2,128)} %picks_hbm.1, s32[2]{0:T(128)} %ranks_hbm.1, bf16[128,512]{1,0:T(8,128)(2,1)} %x_hbm.1, f32[1,512]{1,0:T(1,128)} %bitcast.24), custom_call_target="tpu_custom_call" | custom-call | flops 2097152 | bytes 151552 | tf_op jit(solution)/shard_map/shift/pallas_call | solution.py:182
  20.1 3.5 %all-to-all-start = ((bf16[4,144,512]{2,1,0:T(8,128)(2,1)}), bf16[4,144,512]{2,1,0:T(8,128)(2,1)S(1)}, u32[]{:S(2)}, u32[]{:S(2)}) async-start(bf16[4,144,512]{2,1,0:T(8,128)(2,1)} %shift.1), calls=%async_computation | async-start | bytes 1179648 | tf_op jit(solution)/shard_map/all_to_all | solution.py:213
  23.6 0.0 all-gather.7.cloned.1.call-start
  23.7 0.0 copy-done.4
  23.7 2.3 %collective-permute-start.4 = (bf16[256,512]{1,0:T(8,128)(2,1)S(1)}, bf16[256,512]{1,0:T(8,128)(2,1)S(1)}, u32[]{:S(2)}, u32[]{:S(2)}) collective-permute-start(bf16[256,512]{1,0:T(8,128)(2,1)S(1)} %copy-done.4), channel_id=1, source_target_pairs={{0,1},{1,0},{2,3},{3,2},{4,5},{5,4},{6,7},{7,6},{8,9},{9,8},{10,11... | collective-permute-start | bytes 786440 | tf_op jit(solution)/shard_map/ppermute | solution.py:28
  26.0 13.7 %all-to-all-done.refs_0_ = bf16[4,144,512]{2,1,0:T(8,128)(2,1)S(1)} async-done(((bf16[4,144,512]{2,1,0:T(8,128)(2,1)}), bf16[4,144,512]{2,1,0:T(8,128)(2,1)S(1)}, u32[]{:S(2)}, u32[]{:S(2)}) %all-to-all-start) | async-done | bytes 589856 | tf_op jit(solution)/shard_map/all_to_all | solution.py:213
  39.7 1.9 %collective-permute-start = (bf16[4,144,512]{2,1,0:T(8,128)(2,1)S(1)}, bf16[4,144,512]{2,1,0:T(8,128)(2,1)S(1)}, u32[]{:S(2)}, u32[]{:S(2)}) collective-permute-start(bf16[4,144,512]{2,1,0:T(8,128)(2,1)S(1)} %all-to-all-done.refs_0_), channel_id=1, source_target_pairs={{0,8},{1,57},{8,0},{9,17},{16,24},{17,9},{24,16},{25,33},{32,40},{... | collective-permute-start | bytes 1769480 | tf_op jit(solution)/shard_map/ppermute | solution.py:46
  41.6 0.0 copy-done.3
  41.6 2.9 %collective-permute-start.5 = (f32[64,512]{1,0:T(8,128)S(1)}, f32[64,512]{1,0:T(8,128)S(1)}, u32[]{:S(2)}, u32[]{:S(2)}) collective-permute-start(f32[64,512]{1,0:T(8,128)S(1)} %copy-done.3), channel_id=1, source_target_pairs={{0,1},{1,0},{2,3},{3,2},{4,5},{5,4},{6,7},{7,6},{8,9},{9,8},{10,11... | collective-permute-start | bytes 393224 | tf_op jit(solution)/shard_map/ppermute | solution.py:28
  44.5 0.9 collective-permute-done.5.refs_6_.refs_5_
  45.5 0.0 collective-permute-done.4
  45.5 6.0 %collective-permute-done.refs_1_ = bf16[4,144,512]{2,1,0:T(8,128)(2,1)S(1)} collective-permute-done((bf16[4,144,512]{2,1,0:T(8,128)(2,1)S(1)}, bf16[4,144,512]{2,1,0:T(8,128)(2,1)S(1)}, u32[]{:S(2)}, u32[]{:S(2)}) %collective-permute-start) | collective-permute-done | bytes 589856 | tf_op jit(solution)/shard_map/ppermute | solution.py:46
  51.5 0.7 fusion.1
  52.3 0.0 all-gather.7.cloned.1.call-update
  52.3 2.8 %collective-permute-start.1 = (bf16[4,144,512]{2,1,0:T(8,128)(2,1)S(1)}, bf16[4,144,512]{2,1,0:T(8,128)(2,1)S(1)}, u32[]{:S(2)}, u32[]{:S(2)}) collective-permute-start(bf16[4,144,512]{2,1,0:T(8,128)(2,1)S(1)} %all-to-all-done.refs_0_), channel_id=1, source_target_pairs={{0,1},{1,0},{2,3},{3,2},{4,5},{5,4},{6,7},{7,6},{8,9},{9,8},{10,11... | collective-permute-start | bytes 1769480 | tf_op jit(solution)/shard_map/ppermute | solution.py:28
  55.1 1.9 %collective-permute-start.2 = (bf16[4,144,512]{2,1,0:T(8,128)(2,1)S(1)}, bf16[4,144,512]{2,1,0:T(8,128)(2,1)S(1)}, u32[]{:S(2)}, u32[]{:S(2)}) collective-permute-start(bf16[4,144,512]{2,1,0:T(8,128)(2,1)S(1)} %collective-permute-done.refs_1_), channel_id=1, source_target_pairs={{0,1},{1,0},{2,3},{3,2},{4,5},{5,4},{6,7},{7,6},{8,9},{9,8},{10,11... | collective-permute-start | bytes 1769480 | tf_op jit(solution)/shard_map/ppermute | solution.py:28
  57.1 0.1 pad_add_fusion.1.at_ref
  57.1 1.5 hidden.1.refs_7_.refs_6_
  58.7 0.1 pad_add_fusion.order_ref
  58.7 0.0 collective-permute-done.1.refs_2_
  58.7 0.3 collective-permute-done.2.refs_3_
  59.0 1.6 copy-done
  60.6 1.4 key_part.5
  62.0 3.3 %collective-permute-start.7 = (bf16[256,1024]{1,0:T(8,128)(2,1)S(1)}, bf16[256,1024]{1,0:T(8,128)(2,1)S(1)}, u32[]{:S(2)}, u32[]{:S(2)}) collective-permute-start(bf16[256,1024]{1,0:T(8,128)(2,1)S(1)} %key_part.5), channel_id=1, source_target_pairs={{0,2},{1,7},{2,0},{3,5},{4,6},{5,3},{6,4},{7,1},{8,10},{9,15},{10,... | collective-permute-start | bytes 1572872 | tf_op jit(solution)/shard_map/ppermute | solution.py:37
  65.3 1.4 key_part.4
  66.7 3.2 %collective-permute-start.6 = (bf16[256,1024]{1,0:T(8,128)(2,1)S(1)}, bf16[256,1024]{1,0:T(8,128)(2,1)S(1)}, u32[]{:S(2)}, u32[]{:S(2)}) collective-permute-start(bf16[256,1024]{1,0:T(8,128)(2,1)S(1)} %key_part.4), channel_id=1, source_target_pairs={{0,2},{1,7},{2,0},{3,5},{4,6},{5,3},{6,4},{7,1},{8,10},{9,15},{10,... | collective-permute-start | bytes 1572872 | tf_op jit(solution)/shard_map/ppermute | solution.py:37
  69.9 2.0 %key_part.3 = (f32[256,1024]{1,0:T(8,128)S(1)}, f32[256,1024]{1,0:T(8,128)S(1)}) custom-call(s32[4]{0:T(128)S(1)} %pad_add_fusion.order_ref, s32[16,4]{1,0:T(8,128)S(1)} %slice_convert_fusion.ids_ref, bf16[4,144,512]{2,1,0:T(8,128)(2,1)S(1)} %all-to-all-done.refs_0_, bf16[4,144,512]{2,1,0:T(8,128)(2,1)S(1)} %collective-permute-done.refs_1_, ...), custom_call_target="tpu_custom_call" | custom-call | flops 1073741824 | bytes 4194304 | tf_op jit(solution)/shard_map/key_part/pallas_call | solution.py:182
  71.9 1.2 collective-permute-done.7.came_ref
  73.1 0.1 add.52
  73.2 1.9 %collective-permute-start.8 = (bf16[256,1024]{1,0:T(8,128)(2,1)S(1)}, bf16[256,1024]{1,0:T(8,128)(2,1)S(1)}, u32[]{:S(2)}, u32[]{:S(2)}) collective-permute-start(bf16[256,1024]{1,0:T(8,128)(2,1)S(1)} %add.52), channel_id=1, source_target_pairs={{0,6},{1,3},{2,4},{3,1},{4,2},{5,7},{6,0},{7,5},{8,14},{9,11},{10,... | collective-permute-start | bytes 1572872 | tf_op jit(solution)/shard_map/ppermute | solution.py:37
  75.2 3.6 %collective-permute-done.6.first_ref = bf16[256,1024]{1,0:T(8,128)(2,1)S(1)} collective-permute-done((bf16[256,1024]{1,0:T(8,128)(2,1)S(1)}, bf16[256,1024]{1,0:T(8,128)(2,1)S(1)}, u32[]{:S(2)}, u32[]{:S(2)}) %collective-permute-start.6) | collective-permute-done | bytes 524320 | tf_op jit(solution)/shard_map/ppermute | solution.py:37
  78.8 9.0 %collective-permute-done.8.second_ref = bf16[256,1024]{1,0:T(8,128)(2,1)S(1)} collective-permute-done((bf16[256,1024]{1,0:T(8,128)(2,1)S(1)}, bf16[256,1024]{1,0:T(8,128)(2,1)S(1)}, u32[]{:S(2)}, u32[]{:S(2)}) %collective-permute-start.8) | collective-permute-done | bytes 524320 | tf_op jit(solution)/shard_map/ppermute | solution.py:37
  87.8 0.2 square.1.refs_0_
  88.0 3.1 %collective-permute-start.9 = (bf16[256,1024]{1,0:T(8,128)(2,1)S(1)}, bf16[256,1024]{1,0:T(8,128)(2,1)S(1)}, u32[]{:S(2)}, u32[]{:S(2)}) collective-permute-start(bf16[256,1024]{1,0:T(8,128)(2,1)S(1)} %square.1.refs_0_), channel_id=1, source_target_pairs={{0,6},{1,3},{2,4},{3,1},{4,2},{5,7},{6,0},{7,5},{8,14},{9,11},{10,... | collective-permute-start | bytes 1572872 | tf_op jit(solution)/shard_map/ppermute | solution.py:37
  91.1 7.2 %collective-permute-done.9.refs_1_ = bf16[256,1024]{1,0:T(8,128)(2,1)S(1)} collective-permute-done((bf16[256,1024]{1,0:T(8,128)(2,1)S(1)}, bf16[256,1024]{1,0:T(8,128)(2,1)S(1)}, u32[]{:S(2)}, u32[]{:S(2)}) %collective-permute-start.9) | collective-permute-done | bytes 524320 | tf_op jit(solution)/shard_map/ppermute | solution.py:37
  98.3 4.3 %collective-permute-start.10 = (bf16[256,1024]{1,0:T(8,128)(2,1)S(1)}, bf16[256,1024]{1,0:T(8,128)(2,1)S(1)}, u32[]{:S(2)}, u32[]{:S(2)}) collective-permute-start(bf16[256,1024]{1,0:T(8,128)(2,1)S(1)} %collective-permute-done.9.refs_1_), channel_id=1, source_target_pairs={{0,2},{1,7},{2,0},{3,5},{4,6},{5,3},{6,4},{7,1},{8,10},{9,15},{10,... | collective-permute-start | bytes 1572872 | tf_op jit(solution)/shard_map/ppermute | solution.py:37
  102.6 2.2 %collective-permute-start.11 = (bf16[256,1024]{1,0:T(8,128)(2,1)S(1)}, bf16[256,1024]{1,0:T(8,128)(2,1)S(1)}, u32[]{:S(2)}, u32[]{:S(2)}) collective-permute-start(bf16[256,1024]{1,0:T(8,128)(2,1)S(1)} %square.1.refs_0_), channel_id=1, source_target_pairs={{0,2},{1,7},{2,0},{3,5},{4,6},{5,3},{6,4},{7,1},{8,10},{9,15},{10,... | collective-permute-start | bytes 1572872 | tf_op jit(solution)/shard_map/ppermute | solution.py:37
  104.8 0.0 all-gather.7.cloned.1.call-done
  104.8 4.6 %collective-permute-done.10.refs_2_ = bf16[256,1024]{1,0:T(8,128)(2,1)S(1)} collective-permute-done((bf16[256,1024]{1,0:T(8,128)(2,1)S(1)}, bf16[256,1024]{1,0:T(8,128)(2,1)S(1)}, u32[]{:S(2)}, u32[]{:S(2)}) %collective-permute-start.10) | collective-permute-done | bytes 524320 | tf_op jit(solution)/shard_map/ppermute | solution.py:37
  109.4 5.6 %collective-permute-done.11.refs_3_ = bf16[256,1024]{1,0:T(8,128)(2,1)S(1)} collective-permute-done((bf16[256,1024]{1,0:T(8,128)(2,1)S(1)}, bf16[256,1024]{1,0:T(8,128)(2,1)S(1)}, u32[]{:S(2)}, u32[]{:S(2)}) %collective-permute-start.11) | collective-permute-done | bytes 524320 | tf_op jit(solution)/shard_map/ppermute | solution.py:37
  115.1 1.7 copy-done.1
  116.7 2.2 %out_part.2 = (bf16[4,128,512]{2,1,0:T(8,128)(2,1)S(1)}, bf16[4,128,512]{2,1,0:T(8,128)(2,1)S(1)}) custom-call(s32[4]{0:T(128)S(1)} %pad_add_fusion.order_ref, s32[16,4]{1,0:T(8,128)S(1)} %slice_convert_fusion.ids_ref, bf16[256,1024]{1,0:T(8,128)(2,1)S(1)} %square.1.refs_0_, bf16[256,1024]{1,0:T(8,128)(2,1)S(1)} %collective-permute-done.9.refs_1_, ...), custom_call_target="tpu_custom_call" | custom-call | flops 1073741824 | bytes 4194304 | tf_op jit(solution)/shard_map/out_part/pallas_call | solution.py:182
  118.9 5.2 %collective-permute-start.12 = (bf16[4,128,512]{2,1,0:T(8,128)(2,1)S(1)}, bf16[4,128,512]{2,1,0:T(8,128)(2,1)S(1)}, u32[]{:S(2)}, u32[]{:S(2)}) collective-permute-start(bf16[4,128,512]{2,1,0:T(8,128)(2,1)S(1)} %get-tuple-element.23), channel_id=1, source_target_pairs={{0,1},{1,0},{2,3},{3,2},{4,5},{5,4},{6,7},{7,6},{8,9},{9,8},{10,11... | collective-permute-start | bytes 1572872 | tf_op jit(solution)/shard_map/ppermute | solution.py:28
  124.1 1.9 %collective-permute-start.13 = (bf16[4,128,512]{2,1,0:T(8,128)(2,1)S(1)}, bf16[4,128,512]{2,1,0:T(8,128)(2,1)S(1)}, u32[]{:S(2)}, u32[]{:S(2)}) collective-permute-start(bf16[4,128,512]{2,1,0:T(8,128)(2,1)S(1)} %get-tuple-element.24), channel_id=1, source_target_pairs={{0,1},{1,0},{2,3},{3,2},{4,5},{5,4},{6,7},{7,6},{8,9},{9,8},{10,11... | collective-permute-start | bytes 1572872 | tf_op jit(solution)/shard_map/ppermute | solution.py:28
  126.1 0.0 collective-permute-done.12.refs_7_
  126.1 1.9 %collective-permute-done.13.refs_8_ = bf16[4,128,512]{2,1,0:T(8,128)(2,1)S(1)} collective-permute-done((bf16[4,128,512]{2,1,0:T(8,128)(2,1)S(1)}, bf16[4,128,512]{2,1,0:T(8,128)(2,1)S(1)}, u32[]{:S(2)}, u32[]{:S(2)}) %collective-permute-start.13) | collective-permute-done | bytes 524320 | tf_op jit(solution)/shard_map/ppermute | solution.py:28
  127.9 2.3 %out_part.3 = (f32[4,128,512]{2,1,0:T(8,128)S(1)}, bf16[4,128,512]{2,1,0:T(8,128)(2,1)S(1)}) custom-call(s32[4]{0:T(128)S(1)} %pad_add_fusion.order_ref, s32[16,4]{1,0:T(8,128)S(1)} %slice_convert_fusion.ids_ref, bf16[256,1024]{1,0:T(8,128)(2,1)S(1)} %square.1.refs_0_, bf16[256,1024]{1,0:T(8,128)(2,1)S(1)} %collective-permute-done.9.refs_1_, ...), custom_call_target="tpu_custom_call" | custom-call | flops 1073741824 | bytes 4194304 | tf_op jit(solution)/shard_map/out_part/pallas_call | solution.py:182
  130.3 0.0 copy-start.2
  130.3 4.6 %collective-permute-start.14 = (bf16[4,128,512]{2,1,0:T(8,128)(2,1)S(1)}, bf16[4,128,512]{2,1,0:T(8,128)(2,1)S(1)}, u32[]{:S(2)}, u32[]{:S(2)}) collective-permute-start(bf16[4,128,512]{2,1,0:T(8,128)(2,1)S(1)} %get-tuple-element.26), channel_id=1, source_target_pairs={{0,8},{1,57},{8,0},{9,17},{16,24},{17,9},{24,16},{25,33},{32,40},{... | collective-permute-start | bytes 1572872 | tf_op jit(solution)/shard_map/ppermute | solution.py:46
  134.9 6.6 %collective-permute-done.14 = bf16[4,128,512]{2,1,0:T(8,128)(2,1)S(1)} collective-permute-done((bf16[4,128,512]{2,1,0:T(8,128)(2,1)S(1)}, bf16[4,128,512]{2,1,0:T(8,128)(2,1)S(1)}, u32[]{:S(2)}, u32[]{:S(2)}) %collective-permute-start.14) | collective-permute-done | bytes 524320 | tf_op jit(solution)/shard_map/ppermute | solution.py:46
  141.5 1.0 add_convert_fusion
  142.5 6.4 %all-to-all-start.1 = ((bf16[4,128,512]{2,1,0:T(8,128)(2,1)}), bf16[4,128,512]{2,1,0:T(8,128)(2,1)S(1)}, u32[]{:S(2)}, u32[]{:S(2)}) async-start(bf16[4,128,512]{2,1,0:T(8,128)(2,1)} %add_convert_fusion), calls=%async_computation.1 | async-start | bytes 1048576 | tf_op jit(solution)/shard_map/all_to_all | solution.py:277
  149.0 0.0 copy-done.2
  149.0 3.0 %steps.1 = (f32[512,256]{1,0:T(8,128)}, f32[256,512]{1,0:T(8,128)}) custom-call(s32[2]{0:T(128)S(1)} %pad_add_fusion.1.at_ref, bf16[128,128]{1,0:T(8,128)(2,1)S(1)} %bitcast.21, f32[64,512]{1,0:T(8,128)S(1)} %copy-done.3, f32[64,4096]{1,0:T(8,128)S(1)} %copy-done.2), custom_call_target="tpu_custom_call" | custom-call | flops 134217728 | bytes 1048576 | tf_op jit(solution)/shard_map/steps/pallas_call | solution.py:182
  152.0 11.4 %all-to-all-done.1 = bf16[4,128,512]{2,1,0:T(8,128)(2,1)S(1)} async-done(((bf16[4,128,512]{2,1,0:T(8,128)(2,1)}), bf16[4,128,512]{2,1,0:T(8,128)(2,1)S(1)}, u32[]{:S(2)}, u32[]{:S(2)}) %all-to-all-start.1) | async-done | bytes 524320 | tf_op jit(solution)/shard_map/all_to_all | solution.py:277
  163.4 0.7 reduce_sum.12
  (11 shorter events, 0.1 us)
Async XLA Ops:
  7.2 16.5 %copy-start.4 = (bf16[256,512]{1,0:T(8,128)(2,1)S(1)}, bf16[256,512]{1,0:T(8,128)(2,1)}, u32[]{:S(2)}) copy-start(bf16[256,512]{1,0:T(8,128)(2,1)} %param.11) | copy-start | bytes 786436
  7.2 34.4 %copy-start.3 = (f32[64,512]{1,0:T(8,128)S(1)}, f32[64,512]{1,0:T(8,128)}, u32[]{:S(2)}) copy-start(f32[64,512]{1,0:T(8,128)} %bank_ref.1) | copy-start | bytes 393220
  7.2 51.8 %all-gather.5.cloned.1.call-start = ((), (), s32[]{:S(2)}) async-start(), calls=%async_computation.2 | async-start | bytes 2359296 | tf_op jit(solution)/shard_map/all_gather | solution.py:224
  7.2 10.3 %collective-permute-start.3 = (bf16[512,256]{1,0:T(8,128)(2,1)}, bf16[512,256]{1,0:T(8,128)(2,1)S(1)}, u32[]{:S(2)}, u32[]{:S(2)}) collective-permute-start(bf16[512,256]{1,0:T(8,128)(2,1)} %param.10), channel_id=1, source_target_pairs={{0,1},{1,0},{2,3},{3,2},{4,5},{5,4},{6,7},{7,6},{8,9},{9,8},{10,11... | collective-permute-start | bytes 786440 | tf_op jit(solution)/shard_map/ppermute | solution.py:28
  20.1 19.6 %all-to-all-start = ((bf16[4,144,512]{2,1,0:T(8,128)(2,1)}), bf16[4,144,512]{2,1,0:T(8,128)(2,1)S(1)}, u32[]{:S(2)}, u32[]{:S(2)}) async-start(bf16[4,144,512]{2,1,0:T(8,128)(2,1)} %shift.1), calls=%async_computation | async-start | bytes 1179648 | tf_op jit(solution)/shard_map/all_to_all | solution.py:213
  23.6 81.2 %all-gather.7.cloned.1.call-start = ((), (), s32[]{:S(2)}) async-start(), calls=%async_computation.3 | async-start | bytes 2654208 | tf_op jit(solution)/shard_map/all_gather | solution.py:228
  23.7 21.8 %collective-permute-start.4 = (bf16[256,512]{1,0:T(8,128)(2,1)S(1)}, bf16[256,512]{1,0:T(8,128)(2,1)S(1)}, u32[]{:S(2)}, u32[]{:S(2)}) collective-permute-start(bf16[256,512]{1,0:T(8,128)(2,1)S(1)} %copy-done.4), channel_id=1, source_target_pairs={{0,1},{1,0},{2,3},{3,2},{4,5},{5,4},{6,7},{7,6},{8,9},{9,8},{10,11... | collective-permute-start | bytes 786440 | tf_op jit(solution)/shard_map/ppermute | solution.py:28
  39.7 11.8 %collective-permute-start = (bf16[4,144,512]{2,1,0:T(8,128)(2,1)S(1)}, bf16[4,144,512]{2,1,0:T(8,128)(2,1)S(1)}, u32[]{:S(2)}, u32[]{:S(2)}) collective-permute-start(bf16[4,144,512]{2,1,0:T(8,128)(2,1)S(1)} %all-to-all-done.refs_0_), channel_id=1, source_target_pairs={{0,8},{1,57},{8,0},{9,17},{16,24},{17,9},{24,16},{25,33},{32,40},{... | collective-permute-start | bytes 1769480 | tf_op jit(solution)/shard_map/ppermute | solution.py:46
  41.6 3.8 %collective-permute-start.5 = (f32[64,512]{1,0:T(8,128)S(1)}, f32[64,512]{1,0:T(8,128)S(1)}, u32[]{:S(2)}, u32[]{:S(2)}) collective-permute-start(f32[64,512]{1,0:T(8,128)S(1)} %copy-done.3), channel_id=1, source_target_pairs={{0,1},{1,0},{2,3},{3,2},{4,5},{5,4},{6,7},{7,6},{8,9},{9,8},{10,11... | collective-permute-start | bytes 393224 | tf_op jit(solution)/shard_map/ppermute | solution.py:28
  52.3 6.4 %collective-permute-start.1 = (bf16[4,144,512]{2,1,0:T(8,128)(2,1)S(1)}, bf16[4,144,512]{2,1,0:T(8,128)(2,1)S(1)}, u32[]{:S(2)}, u32[]{:S(2)}) collective-permute-start(bf16[4,144,512]{2,1,0:T(8,128)(2,1)S(1)} %all-to-all-done.refs_0_), channel_id=1, source_target_pairs={{0,1},{1,0},{2,3},{3,2},{4,5},{5,4},{6,7},{7,6},{8,9},{9,8},{10,11... | collective-permute-start | bytes 1769480 | tf_op jit(solution)/shard_map/ppermute | solution.py:28
  55.1 3.9 %collective-permute-start.2 = (bf16[4,144,512]{2,1,0:T(8,128)(2,1)S(1)}, bf16[4,144,512]{2,1,0:T(8,128)(2,1)S(1)}, u32[]{:S(2)}, u32[]{:S(2)}) collective-permute-start(bf16[4,144,512]{2,1,0:T(8,128)(2,1)S(1)} %collective-permute-done.refs_1_), channel_id=1, source_target_pairs={{0,1},{1,0},{2,3},{3,2},{4,5},{5,4},{6,7},{7,6},{8,9},{9,8},{10,11... | collective-permute-start | bytes 1769480 | tf_op jit(solution)/shard_map/ppermute | solution.py:28
  59.0 1.6 copy-start
  62.0 11.1 %collective-permute-start.7 = (bf16[256,1024]{1,0:T(8,128)(2,1)S(1)}, bf16[256,1024]{1,0:T(8,128)(2,1)S(1)}, u32[]{:S(2)}, u32[]{:S(2)}) collective-permute-start(bf16[256,1024]{1,0:T(8,128)(2,1)S(1)} %key_part.5), channel_id=1, source_target_pairs={{0,2},{1,7},{2,0},{3,5},{4,6},{5,3},{6,4},{7,1},{8,10},{9,15},{10,... | collective-permute-start | bytes 1572872 | tf_op jit(solution)/shard_map/ppermute | solution.py:37
  66.7 12.0 %collective-permute-start.6 = (bf16[256,1024]{1,0:T(8,128)(2,1)S(1)}, bf16[256,1024]{1,0:T(8,128)(2,1)S(1)}, u32[]{:S(2)}, u32[]{:S(2)}) collective-permute-start(bf16[256,1024]{1,0:T(8,128)(2,1)S(1)} %key_part.4), channel_id=1, source_target_pairs={{0,2},{1,7},{2,0},{3,5},{4,6},{5,3},{6,4},{7,1},{8,10},{9,15},{10,... | collective-permute-start | bytes 1572872 | tf_op jit(solution)/shard_map/ppermute | solution.py:37
  73.2 14.5 %collective-permute-start.8 = (bf16[256,1024]{1,0:T(8,128)(2,1)S(1)}, bf16[256,1024]{1,0:T(8,128)(2,1)S(1)}, u32[]{:S(2)}, u32[]{:S(2)}) collective-permute-start(bf16[256,1024]{1,0:T(8,128)(2,1)S(1)} %add.52), channel_id=1, source_target_pairs={{0,6},{1,3},{2,4},{3,1},{4,2},{5,7},{6,0},{7,5},{8,14},{9,11},{10,... | collective-permute-start | bytes 1572872 | tf_op jit(solution)/shard_map/ppermute | solution.py:37
  88.0 10.3 %collective-permute-start.9 = (bf16[256,1024]{1,0:T(8,128)(2,1)S(1)}, bf16[256,1024]{1,0:T(8,128)(2,1)S(1)}, u32[]{:S(2)}, u32[]{:S(2)}) collective-permute-start(bf16[256,1024]{1,0:T(8,128)(2,1)S(1)} %square.1.refs_0_), channel_id=1, source_target_pairs={{0,6},{1,3},{2,4},{3,1},{4,2},{5,7},{6,0},{7,5},{8,14},{9,11},{10,... | collective-permute-start | bytes 1572872 | tf_op jit(solution)/shard_map/ppermute | solution.py:37
  98.3 11.1 %collective-permute-start.10 = (bf16[256,1024]{1,0:T(8,128)(2,1)S(1)}, bf16[256,1024]{1,0:T(8,128)(2,1)S(1)}, u32[]{:S(2)}, u32[]{:S(2)}) collective-permute-start(bf16[256,1024]{1,0:T(8,128)(2,1)S(1)} %collective-permute-done.9.refs_1_), channel_id=1, source_target_pairs={{0,2},{1,7},{2,0},{3,5},{4,6},{5,3},{6,4},{7,1},{8,10},{9,15},{10,... | collective-permute-start | bytes 1572872 | tf_op jit(solution)/shard_map/ppermute | solution.py:37
  102.6 12.4 %collective-permute-start.11 = (bf16[256,1024]{1,0:T(8,128)(2,1)S(1)}, bf16[256,1024]{1,0:T(8,128)(2,1)S(1)}, u32[]{:S(2)}, u32[]{:S(2)}) collective-permute-start(bf16[256,1024]{1,0:T(8,128)(2,1)S(1)} %square.1.refs_0_), channel_id=1, source_target_pairs={{0,2},{1,7},{2,0},{3,5},{4,6},{5,3},{6,4},{7,1},{8,10},{9,15},{10,... | collective-permute-start | bytes 1572872 | tf_op jit(solution)/shard_map/ppermute | solution.py:37
  115.1 1.7 copy-start.1
  118.9 7.2 %collective-permute-start.12 = (bf16[4,128,512]{2,1,0:T(8,128)(2,1)S(1)}, bf16[4,128,512]{2,1,0:T(8,128)(2,1)S(1)}, u32[]{:S(2)}, u32[]{:S(2)}) collective-permute-start(bf16[4,128,512]{2,1,0:T(8,128)(2,1)S(1)} %get-tuple-element.23), channel_id=1, source_target_pairs={{0,1},{1,0},{2,3},{3,2},{4,5},{5,4},{6,7},{7,6},{8,9},{9,8},{10,11... | collective-permute-start | bytes 1572872 | tf_op jit(solution)/shard_map/ppermute | solution.py:28
  124.1 3.8 %collective-permute-start.13 = (bf16[4,128,512]{2,1,0:T(8,128)(2,1)S(1)}, bf16[4,128,512]{2,1,0:T(8,128)(2,1)S(1)}, u32[]{:S(2)}, u32[]{:S(2)}) collective-permute-start(bf16[4,128,512]{2,1,0:T(8,128)(2,1)S(1)} %get-tuple-element.24), channel_id=1, source_target_pairs={{0,1},{1,0},{2,3},{3,2},{4,5},{5,4},{6,7},{7,6},{8,9},{9,8},{10,11... | collective-permute-start | bytes 1572872 | tf_op jit(solution)/shard_map/ppermute | solution.py:28
  130.3 18.7 %copy-start.2 = (f32[64,4096]{1,0:T(8,128)S(1)}, f32[64,4096]{1,0:T(8,128)}, u32[]{:S(2)}) copy-start(f32[64,4096]{1,0:T(8,128)} %hid_ref.1) | copy-start | bytes 3145732
  130.3 11.3 %collective-permute-start.14 = (bf16[4,128,512]{2,1,0:T(8,128)(2,1)S(1)}, bf16[4,128,512]{2,1,0:T(8,128)(2,1)S(1)}, u32[]{:S(2)}, u32[]{:S(2)}) collective-permute-start(bf16[4,128,512]{2,1,0:T(8,128)(2,1)S(1)} %get-tuple-element.26), channel_id=1, source_target_pairs={{0,8},{1,57},{8,0},{9,17},{16,24},{17,9},{24,16},{25,33},{32,40},{... | collective-permute-start | bytes 1572872 | tf_op jit(solution)/shard_map/ppermute | solution.py:46
  142.5 20.9 %all-to-all-start.1 = ((bf16[4,128,512]{2,1,0:T(8,128)(2,1)}), bf16[4,128,512]{2,1,0:T(8,128)(2,1)S(1)}, u32[]{:S(2)}, u32[]{:S(2)}) async-start(bf16[4,128,512]{2,1,0:T(8,128)(2,1)} %add_convert_fusion), calls=%async_computation.1 | async-start | bytes 1048576 | tf_op jit(solution)/shard_map/all_to_all | solution.py:277
Sparse Core Ops, SparseCore 0:
  18.4 39.5 all-gather.4
  60.6 44.0 all-gather.6

commit v5 on v4

--- a/solution.py
+++ b/solution.py
@@ -21,6 +21,7 @@
 SIGMA_V = 0.5 / FF**0.5
 VMEM = pl.BlockSpec(memory_space=pltpu.VMEM)
 HBM = pl.BlockSpec(memory_space=pltpu.HBM)
+ANY = pl.BlockSpec(memory_space=pl.ANY)
 SMEM = pl.BlockSpec(memory_space=pltpu.SMEM)
 
 
@@ -120,34 +121,41 @@
     out_ref[...] = (jnp.maximum(total, 0.0) ** 2).astype(jnp.bfloat16)
 
 
-def out_kernel(half, order_ref, ids_ref, *refs):
-    keys, (v_ref, bank_ref, hid_ref), rest = refs[:NX], refs[NX : NX + 3], refs[NX + 3 :]
-    came, out_refs = rest[:-2], rest[-2:]
-    feat, width = out_refs[0].shape[2], hid_ref.shape[1] // NZ
-    tok = out_refs[0].shape[1]
+def out_kernel(half, order, order_ref, ids_ref, *refs):
+    keys, (v_ref, bank_ref, hid_ref, *_, out_ref) = refs[: len(order)], refs[len(order) :]
+    feat, width = out_ref.shape[3], hid_ref.shape[1] // NZ
+    tok = out_ref.shape[2]
     own, wide = tok // BATCH, 256
     inner, picks, places = [], [], []
-    for i in range(NX):
+    for i, o in enumerate(order):
         for s in range(2):
             for j in range(own):
-                m = (s * NX + order_ref[i]) * own + j
+                m = (s * NX + order_ref[o]) * own + j
                 fac_c = hid_ref[pl.ds(ids_ref[m, 2], 1), :]
                 at = s * tok + j * BATCH
                 part = keys[i][at : at + BATCH, :].astype(jnp.float32)
                 inner.append(SIGMA_V * jnp.sum(part * fac_c, axis=1, keepdims=True))
                 picks.append(ids_ref[m, 3])
-                places.append((s, order_ref[i], slice(j * BATCH, (j + 1) * BATCH)))
+                places.append((i, s, slice(j * BATCH, (j + 1) * BATCH)))
     rows = jnp.concatenate([k[...] for k in keys], axis=0)
     for n in range(feat // wide):
         cols = slice(n * wide, (n + 1) * wide)
         from_v = slice(half * feat + n * wide, half * feat + (n + 1) * wide)
         v = jnp.concatenate([v_ref[i, :width, from_v] for i in range(NZ)], axis=0)
         acc = jnp.dot(rows, v, preferred_element_type=jnp.float32)
-        for k, (s, u, at) in enumerate(places):
+        for k, (i, s, at) in enumerate(places):
             part = acc[k * BATCH : (k + 1) * BATCH] + inner[k] * bank_ref[pl.ds(picks[k], 1), cols]
-            if came:
-                part = part + came[s][u, at, cols].astype(jnp.float32)
-            out_refs[s][u, at, cols] = part.astype(out_refs[s].dtype)
+            out_ref[i, s, at, cols] = part.astype(out_ref.dtype)
+
+
+def place_kernel(orders, order_ref, at_ref, *refs):
+    parts, out_ref = refs[:-1], refs[-1]
+    twins = (0, 2, 1)
+    for order, mine_ref, came_ref in zip(orders, parts[::2], parts[1::2]):
+        for i, o in enumerate(order):
+            for s in range(2):
+                total = mine_ref[i, s] + came_ref[twins[i], s].astype(jnp.float32)
+                out_ref[2 * order_ref[o] + lax.rem(at_ref[2] + s, 2)] = total.astype(jnp.bfloat16)
 
 
 def step_kernel(at_ref, info_ref, bank_ref, hid_ref, key_ref, value_ref):
@@ -198,7 +206,8 @@
     own = tok // BATCH
     core, x, z = lax.axis_index("core"), lax.axis_index("x"), lax.axis_index("z")
     block = (z * 2 + lax.axis_index("y_hi")) * hid
-    at = jnp.stack([lax.axis_index("y_hi") * hid + core * half, block]).astype(jnp.int32)
+    at = [lax.axis_index("y_hi") * hid + core * half, block, lax.axis_index("y_low")]
+    at = jnp.stack(at).astype(jnp.int32)
 
     key_other, value_other, bank_other = swap(key_weight), swap(value_weight), swap(dim_bank)
     scratch = [
@@ -231,7 +240,9 @@
     lo, hi = lax.rem(x, 2), x // 2
     f, g = jnp.where(core == 0, lax.rem(lo + hi, 2), hi), jnp.where(core == 0, hi, lo)
     turned = jnp.where(core == 0, 1 - g, g)
-    order = [2 * f + g, 2 * f + 1 - g, 2 * (1 - f) + turned, 2 * (1 - f) + 1 - turned]
+    order = []
+    for upper, lower in ((f, g), (f, 1 - g), (1 - f, turned), (1 - f, 1 - turned)):
+        order.append(jnp.where(core == 0, 2 * lower + lax.rem(upper + lower, 2), 2 * upper + lower))
     order = jnp.stack(order).astype(jnp.int32)
     deep, wide, quarter = 2 * feat, NZ * half, NY * tok // NX
     low, high = ((quarter, wide), jnp.bfloat16), ((quarter, wide), jnp.float32)
@@ -256,25 +267,32 @@
     came_next = exchange(local(add_kernel, "add", following, came_first), 1)
     key_own = local(square_kernel, "square", kept, came_second, came_next)
 
+    before, after = NX - 1 - x, x + 1 - 2 * lo
+    around = [x, jnp.where(core == 0, before, after), jnp.where(core == 0, after, before), lax.rem(x + 2, NX)]
+    around = jnp.stack(around).astype(jnp.int32)
     key_next = exchange(key_own, 1)
-    key_own, key_next = lax.optimization_barrier((key_own, key_next))
     key_second = exchange(key_own, 0)
-    key_first = exchange(key_next, 0)
-    keys = key_own, key_next, key_first, key_second
-
-    def out_part(half, bank, kept, *came):
-        out = NQ, tok, feat
+    keys = key_own, key_next, key_second, exchange(key_next, 0)
+
+    def out_part(half, which, bank, kept, *after):
+        out = len(which), 2, tok, feat
         return call(
-            functools.partial(out_kernel, half), "out_part", [(out, kept), (out, jnp.bfloat16)],
-            [SMEM] * 2 + [VMEM] * (NX + 3 + len(came)), cost(NY * tok, wide, feat),
-            (order, ids, *keys, value_all, bank, hidden, *came),
-        )
-
-    came = [swap(rest) for rest in out_part(1, bank_other, jnp.bfloat16)]
-    same, other = out_part(0, dim_bank, jnp.float32, *came)
-    pieces = (same + beside(other).astype(jnp.float32)).astype(jnp.bfloat16)
-    pieces, everyone = lax.optimization_barrier((pieces, everyone))
-    pieces = lax.all_to_all(pieces, YQ, 0, 0)
+            functools.partial(out_kernel, half, which), "out_part", [(out, kept)],
+            [SMEM] * 2 + [VMEM] * (len(which) + 3) + [ANY] * len(after), cost(len(which) * quarter, wide, feat),
+            (around, ids, *[keys[i] for i in which], value_all, bank, hidden, *after),
+        )[0]
+
+    sets = (0, 1, 2), (3,)
+    parts = []
+    for which in sets:
+        came = swap(out_part(1, which, bank_other, jnp.bfloat16, *parts[:1]))
+        parts += [out_part(0, which, dim_bank, jnp.float32), came]
+    result = call(
+        functools.partial(place_kernel, sets), "place", [((NY, tok, feat), jnp.bfloat16)],
+        [SMEM] * 2 + [VMEM] * 4, cost(NY * tok, 1, feat), (around, at, *parts),
+    )[0]
+    result, everyone = lax.optimization_barrier((result, everyone))
+    pieces = lax.all_to_all(result, YQ + ("y_low",), 0, 0)
     outputs = jnp.sum(pieces.astype(jnp.float32), axis=0).astype(jnp.bfloat16)
     key_step, value_step = call(
         step_kernel, "steps", [(key_weight.shape, jnp.float32), (value_weight.shape, jnp.float32)],

time: 172 us -> 168 us (0.977)
  waiting for transfers between devices: 72.7 us -> 67.7 us
  Pallas kernels: 15.9 us -> 19.1 us
    all_to_all x1, waiting for transfers between devices: 11.4 us -> 26.2 us  [shards(): pieces = lax.all_to_all(result, YQ + ('y_low',), 0, 0)]
    ppermute x6, waiting for transfers between devices: 31.3 us -> 20.1 us  [exchange(): return lax.ppermute(x, ('x', 'core'), pairs)]
    ppermute x2 -> x1, waiting for transfers between devices: 12.7 us -> 6.03 us  [beside(): return lax.ppermute(x, YQ + ('y_low', 'core'), pairs)]
    ppermute x2 -> x1, starting transfers between devices: 6.5 us -> 1.91 us  [beside(): return lax.ppermute(x, YQ + ('y_low', 'core'), pairs)]
    pallas_call x10 -> x13, Pallas kernels: 15.9 us -> 19.1 us  [call(): pl.pallas_call(kernel, out_shape=[jax.ShapeDtypeStruct(*out) for out in o...]
    ppermute x6, starting transfers between devices: 18 us -> 20.6 us  [exchange(): return lax.ppermute(x, ('x', 'core'), pairs)]
    ppermute x7, waiting for transfers between devices: 3.5 us -> 1.59 us  [swap(): return lax.ppermute(x, 'core', [(0, 1), (1, 0)])]
  transfers between devices with their start and end apart: 19 -> 18, of which waited for: 14 -> 11; matrix products, arithmetic and copies ran while one was open for 1% -> 1% of each run, Pallas kernels for 7% -> 10%
where the time goes in v5:
time: 168 us; the launch traced here: 167 us
  waiting for transfers between devices  67.7 us (40%)
  starting transfers between devices  59.1 us (35%)
  Pallas kernels  19.1 us (11%)
  between operations  14.5 us (9%)
  local copies, waits for them, and re-layouts  4.25 us (3%)
  other arithmetic  2.53 us (2%)
    all_to_all x1, waiting for transfers between devices, shards(): pieces = lax.all_to_all(result, YQ + ('y_low',), 0, 0)  26.2 us
    ppermute x7, starting transfers between devices, swap(): return lax.ppermute(x, 'core', [(0, 1), (1, 0)])  25.9 us
    ppermute x6, starting transfers between devices, exchange(): return lax.ppermute(x, ('x', 'core'), pairs)  20.6 us
    ppermute x6, waiting for transfers between devices, exchange(): return lax.ppermute(x, ('x', 'core'), pairs)  20.1 us
    pallas_call x13, Pallas kernels, call(): pl.pallas_call(kernel, out_shape=[jax.ShapeDtypeStruct(*out) for out in o...  19.1 us
    all_to_all x1, waiting for transfers between devices, shards(): same = lax.all_to_all(shifted, YQ, 0, 0)  13.7 us
    all_to_all x1, starting transfers between devices, shards(): pieces = lax.all_to_all(result, YQ + ('y_low',), 0, 0)  7.04 us
    ppermute x1, waiting for transfers between devices, beside(): return lax.ppermute(x, YQ + ('y_low', 'core'), pairs)  6.03 us
  transfers between devices with their start and end apart: 18, of which 11 were waited for; matrix products, arithmetic and copies ran while one was open for 1% of the time, Pallas kernels for 10%

profile of v5, /device:TPU:1, one launch (start us, length us, event | category | flops | bytes accessed | tf_op | source)
XLA Modules:
  0.0 167.1 jit_solution(1323858184293134259)
XLA Ops:
  7.2 0.0 copy-start.5
  7.2 0.0 copy-start.3
  7.2 0.0 all-gather.5.cloned.1.call-start
  7.2 8.9 %collective-permute-start.3 = (bf16[512,256]{1,0:T(8,128)(2,1)}, bf16[512,256]{1,0:T(8,128)(2,1)S(1)}, u32[]{:S(2)}, u32[]{:S(2)}) collective-permute-start(bf16[512,256]{1,0:T(8,128)(2,1)} %param.10), channel_id=1, source_target_pairs={{0,1},{1,0},{2,3},{3,2},{4,5},{5,4},{6,7},{7,6},{8,9},{9,8},{10,11... | collective-permute-start | bytes 786440 | tf_op jit(solution)/shard_map/ppermute | solution.py:29
  16.2 0.9 constant_dynamic-slice_fusion.3
  17.1 0.4 collective-permute-done.3
  17.5 0.7 pad_maximum_fusion
  18.2 0.0 all-gather.5.cloned.1.call-update
  18.3 1.9 %shift.1 = bf16[4,144,512]{2,1,0:T(8,128)(2,1)} custom-call(s32[2,4]{1,0:T(2,128)} %picks_hbm.1, s32[2]{0:T(128)} %ranks_hbm.1, bf16[128,512]{1,0:T(8,128)(2,1)} %x_hbm.1, f32[1,512]{1,0:T(1,128)} %bitcast.31), custom_call_target="tpu_custom_call" | custom-call | flops 2097152 | bytes 151552 | tf_op jit(solution)/shard_map/shift/pallas_call | solution.py:190
  20.1 3.5 %all-to-all-start = ((bf16[4,144,512]{2,1,0:T(8,128)(2,1)}), bf16[4,144,512]{2,1,0:T(8,128)(2,1)S(1)}, u32[]{:S(2)}, u32[]{:S(2)}) async-start(bf16[4,144,512]{2,1,0:T(8,128)(2,1)} %shift.1), calls=%async_computation | async-start | bytes 1179648 | tf_op jit(solution)/shard_map/all_to_all | solution.py:222
  23.6 0.0 all-gather.7.cloned.1.call-start
  23.7 0.0 copy-done.5
  23.7 2.3 %collective-permute-start.4 = (bf16[256,512]{1,0:T(8,128)(2,1)S(1)}, bf16[256,512]{1,0:T(8,128)(2,1)S(1)}, u32[]{:S(2)}, u32[]{:S(2)}) collective-permute-start(bf16[256,512]{1,0:T(8,128)(2,1)S(1)} %copy-done.5), channel_id=1, source_target_pairs={{0,1},{1,0},{2,3},{3,2},{4,5},{5,4},{6,7},{7,6},{8,9},{9,8},{10,11... | collective-permute-start | bytes 786440 | tf_op jit(solution)/shard_map/ppermute | solution.py:29
  26.0 13.7 %all-to-all-done.refs_0_ = bf16[4,144,512]{2,1,0:T(8,128)(2,1)S(1)} async-done(((bf16[4,144,512]{2,1,0:T(8,128)(2,1)}), bf16[4,144,512]{2,1,0:T(8,128)(2,1)S(1)}, u32[]{:S(2)}, u32[]{:S(2)}) %all-to-all-start) | async-done | bytes 589856 | tf_op jit(solution)/shard_map/all_to_all | solution.py:222
  39.7 1.9 %collective-permute-start = (bf16[4,144,512]{2,1,0:T(8,128)(2,1)S(1)}, bf16[4,144,512]{2,1,0:T(8,128)(2,1)S(1)}, u32[]{:S(2)}, u32[]{:S(2)}) collective-permute-start(bf16[4,144,512]{2,1,0:T(8,128)(2,1)S(1)} %all-to-all-done.refs_0_), channel_id=1, source_target_pairs={{0,8},{1,57},{8,0},{9,17},{16,24},{17,9},{24,16},{25,33},{32,40},{... | collective-permute-start | bytes 1769480 | tf_op jit(solution)/shard_map/ppermute | solution.py:47
  41.6 0.0 copy-done.3
  41.6 2.9 %collective-permute-start.5 = (f32[64,512]{1,0:T(8,128)S(1)}, f32[64,512]{1,0:T(8,128)S(1)}, u32[]{:S(2)}, u32[]{:S(2)}) collective-permute-start(f32[64,512]{1,0:T(8,128)S(1)} %copy-done.3), channel_id=1, source_target_pairs={{0,1},{1,0},{2,3},{3,2},{4,5},{5,4},{6,7},{7,6},{8,9},{9,8},{10,11... | collective-permute-start | bytes 393224 | tf_op jit(solution)/shard_map/ppermute | solution.py:29
  44.5 0.9 collective-permute-done.5.refs_6_.refs_4_.refs_2_
  45.5 0.0 collective-permute-done.4
  45.5 6.0 %collective-permute-done.refs_1_ = bf16[4,144,512]{2,1,0:T(8,128)(2,1)S(1)} collective-permute-done((bf16[4,144,512]{2,1,0:T(8,128)(2,1)S(1)}, bf16[4,144,512]{2,1,0:T(8,128)(2,1)S(1)}, u32[]{:S(2)}, u32[]{:S(2)}) %collective-permute-start) | collective-permute-done | bytes 589856 | tf_op jit(solution)/shard_map/ppermute | solution.py:47
  51.6 0.7 fusion.1
  52.3 0.0 all-gather.7.cloned.1.call-update
  52.3 2.8 %collective-permute-start.1 = (bf16[4,144,512]{2,1,0:T(8,128)(2,1)S(1)}, bf16[4,144,512]{2,1,0:T(8,128)(2,1)S(1)}, u32[]{:S(2)}, u32[]{:S(2)}) collective-permute-start(bf16[4,144,512]{2,1,0:T(8,128)(2,1)S(1)} %all-to-all-done.refs_0_), channel_id=1, source_target_pairs={{0,1},{1,0},{2,3},{3,2},{4,5},{5,4},{6,7},{7,6},{8,9},{9,8},{10,11... | collective-permute-start | bytes 1769480 | tf_op jit(solution)/shard_map/ppermute | solution.py:29
  55.1 1.9 %collective-permute-start.2 = (bf16[4,144,512]{2,1,0:T(8,128)(2,1)S(1)}, bf16[4,144,512]{2,1,0:T(8,128)(2,1)S(1)}, u32[]{:S(2)}, u32[]{:S(2)}) collective-permute-start(bf16[4,144,512]{2,1,0:T(8,128)(2,1)S(1)} %collective-permute-done.refs_1_), channel_id=1, source_target_pairs={{0,1},{1,0},{2,3},{3,2},{4,5},{5,4},{6,7},{7,6},{8,9},{9,8},{10,11... | collective-permute-start | bytes 1769480 | tf_op jit(solution)/shard_map/ppermute | solution.py:29
  57.1 0.1 pad_add_fusion.1.at_ref
  57.1 1.5 hidden.1.refs_7_.refs_5_.refs_3_
  58.7 0.1 pad_add_fusion.2.order_ref
  58.8 0.0 collective-permute-done.1.refs_2_
  58.8 0.2 collective-permute-done.2.refs_3_
  59.0 1.6 copy-done.2
  60.6 1.4 key_part.5
  62.0 3.3 %collective-permute-start.7 = (bf16[256,1024]{1,0:T(8,128)(2,1)S(1)}, bf16[256,1024]{1,0:T(8,128)(2,1)S(1)}, u32[]{:S(2)}, u32[]{:S(2)}) collective-permute-start(bf16[256,1024]{1,0:T(8,128)(2,1)S(1)} %key_part.5), channel_id=1, source_target_pairs={{0,2},{1,7},{2,0},{3,5},{4,6},{5,3},{6,4},{7,1},{8,10},{9,15},{10,... | collective-permute-start | bytes 1572872 | tf_op jit(solution)/shard_map/ppermute | solution.py:38
  65.3 1.4 key_part.4
  66.7 3.2 %collective-permute-start.6 = (bf16[256,1024]{1,0:T(8,128)(2,1)S(1)}, bf16[256,1024]{1,0:T(8,128)(2,1)S(1)}, u32[]{:S(2)}, u32[]{:S(2)}) collective-permute-start(bf16[256,1024]{1,0:T(8,128)(2,1)S(1)} %key_part.4), channel_id=1, source_target_pairs={{0,2},{1,7},{2,0},{3,5},{4,6},{5,3},{6,4},{7,1},{8,10},{9,15},{10,... | collective-permute-start | bytes 1572872 | tf_op jit(solution)/shard_map/ppermute | solution.py:38
  69.9 2.0 %key_part.3 = (f32[256,1024]{1,0:T(8,128)S(1)}, f32[256,1024]{1,0:T(8,128)S(1)}) custom-call(s32[4]{0:T(128)S(1)} %pad_add_fusion.2.order_ref, s32[16,4]{1,0:T(8,128)S(1)} %slice_convert_fusion.ids_ref, bf16[4,144,512]{2,1,0:T(8,128)(2,1)S(1)} %all-to-all-done.refs_0_, bf16[4,144,512]{2,1,0:T(8,128)(2,1)S(1)} %collective-permute-done.refs_1_, ...), custom_call_target="tpu_custom_call" | custom-call | flops 1073741824 | bytes 4194304 | tf_op jit(solution)/shard_map/key_part/pallas_call | solution.py:190
  71.9 1.2 collective-permute-done.7.came_ref
  73.2 0.1 add.95
  73.3 1.9 %collective-permute-start.8 = (bf16[256,1024]{1,0:T(8,128)(2,1)S(1)}, bf16[256,1024]{1,0:T(8,128)(2,1)S(1)}, u32[]{:S(2)}, u32[]{:S(2)}) collective-permute-start(bf16[256,1024]{1,0:T(8,128)(2,1)S(1)} %add.95), channel_id=1, source_target_pairs={{0,6},{1,3},{2,4},{3,1},{4,2},{5,7},{6,0},{7,5},{8,14},{9,11},{10,... | collective-permute-start | bytes 1572872 | tf_op jit(solution)/shard_map/ppermute | solution.py:38
  75.2 3.6 %collective-permute-done.6.first_ref = bf16[256,1024]{1,0:T(8,128)(2,1)S(1)} collective-permute-done((bf16[256,1024]{1,0:T(8,128)(2,1)S(1)}, bf16[256,1024]{1,0:T(8,128)(2,1)S(1)}, u32[]{:S(2)}, u32[]{:S(2)}) %collective-permute-start.6) | collective-permute-done | bytes 524320 | tf_op jit(solution)/shard_map/ppermute | solution.py:38
  78.8 9.0 %collective-permute-done.8.second_ref = bf16[256,1024]{1,0:T(8,128)(2,1)S(1)} collective-permute-done((bf16[256,1024]{1,0:T(8,128)(2,1)S(1)}, bf16[256,1024]{1,0:T(8,128)(2,1)S(1)}, u32[]{:S(2)}, u32[]{:S(2)}) %collective-permute-start.8) | collective-permute-done | bytes 524320 | tf_op jit(solution)/shard_map/ppermute | solution.py:38
  87.8 0.2 square.1.refs_0_
  88.0 3.1 %collective-permute-start.9 = (bf16[256,1024]{1,0:T(8,128)(2,1)S(1)}, bf16[256,1024]{1,0:T(8,128)(2,1)S(1)}, u32[]{:S(2)}, u32[]{:S(2)}) collective-permute-start(bf16[256,1024]{1,0:T(8,128)(2,1)S(1)} %square.1.refs_0_), channel_id=1, source_target_pairs={{0,6},{1,3},{2,4},{3,1},{4,2},{5,7},{6,0},{7,5},{8,14},{9,11},{10,... | collective-permute-start | bytes 1572872 | tf_op jit(solution)/shard_map/ppermute | solution.py:38
  91.1 3.6 %collective-permute-start.10 = (bf16[256,1024]{1,0:T(8,128)(2,1)S(1)}, bf16[256,1024]{1,0:T(8,128)(2,1)S(1)}, u32[]{:S(2)}, u32[]{:S(2)}) collective-permute-start(bf16[256,1024]{1,0:T(8,128)(2,1)S(1)} %square.1.refs_0_), channel_id=1, source_target_pairs={{0,2},{1,7},{2,0},{3,5},{4,6},{5,3},{6,4},{7,1},{8,10},{9,15},{10,... | collective-permute-start | bytes 1572872 | tf_op jit(solution)/shard_map/ppermute | solution.py:38
  94.8 0.1 pad_add_fusion.order_ref
  94.8 3.5 %collective-permute-done.9.refs_1_ = bf16[256,1024]{1,0:T(8,128)(2,1)S(1)} collective-permute-done((bf16[256,1024]{1,0:T(8,128)(2,1)S(1)}, bf16[256,1024]{1,0:T(8,128)(2,1)S(1)}, u32[]{:S(2)}, u32[]{:S(2)}) %collective-permute-start.9) | collective-permute-done | bytes 524320 | tf_op jit(solution)/shard_map/ppermute | solution.py:38
  98.3 5.5 %collective-permute-start.12 = (bf16[256,1024]{1,0:T(8,128)(2,1)S(1)}, bf16[256,1024]{1,0:T(8,128)(2,1)S(1)}, u32[]{:S(2)}, u32[]{:S(2)}) collective-permute-start(bf16[256,1024]{1,0:T(8,128)(2,1)S(1)} %collective-permute-done.9.refs_1_), channel_id=1, source_target_pairs={{0,2},{1,7},{2,0},{3,5},{4,6},{5,3},{6,4},{7,1},{8,10},{9,15},{10,... | collective-permute-start | bytes 1572872 | tf_op jit(solution)/shard_map/ppermute | solution.py:38
  103.8 2.9 %collective-permute-done.10.refs_2_ = bf16[256,1024]{1,0:T(8,128)(2,1)S(1)} collective-permute-done((bf16[256,1024]{1,0:T(8,128)(2,1)S(1)}, bf16[256,1024]{1,0:T(8,128)(2,1)S(1)}, u32[]{:S(2)}, u32[]{:S(2)}) %collective-permute-start.10) | collective-permute-done | bytes 524320 | tf_op jit(solution)/shard_map/ppermute | solution.py:38
  106.7 1.7 copy-done
  108.3 1.8 %out_part.5 = bf16[3,2,128,512]{3,2,1,0:T(8,128)(2,1)S(1)} custom-call(s32[4]{0:T(128)S(1)} %pad_add_fusion.order_ref, s32[16,4]{1,0:T(8,128)S(1)} %slice_convert_fusion.ids_ref, bf16[256,1024]{1,0:T(8,128)(2,1)S(1)} %square.1.refs_0_, bf16[256,1024]{1,0:T(8,128)(2,1)S(1)} %collective-permute-done.9.refs_1_, ...), custom_call_target="tpu_custom_call" | custom-call | flops 805306368 | bytes 3407872 | tf_op jit(solution)/shard_map/out_part/pallas_call | solution.py:190
  110.1 0.0 copy-start.1
  110.1 4.0 %collective-permute-start.11 = (bf16[3,2,128,512]{3,2,1,0:T(8,128)(2,1)S(1)}, bf16[3,2,128,512]{3,2,1,0:T(8,128)(2,1)S(1)}, u32[]{:S(2)}, u32[]{:S(2)}) collective-permute-start(bf16[3,2,128,512]{3,2,1,0:T(8,128)(2,1)S(1)} %out_part.5), channel_id=1, source_target_pairs={{0,1},{1,0},{2,3},{3,2},{4,5},{5,4},{6,7},{7,6},{8,9},{9,8},{10,11... | collective-permute-start | bytes 2359304 | tf_op jit(solution)/shard_map/ppermute | solution.py:29
  114.1 1.8 %out_part.4.refs_4_.refs_0_ = f32[3,2,128,512]{3,2,1,0:T(8,128)S(1)} custom-call(s32[4]{0:T(128)S(1)} %pad_add_fusion.order_ref, s32[16,4]{1,0:T(8,128)S(1)} %slice_convert_fusion.ids_ref, bf16[256,1024]{1,0:T(8,128)(2,1)S(1)} %square.1.refs_0_, bf16[256,1024]{1,0:T(8,128)(2,1)S(1)} %collective-permute-done.9.refs_1_, ...), custom_call_target="tpu_custom_call" | custom-call | flops 805306368 | bytes 3407872 | tf_op jit(solution)/shard_map/out_part/pallas_call | solution.py:190
  115.9 0.0 collective-permute-done.12.refs_0_
  115.9 0.0 copy-done.1
  115.9 1.1 out_part.7
  117.0 3.2 %collective-permute-start.13 = (bf16[1,2,128,512]{3,2,1,0:T(8,128)(2,1)S(1)}, bf16[1,2,128,512]{3,2,1,0:T(8,128)(2,1)S(1)}, u32[]{:S(2)}, u32[]{:S(2)}) collective-permute-start(bf16[1,2,128,512]{3,2,1,0:T(8,128)(2,1)S(1)} %out_part.7), channel_id=1, source_target_pairs={{0,1},{1,0},{2,3},{3,2},{4,5},{5,4},{6,7},{7,6},{8,9},{9,8},{10,11... | collective-permute-start | bytes 786440 | tf_op jit(solution)/shard_map/ppermute | solution.py:29
  120.3 1.1 out_part.6.refs_2_
  121.4 0.0 collective-permute-done.13.refs_3_
  121.4 0.0 collective-permute-done.11.refs_1_
  121.4 1.7 %place.1 = bf16[8,128,512]{2,1,0:T(8,128)(2,1)} custom-call(s32[4]{0:T(128)S(1)} %pad_add_fusion.order_ref, s32[3]{0:T(128)S(1)} %pad_add_fusion.1.at_ref, f32[3,2,128,512]{3,2,1,0:T(8,128)S(1)} %out_part.4.refs_4_.refs_0_, bf16[3,2,128,512]{3,2,1,0:T(8,128)(2,1)S(1)} %collective-permute-done.11.refs_1_, f32[1,2,128,512]{3,2,1,0:T(8,128)S(1)} %out_part.6.refs_2_, ...), custom_call_target="tpu_custom_call" | custom-call | flops 1048576 | bytes 1051648 | tf_op jit(solution)/shard_map/place/pallas_call | solution.py:190
  123.2 7.0 %all-to-all-start.1 = ((bf16[8,128,512]{2,1,0:T(8,128)(2,1)}), bf16[8,128,512]{2,1,0:T(8,128)(2,1)S(1)}, u32[]{:S(2)}, u32[]{:S(2)}) async-start(bf16[8,128,512]{2,1,0:T(8,128)(2,1)} %place.1), calls=%async_computation.1 | async-start | bytes 2097152 | tf_op jit(solution)/shard_map/all_to_all | solution.py:295
  130.2 3.0 %steps.1 = (f32[512,256]{1,0:T(8,128)}, f32[256,512]{1,0:T(8,128)}) custom-call(s32[3]{0:T(128)S(1)} %pad_add_fusion.1.at_ref, bf16[128,128]{1,0:T(8,128)(2,1)S(1)} %bitcast.28, f32[64,512]{1,0:T(8,128)S(1)} %copy-done.3, f32[64,4096]{1,0:T(8,128)S(1)} %copy-done.4), custom_call_target="tpu_custom_call" | custom-call | flops 134217728 | bytes 1048576 | tf_op jit(solution)/shard_map/steps/pallas_call | solution.py:190
  133.2 26.2 %all-to-all-done.1 = bf16[8,128,512]{2,1,0:T(8,128)(2,1)S(1)} async-done(((bf16[8,128,512]{2,1,0:T(8,128)(2,1)}), bf16[8,128,512]{2,1,0:T(8,128)(2,1)S(1)}, u32[]{:S(2)}, u32[]{:S(2)}) %all-to-all-start.1) | async-done | bytes 1048608 | tf_op jit(solution)/shard_map/all_to_all | solution.py:295
  159.4 0.8 reduce_sum.12
  (14 shorter events, 0.1 us)
Async XLA Ops:
  7.2 16.5 %copy-start.5 = (bf16[256,512]{1,0:T(8,128)(2,1)S(1)}, bf16[256,512]{1,0:T(8,128)(2,1)}, u32[]{:S(2)}) copy-start(bf16[256,512]{1,0:T(8,128)(2,1)} %param.11) | copy-start | bytes 786436
  7.2 34.5 %copy-start.3 = (f32[64,512]{1,0:T(8,128)S(1)}, f32[64,512]{1,0:T(8,128)}, u32[]{:S(2)}) copy-start(f32[64,512]{1,0:T(8,128)} %bank_ref.1) | copy-start | bytes 393220
  7.2 51.8 %all-gather.5.cloned.1.call-start = ((), (), s32[]{:S(2)}) async-start(), calls=%async_computation.2 | async-start | bytes 2359296 | tf_op jit(solution)/shard_map/all_gather | solution.py:233
  7.2 10.3 %collective-permute-start.3 = (bf16[512,256]{1,0:T(8,128)(2,1)}, bf16[512,256]{1,0:T(8,128)(2,1)S(1)}, u32[]{:S(2)}, u32[]{:S(2)}) collective-permute-start(bf16[512,256]{1,0:T(8,128)(2,1)} %param.10), channel_id=1, source_target_pairs={{0,1},{1,0},{2,3},{3,2},{4,5},{5,4},{6,7},{7,6},{8,9},{9,8},{10,11... | collective-permute-start | bytes 786440 | tf_op jit(solution)/shard_map/ppermute | solution.py:29
  20.1 19.6 %all-to-all-start = ((bf16[4,144,512]{2,1,0:T(8,128)(2,1)}), bf16[4,144,512]{2,1,0:T(8,128)(2,1)S(1)}, u32[]{:S(2)}, u32[]{:S(2)}) async-start(bf16[4,144,512]{2,1,0:T(8,128)(2,1)} %shift.1), calls=%async_computation | async-start | bytes 1179648 | tf_op jit(solution)/shard_map/all_to_all | solution.py:222
  23.6 83.0 %all-gather.7.cloned.1.call-start = ((), (), s32[]{:S(2)}) async-start(), calls=%async_computation.3 | async-start | bytes 2654208 | tf_op jit(solution)/shard_map/all_gather | solution.py:237
  23.7 21.8 %collective-permute-start.4 = (bf16[256,512]{1,0:T(8,128)(2,1)S(1)}, bf16[256,512]{1,0:T(8,128)(2,1)S(1)}, u32[]{:S(2)}, u32[]{:S(2)}) collective-permute-start(bf16[256,512]{1,0:T(8,128)(2,1)S(1)} %copy-done.5), channel_id=1, source_target_pairs={{0,1},{1,0},{2,3},{3,2},{4,5},{5,4},{6,7},{7,6},{8,9},{9,8},{10,11... | collective-permute-start | bytes 786440 | tf_op jit(solution)/shard_map/ppermute | solution.py:29
  39.7 11.8 %collective-permute-start = (bf16[4,144,512]{2,1,0:T(8,128)(2,1)S(1)}, bf16[4,144,512]{2,1,0:T(8,128)(2,1)S(1)}, u32[]{:S(2)}, u32[]{:S(2)}) collective-permute-start(bf16[4,144,512]{2,1,0:T(8,128)(2,1)S(1)} %all-to-all-done.refs_0_), channel_id=1, source_target_pairs={{0,8},{1,57},{8,0},{9,17},{16,24},{17,9},{24,16},{25,33},{32,40},{... | collective-permute-start | bytes 1769480 | tf_op jit(solution)/shard_map/ppermute | solution.py:47
  41.6 3.8 %collective-permute-start.5 = (f32[64,512]{1,0:T(8,128)S(1)}, f32[64,512]{1,0:T(8,128)S(1)}, u32[]{:S(2)}, u32[]{:S(2)}) collective-permute-start(f32[64,512]{1,0:T(8,128)S(1)} %copy-done.3), channel_id=1, source_target_pairs={{0,1},{1,0},{2,3},{3,2},{4,5},{5,4},{6,7},{7,6},{8,9},{9,8},{10,11... | collective-permute-start | bytes 393224 | tf_op jit(solution)/shard_map/ppermute | solution.py:29
  52.3 6.5 %collective-permute-start.1 = (bf16[4,144,512]{2,1,0:T(8,128)(2,1)S(1)}, bf16[4,144,512]{2,1,0:T(8,128)(2,1)S(1)}, u32[]{:S(2)}, u32[]{:S(2)}) collective-permute-start(bf16[4,144,512]{2,1,0:T(8,128)(2,1)S(1)} %all-to-all-done.refs_0_), channel_id=1, source_target_pairs={{0,1},{1,0},{2,3},{3,2},{4,5},{5,4},{6,7},{7,6},{8,9},{9,8},{10,11... | collective-permute-start | bytes 1769480 | tf_op jit(solution)/shard_map/ppermute | solution.py:29
  55.1 3.9 %collective-permute-start.2 = (bf16[4,144,512]{2,1,0:T(8,128)(2,1)S(1)}, bf16[4,144,512]{2,1,0:T(8,128)(2,1)S(1)}, u32[]{:S(2)}, u32[]{:S(2)}) collective-permute-start(bf16[4,144,512]{2,1,0:T(8,128)(2,1)S(1)} %collective-permute-done.refs_1_), channel_id=1, source_target_pairs={{0,1},{1,0},{2,3},{3,2},{4,5},{5,4},{6,7},{7,6},{8,9},{9,8},{10,11... | collective-permute-start | bytes 1769480 | tf_op jit(solution)/shard_map/ppermute | solution.py:29
  59.0 1.6 copy-start.2
  62.0 11.1 %collective-permute-start.7 = (bf16[256,1024]{1,0:T(8,128)(2,1)S(1)}, bf16[256,1024]{1,0:T(8,128)(2,1)S(1)}, u32[]{:S(2)}, u32[]{:S(2)}) collective-permute-start(bf16[256,1024]{1,0:T(8,128)(2,1)S(1)} %key_part.5), channel_id=1, source_target_pairs={{0,2},{1,7},{2,0},{3,5},{4,6},{5,3},{6,4},{7,1},{8,10},{9,15},{10,... | collective-permute-start | bytes 1572872 | tf_op jit(solution)/shard_map/ppermute | solution.py:38
  66.7 12.1 %collective-permute-start.6 = (bf16[256,1024]{1,0:T(8,128)(2,1)S(1)}, bf16[256,1024]{1,0:T(8,128)(2,1)S(1)}, u32[]{:S(2)}, u32[]{:S(2)}) collective-permute-start(bf16[256,1024]{1,0:T(8,128)(2,1)S(1)} %key_part.4), channel_id=1, source_target_pairs={{0,2},{1,7},{2,0},{3,5},{4,6},{5,3},{6,4},{7,1},{8,10},{9,15},{10,... | collective-permute-start | bytes 1572872 | tf_op jit(solution)/shard_map/ppermute | solution.py:38
  73.3 14.5 %collective-permute-start.8 = (bf16[256,1024]{1,0:T(8,128)(2,1)S(1)}, bf16[256,1024]{1,0:T(8,128)(2,1)S(1)}, u32[]{:S(2)}, u32[]{:S(2)}) collective-permute-start(bf16[256,1024]{1,0:T(8,128)(2,1)S(1)} %add.95), channel_id=1, source_target_pairs={{0,6},{1,3},{2,4},{3,1},{4,2},{5,7},{6,0},{7,5},{8,14},{9,11},{10,... | collective-permute-start | bytes 1572872 | tf_op jit(solution)/shard_map/ppermute | solution.py:38
  88.0 10.3 %collective-permute-start.9 = (bf16[256,1024]{1,0:T(8,128)(2,1)S(1)}, bf16[256,1024]{1,0:T(8,128)(2,1)S(1)}, u32[]{:S(2)}, u32[]{:S(2)}) collective-permute-start(bf16[256,1024]{1,0:T(8,128)(2,1)S(1)} %square.1.refs_0_), channel_id=1, source_target_pairs={{0,6},{1,3},{2,4},{3,1},{4,2},{5,7},{6,0},{7,5},{8,14},{9,11},{10,... | collective-permute-start | bytes 1572872 | tf_op jit(solution)/shard_map/ppermute | solution.py:38
  91.1 15.6 %collective-permute-start.10 = (bf16[256,1024]{1,0:T(8,128)(2,1)S(1)}, bf16[256,1024]{1,0:T(8,128)(2,1)S(1)}, u32[]{:S(2)}, u32[]{:S(2)}) collective-permute-start(bf16[256,1024]{1,0:T(8,128)(2,1)S(1)} %square.1.refs_0_), channel_id=1, source_target_pairs={{0,2},{1,7},{2,0},{3,5},{4,6},{5,3},{6,4},{7,1},{8,10},{9,15},{10,... | collective-permute-start | bytes 1572872 | tf_op jit(solution)/shard_map/ppermute | solution.py:38
  98.3 17.6 %collective-permute-start.12 = (bf16[256,1024]{1,0:T(8,128)(2,1)S(1)}, bf16[256,1024]{1,0:T(8,128)(2,1)S(1)}, u32[]{:S(2)}, u32[]{:S(2)}) collective-permute-start(bf16[256,1024]{1,0:T(8,128)(2,1)S(1)} %collective-permute-done.9.refs_1_), channel_id=1, source_target_pairs={{0,2},{1,7},{2,0},{3,5},{4,6},{5,3},{6,4},{7,1},{8,10},{9,15},{10,... | collective-permute-start | bytes 1572872 | tf_op jit(solution)/shard_map/ppermute | solution.py:38
  106.7 1.7 copy-start
  110.1 5.8 %copy-start.1 = (bf16[1152,1024]{1,0:T(8,128)(2,1)S(1)}, bf16[1152,1024]{1,0:T(8,128)(2,1)}, u32[]{:S(2)}) copy-start(bf16[1152,1024]{1,0:T(8,128)(2,1)} %all-gather.7.cloned.1.call-done) | copy-start | bytes 7077892
  110.1 11.3 %collective-permute-start.11 = (bf16[3,2,128,512]{3,2,1,0:T(8,128)(2,1)S(1)}, bf16[3,2,128,512]{3,2,1,0:T(8,128)(2,1)S(1)}, u32[]{:S(2)}, u32[]{:S(2)}) collective-permute-start(bf16[3,2,128,512]{3,2,1,0:T(8,128)(2,1)S(1)} %out_part.5), channel_id=1, source_target_pairs={{0,1},{1,0},{2,3},{3,2},{4,5},{5,4},{6,7},{7,6},{8,9},{9,8},{10,11... | collective-permute-start | bytes 2359304 | tf_op jit(solution)/shard_map/ppermute | solution.py:29
  117.0 4.3 %collective-permute-start.13 = (bf16[1,2,128,512]{3,2,1,0:T(8,128)(2,1)S(1)}, bf16[1,2,128,512]{3,2,1,0:T(8,128)(2,1)S(1)}, u32[]{:S(2)}, u32[]{:S(2)}) collective-permute-start(bf16[1,2,128,512]{3,2,1,0:T(8,128)(2,1)S(1)} %out_part.7), channel_id=1, source_target_pairs={{0,1},{1,0},{2,3},{3,2},{4,5},{5,4},{6,7},{7,6},{8,9},{9,8},{10,11... | collective-permute-start | bytes 786440 | tf_op jit(solution)/shard_map/ppermute | solution.py:29
  123.2 7.0 %copy-start.4 = (f32[64,4096]{1,0:T(8,128)S(1)}, f32[64,4096]{1,0:T(8,128)}, u32[]{:S(2)}) copy-start(f32[64,4096]{1,0:T(8,128)} %hid_ref.1) | copy-start | bytes 3145732
  123.2 36.3 %all-to-all-start.1 = ((bf16[8,128,512]{2,1,0:T(8,128)(2,1)}), bf16[8,128,512]{2,1,0:T(8,128)(2,1)S(1)}, u32[]{:S(2)}, u32[]{:S(2)}) async-start(bf16[8,128,512]{2,1,0:T(8,128)(2,1)} %place.1), calls=%async_computation.1 | async-start | bytes 2097152 | tf_op jit(solution)/shard_map/all_to_all | solution.py:295
Sparse Core Ops, SparseCore 0:
  18.4 39.5 all-gather.4
  60.6 44.0 all-gather.6

commit v6 on v5

--- a/solution.py
+++ b/solution.py
@@ -21,7 +21,6 @@
 SIGMA_V = 0.5 / FF**0.5
 VMEM = pl.BlockSpec(memory_space=pltpu.VMEM)
 HBM = pl.BlockSpec(memory_space=pltpu.HBM)
-ANY = pl.BlockSpec(memory_space=pl.ANY)
 SMEM = pl.BlockSpec(memory_space=pltpu.SMEM)
 
 
@@ -116,16 +115,18 @@
     out_ref[...] = (kept_ref[...] + came_ref[...].astype(jnp.float32)).astype(jnp.bfloat16)
 
 
-def square_kernel(kept_ref, first_ref, second_ref, out_ref):
-    total = kept_ref[...] + first_ref[...].astype(jnp.float32) + second_ref[...].astype(jnp.float32)
+def square_kernel(mine_ref, came_ref, out_ref):
+    total = mine_ref[...].astype(jnp.float32) + came_ref[...].astype(jnp.float32)
     out_ref[...] = (jnp.maximum(total, 0.0) ** 2).astype(jnp.bfloat16)
 
 
 def out_kernel(half, order, order_ref, ids_ref, *refs):
-    keys, (v_ref, bank_ref, hid_ref, *_, out_ref) = refs[: len(order)], refs[len(order) :]
+    keys, (v_ref, bank_ref, hid_ref, *done, out_ref) = refs[: len(order)], refs[len(order) :]
     feat, width = out_ref.shape[3], hid_ref.shape[1] // NZ
     tok = out_ref.shape[2]
     own, wide = tok // BATCH, 256
+    for ref in done:
+        out_ref[: ref.shape[0]] = ref[...]
     inner, picks, places = [], [], []
     for i, o in enumerate(order):
         for s in range(2):
@@ -136,7 +137,7 @@
                 part = keys[i][at : at + BATCH, :].astype(jnp.float32)
                 inner.append(SIGMA_V * jnp.sum(part * fac_c, axis=1, keepdims=True))
                 picks.append(ids_ref[m, 3])
-                places.append((i, s, slice(j * BATCH, (j + 1) * BATCH)))
+                places.append((out_ref.shape[0] - len(order) + i, s, slice(j * BATCH, (j + 1) * BATCH)))
     rows = jnp.concatenate([k[...] for k in keys], axis=0)
     for n in range(feat // wide):
         cols = slice(n * wide, (n + 1) * wide)
@@ -148,14 +149,12 @@
             out_ref[i, s, at, cols] = part.astype(out_ref.dtype)
 
 
-def place_kernel(orders, order_ref, at_ref, *refs):
-    parts, out_ref = refs[:-1], refs[-1]
-    twins = (0, 2, 1)
-    for order, mine_ref, came_ref in zip(orders, parts[::2], parts[1::2]):
-        for i, o in enumerate(order):
-            for s in range(2):
-                total = mine_ref[i, s] + came_ref[twins[i], s].astype(jnp.float32)
-                out_ref[2 * order_ref[o] + lax.rem(at_ref[2] + s, 2)] = total.astype(jnp.bfloat16)
+def place_kernel(order_ref, at_ref, mine_ref, came_ref, out_ref):
+    twins = (0, 2, 1, 3)
+    for i in range(NX):
+        for s in range(2):
+            total = mine_ref[i, s] + came_ref[twins[i], s].astype(jnp.float32)
+            out_ref[2 * order_ref[i] + lax.rem(at_ref[2] + s, 2)] = total.astype(jnp.bfloat16)
 
 
 def step_kernel(at_ref, info_ref, bank_ref, hid_ref, key_ref, value_ref):
@@ -237,12 +236,8 @@
     value_all = lax.all_gather(jnp.concatenate([value_pack, info], axis=0), "z", axis=0)
     everyone = value_all[:, half : half + members, :128].reshape(NZ * members, 128)
 
-    lo, hi = lax.rem(x, 2), x // 2
-    f, g = jnp.where(core == 0, lax.rem(lo + hi, 2), hi), jnp.where(core == 0, hi, lo)
-    turned = jnp.where(core == 0, 1 - g, g)
-    order = []
-    for upper, lower in ((f, g), (f, 1 - g), (1 - f, turned), (1 - f, 1 - turned)):
-        order.append(jnp.where(core == 0, 2 * lower + lax.rem(upper + lower, 2), 2 * upper + lower))
+    before, after = NX - 1 - x, x + 1 - 2 * lax.rem(x, 2)
+    order = [x, jnp.where(core == 0, before, after), jnp.where(core == 0, after, before), lax.rem(x + 2, NX)]
     order = jnp.stack(order).astype(jnp.int32)
     deep, wide, quarter = 2 * feat, NZ * half, NY * tok // NX
     low, high = ((quarter, wide), jnp.bfloat16), ((quarter, wide), jnp.float32)
@@ -261,35 +256,31 @@
     def local(kernel, name, *args):
         return call(kernel, name, [low], [VMEM] * len(args), cost(quarter, 4, wide), args)[0]
 
-    came_first = exchange(key_part((2,), [low])[0], 0)
-    came_second = exchange(key_part((3,), [low])[0], 0)
-    following, kept = key_part((1, 0), [high, high])
-    came_next = exchange(local(add_kernel, "add", following, came_first), 1)
-    key_own = local(square_kernel, "square", kept, came_second, came_next)
-
-    before, after = NX - 1 - x, x + 1 - 2 * lo
-    around = [x, jnp.where(core == 0, before, after), jnp.where(core == 0, after, before), lax.rem(x + 2, NX)]
-    around = jnp.stack(around).astype(jnp.int32)
-    key_next = exchange(key_own, 1)
-    key_second = exchange(key_own, 0)
-    keys = key_own, key_next, key_second, exchange(key_next, 0)
-
-    def out_part(half, which, bank, kept, *after):
-        out = len(which), 2, tok, feat
+    came_next = exchange(key_part((3,), [low])[0], 0)
+    came_own = exchange(key_part((2,), [low])[0], 0)
+    sum_next, sum_own = key_part((1, 0), [high, high])
+    sum_next = local(add_kernel, "add", sum_next, came_next)
+    other_own = exchange(sum_next, 1)
+    sum_own = local(add_kernel, "add", sum_own, came_own)
+    other_next = exchange(sum_own, 1)
+    key_own = local(square_kernel, "square", sum_own, other_own)
+    key_first = exchange(key_own, 0)
+    key_next = local(square_kernel, "square", sum_next, other_next)
+    keys = key_own, key_next, key_first, exchange(key_next, 0)
+
+    def out_part(half, which, bank, kept, *done):
+        out = sum(d.shape[0] for d in done) + len(which), 2, tok, feat
         return call(
             functools.partial(out_kernel, half, which), "out_part", [(out, kept)],
-            [SMEM] * 2 + [VMEM] * (len(which) + 3) + [ANY] * len(after), cost(len(which) * quarter, wide, feat),
-            (around, ids, *[keys[i] for i in which], value_all, bank, hidden, *after),
+            [SMEM] * 2 + [VMEM] * (len(which) + 3 + len(done)), cost(len(which) * quarter, wide, feat),
+            (order, ids, *[keys[i] for i in which], value_all, bank, hidden, *done),
         )[0]
 
-    sets = (0, 1, 2), (3,)
-    parts = []
-    for which in sets:
-        came = swap(out_part(1, which, bank_other, jnp.bfloat16, *parts[:1]))
-        parts += [out_part(0, which, dim_bank, jnp.float32), came]
+    rest = out_part(1, (0, 1, 2), bank_other, jnp.bfloat16)
+    came = swap(out_part(1, (3,), bank_other, jnp.bfloat16, rest))
     result = call(
-        functools.partial(place_kernel, sets), "place", [((NY, tok, feat), jnp.bfloat16)],
-        [SMEM] * 2 + [VMEM] * 4, cost(NY * tok, 1, feat), (around, at, *parts),
+        place_kernel, "place", [((NY, tok, feat), jnp.bfloat16)], [SMEM] * 2 + [VMEM] * 2,
+        cost(NY * tok, 1, feat), (order, at, out_part(0, (0, 1, 2, 3), dim_bank, jnp.float32), came),
     )[0]
     result, everyone = lax.optimization_barrier((result, everyone))
     pieces = lax.all_to_all(result, YQ + ("y_low",), 0, 0)

time: 168 us -> 168 us (level)
    ppermute x7 -> x6, starting transfers between devices: 25.9 us -> 26.8 us  [swap(): return lax.ppermute(x, 'core', [(0, 1), (1, 0)])]
    pallas_call x13 -> x14, Pallas kernels: 19.1 us -> 18.7 us  [call(): pl.pallas_call(kernel, out_shape=[jax.ShapeDtypeStruct(*out) for out in o...]
  transfers between devices with their start and end apart: 18 -> 17, of which waited for: 11 -> 13; matrix products, arithmetic and copies ran while one was open for 1% -> 1% of each run, Pallas kernels for 10% -> 9%
where the time goes in v6:
time: 168 us; the launch traced here: 167 us
  waiting for transfers between devices  69.2 us (41%)
  starting transfers between devices  58.6 us (35%)
  Pallas kernels  18.7 us (11%)
  between operations  14.3 us (9%)
  local copies, waits for them, and re-layouts  4.25 us (3%)
  other arithmetic  2.45 us (1%)
    ppermute x6, starting transfers between devices, swap(): return lax.ppermute(x, 'core', [(0, 1), (1, 0)])  26.8 us
    all_to_all x1, waiting for transfers between devices, shards(): pieces = lax.all_to_all(result, YQ + ('y_low',), 0, 0)  26.2 us
    ppermute x6, waiting for transfers between devices, exchange(): return lax.ppermute(x, ('x', 'core'), pairs)  21.5 us
    ppermute x6, starting transfers between devices, exchange(): return lax.ppermute(x, ('x', 'core'), pairs)  19 us
    pallas_call x14, Pallas kernels, call(): pl.pallas_call(kernel, out_shape=[jax.ShapeDtypeStruct(*out) for out in o...  18.7 us
    all_to_all x1, waiting for transfers between devices, shards(): same = lax.all_to_all(shifted, YQ, 0, 0)  13.7 us
    all_to_all x1, starting transfers between devices, shards(): pieces = lax.all_to_all(result, YQ + ('y_low',), 0, 0)  7.37 us
    ppermute x1, waiting for transfers between devices, beside(): return lax.ppermute(x, YQ + ('y_low', 'core'), pairs)  6.03 us
  transfers between devices with their start and end apart: 17, of which 13 were waited for; matrix products, arithmetic and copies ran while one was open for 1% of the time, Pallas kernels for 9%

profile of v6, /device:TPU:1, one launch (start us, length us, event | category | flops | bytes accessed | tf_op | source)
XLA Modules:
  0.0 167.5 jit_solution(1921290595792214501)
XLA Ops:
  7.2 0.0 copy-start.5
  7.2 0.0 copy-start.4
  7.2 0.0 all-gather.5.cloned.1.call-start
  7.2 8.9 %collective-permute-start.3 = (bf16[512,256]{1,0:T(8,128)(2,1)}, bf16[512,256]{1,0:T(8,128)(2,1)S(1)}, u32[]{:S(2)}, u32[]{:S(2)}) collective-permute-start(bf16[512,256]{1,0:T(8,128)(2,1)} %param.10), channel_id=1, source_target_pairs={{0,1},{1,0},{2,3},{3,2},{4,5},{5,4},{6,7},{7,6},{8,9},{9,8},{10,11... | collective-permute-start | bytes 786440 | tf_op jit(solution)/shard_map/ppermute | solution.py:28
  16.2 0.9 constant_dynamic-slice_fusion.3
  17.1 0.4 collective-permute-done.3
  17.5 0.7 pad_maximum_fusion
  18.2 0.0 all-gather.5.cloned.1.call-update
  18.3 1.9 %shift.1 = bf16[4,144,512]{2,1,0:T(8,128)(2,1)} custom-call(s32[2,4]{1,0:T(2,128)} %picks_hbm.1, s32[2]{0:T(128)} %ranks_hbm.1, bf16[128,512]{1,0:T(8,128)(2,1)} %x_hbm.1, f32[1,512]{1,0:T(1,128)} %bitcast.26), custom_call_target="tpu_custom_call" | custom-call | flops 2097152 | bytes 151552 | tf_op jit(solution)/shard_map/shift/pallas_call | solution.py:189
  20.2 3.5 %all-to-all-start = ((bf16[4,144,512]{2,1,0:T(8,128)(2,1)}), bf16[4,144,512]{2,1,0:T(8,128)(2,1)S(1)}, u32[]{:S(2)}, u32[]{:S(2)}) async-start(bf16[4,144,512]{2,1,0:T(8,128)(2,1)} %shift.1), calls=%async_computation | async-start | bytes 1179648 | tf_op jit(solution)/shard_map/all_to_all | solution.py:221
  23.6 0.0 all-gather.7.cloned.1.call-start
  23.7 0.0 copy-done.5
  23.7 2.3 %collective-permute-start.4 = (bf16[256,512]{1,0:T(8,128)(2,1)S(1)}, bf16[256,512]{1,0:T(8,128)(2,1)S(1)}, u32[]{:S(2)}, u32[]{:S(2)}) collective-permute-start(bf16[256,512]{1,0:T(8,128)(2,1)S(1)} %copy-done.5), channel_id=1, source_target_pairs={{0,1},{1,0},{2,3},{3,2},{4,5},{5,4},{6,7},{7,6},{8,9},{9,8},{10,11... | collective-permute-start | bytes 786440 | tf_op jit(solution)/shard_map/ppermute | solution.py:28
  26.0 13.7 %all-to-all-done.refs_0_ = bf16[4,144,512]{2,1,0:T(8,128)(2,1)S(1)} async-done(((bf16[4,144,512]{2,1,0:T(8,128)(2,1)}), bf16[4,144,512]{2,1,0:T(8,128)(2,1)S(1)}, u32[]{:S(2)}, u32[]{:S(2)}) %all-to-all-start) | async-done | bytes 589856 | tf_op jit(solution)/shard_map/all_to_all | solution.py:221
  39.7 1.9 %collective-permute-start = (bf16[4,144,512]{2,1,0:T(8,128)(2,1)S(1)}, bf16[4,144,512]{2,1,0:T(8,128)(2,1)S(1)}, u32[]{:S(2)}, u32[]{:S(2)}) collective-permute-start(bf16[4,144,512]{2,1,0:T(8,128)(2,1)S(1)} %all-to-all-done.refs_0_), channel_id=1, source_target_pairs={{0,8},{1,57},{8,0},{9,17},{16,24},{17,9},{24,16},{25,33},{32,40},{... | collective-permute-start | bytes 1769480 | tf_op jit(solution)/shard_map/ppermute | solution.py:46
  41.6 0.0 copy-done.4
  41.7 2.9 %collective-permute-start.5 = (f32[64,512]{1,0:T(8,128)S(1)}, f32[64,512]{1,0:T(8,128)S(1)}, u32[]{:S(2)}, u32[]{:S(2)}) collective-permute-start(f32[64,512]{1,0:T(8,128)S(1)} %copy-done.4), channel_id=1, source_target_pairs={{0,1},{1,0},{2,3},{3,2},{4,5},{5,4},{6,7},{7,6},{8,9},{9,8},{10,11... | collective-permute-start | bytes 393224 | tf_op jit(solution)/shard_map/ppermute | solution.py:28
  44.6 0.9 collective-permute-done.5.refs_6_.refs_4_.refs_2_
  45.5 0.0 collective-permute-done.4
  45.5 6.0 %collective-permute-done.refs_1_ = bf16[4,144,512]{2,1,0:T(8,128)(2,1)S(1)} collective-permute-done((bf16[4,144,512]{2,1,0:T(8,128)(2,1)S(1)}, bf16[4,144,512]{2,1,0:T(8,128)(2,1)S(1)}, u32[]{:S(2)}, u32[]{:S(2)}) %collective-permute-start) | collective-permute-done | bytes 589856 | tf_op jit(solution)/shard_map/ppermute | solution.py:46
  51.6 0.7 fusion.1
  52.3 0.0 all-gather.7.cloned.1.call-update
  52.3 2.8 %collective-permute-start.1 = (bf16[4,144,512]{2,1,0:T(8,128)(2,1)S(1)}, bf16[4,144,512]{2,1,0:T(8,128)(2,1)S(1)}, u32[]{:S(2)}, u32[]{:S(2)}) collective-permute-start(bf16[4,144,512]{2,1,0:T(8,128)(2,1)S(1)} %all-to-all-done.refs_0_), channel_id=1, source_target_pairs={{0,1},{1,0},{2,3},{3,2},{4,5},{5,4},{6,7},{7,6},{8,9},{9,8},{10,11... | collective-permute-start | bytes 1769480 | tf_op jit(solution)/shard_map/ppermute | solution.py:28
  55.2 1.9 %collective-permute-start.2 = (bf16[4,144,512]{2,1,0:T(8,128)(2,1)S(1)}, bf16[4,144,512]{2,1,0:T(8,128)(2,1)S(1)}, u32[]{:S(2)}, u32[]{:S(2)}) collective-permute-start(bf16[4,144,512]{2,1,0:T(8,128)(2,1)S(1)} %collective-permute-done.refs_1_), channel_id=1, source_target_pairs={{0,1},{1,0},{2,3},{3,2},{4,5},{5,4},{6,7},{7,6},{8,9},{9,8},{10,11... | collective-permute-start | bytes 1769480 | tf_op jit(solution)/shard_map/ppermute | solution.py:28
  57.1 0.1 pad_add_fusion.1.at_ref
  57.2 1.5 hidden.1.refs_7_.refs_6_.refs_5_.refs_3_
  58.7 0.1 pad_add_fusion.order_ref
  58.8 0.0 collective-permute-done.1.refs_2_
  58.8 0.3 collective-permute-done.2.refs_3_
  59.1 0.0 all-gather.5.cloned.1.call-done
  59.1 0.0 copy-start.2
  59.1 1.6 copy-done.2
  60.6 1.4 key_part.5
  62.0 3.3 %collective-permute-start.7 = (bf16[256,1024]{1,0:T(8,128)(2,1)S(1)}, bf16[256,1024]{1,0:T(8,128)(2,1)S(1)}, u32[]{:S(2)}, u32[]{:S(2)}) collective-permute-start(bf16[256,1024]{1,0:T(8,128)(2,1)S(1)} %key_part.5), channel_id=1, source_target_pairs={{0,2},{1,7},{2,0},{3,5},{4,6},{5,3},{6,4},{7,1},{8,10},{9,15},{10,... | collective-permute-start | bytes 1572872 | tf_op jit(solution)/shard_map/ppermute | solution.py:37
  65.3 1.4 key_part.4
  66.7 3.2 %collective-permute-start.6 = (bf16[256,1024]{1,0:T(8,128)(2,1)S(1)}, bf16[256,1024]{1,0:T(8,128)(2,1)S(1)}, u32[]{:S(2)}, u32[]{:S(2)}) collective-permute-start(bf16[256,1024]{1,0:T(8,128)(2,1)S(1)} %key_part.4), channel_id=1, source_target_pairs={{0,2},{1,7},{2,0},{3,5},{4,6},{5,3},{6,4},{7,1},{8,10},{9,15},{10,... | collective-permute-start | bytes 1572872 | tf_op jit(solution)/shard_map/ppermute | solution.py:37
  70.0 2.0 %key_part.3 = (f32[256,1024]{1,0:T(8,128)S(1)}, f32[256,1024]{1,0:T(8,128)S(1)}) custom-call(s32[4]{0:T(128)S(1)} %pad_add_fusion.order_ref, s32[16,4]{1,0:T(8,128)S(1)} %slice_convert_fusion.ids_ref, bf16[4,144,512]{2,1,0:T(8,128)(2,1)S(1)} %all-to-all-done.refs_0_, bf16[4,144,512]{2,1,0:T(8,128)(2,1)S(1)} %collective-permute-done.refs_1_, ...), custom_call_target="tpu_custom_call" | custom-call | flops 1073741824 | bytes 4194304 | tf_op jit(solution)/shard_map/key_part/pallas_call | solution.py:189
  72.0 1.2 collective-permute-done.7.came_ref
  73.2 0.1 add.38.mine_ref
  73.3 1.9 %collective-permute-start.8 = (bf16[256,1024]{1,0:T(8,128)(2,1)S(1)}, bf16[256,1024]{1,0:T(8,128)(2,1)S(1)}, u32[]{:S(2)}, u32[]{:S(2)}) collective-permute-start(bf16[256,1024]{1,0:T(8,128)(2,1)S(1)} %add.38.mine_ref), channel_id=1, source_target_pairs={{0,6},{1,3},{2,4},{3,1},{4,2},{5,7},{6,0},{7,5},{8,14},{9,11},{10,... | collective-permute-start | bytes 1572872 | tf_op jit(solution)/shard_map/ppermute | solution.py:37
  75.2 3.6 %collective-permute-done.6.came_ref = bf16[256,1024]{1,0:T(8,128)(2,1)S(1)} collective-permute-done((bf16[256,1024]{1,0:T(8,128)(2,1)S(1)}, bf16[256,1024]{1,0:T(8,128)(2,1)S(1)}, u32[]{:S(2)}, u32[]{:S(2)}) %collective-permute-start.6) | collective-permute-done | bytes 524320 | tf_op jit(solution)/shard_map/ppermute | solution.py:37
  78.8 0.1 add.37.mine_ref
  78.9 1.9 %collective-permute-start.9 = (bf16[256,1024]{1,0:T(8,128)(2,1)S(1)}, bf16[256,1024]{1,0:T(8,128)(2,1)S(1)}, u32[]{:S(2)}, u32[]{:S(2)}) collective-permute-start(bf16[256,1024]{1,0:T(8,128)(2,1)S(1)} %add.37.mine_ref), channel_id=1, source_target_pairs={{0,6},{1,3},{2,4},{3,1},{4,2},{5,7},{6,0},{7,5},{8,14},{9,11},{10,... | collective-permute-start | bytes 1572872 | tf_op jit(solution)/shard_map/ppermute | solution.py:37
  80.8 6.9 %collective-permute-done.8.came_ref = bf16[256,1024]{1,0:T(8,128)(2,1)S(1)} collective-permute-done((bf16[256,1024]{1,0:T(8,128)(2,1)S(1)}, bf16[256,1024]{1,0:T(8,128)(2,1)S(1)}, u32[]{:S(2)}, u32[]{:S(2)}) %collective-permute-start.8) | collective-permute-done | bytes 524320 | tf_op jit(solution)/shard_map/ppermute | solution.py:37
  87.8 0.2 square.2.refs_0_
  87.9 4.3 %collective-permute-start.10 = (bf16[256,1024]{1,0:T(8,128)(2,1)S(1)}, bf16[256,1024]{1,0:T(8,128)(2,1)S(1)}, u32[]{:S(2)}, u32[]{:S(2)}) collective-permute-start(bf16[256,1024]{1,0:T(8,128)(2,1)S(1)} %square.2.refs_0_), channel_id=1, source_target_pairs={{0,2},{1,7},{2,0},{3,5},{4,6},{5,3},{6,4},{7,1},{8,10},{9,15},{10,... | collective-permute-start | bytes 1572872 | tf_op jit(solution)/shard_map/ppermute | solution.py:37
  92.3 1.1 collective-permute-done.9.came_ref
  93.4 0.2 square.3.refs_1_
  93.6 4.3 %collective-permute-start.11 = (bf16[256,1024]{1,0:T(8,128)(2,1)S(1)}, bf16[256,1024]{1,0:T(8,128)(2,1)S(1)}, u32[]{:S(2)}, u32[]{:S(2)}) collective-permute-start(bf16[256,1024]{1,0:T(8,128)(2,1)S(1)} %square.3.refs_1_), channel_id=1, source_target_pairs={{0,2},{1,7},{2,0},{3,5},{4,6},{5,3},{6,4},{7,1},{8,10},{9,15},{10,... | collective-permute-start | bytes 1572872 | tf_op jit(solution)/shard_map/ppermute | solution.py:37
  97.9 6.8 %collective-permute-done.10.refs_2_ = bf16[256,1024]{1,0:T(8,128)(2,1)S(1)} collective-permute-done((bf16[256,1024]{1,0:T(8,128)(2,1)S(1)}, bf16[256,1024]{1,0:T(8,128)(2,1)S(1)}, u32[]{:S(2)}, u32[]{:S(2)}) %collective-permute-start.10) | collective-permute-done | bytes 524320 | tf_op jit(solution)/shard_map/ppermute | solution.py:37
  104.7 1.7 copy-done
  106.4 1.8 %out_part.4.refs_4_ = bf16[3,2,128,512]{3,2,1,0:T(8,128)(2,1)S(1)} custom-call(s32[4]{0:T(128)S(1)} %pad_add_fusion.order_ref, s32[16,4]{1,0:T(8,128)S(1)} %slice_convert_fusion.ids_ref, bf16[256,1024]{1,0:T(8,128)(2,1)S(1)} %square.2.refs_0_, bf16[256,1024]{1,0:T(8,128)(2,1)S(1)} %square.3.refs_1_, bf16[256,1024]{1,0:T(8,128)(2,1)S(1)} %collective-permute-done.10.refs_2_, ...), custom_call_target="tpu_custom_call" | custom-call | flops 805306368 | bytes 3407872 | tf_op jit(solution)/shard_map/out_part/pallas_call | solution.py:189
  108.2 1.8 %collective-permute-done.11.refs_3_.refs_0_ = bf16[256,1024]{1,0:T(8,128)(2,1)S(1)} collective-permute-done((bf16[256,1024]{1,0:T(8,128)(2,1)S(1)}, bf16[256,1024]{1,0:T(8,128)(2,1)S(1)}, u32[]{:S(2)}, u32[]{:S(2)}) %collective-permute-start.11) | collective-permute-done | bytes 524320 | tf_op jit(solution)/shard_map/ppermute | solution.py:37
  109.9 0.0 copy-done.1
  110.0 1.2 out_part.5
  111.1 8.0 %collective-permute-start.12 = (bf16[4,2,128,512]{3,2,1,0:T(8,128)(2,1)S(1)}, bf16[4,2,128,512]{3,2,1,0:T(8,128)(2,1)S(1)}, u32[]{:S(2)}, u32[]{:S(2)}) collective-permute-start(bf16[4,2,128,512]{3,2,1,0:T(8,128)(2,1)S(1)} %out_part.5), channel_id=1, source_target_pairs={{0,1},{1,0},{2,3},{3,2},{4,5},{5,4},{6,7},{7,6},{8,9},{9,8},{10,11... | collective-permute-start | bytes 3145736 | tf_op jit(solution)/shard_map/ppermute | solution.py:28
  119.1 2.1 %out_part.3.mine_ref = f32[4,2,128,512]{3,2,1,0:T(8,128)S(1)} custom-call(s32[4]{0:T(128)S(1)} %pad_add_fusion.order_ref, s32[16,4]{1,0:T(8,128)S(1)} %slice_convert_fusion.ids_ref, bf16[256,1024]{1,0:T(8,128)(2,1)S(1)} %square.2.refs_0_, bf16[256,1024]{1,0:T(8,128)(2,1)S(1)} %square.3.refs_1_, bf16[256,1024]{1,0:T(8,128)(2,1)S(1)} %collective-permute-done.10.refs_2_, ...), custom_call_target="tpu_custom_call" | custom-call | flops 1073741824 | bytes 4194304 | tf_op jit(solution)/shard_map/out_part/pallas_call | solution.py:189
  121.3 0.1 collective-permute-done.12.came_ref
  121.4 1.8 %place.1 = bf16[8,128,512]{2,1,0:T(8,128)(2,1)} custom-call(s32[4]{0:T(128)S(1)} %pad_add_fusion.order_ref, s32[3]{0:T(128)S(1)} %pad_add_fusion.1.at_ref, f32[4,2,128,512]{3,2,1,0:T(8,128)S(1)} %out_part.3.mine_ref, bf16[4,2,128,512]{3,2,1,0:T(8,128)(2,1)S(1)} %collective-permute-done.12.came_ref), custom_call_target="tpu_custom_call" | custom-call | flops 1048576 | bytes 1051648 | tf_op jit(solution)/shard_map/place/pallas_call | solution.py:189
  123.2 7.4 %all-to-all-start.1 = ((bf16[8,128,512]{2,1,0:T(8,128)(2,1)}), bf16[8,128,512]{2,1,0:T(8,128)(2,1)S(1)}, u32[]{:S(2)}, u32[]{:S(2)}) async-start(bf16[8,128,512]{2,1,0:T(8,128)(2,1)} %place.1), calls=%async_computation.1 | async-start | bytes 2097152 | tf_op jit(solution)/shard_map/all_to_all | solution.py:286
  130.6 0.0 copy-done.3
  130.6 3.0 %steps.1 = (f32[512,256]{1,0:T(8,128)}, f32[256,512]{1,0:T(8,128)}) custom-call(s32[3]{0:T(128)S(1)} %pad_add_fusion.1.at_ref, bf16[128,128]{1,0:T(8,128)(2,1)S(1)} %bitcast.23, f32[64,512]{1,0:T(8,128)S(1)} %copy-done.4, f32[64,4096]{1,0:T(8,128)S(1)} %copy-done.3), custom_call_target="tpu_custom_call" | custom-call | flops 134217728 | bytes 1048576 | tf_op jit(solution)/shard_map/steps/pallas_call | solution.py:189
  133.6 26.2 %all-to-all-done.1 = bf16[8,128,512]{2,1,0:T(8,128)(2,1)S(1)} async-done(((bf16[8,128,512]{2,1,0:T(8,128)(2,1)}), bf16[8,128,512]{2,1,0:T(8,128)(2,1)S(1)}, u32[]{:S(2)}, u32[]{:S(2)}) %all-to-all-start.1) | async-done | bytes 1048608 | tf_op jit(solution)/shard_map/all_to_all | solution.py:286
  159.8 0.8 reduce_sum.12
  (12 shorter events, 0.1 us)
Async XLA Ops:
  7.2 16.5 %copy-start.5 = (bf16[256,512]{1,0:T(8,128)(2,1)S(1)}, bf16[256,512]{1,0:T(8,128)(2,1)}, u32[]{:S(2)}) copy-start(bf16[256,512]{1,0:T(8,128)(2,1)} %param.11) | copy-start | bytes 786436
  7.2 34.5 %copy-start.4 = (f32[64,512]{1,0:T(8,128)S(1)}, f32[64,512]{1,0:T(8,128)}, u32[]{:S(2)}) copy-start(f32[64,512]{1,0:T(8,128)} %bank_ref.1) | copy-start | bytes 393220
  7.2 51.9 %all-gather.5.cloned.1.call-start = ((), (), s32[]{:S(2)}) async-start(), calls=%async_computation.2 | async-start | bytes 2359296 | tf_op jit(solution)/shard_map/all_gather | solution.py:232
  7.2 10.3 %collective-permute-start.3 = (bf16[512,256]{1,0:T(8,128)(2,1)}, bf16[512,256]{1,0:T(8,128)(2,1)S(1)}, u32[]{:S(2)}, u32[]{:S(2)}) collective-permute-start(bf16[512,256]{1,0:T(8,128)(2,1)} %param.10), channel_id=1, source_target_pairs={{0,1},{1,0},{2,3},{3,2},{4,5},{5,4},{6,7},{7,6},{8,9},{9,8},{10,11... | collective-permute-start | bytes 786440 | tf_op jit(solution)/shard_map/ppermute | solution.py:28
  20.2 19.6 %all-to-all-start = ((bf16[4,144,512]{2,1,0:T(8,128)(2,1)}), bf16[4,144,512]{2,1,0:T(8,128)(2,1)S(1)}, u32[]{:S(2)}, u32[]{:S(2)}) async-start(bf16[4,144,512]{2,1,0:T(8,128)(2,1)} %shift.1), calls=%async_computation | async-start | bytes 1179648 | tf_op jit(solution)/shard_map/all_to_all | solution.py:221
  23.6 81.1 %all-gather.7.cloned.1.call-start = ((), (), s32[]{:S(2)}) async-start(), calls=%async_computation.3 | async-start | bytes 2654208 | tf_op jit(solution)/shard_map/all_gather | solution.py:236
  23.7 21.8 %collective-permute-start.4 = (bf16[256,512]{1,0:T(8,128)(2,1)S(1)}, bf16[256,512]{1,0:T(8,128)(2,1)S(1)}, u32[]{:S(2)}, u32[]{:S(2)}) collective-permute-start(bf16[256,512]{1,0:T(8,128)(2,1)S(1)} %copy-done.5), channel_id=1, source_target_pairs={{0,1},{1,0},{2,3},{3,2},{4,5},{5,4},{6,7},{7,6},{8,9},{9,8},{10,11... | collective-permute-start | bytes 786440 | tf_op jit(solution)/shard_map/ppermute | solution.py:28
  39.7 11.8 %collective-permute-start = (bf16[4,144,512]{2,1,0:T(8,128)(2,1)S(1)}, bf16[4,144,512]{2,1,0:T(8,128)(2,1)S(1)}, u32[]{:S(2)}, u32[]{:S(2)}) collective-permute-start(bf16[4,144,512]{2,1,0:T(8,128)(2,1)S(1)} %all-to-all-done.refs_0_), channel_id=1, source_target_pairs={{0,8},{1,57},{8,0},{9,17},{16,24},{17,9},{24,16},{25,33},{32,40},{... | collective-permute-start | bytes 1769480 | tf_op jit(solution)/shard_map/ppermute | solution.py:46
  41.7 3.8 %collective-permute-start.5 = (f32[64,512]{1,0:T(8,128)S(1)}, f32[64,512]{1,0:T(8,128)S(1)}, u32[]{:S(2)}, u32[]{:S(2)}) collective-permute-start(f32[64,512]{1,0:T(8,128)S(1)} %copy-done.4), channel_id=1, source_target_pairs={{0,1},{1,0},{2,3},{3,2},{4,5},{5,4},{6,7},{7,6},{8,9},{9,8},{10,11... | collective-permute-start | bytes 393224 | tf_op jit(solution)/shard_map/ppermute | solution.py:28
  52.3 6.4 %collective-permute-start.1 = (bf16[4,144,512]{2,1,0:T(8,128)(2,1)S(1)}, bf16[4,144,512]{2,1,0:T(8,128)(2,1)S(1)}, u32[]{:S(2)}, u32[]{:S(2)}) collective-permute-start(bf16[4,144,512]{2,1,0:T(8,128)(2,1)S(1)} %all-to-all-done.refs_0_), channel_id=1, source_target_pairs={{0,1},{1,0},{2,3},{3,2},{4,5},{5,4},{6,7},{7,6},{8,9},{9,8},{10,11... | collective-permute-start | bytes 1769480 | tf_op jit(solution)/shard_map/ppermute | solution.py:28
  55.2 3.9 %collective-permute-start.2 = (bf16[4,144,512]{2,1,0:T(8,128)(2,1)S(1)}, bf16[4,144,512]{2,1,0:T(8,128)(2,1)S(1)}, u32[]{:S(2)}, u32[]{:S(2)}) collective-permute-start(bf16[4,144,512]{2,1,0:T(8,128)(2,1)S(1)} %collective-permute-done.refs_1_), channel_id=1, source_target_pairs={{0,1},{1,0},{2,3},{3,2},{4,5},{5,4},{6,7},{7,6},{8,9},{9,8},{10,11... | collective-permute-start | bytes 1769480 | tf_op jit(solution)/shard_map/ppermute | solution.py:28
  59.1 1.6 copy-start.2
  62.0 11.1 %collective-permute-start.7 = (bf16[256,1024]{1,0:T(8,128)(2,1)S(1)}, bf16[256,1024]{1,0:T(8,128)(2,1)S(1)}, u32[]{:S(2)}, u32[]{:S(2)}) collective-permute-start(bf16[256,1024]{1,0:T(8,128)(2,1)S(1)} %key_part.5), channel_id=1, source_target_pairs={{0,2},{1,7},{2,0},{3,5},{4,6},{5,3},{6,4},{7,1},{8,10},{9,15},{10,... | collective-permute-start | bytes 1572872 | tf_op jit(solution)/shard_map/ppermute | solution.py:37
  66.7 12.1 %collective-permute-start.6 = (bf16[256,1024]{1,0:T(8,128)(2,1)S(1)}, bf16[256,1024]{1,0:T(8,128)(2,1)S(1)}, u32[]{:S(2)}, u32[]{:S(2)}) collective-permute-start(bf16[256,1024]{1,0:T(8,128)(2,1)S(1)} %key_part.4), channel_id=1, source_target_pairs={{0,2},{1,7},{2,0},{3,5},{4,6},{5,3},{6,4},{7,1},{8,10},{9,15},{10,... | collective-permute-start | bytes 1572872 | tf_op jit(solution)/shard_map/ppermute | solution.py:37
  73.3 14.5 %collective-permute-start.8 = (bf16[256,1024]{1,0:T(8,128)(2,1)S(1)}, bf16[256,1024]{1,0:T(8,128)(2,1)S(1)}, u32[]{:S(2)}, u32[]{:S(2)}) collective-permute-start(bf16[256,1024]{1,0:T(8,128)(2,1)S(1)} %add.38.mine_ref), channel_id=1, source_target_pairs={{0,6},{1,3},{2,4},{3,1},{4,2},{5,7},{6,0},{7,5},{8,14},{9,11},{10,... | collective-permute-start | bytes 1572872 | tf_op jit(solution)/shard_map/ppermute | solution.py:37
  78.9 14.5 %collective-permute-start.9 = (bf16[256,1024]{1,0:T(8,128)(2,1)S(1)}, bf16[256,1024]{1,0:T(8,128)(2,1)S(1)}, u32[]{:S(2)}, u32[]{:S(2)}) collective-permute-start(bf16[256,1024]{1,0:T(8,128)(2,1)S(1)} %add.37.mine_ref), channel_id=1, source_target_pairs={{0,6},{1,3},{2,4},{3,1},{4,2},{5,7},{6,0},{7,5},{8,14},{9,11},{10,... | collective-permute-start | bytes 1572872 | tf_op jit(solution)/shard_map/ppermute | solution.py:37
  87.9 16.8 %collective-permute-start.10 = (bf16[256,1024]{1,0:T(8,128)(2,1)S(1)}, bf16[256,1024]{1,0:T(8,128)(2,1)S(1)}, u32[]{:S(2)}, u32[]{:S(2)}) collective-permute-start(bf16[256,1024]{1,0:T(8,128)(2,1)S(1)} %square.2.refs_0_), channel_id=1, source_target_pairs={{0,2},{1,7},{2,0},{3,5},{4,6},{5,3},{6,4},{7,1},{8,10},{9,15},{10,... | collective-permute-start | bytes 1572872 | tf_op jit(solution)/shard_map/ppermute | solution.py:37
  93.6 16.4 %collective-permute-start.11 = (bf16[256,1024]{1,0:T(8,128)(2,1)S(1)}, bf16[256,1024]{1,0:T(8,128)(2,1)S(1)}, u32[]{:S(2)}, u32[]{:S(2)}) collective-permute-start(bf16[256,1024]{1,0:T(8,128)(2,1)S(1)} %square.3.refs_1_), channel_id=1, source_target_pairs={{0,2},{1,7},{2,0},{3,5},{4,6},{5,3},{6,4},{7,1},{8,10},{9,15},{10,... | collective-permute-start | bytes 1572872 | tf_op jit(solution)/shard_map/ppermute | solution.py:37
  104.7 1.7 copy-start
  106.4 3.6 %copy-start.1 = (bf16[1152,1024]{1,0:T(8,128)(2,1)S(1)}, bf16[1152,1024]{1,0:T(8,128)(2,1)}, u32[]{:S(2)}) copy-start(bf16[1152,1024]{1,0:T(8,128)(2,1)} %all-gather.7.cloned.1.call-done) | copy-start | bytes 7077892
  111.1 10.3 %collective-permute-start.12 = (bf16[4,2,128,512]{3,2,1,0:T(8,128)(2,1)S(1)}, bf16[4,2,128,512]{3,2,1,0:T(8,128)(2,1)S(1)}, u32[]{:S(2)}, u32[]{:S(2)}) collective-permute-start(bf16[4,2,128,512]{3,2,1,0:T(8,128)(2,1)S(1)} %out_part.5), channel_id=1, source_target_pairs={{0,1},{1,0},{2,3},{3,2},{4,5},{5,4},{6,7},{7,6},{8,9},{9,8},{10,11... | collective-permute-start | bytes 3145736 | tf_op jit(solution)/shard_map/ppermute | solution.py:28
  123.2 7.4 %copy-start.3 = (f32[64,4096]{1,0:T(8,128)S(1)}, f32[64,4096]{1,0:T(8,128)}, u32[]{:S(2)}) copy-start(f32[64,4096]{1,0:T(8,128)} %hid_ref.1) | copy-start | bytes 3145732
  123.2 36.6 %all-to-all-start.1 = ((bf16[8,128,512]{2,1,0:T(8,128)(2,1)}), bf16[8,128,512]{2,1,0:T(8,128)(2,1)S(1)}, u32[]{:S(2)}, u32[]{:S(2)}) async-start(bf16[8,128,512]{2,1,0:T(8,128)(2,1)} %place.1), calls=%async_computation.1 | async-start | bytes 2097152 | tf_op jit(solution)/shard_map/all_to_all | solution.py:286
Sparse Core Ops, SparseCore 0:
  18.4 39.5 all-gather.4
  60.6 44.0 all-gather.6

commit v7 on v5

--- a/solution.py
+++ b/solution.py
@@ -116,8 +116,8 @@
     out_ref[...] = (kept_ref[...] + came_ref[...].astype(jnp.float32)).astype(jnp.bfloat16)
 
 
-def square_kernel(kept_ref, first_ref, second_ref, out_ref):
-    total = kept_ref[...] + first_ref[...].astype(jnp.float32) + second_ref[...].astype(jnp.float32)
+def square_kernel(mine_ref, came_ref, out_ref):
+    total = mine_ref[...].astype(jnp.float32) + came_ref[...].astype(jnp.float32)
     out_ref[...] = (jnp.maximum(total, 0.0) ** 2).astype(jnp.bfloat16)
 
 
@@ -237,12 +237,8 @@
     value_all = lax.all_gather(jnp.concatenate([value_pack, info], axis=0), "z", axis=0)
     everyone = value_all[:, half : half + members, :128].reshape(NZ * members, 128)
 
-    lo, hi = lax.rem(x, 2), x // 2
-    f, g = jnp.where(core == 0, lax.rem(lo + hi, 2), hi), jnp.where(core == 0, hi, lo)
-    turned = jnp.where(core == 0, 1 - g, g)
-    order = []
-    for upper, lower in ((f, g), (f, 1 - g), (1 - f, turned), (1 - f, 1 - turned)):
-        order.append(jnp.where(core == 0, 2 * lower + lax.rem(upper + lower, 2), 2 * upper + lower))
+    before, after = NX - 1 - x, x + 1 - 2 * lax.rem(x, 2)
+    order = [x, jnp.where(core == 0, before, after), jnp.where(core == 0, after, before), lax.rem(x + 2, NX)]
     order = jnp.stack(order).astype(jnp.int32)
     deep, wide, quarter = 2 * feat, NZ * half, NY * tok // NX
     low, high = ((quarter, wide), jnp.bfloat16), ((quarter, wide), jnp.float32)
@@ -261,25 +257,24 @@
     def local(kernel, name, *args):
         return call(kernel, name, [low], [VMEM] * len(args), cost(quarter, 4, wide), args)[0]
 
-    came_first = exchange(key_part((2,), [low])[0], 0)
-    came_second = exchange(key_part((3,), [low])[0], 0)
-    following, kept = key_part((1, 0), [high, high])
-    came_next = exchange(local(add_kernel, "add", following, came_first), 1)
-    key_own = local(square_kernel, "square", kept, came_second, came_next)
-
-    before, after = NX - 1 - x, x + 1 - 2 * lo
-    around = [x, jnp.where(core == 0, before, after), jnp.where(core == 0, after, before), lax.rem(x + 2, NX)]
-    around = jnp.stack(around).astype(jnp.int32)
-    key_next = exchange(key_own, 1)
-    key_second = exchange(key_own, 0)
-    keys = key_own, key_next, key_second, exchange(key_next, 0)
+    came_next = exchange(key_part((3,), [low])[0], 0)
+    came_own = exchange(key_part((2,), [low])[0], 0)
+    sum_next, sum_own = key_part((1, 0), [high, high])
+    sum_next = local(add_kernel, "add", sum_next, came_next)
+    other_own = exchange(sum_next, 1)
+    sum_own = local(add_kernel, "add", sum_own, came_own)
+    other_next = exchange(sum_own, 1)
+    key_own = local(square_kernel, "square", sum_own, other_own)
+    key_first = exchange(key_own, 0)
+    key_next = local(square_kernel, "square", sum_next, other_next)
+    keys = key_own, key_next, key_first, exchange(key_next, 0)
 
     def out_part(half, which, bank, kept, *after):
         out = len(which), 2, tok, feat
         return call(
             functools.partial(out_kernel, half, which), "out_part", [(out, kept)],
             [SMEM] * 2 + [VMEM] * (len(which) + 3) + [ANY] * len(after), cost(len(which) * quarter, wide, feat),
-            (around, ids, *[keys[i] for i in which], value_all, bank, hidden, *after),
+            (order, ids, *[keys[i] for i in which], value_all, bank, hidden, *after),
         )[0]
 
     sets = (0, 1, 2), (3,)
@@ -289,7 +284,7 @@
         parts += [out_part(0, which, dim_bank, jnp.float32), came]
     result = call(
         functools.partial(place_kernel, sets), "place", [((NY, tok, feat), jnp.bfloat16)],
-        [SMEM] * 2 + [VMEM] * 4, cost(NY * tok, 1, feat), (around, at, *parts),
+        [SMEM] * 2 + [VMEM] * 4, cost(NY * tok, 1, feat), (order, at, *parts),
     )[0]
     result, everyone = lax.optimization_barrier((result, everyone))
     pieces = lax.all_to_all(result, YQ + ("y_low",), 0, 0)

time: 168 us -> 167 us (level)
    pallas_call x13 -> x15, Pallas kernels: 19.1 us -> 19.2 us  [call(): pl.pallas_call(kernel, out_shape=[jax.ShapeDtypeStruct(*out) for out in o...]
  transfers between devices with their start and end apart: 18 -> 18, of which waited for: 11 -> 12; matrix products, arithmetic and copies ran while one was open for 1% -> 1% of each run, Pallas kernels for 10% -> 11%
where the time goes in v7:
time: 167 us; the launch traced here: 166 us
  waiting for transfers between devices  67.7 us (41%)
  starting transfers between devices  58.3 us (35%)
  Pallas kernels  19.2 us (11%)
  between operations  14.4 us (9%)
  local copies, waits for them, and re-layouts  4.25 us (3%)
  other arithmetic  2.45 us (1%)
    ppermute x7, starting transfers between devices, swap(): return lax.ppermute(x, 'core', [(0, 1), (1, 0)])  26.7 us
    all_to_all x1, waiting for transfers between devices, shards(): pieces = lax.all_to_all(result, YQ + ('y_low',), 0, 0)  26.2 us
    ppermute x6, waiting for transfers between devices, exchange(): return lax.ppermute(x, ('x', 'core'), pairs)  19.7 us
    pallas_call x15, Pallas kernels, call(): pl.pallas_call(kernel, out_shape=[jax.ShapeDtypeStruct(*out) for out in o...  19.2 us
    ppermute x6, starting transfers between devices, exchange(): return lax.ppermute(x, ('x', 'core'), pairs)  19 us
    all_to_all x1, waiting for transfers between devices, shards(): same = lax.all_to_all(shifted, YQ, 0, 0)  13.7 us
    all_to_all x1, starting transfers between devices, shards(): pieces = lax.all_to_all(result, YQ + ('y_low',), 0, 0)  7.12 us
    ppermute x1, waiting for transfers between devices, beside(): return lax.ppermute(x, YQ + ('y_low', 'core'), pairs)  6.03 us
  transfers between devices with their start and end apart: 18, of which 12 were waited for; matrix products, arithmetic and copies ran while one was open for 1% of the time, Pallas kernels for 11%

profile of v7, /device:TPU:1, one launch (start us, length us, event | category | flops | bytes accessed | tf_op | source)
XLA Modules:
  0.0 166.2 jit_solution(2701677471293341570)
XLA Ops:
  7.2 0.0 copy-start.5
  7.2 0.0 copy-start.3
  7.2 0.0 all-gather.5.cloned.1.call-start
  7.2 8.9 %collective-permute-start.3 = (bf16[512,256]{1,0:T(8,128)(2,1)}, bf16[512,256]{1,0:T(8,128)(2,1)S(1)}, u32[]{:S(2)}, u32[]{:S(2)}) collective-permute-start(bf16[512,256]{1,0:T(8,128)(2,1)} %param.10), channel_id=1, source_target_pairs={{0,1},{1,0},{2,3},{3,2},{4,5},{5,4},{6,7},{7,6},{8,9},{9,8},{10,11... | collective-permute-start | bytes 786440 | tf_op jit(solution)/shard_map/ppermute | solution.py:29
  16.2 0.9 constant_dynamic-slice_fusion.3
  17.1 0.4 collective-permute-done.3
  17.5 0.7 pad_maximum_fusion
  18.2 0.0 all-gather.5.cloned.1.call-update
  18.3 1.9 %shift.1 = bf16[4,144,512]{2,1,0:T(8,128)(2,1)} custom-call(s32[2,4]{1,0:T(2,128)} %picks_hbm.1, s32[2]{0:T(128)} %ranks_hbm.1, bf16[128,512]{1,0:T(8,128)(2,1)} %x_hbm.1, f32[1,512]{1,0:T(1,128)} %bitcast.27), custom_call_target="tpu_custom_call" | custom-call | flops 2097152 | bytes 151552 | tf_op jit(solution)/shard_map/shift/pallas_call | solution.py:190
  20.1 3.5 %all-to-all-start = ((bf16[4,144,512]{2,1,0:T(8,128)(2,1)}), bf16[4,144,512]{2,1,0:T(8,128)(2,1)S(1)}, u32[]{:S(2)}, u32[]{:S(2)}) async-start(bf16[4,144,512]{2,1,0:T(8,128)(2,1)} %shift.1), calls=%async_computation | async-start | bytes 1179648 | tf_op jit(solution)/shard_map/all_to_all | solution.py:222
  23.6 0.0 all-gather.7.cloned.1.call-start
  23.7 0.0 copy-done.5
  23.7 2.3 %collective-permute-start.4 = (bf16[256,512]{1,0:T(8,128)(2,1)S(1)}, bf16[256,512]{1,0:T(8,128)(2,1)S(1)}, u32[]{:S(2)}, u32[]{:S(2)}) collective-permute-start(bf16[256,512]{1,0:T(8,128)(2,1)S(1)} %copy-done.5), channel_id=1, source_target_pairs={{0,1},{1,0},{2,3},{3,2},{4,5},{5,4},{6,7},{7,6},{8,9},{9,8},{10,11... | collective-permute-start | bytes 786440 | tf_op jit(solution)/shard_map/ppermute | solution.py:29
  26.0 13.7 %all-to-all-done.refs_0_ = bf16[4,144,512]{2,1,0:T(8,128)(2,1)S(1)} async-done(((bf16[4,144,512]{2,1,0:T(8,128)(2,1)}), bf16[4,144,512]{2,1,0:T(8,128)(2,1)S(1)}, u32[]{:S(2)}, u32[]{:S(2)}) %all-to-all-start) | async-done | bytes 589856 | tf_op jit(solution)/shard_map/all_to_all | solution.py:222
  39.7 1.9 %collective-permute-start = (bf16[4,144,512]{2,1,0:T(8,128)(2,1)S(1)}, bf16[4,144,512]{2,1,0:T(8,128)(2,1)S(1)}, u32[]{:S(2)}, u32[]{:S(2)}) collective-permute-start(bf16[4,144,512]{2,1,0:T(8,128)(2,1)S(1)} %all-to-all-done.refs_0_), channel_id=1, source_target_pairs={{0,8},{1,57},{8,0},{9,17},{16,24},{17,9},{24,16},{25,33},{32,40},{... | collective-permute-start | bytes 1769480 | tf_op jit(solution)/shard_map/ppermute | solution.py:47
  41.6 0.0 copy-done.3
  41.6 2.9 %collective-permute-start.5 = (f32[64,512]{1,0:T(8,128)S(1)}, f32[64,512]{1,0:T(8,128)S(1)}, u32[]{:S(2)}, u32[]{:S(2)}) collective-permute-start(f32[64,512]{1,0:T(8,128)S(1)} %copy-done.3), channel_id=1, source_target_pairs={{0,1},{1,0},{2,3},{3,2},{4,5},{5,4},{6,7},{7,6},{8,9},{9,8},{10,11... | collective-permute-start | bytes 393224 | tf_op jit(solution)/shard_map/ppermute | solution.py:29
  44.5 0.9 collective-permute-done.5.refs_6_.refs_4_.refs_2_
  45.5 0.0 collective-permute-done.4
  45.5 6.0 %collective-permute-done.refs_1_ = bf16[4,144,512]{2,1,0:T(8,128)(2,1)S(1)} collective-permute-done((bf16[4,144,512]{2,1,0:T(8,128)(2,1)S(1)}, bf16[4,144,512]{2,1,0:T(8,128)(2,1)S(1)}, u32[]{:S(2)}, u32[]{:S(2)}) %collective-permute-start) | collective-permute-done | bytes 589856 | tf_op jit(solution)/shard_map/ppermute | solution.py:47
  51.6 0.7 fusion.1
  52.3 0.0 all-gather.7.cloned.1.call-update
  52.3 2.8 %collective-permute-start.1 = (bf16[4,144,512]{2,1,0:T(8,128)(2,1)S(1)}, bf16[4,144,512]{2,1,0:T(8,128)(2,1)S(1)}, u32[]{:S(2)}, u32[]{:S(2)}) collective-permute-start(bf16[4,144,512]{2,1,0:T(8,128)(2,1)S(1)} %all-to-all-done.refs_0_), channel_id=1, source_target_pairs={{0,1},{1,0},{2,3},{3,2},{4,5},{5,4},{6,7},{7,6},{8,9},{9,8},{10,11... | collective-permute-start | bytes 1769480 | tf_op jit(solution)/shard_map/ppermute | solution.py:29
  55.1 1.9 %collective-permute-start.2 = (bf16[4,144,512]{2,1,0:T(8,128)(2,1)S(1)}, bf16[4,144,512]{2,1,0:T(8,128)(2,1)S(1)}, u32[]{:S(2)}, u32[]{:S(2)}) collective-permute-start(bf16[4,144,512]{2,1,0:T(8,128)(2,1)S(1)} %collective-permute-done.refs_1_), channel_id=1, source_target_pairs={{0,1},{1,0},{2,3},{3,2},{4,5},{5,4},{6,7},{7,6},{8,9},{9,8},{10,11... | collective-permute-start | bytes 1769480 | tf_op jit(solution)/shard_map/ppermute | solution.py:29
  57.1 0.1 pad_add_fusion.1.at_ref
  57.1 1.5 hidden.1.refs_7_.refs_5_.refs_3_
  58.7 0.1 pad_add_fusion.order_ref
  58.7 0.0 collective-permute-done.1.refs_2_
  58.7 0.3 collective-permute-done.2.refs_3_
  59.0 1.6 copy-done.2
  60.6 1.4 key_part.5
  62.0 3.3 %collective-permute-start.7 = (bf16[256,1024]{1,0:T(8,128)(2,1)S(1)}, bf16[256,1024]{1,0:T(8,128)(2,1)S(1)}, u32[]{:S(2)}, u32[]{:S(2)}) collective-permute-start(bf16[256,1024]{1,0:T(8,128)(2,1)S(1)} %key_part.5), channel_id=1, source_target_pairs={{0,2},{1,7},{2,0},{3,5},{4,6},{5,3},{6,4},{7,1},{8,10},{9,15},{10,... | collective-permute-start | bytes 1572872 | tf_op jit(solution)/shard_map/ppermute | solution.py:38
  65.3 1.4 key_part.4
  66.7 3.2 %collective-permute-start.6 = (bf16[256,1024]{1,0:T(8,128)(2,1)S(1)}, bf16[256,1024]{1,0:T(8,128)(2,1)S(1)}, u32[]{:S(2)}, u32[]{:S(2)}) collective-permute-start(bf16[256,1024]{1,0:T(8,128)(2,1)S(1)} %key_part.4), channel_id=1, source_target_pairs={{0,2},{1,7},{2,0},{3,5},{4,6},{5,3},{6,4},{7,1},{8,10},{9,15},{10,... | collective-permute-start | bytes 1572872 | tf_op jit(solution)/shard_map/ppermute | solution.py:38
  69.9 2.0 %key_part.3 = (f32[256,1024]{1,0:T(8,128)S(1)}, f32[256,1024]{1,0:T(8,128)S(1)}) custom-call(s32[4]{0:T(128)S(1)} %pad_add_fusion.order_ref, s32[16,4]{1,0:T(8,128)S(1)} %slice_convert_fusion.ids_ref, bf16[4,144,512]{2,1,0:T(8,128)(2,1)S(1)} %all-to-all-done.refs_0_, bf16[4,144,512]{2,1,0:T(8,128)(2,1)S(1)} %collective-permute-done.refs_1_, ...), custom_call_target="tpu_custom_call" | custom-call | flops 1073741824 | bytes 4194304 | tf_op jit(solution)/shard_map/key_part/pallas_call | solution.py:190
  71.9 1.2 collective-permute-done.7.came_ref
  73.2 0.1 add.38.mine_ref
  73.3 1.9 %collective-permute-start.8 = (bf16[256,1024]{1,0:T(8,128)(2,1)S(1)}, bf16[256,1024]{1,0:T(8,128)(2,1)S(1)}, u32[]{:S(2)}, u32[]{:S(2)}) collective-permute-start(bf16[256,1024]{1,0:T(8,128)(2,1)S(1)} %add.38.mine_ref), channel_id=1, source_target_pairs={{0,6},{1,3},{2,4},{3,1},{4,2},{5,7},{6,0},{7,5},{8,14},{9,11},{10,... | collective-permute-start | bytes 1572872 | tf_op jit(solution)/shard_map/ppermute | solution.py:38
  75.2 3.6 %collective-permute-done.6.came_ref = bf16[256,1024]{1,0:T(8,128)(2,1)S(1)} collective-permute-done((bf16[256,1024]{1,0:T(8,128)(2,1)S(1)}, bf16[256,1024]{1,0:T(8,128)(2,1)S(1)}, u32[]{:S(2)}, u32[]{:S(2)}) %collective-permute-start.6) | collective-permute-done | bytes 524320 | tf_op jit(solution)/shard_map/ppermute | solution.py:38
  78.8 0.1 add.37.mine_ref
  78.9 1.9 %collective-permute-start.9 = (bf16[256,1024]{1,0:T(8,128)(2,1)S(1)}, bf16[256,1024]{1,0:T(8,128)(2,1)S(1)}, u32[]{:S(2)}, u32[]{:S(2)}) collective-permute-start(bf16[256,1024]{1,0:T(8,128)(2,1)S(1)} %add.37.mine_ref), channel_id=1, source_target_pairs={{0,6},{1,3},{2,4},{3,1},{4,2},{5,7},{6,0},{7,5},{8,14},{9,11},{10,... | collective-permute-start | bytes 1572872 | tf_op jit(solution)/shard_map/ppermute | solution.py:38
  80.8 6.9 %collective-permute-done.8.came_ref = bf16[256,1024]{1,0:T(8,128)(2,1)S(1)} collective-permute-done((bf16[256,1024]{1,0:T(8,128)(2,1)S(1)}, bf16[256,1024]{1,0:T(8,128)(2,1)S(1)}, u32[]{:S(2)}, u32[]{:S(2)}) %collective-permute-start.8) | collective-permute-done | bytes 524320 | tf_op jit(solution)/shard_map/ppermute | solution.py:38
  87.8 0.2 square.2.refs_0_
  87.9 4.3 %collective-permute-start.10 = (bf16[256,1024]{1,0:T(8,128)(2,1)S(1)}, bf16[256,1024]{1,0:T(8,128)(2,1)S(1)}, u32[]{:S(2)}, u32[]{:S(2)}) collective-permute-start(bf16[256,1024]{1,0:T(8,128)(2,1)S(1)} %square.2.refs_0_), channel_id=1, source_target_pairs={{0,2},{1,7},{2,0},{3,5},{4,6},{5,3},{6,4},{7,1},{8,10},{9,15},{10,... | collective-permute-start | bytes 1572872 | tf_op jit(solution)/shard_map/ppermute | solution.py:38
  92.3 1.1 collective-permute-done.9.came_ref
  93.4 0.2 square.3.refs_1_
  93.6 4.3 %collective-permute-start.12 = (bf16[256,1024]{1,0:T(8,128)(2,1)S(1)}, bf16[256,1024]{1,0:T(8,128)(2,1)S(1)}, u32[]{:S(2)}, u32[]{:S(2)}) collective-permute-start(bf16[256,1024]{1,0:T(8,128)(2,1)S(1)} %square.3.refs_1_), channel_id=1, source_target_pairs={{0,2},{1,7},{2,0},{3,5},{4,6},{5,3},{6,4},{7,1},{8,10},{9,15},{10,... | collective-permute-start | bytes 1572872 | tf_op jit(solution)/shard_map/ppermute | solution.py:38
  97.9 6.8 %collective-permute-done.10.refs_2_ = bf16[256,1024]{1,0:T(8,128)(2,1)S(1)} collective-permute-done((bf16[256,1024]{1,0:T(8,128)(2,1)S(1)}, bf16[256,1024]{1,0:T(8,128)(2,1)S(1)}, u32[]{:S(2)}, u32[]{:S(2)}) %collective-permute-start.10) | collective-permute-done | bytes 524320 | tf_op jit(solution)/shard_map/ppermute | solution.py:38
  104.7 1.7 %copy-done = bf16[1152,1024]{1,0:T(8,128)(2,1)S(1)} copy-done((bf16[1152,1024]{1,0:T(8,128)(2,1)S(1)}, bf16[1152,1024]{1,0:T(8,128)(2,1)}, u32[]{:S(2)}) %copy-start) | copy-done | bytes 2359320
  106.4 1.8 %out_part.5 = bf16[3,2,128,512]{3,2,1,0:T(8,128)(2,1)S(1)} custom-call(s32[4]{0:T(128)S(1)} %pad_add_fusion.order_ref, s32[16,4]{1,0:T(8,128)S(1)} %slice_convert_fusion.ids_ref, bf16[256,1024]{1,0:T(8,128)(2,1)S(1)} %square.2.refs_0_, bf16[256,1024]{1,0:T(8,128)(2,1)S(1)} %square.3.refs_1_, bf16[256,1024]{1,0:T(8,128)(2,1)S(1)} %collective-permute-done.10.refs_2_, ...), custom_call_target="tpu_custom_call" | custom-call | flops 805306368 | bytes 3407872 | tf_op jit(solution)/shard_map/out_part/pallas_call | solution.py:190
  108.2 0.0 copy-start.1
  108.2 5.9 %collective-permute-start.11 = (bf16[3,2,128,512]{3,2,1,0:T(8,128)(2,1)S(1)}, bf16[3,2,128,512]{3,2,1,0:T(8,128)(2,1)S(1)}, u32[]{:S(2)}, u32[]{:S(2)}) collective-permute-start(bf16[3,2,128,512]{3,2,1,0:T(8,128)(2,1)S(1)} %out_part.5), channel_id=1, source_target_pairs={{0,1},{1,0},{2,3},{3,2},{4,5},{5,4},{6,7},{7,6},{8,9},{9,8},{10,11... | collective-permute-start | bytes 2359304 | tf_op jit(solution)/shard_map/ppermute | solution.py:29
  114.1 1.8 %out_part.4.refs_4_.refs_0_ = f32[3,2,128,512]{3,2,1,0:T(8,128)S(1)} custom-call(s32[4]{0:T(128)S(1)} %pad_add_fusion.order_ref, s32[16,4]{1,0:T(8,128)S(1)} %slice_convert_fusion.ids_ref, bf16[256,1024]{1,0:T(8,128)(2,1)S(1)} %square.2.refs_0_, bf16[256,1024]{1,0:T(8,128)(2,1)S(1)} %square.3.refs_1_, bf16[256,1024]{1,0:T(8,128)(2,1)S(1)} %collective-permute-done.10.refs_2_, ...), custom_call_target="tpu_custom_call" | custom-call | flops 805306368 | bytes 3407872 | tf_op jit(solution)/shard_map/out_part/pallas_call | solution.py:190
  115.9 0.0 collective-permute-done.12.refs_0_
  115.9 1.1 out_part.7
  117.0 2.0 %collective-permute-start.13 = (bf16[1,2,128,512]{3,2,1,0:T(8,128)(2,1)S(1)}, bf16[1,2,128,512]{3,2,1,0:T(8,128)(2,1)S(1)}, u32[]{:S(2)}, u32[]{:S(2)}) collective-permute-start(bf16[1,2,128,512]{3,2,1,0:T(8,128)(2,1)S(1)} %out_part.7), channel_id=1, source_target_pairs={{0,1},{1,0},{2,3},{3,2},{4,5},{5,4},{6,7},{7,6},{8,9},{9,8},{10,11... | collective-permute-start | bytes 786440 | tf_op jit(solution)/shard_map/ppermute | solution.py:29
  119.1 1.1 out_part.6.refs_2_
  120.2 0.3 collective-permute-done.13.refs_3_
  120.5 0.0 collective-permute-done.11.refs_1_
  120.5 1.7 %place.1 = bf16[8,128,512]{2,1,0:T(8,128)(2,1)} custom-call(s32[4]{0:T(128)S(1)} %pad_add_fusion.order_ref, s32[3]{0:T(128)S(1)} %pad_add_fusion.1.at_ref, f32[3,2,128,512]{3,2,1,0:T(8,128)S(1)} %out_part.4.refs_4_.refs_0_, bf16[3,2,128,512]{3,2,1,0:T(8,128)(2,1)S(1)} %collective-permute-done.11.refs_1_, f32[1,2,128,512]{3,2,1,0:T(8,128)S(1)} %out_part.6.refs_2_, ...), custom_call_target="tpu_custom_call" | custom-call | flops 1048576 | bytes 1051648 | tf_op jit(solution)/shard_map/place/pallas_call | solution.py:190
  122.2 7.1 %all-to-all-start.1 = ((bf16[8,128,512]{2,1,0:T(8,128)(2,1)}), bf16[8,128,512]{2,1,0:T(8,128)(2,1)S(1)}, u32[]{:S(2)}, u32[]{:S(2)}) async-start(bf16[8,128,512]{2,1,0:T(8,128)(2,1)} %place.1), calls=%async_computation.1 | async-start | bytes 2097152 | tf_op jit(solution)/shard_map/all_to_all | solution.py:290
  129.3 3.0 %steps.1 = (f32[512,256]{1,0:T(8,128)}, f32[256,512]{1,0:T(8,128)}) custom-call(s32[3]{0:T(128)S(1)} %pad_add_fusion.1.at_ref, bf16[128,128]{1,0:T(8,128)(2,1)S(1)} %bitcast.24, f32[64,512]{1,0:T(8,128)S(1)} %copy-done.3, f32[64,4096]{1,0:T(8,128)S(1)} %copy-done.4), custom_call_target="tpu_custom_call" | custom-call | flops 134217728 | bytes 1048576 | tf_op jit(solution)/shard_map/steps/pallas_call | solution.py:190
  132.3 26.2 %all-to-all-done.1 = bf16[8,128,512]{2,1,0:T(8,128)(2,1)S(1)} async-done(((bf16[8,128,512]{2,1,0:T(8,128)(2,1)}), bf16[8,128,512]{2,1,0:T(8,128)(2,1)S(1)}, u32[]{:S(2)}, u32[]{:S(2)}) %all-to-all-start.1) | async-done | bytes 1048608 | tf_op jit(solution)/shard_map/all_to_all | solution.py:290
  158.5 0.8 reduce_sum.12
  (15 shorter events, 0.1 us)
Async XLA Ops:
  7.2 16.5 %copy-start.5 = (bf16[256,512]{1,0:T(8,128)(2,1)S(1)}, bf16[256,512]{1,0:T(8,128)(2,1)}, u32[]{:S(2)}) copy-start(bf16[256,512]{1,0:T(8,128)(2,1)} %param.11) | copy-start | bytes 786436
  7.2 34.5 %copy-start.3 = (f32[64,512]{1,0:T(8,128)S(1)}, f32[64,512]{1,0:T(8,128)}, u32[]{:S(2)}) copy-start(f32[64,512]{1,0:T(8,128)} %bank_ref.1) | copy-start | bytes 393220
  7.2 51.8 %all-gather.5.cloned.1.call-start = ((), (), s32[]{:S(2)}) async-start(), calls=%async_computation.2 | async-start | bytes 2359296 | tf_op jit(solution)/shard_map/all_gather | solution.py:233
  7.2 10.3 %collective-permute-start.3 = (bf16[512,256]{1,0:T(8,128)(2,1)}, bf16[512,256]{1,0:T(8,128)(2,1)S(1)}, u32[]{:S(2)}, u32[]{:S(2)}) collective-permute-start(bf16[512,256]{1,0:T(8,128)(2,1)} %param.10), channel_id=1, source_target_pairs={{0,1},{1,0},{2,3},{3,2},{4,5},{5,4},{6,7},{7,6},{8,9},{9,8},{10,11... | collective-permute-start | bytes 786440 | tf_op jit(solution)/shard_map/ppermute | solution.py:29
  20.1 19.6 %all-to-all-start = ((bf16[4,144,512]{2,1,0:T(8,128)(2,1)}), bf16[4,144,512]{2,1,0:T(8,128)(2,1)S(1)}, u32[]{:S(2)}, u32[]{:S(2)}) async-start(bf16[4,144,512]{2,1,0:T(8,128)(2,1)} %shift.1), calls=%async_computation | async-start | bytes 1179648 | tf_op jit(solution)/shard_map/all_to_all | solution.py:222
  23.6 81.1 %all-gather.7.cloned.1.call-start = ((), (), s32[]{:S(2)}) async-start(), calls=%async_computation.3 | async-start | bytes 2654208 | tf_op jit(solution)/shard_map/all_gather | solution.py:237
  23.7 21.8 %collective-permute-start.4 = (bf16[256,512]{1,0:T(8,128)(2,1)S(1)}, bf16[256,512]{1,0:T(8,128)(2,1)S(1)}, u32[]{:S(2)}, u32[]{:S(2)}) collective-permute-start(bf16[256,512]{1,0:T(8,128)(2,1)S(1)} %copy-done.5), channel_id=1, source_target_pairs={{0,1},{1,0},{2,3},{3,2},{4,5},{5,4},{6,7},{7,6},{8,9},{9,8},{10,11... | collective-permute-start | bytes 786440 | tf_op jit(solution)/shard_map/ppermute | solution.py:29
  39.7 11.8 %collective-permute-start = (bf16[4,144,512]{2,1,0:T(8,128)(2,1)S(1)}, bf16[4,144,512]{2,1,0:T(8,128)(2,1)S(1)}, u32[]{:S(2)}, u32[]{:S(2)}) collective-permute-start(bf16[4,144,512]{2,1,0:T(8,128)(2,1)S(1)} %all-to-all-done.refs_0_), channel_id=1, source_target_pairs={{0,8},{1,57},{8,0},{9,17},{16,24},{17,9},{24,16},{25,33},{32,40},{... | collective-permute-start | bytes 1769480 | tf_op jit(solution)/shard_map/ppermute | solution.py:47
  41.6 3.8 %collective-permute-start.5 = (f32[64,512]{1,0:T(8,128)S(1)}, f32[64,512]{1,0:T(8,128)S(1)}, u32[]{:S(2)}, u32[]{:S(2)}) collective-permute-start(f32[64,512]{1,0:T(8,128)S(1)} %copy-done.3), channel_id=1, source_target_pairs={{0,1},{1,0},{2,3},{3,2},{4,5},{5,4},{6,7},{7,6},{8,9},{9,8},{10,11... | collective-permute-start | bytes 393224 | tf_op jit(solution)/shard_map/ppermute | solution.py:29
  52.3 6.4 %collective-permute-start.1 = (bf16[4,144,512]{2,1,0:T(8,128)(2,1)S(1)}, bf16[4,144,512]{2,1,0:T(8,128)(2,1)S(1)}, u32[]{:S(2)}, u32[]{:S(2)}) collective-permute-start(bf16[4,144,512]{2,1,0:T(8,128)(2,1)S(1)} %all-to-all-done.refs_0_), channel_id=1, source_target_pairs={{0,1},{1,0},{2,3},{3,2},{4,5},{5,4},{6,7},{7,6},{8,9},{9,8},{10,11... | collective-permute-start | bytes 1769480 | tf_op jit(solution)/shard_map/ppermute | solution.py:29
  55.1 3.9 %collective-permute-start.2 = (bf16[4,144,512]{2,1,0:T(8,128)(2,1)S(1)}, bf16[4,144,512]{2,1,0:T(8,128)(2,1)S(1)}, u32[]{:S(2)}, u32[]{:S(2)}) collective-permute-start(bf16[4,144,512]{2,1,0:T(8,128)(2,1)S(1)} %collective-permute-done.refs_1_), channel_id=1, source_target_pairs={{0,1},{1,0},{2,3},{3,2},{4,5},{5,4},{6,7},{7,6},{8,9},{9,8},{10,11... | collective-permute-start | bytes 1769480 | tf_op jit(solution)/shard_map/ppermute | solution.py:29
  59.0 1.6 copy-start.2
  62.0 11.1 %collective-permute-start.7 = (bf16[256,1024]{1,0:T(8,128)(2,1)S(1)}, bf16[256,1024]{1,0:T(8,128)(2,1)S(1)}, u32[]{:S(2)}, u32[]{:S(2)}) collective-permute-start(bf16[256,1024]{1,0:T(8,128)(2,1)S(1)} %key_part.5), channel_id=1, source_target_pairs={{0,2},{1,7},{2,0},{3,5},{4,6},{5,3},{6,4},{7,1},{8,10},{9,15},{10,... | collective-permute-start | bytes 1572872 | tf_op jit(solution)/shard_map/ppermute | solution.py:38
  66.7 12.1 %collective-permute-start.6 = (bf16[256,1024]{1,0:T(8,128)(2,1)S(1)}, bf16[256,1024]{1,0:T(8,128)(2,1)S(1)}, u32[]{:S(2)}, u32[]{:S(2)}) collective-permute-start(bf16[256,1024]{1,0:T(8,128)(2,1)S(1)} %key_part.4), channel_id=1, source_target_pairs={{0,2},{1,7},{2,0},{3,5},{4,6},{5,3},{6,4},{7,1},{8,10},{9,15},{10,... | collective-permute-start | bytes 1572872 | tf_op jit(solution)/shard_map/ppermute | solution.py:38
  73.3 14.5 %collective-permute-start.8 = (bf16[256,1024]{1,0:T(8,128)(2,1)S(1)}, bf16[256,1024]{1,0:T(8,128)(2,1)S(1)}, u32[]{:S(2)}, u32[]{:S(2)}) collective-permute-start(bf16[256,1024]{1,0:T(8,128)(2,1)S(1)} %add.38.mine_ref), channel_id=1, source_target_pairs={{0,6},{1,3},{2,4},{3,1},{4,2},{5,7},{6,0},{7,5},{8,14},{9,11},{10,... | collective-permute-start | bytes 1572872 | tf_op jit(solution)/shard_map/ppermute | solution.py:38
  78.9 14.5 %collective-permute-start.9 = (bf16[256,1024]{1,0:T(8,128)(2,1)S(1)}, bf16[256,1024]{1,0:T(8,128)(2,1)S(1)}, u32[]{:S(2)}, u32[]{:S(2)}) collective-permute-start(bf16[256,1024]{1,0:T(8,128)(2,1)S(1)} %add.37.mine_ref), channel_id=1, source_target_pairs={{0,6},{1,3},{2,4},{3,1},{4,2},{5,7},{6,0},{7,5},{8,14},{9,11},{10,... | collective-permute-start | bytes 1572872 | tf_op jit(solution)/shard_map/ppermute | solution.py:38
  87.9 16.8 %collective-permute-start.10 = (bf16[256,1024]{1,0:T(8,128)(2,1)S(1)}, bf16[256,1024]{1,0:T(8,128)(2,1)S(1)}, u32[]{:S(2)}, u32[]{:S(2)}) collective-permute-start(bf16[256,1024]{1,0:T(8,128)(2,1)S(1)} %square.2.refs_0_), channel_id=1, source_target_pairs={{0,2},{1,7},{2,0},{3,5},{4,6},{5,3},{6,4},{7,1},{8,10},{9,15},{10,... | collective-permute-start | bytes 1572872 | tf_op jit(solution)/shard_map/ppermute | solution.py:38
  93.6 22.3 %collective-permute-start.12 = (bf16[256,1024]{1,0:T(8,128)(2,1)S(1)}, bf16[256,1024]{1,0:T(8,128)(2,1)S(1)}, u32[]{:S(2)}, u32[]{:S(2)}) collective-permute-start(bf16[256,1024]{1,0:T(8,128)(2,1)S(1)} %square.3.refs_1_), channel_id=1, source_target_pairs={{0,2},{1,7},{2,0},{3,5},{4,6},{5,3},{6,4},{7,1},{8,10},{9,15},{10,... | collective-permute-start | bytes 1572872 | tf_op jit(solution)/shard_map/ppermute | solution.py:38
  104.7 1.7 %copy-start = (bf16[1152,1024]{1,0:T(8,128)(2,1)S(1)}, bf16[1152,1024]{1,0:T(8,128)(2,1)}, u32[]{:S(2)}) copy-start(bf16[1152,1024]{1,0:T(8,128)(2,1)} %all-gather.7.cloned.1.call-done) | copy-start | bytes 7077892
  108.2 7.7 %copy-start.1 = (bf16[1152,1024]{1,0:T(8,128)(2,1)S(1)}, bf16[1152,1024]{1,0:T(8,128)(2,1)}, u32[]{:S(2)}) copy-start(bf16[1152,1024]{1,0:T(8,128)(2,1)} %all-gather.7.cloned.1.call-done) | copy-start | bytes 7077892
  108.2 12.3 %collective-permute-start.11 = (bf16[3,2,128,512]{3,2,1,0:T(8,128)(2,1)S(1)}, bf16[3,2,128,512]{3,2,1,0:T(8,128)(2,1)S(1)}, u32[]{:S(2)}, u32[]{:S(2)}) collective-permute-start(bf16[3,2,128,512]{3,2,1,0:T(8,128)(2,1)S(1)} %out_part.5), channel_id=1, source_target_pairs={{0,1},{1,0},{2,3},{3,2},{4,5},{5,4},{6,7},{7,6},{8,9},{9,8},{10,11... | collective-permute-start | bytes 2359304 | tf_op jit(solution)/shard_map/ppermute | solution.py:29
  117.0 3.4 %collective-permute-start.13 = (bf16[1,2,128,512]{3,2,1,0:T(8,128)(2,1)S(1)}, bf16[1,2,128,512]{3,2,1,0:T(8,128)(2,1)S(1)}, u32[]{:S(2)}, u32[]{:S(2)}) collective-permute-start(bf16[1,2,128,512]{3,2,1,0:T(8,128)(2,1)S(1)} %out_part.7), channel_id=1, source_target_pairs={{0,1},{1,0},{2,3},{3,2},{4,5},{5,4},{6,7},{7,6},{8,9},{9,8},{10,11... | collective-permute-start | bytes 786440 | tf_op jit(solution)/shard_map/ppermute | solution.py:29
  122.2 7.1 %copy-start.4 = (f32[64,4096]{1,0:T(8,128)S(1)}, f32[64,4096]{1,0:T(8,128)}, u32[]{:S(2)}) copy-start(f32[64,4096]{1,0:T(8,128)} %hid_ref.1) | copy-start | bytes 3145732
  122.2 36.4 %all-to-all-start.1 = ((bf16[8,128,512]{2,1,0:T(8,128)(2,1)}), bf16[8,128,512]{2,1,0:T(8,128)(2,1)S(1)}, u32[]{:S(2)}, u32[]{:S(2)}) async-start(bf16[8,128,512]{2,1,0:T(8,128)(2,1)} %place.1), calls=%async_computation.1 | async-start | bytes 2097152 | tf_op jit(solution)/shard_map/all_to_all | solution.py:290
Sparse Core Ops, SparseCore 0:
  18.4 39.5 all-gather.4
  60.6 44.0 all-gather.6

commit v8 on v6

--- a/solution.py
+++ b/solution.py
@@ -21,6 +21,7 @@
 SIGMA_V = 0.5 / FF**0.5
 VMEM = pl.BlockSpec(memory_space=pltpu.VMEM)
 HBM = pl.BlockSpec(memory_space=pltpu.HBM)
+ANY = pl.BlockSpec(memory_space=pl.ANY)
 SMEM = pl.BlockSpec(memory_space=pltpu.SMEM)
 
 
@@ -69,6 +70,10 @@
     for i in range(copies):
         out_ref[i, :tok, :] = shifted
         out_ref[i, tok:, :] = info
+
+
+def copy_kernel(x_ref, _, out_ref):
+    out_ref[...] = x_ref[...]
 
 
 def hidden_kernel(at_ref, hid_hbm, out_ref, sems):
@@ -208,7 +213,7 @@
     at = [lax.axis_index("y_hi") * hid + core * half, block, lax.axis_index("y_low")]
     at = jnp.stack(at).astype(jnp.int32)
 
-    key_other, value_other, bank_other = swap(key_weight), swap(value_weight), swap(dim_bank)
+    key_other, value_other = swap(key_weight), swap(value_weight)
     scratch = [
         pltpu.SMEM(member_picks.shape, jnp.int32), pltpu.SMEM(ranks.shape, jnp.int32),
         pltpu.VMEM(inputs.shape, jnp.bfloat16), pltpu.VMEM((1, feat), jnp.float32),
@@ -230,7 +235,10 @@
 
     key_pack = jnp.concatenate([hidden_half(key_weight, 1), hidden_half(key_other, 1)], axis=0)
     key_all = lax.all_gather(key_pack, "z", axis=0)
-    value_other, bank_other = lax.optimization_barrier((value_other, bank_other))
+    bank_other = swap(call(
+        copy_kernel, "bank", [(dim_bank.shape, jnp.float32)], [VMEM, ANY], cost(dim_bank.shape[0], 1, feat),
+        (dim_bank, key_all),
+    )[0])
     value_pack = jnp.concatenate([hidden_half(value_weight, 0), hidden_half(value_other, 0)], axis=1)
     info = jnp.pad(info, ((0, INFO - members), (0, 2 * feat - 128)))
     value_all = lax.all_gather(jnp.concatenate([value_pack, info], axis=0), "z", axis=0)

time: 168 us -> 164 us (0.976)
  waiting for transfers between devices: 69.2 us -> 65.4 us
    ppermute x6, waiting for transfers between devices: 21.5 us -> 10.5 us  [exchange(): return lax.ppermute(x, ('x', 'core'), pairs)]
    ppermute x1, waiting for transfers between devices: 6.03 us -> 9.83 us  [beside(): return lax.ppermute(x, YQ + ('y_low', 'core'), pairs)]
    all_gather x1, waiting for transfers between devices: 0.01 us -> 3.58 us  [shards(): lax.all_gather(jnp.concatenate([value_pack, info], axis=0), 'z', axis=0)]
    pallas_call x14 -> x15, Pallas kernels: 18.7 us -> 18.6 us  [call(): pl.pallas_call(kernel, out_shape=[jax.ShapeDtypeStruct(*out) for out in o...]
  transfers between devices with their start and end apart: 17 -> 17, of which waited for: 13 -> 12; matrix products, arithmetic and copies ran while one was open for 1% -> 1% of each run, Pallas kernels for 9% -> 10%
where the time goes in v8:
time: 164 us; the launch traced here: 163 us
  waiting for transfers between devices  65.4 us (40%)
  starting transfers between devices  57.7 us (35%)
  Pallas kernels  18.6 us (11%)
  between operations  14.4 us (9%)
  local copies, waits for them, and re-layouts  4.26 us (3%)
  other arithmetic  2.45 us (1%)
    ppermute x6, starting transfers between devices, swap(): return lax.ppermute(x, 'core', [(0, 1), (1, 0)])  26.2 us
    all_to_all x1, waiting for transfers between devices, shards(): pieces = lax.all_to_all(result, YQ + ('y_low',), 0, 0)  26.2 us
    ppermute x6, starting transfers between devices, exchange(): return lax.ppermute(x, ('x', 'core'), pairs)  19.2 us
    pallas_call x15, Pallas kernels, call(): pl.pallas_call(kernel, out_shape=[jax.ShapeDtypeStruct(*out) for out in o...  18.6 us
    all_to_all x1, waiting for transfers between devices, shards(): same = lax.all_to_all(shifted, YQ, 0, 0)  13.7 us
    ppermute x6, waiting for transfers between devices, exchange(): return lax.ppermute(x, ('x', 'core'), pairs)  10.5 us
    ppermute x1, waiting for transfers between devices, beside(): return lax.ppermute(x, YQ + ('y_low', 'core'), pairs)  9.83 us
    all_to_all x1, starting transfers between devices, shards(): pieces = lax.all_to_all(result, YQ + ('y_low',), 0, 0)  6.68 us
  transfers between devices with their start and end apart: 17, of which 12 were waited for; matrix products, arithmetic and copies ran while one was open for 1% of the time, Pallas kernels for 10%

profile of v8, /device:TPU:1, one launch (start us, length us, event | category | flops | bytes accessed | tf_op | source)
XLA Modules:
  0.0 162.8 jit_solution(14438751119916937319)
XLA Ops:
  7.2 0.0 copy-start.5
  7.2 0.0 all-gather.5.cloned.1.call-start
  7.2 8.9 %collective-permute-start.3 = (bf16[512,256]{1,0:T(8,128)(2,1)}, bf16[512,256]{1,0:T(8,128)(2,1)S(1)}, u32[]{:S(2)}, u32[]{:S(2)}) collective-permute-start(bf16[512,256]{1,0:T(8,128)(2,1)} %param.10), channel_id=1, source_target_pairs={{0,1},{1,0},{2,3},{3,2},{4,5},{5,4},{6,7},{7,6},{8,9},{9,8},{10,11... | collective-permute-start | bytes 786440 | tf_op jit(solution)/shard_map/ppermute | solution.py:29
  16.2 0.9 constant_dynamic-slice_fusion.3
  17.1 0.4 collective-permute-done.3
  17.5 0.7 pad_maximum_fusion
  18.2 0.0 all-gather.5.cloned.1.call-update
  18.3 1.9 %shift.1 = bf16[4,144,512]{2,1,0:T(8,128)(2,1)} custom-call(s32[2,4]{1,0:T(2,128)} %picks_hbm.1, s32[2]{0:T(128)} %ranks_hbm.1, bf16[128,512]{1,0:T(8,128)(2,1)} %x_hbm.1, f32[1,512]{1,0:T(1,128)} %bitcast.27), custom_call_target="tpu_custom_call" | custom-call | flops 2097152 | bytes 151552 | tf_op jit(solution)/shard_map/shift/pallas_call | solution.py:194
  20.1 0.0 copy-start.3
  20.2 3.6 %all-to-all-start = ((bf16[4,144,512]{2,1,0:T(8,128)(2,1)}), bf16[4,144,512]{2,1,0:T(8,128)(2,1)S(1)}, u32[]{:S(2)}, u32[]{:S(2)}) async-start(bf16[4,144,512]{2,1,0:T(8,128)(2,1)} %shift.1), calls=%async_computation | async-start | bytes 1179648 | tf_op jit(solution)/shard_map/all_to_all | solution.py:226
  23.8 0.0 all-gather.7.cloned.1.call-start
  23.8 0.0 copy-done.5
  23.8 2.3 %collective-permute-start.11 = (bf16[256,512]{1,0:T(8,128)(2,1)S(1)}, bf16[256,512]{1,0:T(8,128)(2,1)S(1)}, u32[]{:S(2)}, u32[]{:S(2)}) collective-permute-start(bf16[256,512]{1,0:T(8,128)(2,1)S(1)} %copy-done.5), channel_id=1, source_target_pairs={{0,1},{1,0},{2,3},{3,2},{4,5},{5,4},{6,7},{7,6},{8,9},{9,8},{10,11... | collective-permute-start | bytes 786440 | tf_op jit(solution)/shard_map/ppermute | solution.py:29
  26.1 13.7 %all-to-all-done.refs_0_ = bf16[4,144,512]{2,1,0:T(8,128)(2,1)S(1)} async-done(((bf16[4,144,512]{2,1,0:T(8,128)(2,1)}), bf16[4,144,512]{2,1,0:T(8,128)(2,1)S(1)}, u32[]{:S(2)}, u32[]{:S(2)}) %all-to-all-start) | async-done | bytes 589856 | tf_op jit(solution)/shard_map/all_to_all | solution.py:226
  39.9 1.9 %collective-permute-start = (bf16[4,144,512]{2,1,0:T(8,128)(2,1)S(1)}, bf16[4,144,512]{2,1,0:T(8,128)(2,1)S(1)}, u32[]{:S(2)}, u32[]{:S(2)}) collective-permute-start(bf16[4,144,512]{2,1,0:T(8,128)(2,1)S(1)} %all-to-all-done.refs_0_), channel_id=1, source_target_pairs={{0,8},{1,57},{8,0},{9,17},{16,24},{17,9},{24,16},{25,33},{32,40},{... | collective-permute-start | bytes 1769480 | tf_op jit(solution)/shard_map/ppermute | solution.py:47
  41.8 0.0 collective-permute-done.11
  41.9 9.8 %collective-permute-done.refs_1_ = bf16[4,144,512]{2,1,0:T(8,128)(2,1)S(1)} collective-permute-done((bf16[4,144,512]{2,1,0:T(8,128)(2,1)S(1)}, bf16[4,144,512]{2,1,0:T(8,128)(2,1)S(1)}, u32[]{:S(2)}, u32[]{:S(2)}) %collective-permute-start) | collective-permute-done | bytes 589856 | tf_op jit(solution)/shard_map/ppermute | solution.py:47
  51.7 0.7 fusion.1
  52.5 0.0 all-gather.7.cloned.1.call-update
  52.5 2.8 %collective-permute-start.1 = (bf16[4,144,512]{2,1,0:T(8,128)(2,1)S(1)}, bf16[4,144,512]{2,1,0:T(8,128)(2,1)S(1)}, u32[]{:S(2)}, u32[]{:S(2)}) collective-permute-start(bf16[4,144,512]{2,1,0:T(8,128)(2,1)S(1)} %all-to-all-done.refs_0_), channel_id=1, source_target_pairs={{0,1},{1,0},{2,3},{3,2},{4,5},{5,4},{6,7},{7,6},{8,9},{9,8},{10,11... | collective-permute-start | bytes 1769480 | tf_op jit(solution)/shard_map/ppermute | solution.py:29
  55.3 1.9 %collective-permute-start.2 = (bf16[4,144,512]{2,1,0:T(8,128)(2,1)S(1)}, bf16[4,144,512]{2,1,0:T(8,128)(2,1)S(1)}, u32[]{:S(2)}, u32[]{:S(2)}) collective-permute-start(bf16[4,144,512]{2,1,0:T(8,128)(2,1)S(1)} %collective-permute-done.refs_1_), channel_id=1, source_target_pairs={{0,1},{1,0},{2,3},{3,2},{4,5},{5,4},{6,7},{7,6},{8,9},{9,8},{10,11... | collective-permute-start | bytes 1769480 | tf_op jit(solution)/shard_map/ppermute | solution.py:29
  57.2 0.1 pad_add_fusion.1.at_ref
  57.3 1.5 hidden.1.refs_7_.refs_6_.refs_5_.refs_3_
  58.8 0.1 pad_add_fusion.order_ref
  58.9 0.0 all-gather.5.cloned.1.call-done
  58.9 0.0 copy-done.3
  58.9 1.6 copy-done
  60.5 5.7 %collective-permute-start.4 = (f32[64,512]{1,0:T(8,128)S(1)}, f32[64,512]{1,0:T(8,128)S(1)}, u32[]{:S(2)}, u32[]{:S(2)}) collective-permute-start(f32[64,512]{1,0:T(8,128)S(1)} %bank.1), channel_id=1, source_target_pairs={{0,1},{1,0},{2,3},{3,2},{4,5},{5,4},{6,7},{7,6},{8,9},{9,8},{10,11... | collective-permute-start | bytes 393224 | tf_op jit(solution)/shard_map/ppermute | solution.py:29
  66.3 0.0 collective-permute-done.1.refs_2_
  66.3 0.0 collective-permute-done.2.refs_3_
  66.3 0.9 collective-permute-done.4.refs_6_.refs_4_.refs_2_
  67.2 1.4 key_part.5
  68.6 4.3 %collective-permute-start.6 = (bf16[256,1024]{1,0:T(8,128)(2,1)S(1)}, bf16[256,1024]{1,0:T(8,128)(2,1)S(1)}, u32[]{:S(2)}, u32[]{:S(2)}) collective-permute-start(bf16[256,1024]{1,0:T(8,128)(2,1)S(1)} %key_part.5), channel_id=1, source_target_pairs={{0,2},{1,7},{2,0},{3,5},{4,6},{5,3},{6,4},{7,1},{8,10},{9,15},{10,... | collective-permute-start | bytes 1572872 | tf_op jit(solution)/shard_map/ppermute | solution.py:38
  72.9 1.4 key_part.4
  74.3 2.2 %collective-permute-start.5 = (bf16[256,1024]{1,0:T(8,128)(2,1)S(1)}, bf16[256,1024]{1,0:T(8,128)(2,1)S(1)}, u32[]{:S(2)}, u32[]{:S(2)}) collective-permute-start(bf16[256,1024]{1,0:T(8,128)(2,1)S(1)} %key_part.4), channel_id=1, source_target_pairs={{0,2},{1,7},{2,0},{3,5},{4,6},{5,3},{6,4},{7,1},{8,10},{9,15},{10,... | collective-permute-start | bytes 1572872 | tf_op jit(solution)/shard_map/ppermute | solution.py:38
  76.5 1.9 %key_part.3 = (f32[256,1024]{1,0:T(8,128)S(1)}, f32[256,1024]{1,0:T(8,128)S(1)}) custom-call(s32[4]{0:T(128)S(1)} %pad_add_fusion.order_ref, s32[16,4]{1,0:T(8,128)S(1)} %slice_convert_fusion.ids_ref, bf16[4,144,512]{2,1,0:T(8,128)(2,1)S(1)} %all-to-all-done.refs_0_, bf16[4,144,512]{2,1,0:T(8,128)(2,1)S(1)} %collective-permute-done.refs_1_, ...), custom_call_target="tpu_custom_call" | custom-call | flops 1073741824 | bytes 4194304 | tf_op jit(solution)/shard_map/key_part/pallas_call | solution.py:194
  78.4 1.3 collective-permute-done.6.came_ref
  79.7 0.1 add.38.mine_ref
  79.8 2.2 %collective-permute-start.7 = (bf16[256,1024]{1,0:T(8,128)(2,1)S(1)}, bf16[256,1024]{1,0:T(8,128)(2,1)S(1)}, u32[]{:S(2)}, u32[]{:S(2)}) collective-permute-start(bf16[256,1024]{1,0:T(8,128)(2,1)S(1)} %add.38.mine_ref), channel_id=1, source_target_pairs={{0,6},{1,3},{2,4},{3,1},{4,2},{5,7},{6,0},{7,5},{8,14},{9,11},{10,... | collective-permute-start | bytes 1572872 | tf_op jit(solution)/shard_map/ppermute | solution.py:38
  82.0 3.8 %collective-permute-done.5.came_ref = bf16[256,1024]{1,0:T(8,128)(2,1)S(1)} collective-permute-done((bf16[256,1024]{1,0:T(8,128)(2,1)S(1)}, bf16[256,1024]{1,0:T(8,128)(2,1)S(1)}, u32[]{:S(2)}, u32[]{:S(2)}) %collective-permute-start.5) | collective-permute-done | bytes 524320 | tf_op jit(solution)/shard_map/ppermute | solution.py:38
  85.8 0.1 add.37.mine_ref
  85.9 1.9 %collective-permute-start.8 = (bf16[256,1024]{1,0:T(8,128)(2,1)S(1)}, bf16[256,1024]{1,0:T(8,128)(2,1)S(1)}, u32[]{:S(2)}, u32[]{:S(2)}) collective-permute-start(bf16[256,1024]{1,0:T(8,128)(2,1)S(1)} %add.37.mine_ref), channel_id=1, source_target_pairs={{0,6},{1,3},{2,4},{3,1},{4,2},{5,7},{6,0},{7,5},{8,14},{9,11},{10,... | collective-permute-start | bytes 1572872 | tf_op jit(solution)/shard_map/ppermute | solution.py:38
  87.9 3.1 %collective-permute-done.7.came_ref = bf16[256,1024]{1,0:T(8,128)(2,1)S(1)} collective-permute-done((bf16[256,1024]{1,0:T(8,128)(2,1)S(1)}, bf16[256,1024]{1,0:T(8,128)(2,1)S(1)}, u32[]{:S(2)}, u32[]{:S(2)}) %collective-permute-start.7) | collective-permute-done | bytes 524320 | tf_op jit(solution)/shard_map/ppermute | solution.py:38
  91.0 0.2 square.2.refs_0_
  91.2 4.3 %collective-permute-start.9 = (bf16[256,1024]{1,0:T(8,128)(2,1)S(1)}, bf16[256,1024]{1,0:T(8,128)(2,1)S(1)}, u32[]{:S(2)}, u32[]{:S(2)}) collective-permute-start(bf16[256,1024]{1,0:T(8,128)(2,1)S(1)} %square.2.refs_0_), channel_id=1, source_target_pairs={{0,2},{1,7},{2,0},{3,5},{4,6},{5,3},{6,4},{7,1},{8,10},{9,15},{10,... | collective-permute-start | bytes 1572872 | tf_op jit(solution)/shard_map/ppermute | solution.py:38
  95.5 1.1 collective-permute-done.8.came_ref
  96.6 0.2 square.3.refs_1_
  96.8 4.3 %collective-permute-start.10 = (bf16[256,1024]{1,0:T(8,128)(2,1)S(1)}, bf16[256,1024]{1,0:T(8,128)(2,1)S(1)}, u32[]{:S(2)}, u32[]{:S(2)}) collective-permute-start(bf16[256,1024]{1,0:T(8,128)(2,1)S(1)} %square.3.refs_1_), channel_id=1, source_target_pairs={{0,2},{1,7},{2,0},{3,5},{4,6},{5,3},{6,4},{7,1},{8,10},{9,15},{10,... | collective-permute-start | bytes 1572872 | tf_op jit(solution)/shard_map/ppermute | solution.py:38
  101.1 3.6 %all-gather.7.cloned.1.call-done = bf16[1152,1024]{1,0:T(8,128)(2,1)} async-done(((bf16[144,1024]{1,0:T(8,128)(2,1)}), bf16[1152,1024]{1,0:T(8,128)(2,1)}) %all-gather.7.cloned.1.call-update) | async-done | bytes 2359312 | tf_op jit(solution)/shard_map/all_gather | solution.py:244
  104.7 0.0 collective-permute-done.9.refs_2_
  104.7 1.7 %copy-done.1 = bf16[1152,1024]{1,0:T(8,128)(2,1)S(1)} copy-done((bf16[1152,1024]{1,0:T(8,128)(2,1)S(1)}, bf16[1152,1024]{1,0:T(8,128)(2,1)}, u32[]{:S(2)}) %copy-start.1) | copy-done | bytes 2359320
  106.4 1.8 %out_part.4.refs_4_ = bf16[3,2,128,512]{3,2,1,0:T(8,128)(2,1)S(1)} custom-call(s32[4]{0:T(128)S(1)} %pad_add_fusion.order_ref, s32[16,4]{1,0:T(8,128)S(1)} %slice_convert_fusion.ids_ref, bf16[256,1024]{1,0:T(8,128)(2,1)S(1)} %square.2.refs_0_, bf16[256,1024]{1,0:T(8,128)(2,1)S(1)} %square.3.refs_1_, bf16[256,1024]{1,0:T(8,128)(2,1)S(1)} %collective-permute-done.9.refs_2_, ...), custom_call_target="tpu_custom_call" | custom-call | flops 805306368 | bytes 3407872 | tf_op jit(solution)/shard_map/out_part/pallas_call | solution.py:194
  108.2 1.2 collective-permute-done.10.refs_3_.refs_0_
  109.3 0.0 copy-done.2
  109.3 1.2 out_part.5
  110.5 4.6 %collective-permute-start.12 = (bf16[4,2,128,512]{3,2,1,0:T(8,128)(2,1)S(1)}, bf16[4,2,128,512]{3,2,1,0:T(8,128)(2,1)S(1)}, u32[]{:S(2)}, u32[]{:S(2)}) collective-permute-start(bf16[4,2,128,512]{3,2,1,0:T(8,128)(2,1)S(1)} %out_part.5), channel_id=1, source_target_pairs={{0,1},{1,0},{2,3},{3,2},{4,5},{5,4},{6,7},{7,6},{8,9},{9,8},{10,11... | collective-permute-start | bytes 3145736 | tf_op jit(solution)/shard_map/ppermute | solution.py:29
  115.1 2.1 %out_part.3.mine_ref = f32[4,2,128,512]{3,2,1,0:T(8,128)S(1)} custom-call(s32[4]{0:T(128)S(1)} %pad_add_fusion.order_ref, s32[16,4]{1,0:T(8,128)S(1)} %slice_convert_fusion.ids_ref, bf16[256,1024]{1,0:T(8,128)(2,1)S(1)} %square.2.refs_0_, bf16[256,1024]{1,0:T(8,128)(2,1)S(1)} %square.3.refs_1_, bf16[256,1024]{1,0:T(8,128)(2,1)S(1)} %collective-permute-done.9.refs_2_, ...), custom_call_target="tpu_custom_call" | custom-call | flops 1073741824 | bytes 4194304 | tf_op jit(solution)/shard_map/out_part/pallas_call | solution.py:194
  117.2 0.1 collective-permute-done.12.came_ref
  117.3 1.8 %place.1 = bf16[8,128,512]{2,1,0:T(8,128)(2,1)} custom-call(s32[4]{0:T(128)S(1)} %pad_add_fusion.order_ref, s32[3]{0:T(128)S(1)} %pad_add_fusion.1.at_ref, f32[4,2,128,512]{3,2,1,0:T(8,128)S(1)} %out_part.3.mine_ref, bf16[4,2,128,512]{3,2,1,0:T(8,128)(2,1)S(1)} %collective-permute-done.12.came_ref), custom_call_target="tpu_custom_call" | custom-call | flops 1048576 | bytes 1051648 | tf_op jit(solution)/shard_map/place/pallas_call | solution.py:194
  119.2 6.7 %all-to-all-start.1 = ((bf16[8,128,512]{2,1,0:T(8,128)(2,1)}), bf16[8,128,512]{2,1,0:T(8,128)(2,1)S(1)}, u32[]{:S(2)}, u32[]{:S(2)}) async-start(bf16[8,128,512]{2,1,0:T(8,128)(2,1)} %place.1), calls=%async_computation.1 | async-start | bytes 2097152 | tf_op jit(solution)/shard_map/all_to_all | solution.py:294
  125.9 0.0 copy-done.4
  125.9 3.0 %steps.1 = (f32[512,256]{1,0:T(8,128)}, f32[256,512]{1,0:T(8,128)}) custom-call(s32[3]{0:T(128)S(1)} %pad_add_fusion.1.at_ref, bf16[128,128]{1,0:T(8,128)(2,1)S(1)} %bitcast.24, f32[64,512]{1,0:T(8,128)S(1)} %copy-done.3, f32[64,4096]{1,0:T(8,128)S(1)} %copy-done.4), custom_call_target="tpu_custom_call" | custom-call | flops 134217728 | bytes 1048576 | tf_op jit(solution)/shard_map/steps/pallas_call | solution.py:194
  128.9 26.2 %all-to-all-done.1 = bf16[8,128,512]{2,1,0:T(8,128)(2,1)S(1)} async-done(((bf16[8,128,512]{2,1,0:T(8,128)(2,1)}), bf16[8,128,512]{2,1,0:T(8,128)(2,1)S(1)}, u32[]{:S(2)}, u32[]{:S(2)}) %all-to-all-start.1) | async-done | bytes 1048608 | tf_op jit(solution)/shard_map/all_to_all | solution.py:294
  155.1 0.8 reduce_sum.12
  (13 shorter events, 0.1 us)
Async XLA Ops:
  7.2 16.7 %copy-start.5 = (bf16[256,512]{1,0:T(8,128)(2,1)S(1)}, bf16[256,512]{1,0:T(8,128)(2,1)}, u32[]{:S(2)}) copy-start(bf16[256,512]{1,0:T(8,128)(2,1)} %param.11) | copy-start | bytes 786436
  7.2 51.7 %all-gather.5.cloned.1.call-start = ((), (), s32[]{:S(2)}) async-start(), calls=%async_computation.2 | async-start | bytes 2359296 | tf_op jit(solution)/shard_map/all_gather | solution.py:237
  7.2 10.3 %collective-permute-start.3 = (bf16[512,256]{1,0:T(8,128)(2,1)}, bf16[512,256]{1,0:T(8,128)(2,1)S(1)}, u32[]{:S(2)}, u32[]{:S(2)}) collective-permute-start(bf16[512,256]{1,0:T(8,128)(2,1)} %param.10), channel_id=1, source_target_pairs={{0,1},{1,0},{2,3},{3,2},{4,5},{5,4},{6,7},{7,6},{8,9},{9,8},{10,11... | collective-permute-start | bytes 786440 | tf_op jit(solution)/shard_map/ppermute | solution.py:29
  20.1 38.8 %copy-start.3 = (f32[64,512]{1,0:T(8,128)S(1)}, f32[64,512]{1,0:T(8,128)}, u32[]{:S(2)}) copy-start(f32[64,512]{1,0:T(8,128)} %bank_ref.1) | copy-start | bytes 393220
  20.2 19.7 %all-to-all-start = ((bf16[4,144,512]{2,1,0:T(8,128)(2,1)}), bf16[4,144,512]{2,1,0:T(8,128)(2,1)S(1)}, u32[]{:S(2)}, u32[]{:S(2)}) async-start(bf16[4,144,512]{2,1,0:T(8,128)(2,1)} %shift.1), calls=%async_computation | async-start | bytes 1179648 | tf_op jit(solution)/shard_map/all_to_all | solution.py:226
  23.8 80.9 %all-gather.7.cloned.1.call-start = ((), (), s32[]{:S(2)}) async-start(), calls=%async_computation.3 | async-start | bytes 2654208 | tf_op jit(solution)/shard_map/all_gather | solution.py:244
  23.8 18.0 %collective-permute-start.11 = (bf16[256,512]{1,0:T(8,128)(2,1)S(1)}, bf16[256,512]{1,0:T(8,128)(2,1)S(1)}, u32[]{:S(2)}, u32[]{:S(2)}) collective-permute-start(bf16[256,512]{1,0:T(8,128)(2,1)S(1)} %copy-done.5), channel_id=1, source_target_pairs={{0,1},{1,0},{2,3},{3,2},{4,5},{5,4},{6,7},{7,6},{8,9},{9,8},{10,11... | collective-permute-start | bytes 786440 | tf_op jit(solution)/shard_map/ppermute | solution.py:29
  39.9 11.8 %collective-permute-start = (bf16[4,144,512]{2,1,0:T(8,128)(2,1)S(1)}, bf16[4,144,512]{2,1,0:T(8,128)(2,1)S(1)}, u32[]{:S(2)}, u32[]{:S(2)}) collective-permute-start(bf16[4,144,512]{2,1,0:T(8,128)(2,1)S(1)} %all-to-all-done.refs_0_), channel_id=1, source_target_pairs={{0,8},{1,57},{8,0},{9,17},{16,24},{17,9},{24,16},{25,33},{32,40},{... | collective-permute-start | bytes 1769480 | tf_op jit(solution)/shard_map/ppermute | solution.py:47
  52.5 13.8 %collective-permute-start.1 = (bf16[4,144,512]{2,1,0:T(8,128)(2,1)S(1)}, bf16[4,144,512]{2,1,0:T(8,128)(2,1)S(1)}, u32[]{:S(2)}, u32[]{:S(2)}) collective-permute-start(bf16[4,144,512]{2,1,0:T(8,128)(2,1)S(1)} %all-to-all-done.refs_0_), channel_id=1, source_target_pairs={{0,1},{1,0},{2,3},{3,2},{4,5},{5,4},{6,7},{7,6},{8,9},{9,8},{10,11... | collective-permute-start | bytes 1769480 | tf_op jit(solution)/shard_map/ppermute | solution.py:29
  55.3 11.0 %collective-permute-start.2 = (bf16[4,144,512]{2,1,0:T(8,128)(2,1)S(1)}, bf16[4,144,512]{2,1,0:T(8,128)(2,1)S(1)}, u32[]{:S(2)}, u32[]{:S(2)}) collective-permute-start(bf16[4,144,512]{2,1,0:T(8,128)(2,1)S(1)} %collective-permute-done.refs_1_), channel_id=1, source_target_pairs={{0,1},{1,0},{2,3},{3,2},{4,5},{5,4},{6,7},{7,6},{8,9},{9,8},{10,11... | collective-permute-start | bytes 1769480 | tf_op jit(solution)/shard_map/ppermute | solution.py:29
  58.9 1.6 copy-start
  60.5 6.7 %collective-permute-start.4 = (f32[64,512]{1,0:T(8,128)S(1)}, f32[64,512]{1,0:T(8,128)S(1)}, u32[]{:S(2)}, u32[]{:S(2)}) collective-permute-start(f32[64,512]{1,0:T(8,128)S(1)} %bank.1), channel_id=1, source_target_pairs={{0,1},{1,0},{2,3},{3,2},{4,5},{5,4},{6,7},{7,6},{8,9},{9,8},{10,11... | collective-permute-start | bytes 393224 | tf_op jit(solution)/shard_map/ppermute | solution.py:29
  68.6 11.1 %collective-permute-start.6 = (bf16[256,1024]{1,0:T(8,128)(2,1)S(1)}, bf16[256,1024]{1,0:T(8,128)(2,1)S(1)}, u32[]{:S(2)}, u32[]{:S(2)}) collective-permute-start(bf16[256,1024]{1,0:T(8,128)(2,1)S(1)} %key_part.5), channel_id=1, source_target_pairs={{0,2},{1,7},{2,0},{3,5},{4,6},{5,3},{6,4},{7,1},{8,10},{9,15},{10,... | collective-permute-start | bytes 1572872 | tf_op jit(solution)/shard_map/ppermute | solution.py:38
  74.3 11.5 %collective-permute-start.5 = (bf16[256,1024]{1,0:T(8,128)(2,1)S(1)}, bf16[256,1024]{1,0:T(8,128)(2,1)S(1)}, u32[]{:S(2)}, u32[]{:S(2)}) collective-permute-start(bf16[256,1024]{1,0:T(8,128)(2,1)S(1)} %key_part.4), channel_id=1, source_target_pairs={{0,2},{1,7},{2,0},{3,5},{4,6},{5,3},{6,4},{7,1},{8,10},{9,15},{10,... | collective-permute-start | bytes 1572872 | tf_op jit(solution)/shard_map/ppermute | solution.py:38
  79.8 11.2 %collective-permute-start.7 = (bf16[256,1024]{1,0:T(8,128)(2,1)S(1)}, bf16[256,1024]{1,0:T(8,128)(2,1)S(1)}, u32[]{:S(2)}, u32[]{:S(2)}) collective-permute-start(bf16[256,1024]{1,0:T(8,128)(2,1)S(1)} %add.38.mine_ref), channel_id=1, source_target_pairs={{0,6},{1,3},{2,4},{3,1},{4,2},{5,7},{6,0},{7,5},{8,14},{9,11},{10,... | collective-permute-start | bytes 1572872 | tf_op jit(solution)/shard_map/ppermute | solution.py:38
  85.9 10.7 %collective-permute-start.8 = (bf16[256,1024]{1,0:T(8,128)(2,1)S(1)}, bf16[256,1024]{1,0:T(8,128)(2,1)S(1)}, u32[]{:S(2)}, u32[]{:S(2)}) collective-permute-start(bf16[256,1024]{1,0:T(8,128)(2,1)S(1)} %add.37.mine_ref), channel_id=1, source_target_pairs={{0,6},{1,3},{2,4},{3,1},{4,2},{5,7},{6,0},{7,5},{8,14},{9,11},{10,... | collective-permute-start | bytes 1572872 | tf_op jit(solution)/shard_map/ppermute | solution.py:38
  91.2 13.5 %collective-permute-start.9 = (bf16[256,1024]{1,0:T(8,128)(2,1)S(1)}, bf16[256,1024]{1,0:T(8,128)(2,1)S(1)}, u32[]{:S(2)}, u32[]{:S(2)}) collective-permute-start(bf16[256,1024]{1,0:T(8,128)(2,1)S(1)} %square.2.refs_0_), channel_id=1, source_target_pairs={{0,2},{1,7},{2,0},{3,5},{4,6},{5,3},{6,4},{7,1},{8,10},{9,15},{10,... | collective-permute-start | bytes 1572872 | tf_op jit(solution)/shard_map/ppermute | solution.py:38
  96.8 12.5 %collective-permute-start.10 = (bf16[256,1024]{1,0:T(8,128)(2,1)S(1)}, bf16[256,1024]{1,0:T(8,128)(2,1)S(1)}, u32[]{:S(2)}, u32[]{:S(2)}) collective-permute-start(bf16[256,1024]{1,0:T(8,128)(2,1)S(1)} %square.3.refs_1_), channel_id=1, source_target_pairs={{0,2},{1,7},{2,0},{3,5},{4,6},{5,3},{6,4},{7,1},{8,10},{9,15},{10,... | collective-permute-start | bytes 1572872 | tf_op jit(solution)/shard_map/ppermute | solution.py:38
  104.7 1.7 %copy-start.1 = (bf16[1152,1024]{1,0:T(8,128)(2,1)S(1)}, bf16[1152,1024]{1,0:T(8,128)(2,1)}, u32[]{:S(2)}) copy-start(bf16[1152,1024]{1,0:T(8,128)(2,1)} %all-gather.7.cloned.1.call-done) | copy-start | bytes 7077892
  106.4 3.0 %copy-start.2 = (bf16[1152,1024]{1,0:T(8,128)(2,1)S(1)}, bf16[1152,1024]{1,0:T(8,128)(2,1)}, u32[]{:S(2)}) copy-start(bf16[1152,1024]{1,0:T(8,128)(2,1)} %all-gather.7.cloned.1.call-done) | copy-start | bytes 7077892
  110.5 6.8 %collective-permute-start.12 = (bf16[4,2,128,512]{3,2,1,0:T(8,128)(2,1)S(1)}, bf16[4,2,128,512]{3,2,1,0:T(8,128)(2,1)S(1)}, u32[]{:S(2)}, u32[]{:S(2)}) collective-permute-start(bf16[4,2,128,512]{3,2,1,0:T(8,128)(2,1)S(1)} %out_part.5), channel_id=1, source_target_pairs={{0,1},{1,0},{2,3},{3,2},{4,5},{5,4},{6,7},{7,6},{8,9},{9,8},{10,11... | collective-permute-start | bytes 3145736 | tf_op jit(solution)/shard_map/ppermute | solution.py:29
  119.2 6.7 %copy-start.4 = (f32[64,4096]{1,0:T(8,128)S(1)}, f32[64,4096]{1,0:T(8,128)}, u32[]{:S(2)}) copy-start(f32[64,4096]{1,0:T(8,128)} %hid_ref.1) | copy-start | bytes 3145732
  119.2 35.9 %all-to-all-start.1 = ((bf16[8,128,512]{2,1,0:T(8,128)(2,1)}), bf16[8,128,512]{2,1,0:T(8,128)(2,1)S(1)}, u32[]{:S(2)}, u32[]{:S(2)}) async-start(bf16[8,128,512]{2,1,0:T(8,128)(2,1)} %place.1), calls=%async_computation.1 | async-start | bytes 2097152 | tf_op jit(solution)/shard_map/all_to_all | solution.py:294
Sparse Core Ops, SparseCore 0:
  18.4 39.5 all-gather.4
  60.6 44.0 all-gather.6

commit v9 on v8

--- a/solution.py
+++ b/solution.py
@@ -213,7 +213,7 @@
     at = [lax.axis_index("y_hi") * hid + core * half, block, lax.axis_index("y_low")]
     at = jnp.stack(at).astype(jnp.int32)
 
-    key_other, value_other = swap(key_weight), swap(value_weight)
+    key_other, value_other, bank_early = swap(key_weight), swap(value_weight), swap(dim_bank)
     scratch = [
         pltpu.SMEM(member_picks.shape, jnp.int32), pltpu.SMEM(ranks.shape, jnp.int32),
         pltpu.VMEM(inputs.shape, jnp.bfloat16), pltpu.VMEM((1, feat), jnp.float32),
@@ -235,10 +235,6 @@
 
     key_pack = jnp.concatenate([hidden_half(key_weight, 1), hidden_half(key_other, 1)], axis=0)
     key_all = lax.all_gather(key_pack, "z", axis=0)
-    bank_other = swap(call(
-        copy_kernel, "bank", [(dim_bank.shape, jnp.float32)], [VMEM, ANY], cost(dim_bank.shape[0], 1, feat),
-        (dim_bank, key_all),
-    )[0])
     value_pack = jnp.concatenate([hidden_half(value_weight, 0), hidden_half(value_other, 0)], axis=1)
     info = jnp.pad(info, ((0, INFO - members), (0, 2 * feat - 128)))
     value_all = lax.all_gather(jnp.concatenate([value_pack, info], axis=0), "z", axis=0)
@@ -250,11 +246,11 @@
     deep, wide, quarter = 2 * feat, NZ * half, NY * tok // NX
     low, high = ((quarter, wide), jnp.bfloat16), ((quarter, wide), jnp.float32)
     hidden = call(
-        hidden_kernel, "hidden", [((hidden_bank.shape[0], wide), jnp.float32)], [SMEM, HBM],
+        hidden_kernel, "hidden", [((hidden_bank.shape[0], wide), jnp.float32)], [SMEM, VMEM],
         cost(hidden_bank.shape[0], 1, wide), (at, hidden_bank), [pltpu.SemaphoreType.DMA((NZ,))],
     )[0]
 
-    def key_part(which, outs):
+    def key_part(which, outs, bank_other):
         return call(
             functools.partial(key_kernel, which), "key_part", outs,
             [SMEM] * 2 + [VMEM] * 8, cost(len(which) * quarter, deep, wide),
@@ -264,9 +260,14 @@
     def local(kernel, name, *args):
         return call(kernel, name, [low], [VMEM] * len(args), cost(quarter, 4, wide), args)[0]
 
-    came_next = exchange(key_part((3,), [low])[0], 0)
-    came_own = exchange(key_part((2,), [low])[0], 0)
-    sum_next, sum_own = key_part((1, 0), [high, high])
+    first = key_part((3,), [low], bank_early)[0]
+    came_next = exchange(first, 0)
+    bank_other = swap(call(
+        copy_kernel, "bank", [(dim_bank.shape, jnp.float32)], [VMEM, ANY], cost(dim_bank.shape[0], 1, feat),
+        (dim_bank, first),
+    )[0])
+    came_own = exchange(key_part((2,), [low], bank_other)[0], 0)
+    sum_next, sum_own = key_part((1, 0), [high, high], bank_other)
     sum_next = local(add_kernel, "add", sum_next, came_next)
     other_own = exchange(sum_next, 1)
     sum_own = local(add_kernel, "add", sum_own, came_own)

time: 164 us -> 163 us (level)
    unnamed x12 -> x14, local copies, waits for them, and re-layouts: 3.27 us -> 4.49 us
    ppermute x6 -> x7, starting transfers between devices: 26.2 us -> 27 us  [swap(): return lax.ppermute(x, 'core', [(0, 1), (1, 0)])]
  transfers between devices with their start and end apart: 17 -> 18, of which waited for: 12 -> 11; matrix products, arithmetic and copies ran while one was open for 1% -> 1% of each run, Pallas kernels for 10% -> 9%
where the time goes in v9:
time: 163 us
  waiting for transfers between devices  64.2 us (39%)
  starting transfers between devices  58.4 us (36%)
  Pallas kernels  17.9 us (11%)
  between operations  14.4 us (9%)
  local copies, waits for them, and re-layouts  5.48 us (3%)
  other arithmetic  2.45 us (2%)
    ppermute x7, starting transfers between devices, swap(): return lax.ppermute(x, 'core', [(0, 1), (1, 0)])  27 us
    all_to_all x1, waiting for transfers between devices, shards(): pieces = lax.all_to_all(result, YQ + ('y_low',), 0, 0)  26.2 us
    ppermute x6, starting transfers between devices, exchange(): return lax.ppermute(x, ('x', 'core'), pairs)  19.2 us
    pallas_call x15, Pallas kernels, call(): pl.pallas_call(kernel, out_shape=[jax.ShapeDtypeStruct(*out) for out in o...  17.9 us
    all_to_all x1, waiting for transfers between devices, shards(): same = lax.all_to_all(shifted, YQ, 0, 0)  13.7 us
    ppermute x6, waiting for transfers between devices, exchange(): return lax.ppermute(x, ('x', 'core'), pairs)  11.6 us
    ppermute x1, waiting for transfers between devices, beside(): return lax.ppermute(x, YQ + ('y_low', 'core'), pairs)  9.83 us
    all_to_all x1, starting transfers between devices, shards(): pieces = lax.all_to_all(result, YQ + ('y_low',), 0, 0)  6.68 us
  transfers between devices with their start and end apart: 18, of which 11 were waited for; matrix products, arithmetic and copies ran while one was open for 1% of the time, Pallas kernels for 9%

profile of v9, /device:TPU:1, one launch (start us, length us, event | category | flops | bytes accessed | tf_op | source)
XLA Modules:
  0.0 162.7 jit_solution(16332568191395876612)
XLA Ops:
  7.2 0.0 all-gather.5.cloned.1.call-start
  7.2 8.9 %collective-permute-start.3 = (bf16[512,256]{1,0:T(8,128)(2,1)}, bf16[512,256]{1,0:T(8,128)(2,1)S(1)}, u32[]{:S(2)}, u32[]{:S(2)}) collective-permute-start(bf16[512,256]{1,0:T(8,128)(2,1)} %param.10), channel_id=1, source_target_pairs={{0,1},{1,0},{2,3},{3,2},{4,5},{5,4},{6,7},{7,6},{8,9},{9,8},{10,11... | collective-permute-start | bytes 786440 | tf_op jit(solution)/shard_map/ppermute | solution.py:29
  16.2 0.9 constant_dynamic-slice_fusion.3
  17.1 0.4 collective-permute-done.3
  17.5 0.0 copy-start.3
  17.5 0.7 pad_maximum_fusion
  18.2 0.0 all-gather.5.cloned.1.call-update
  18.3 1.9 %shift.1 = bf16[4,144,512]{2,1,0:T(8,128)(2,1)} custom-call(s32[2,4]{1,0:T(2,128)} %picks_hbm.1, s32[2]{0:T(128)} %ranks_hbm.1, bf16[128,512]{1,0:T(8,128)(2,1)} %x_hbm.1, f32[1,512]{1,0:T(1,128)} %bitcast.26), custom_call_target="tpu_custom_call" | custom-call | flops 2097152 | bytes 151552 | tf_op jit(solution)/shard_map/shift/pallas_call | solution.py:194
  20.1 3.5 %all-to-all-start = ((bf16[4,144,512]{2,1,0:T(8,128)(2,1)}), bf16[4,144,512]{2,1,0:T(8,128)(2,1)S(1)}, u32[]{:S(2)}, u32[]{:S(2)}) async-start(bf16[4,144,512]{2,1,0:T(8,128)(2,1)} %shift.1), calls=%async_computation | async-start | bytes 1179648 | tf_op jit(solution)/shard_map/all_to_all | solution.py:226
  23.6 0.0 all-gather.7.cloned.1.call-start
  23.7 0.0 copy-done.6
  23.7 2.3 %collective-permute-start.12 = (bf16[256,512]{1,0:T(8,128)(2,1)S(1)}, bf16[256,512]{1,0:T(8,128)(2,1)S(1)}, u32[]{:S(2)}, u32[]{:S(2)}) collective-permute-start(bf16[256,512]{1,0:T(8,128)(2,1)S(1)} %copy-done.6), channel_id=1, source_target_pairs={{0,1},{1,0},{2,3},{3,2},{4,5},{5,4},{6,7},{7,6},{8,9},{9,8},{10,11... | collective-permute-start | bytes 786440 | tf_op jit(solution)/shard_map/ppermute | solution.py:29
  26.0 13.7 %all-to-all-done.refs_0_ = bf16[4,144,512]{2,1,0:T(8,128)(2,1)S(1)} async-done(((bf16[4,144,512]{2,1,0:T(8,128)(2,1)}), bf16[4,144,512]{2,1,0:T(8,128)(2,1)S(1)}, u32[]{:S(2)}, u32[]{:S(2)}) %all-to-all-start) | async-done | bytes 589856 | tf_op jit(solution)/shard_map/all_to_all | solution.py:226
  39.7 1.9 %collective-permute-start = (bf16[4,144,512]{2,1,0:T(8,128)(2,1)S(1)}, bf16[4,144,512]{2,1,0:T(8,128)(2,1)S(1)}, u32[]{:S(2)}, u32[]{:S(2)}) collective-permute-start(bf16[4,144,512]{2,1,0:T(8,128)(2,1)S(1)} %all-to-all-done.refs_0_), channel_id=1, source_target_pairs={{0,8},{1,57},{8,0},{9,17},{16,24},{17,9},{24,16},{25,33},{32,40},{... | collective-permute-start | bytes 1769480 | tf_op jit(solution)/shard_map/ppermute | solution.py:47
  41.7 0.0 collective-permute-done.12
  41.7 9.8 %collective-permute-done.refs_1_ = bf16[4,144,512]{2,1,0:T(8,128)(2,1)S(1)} collective-permute-done((bf16[4,144,512]{2,1,0:T(8,128)(2,1)S(1)}, bf16[4,144,512]{2,1,0:T(8,128)(2,1)S(1)}, u32[]{:S(2)}, u32[]{:S(2)}) %collective-permute-start) | collective-permute-done | bytes 589856 | tf_op jit(solution)/shard_map/ppermute | solution.py:47
  51.6 0.7 fusion.1
  52.3 0.0 all-gather.7.cloned.1.call-update
  52.3 2.8 %collective-permute-start.1 = (bf16[4,144,512]{2,1,0:T(8,128)(2,1)S(1)}, bf16[4,144,512]{2,1,0:T(8,128)(2,1)S(1)}, u32[]{:S(2)}, u32[]{:S(2)}) collective-permute-start(bf16[4,144,512]{2,1,0:T(8,128)(2,1)S(1)} %all-to-all-done.refs_0_), channel_id=1, source_target_pairs={{0,1},{1,0},{2,3},{3,2},{4,5},{5,4},{6,7},{7,6},{8,9},{9,8},{10,11... | collective-permute-start | bytes 1769480 | tf_op jit(solution)/shard_map/ppermute | solution.py:29
  55.1 1.9 %collective-permute-start.2 = (bf16[4,144,512]{2,1,0:T(8,128)(2,1)S(1)}, bf16[4,144,512]{2,1,0:T(8,128)(2,1)S(1)}, u32[]{:S(2)}, u32[]{:S(2)}) collective-permute-start(bf16[4,144,512]{2,1,0:T(8,128)(2,1)S(1)} %collective-permute-done.refs_1_), channel_id=1, source_target_pairs={{0,1},{1,0},{2,3},{3,2},{4,5},{5,4},{6,7},{7,6},{8,9},{9,8},{10,11... | collective-permute-start | bytes 1769480 | tf_op jit(solution)/shard_map/ppermute | solution.py:29
  57.1 2.4 %collective-permute-start.4 = (f32[64,512]{1,0:T(8,128)S(1)}, f32[64,512]{1,0:T(8,128)S(1)}, u32[]{:S(2)}, u32[]{:S(2)}) collective-permute-start(f32[64,512]{1,0:T(8,128)S(1)} %copy-done.3), channel_id=1, source_target_pairs={{0,1},{1,0},{2,3},{3,2},{4,5},{5,4},{6,7},{7,6},{8,9},{9,8},{10,11... | collective-permute-start | bytes 393224 | tf_op jit(solution)/shard_map/ppermute | solution.py:29
  59.5 0.1 pad_add_fusion.1.at_ref
  59.6 1.2 copy-done.4
  60.8 0.7 hidden.1.refs_7_.refs_6_.refs_5_.refs_3_
  61.5 0.1 pad_add_fusion.order_ref
  61.6 0.0 collective-permute-done.4.refs_6_
  61.6 0.0 collective-permute-done.1.refs_2_
  61.6 0.0 collective-permute-done.2.refs_3_
  61.6 0.0 all-gather.5.cloned.1.call-done
  61.7 1.6 copy-done.2
  63.3 1.4 key_part.3._
  64.7 3.0 %collective-permute-start.5 = (f32[64,512]{1,0:T(8,128)S(1)}, f32[64,512]{1,0:T(8,128)S(1)}, u32[]{:S(2)}, u32[]{:S(2)}) collective-permute-start(f32[64,512]{1,0:T(8,128)S(1)} %bank.1), channel_id=1, source_target_pairs={{0,1},{1,0},{2,3},{3,2},{4,5},{5,4},{6,7},{7,6},{8,9},{9,8},{10,11... | collective-permute-start | bytes 393224 | tf_op jit(solution)/shard_map/ppermute | solution.py:29
  67.7 4.3 %collective-permute-start.7 = (bf16[256,1024]{1,0:T(8,128)(2,1)S(1)}, bf16[256,1024]{1,0:T(8,128)(2,1)S(1)}, u32[]{:S(2)}, u32[]{:S(2)}) collective-permute-start(bf16[256,1024]{1,0:T(8,128)(2,1)S(1)} %key_part.3._), channel_id=1, source_target_pairs={{0,2},{1,7},{2,0},{3,5},{4,6},{5,3},{6,4},{7,1},{8,10},{9,15},{10,... | collective-permute-start | bytes 1572872 | tf_op jit(solution)/shard_map/ppermute | solution.py:38
  72.0 0.0 collective-permute-done.5.refs_6_.refs_4_.refs_2_
  72.0 1.4 key_part.5
  73.4 2.2 %collective-permute-start.6 = (bf16[256,1024]{1,0:T(8,128)(2,1)S(1)}, bf16[256,1024]{1,0:T(8,128)(2,1)S(1)}, u32[]{:S(2)}, u32[]{:S(2)}) collective-permute-start(bf16[256,1024]{1,0:T(8,128)(2,1)S(1)} %key_part.5), channel_id=1, source_target_pairs={{0,2},{1,7},{2,0},{3,5},{4,6},{5,3},{6,4},{7,1},{8,10},{9,15},{10,... | collective-permute-start | bytes 1572872 | tf_op jit(solution)/shard_map/ppermute | solution.py:38
  75.6 2.0 %key_part.4 = (f32[256,1024]{1,0:T(8,128)S(1)}, f32[256,1024]{1,0:T(8,128)S(1)}) custom-call(s32[4]{0:T(128)S(1)} %pad_add_fusion.order_ref, s32[16,4]{1,0:T(8,128)S(1)} %slice_convert_fusion.ids_ref, bf16[4,144,512]{2,1,0:T(8,128)(2,1)S(1)} %all-to-all-done.refs_0_, bf16[4,144,512]{2,1,0:T(8,128)(2,1)S(1)} %collective-permute-done.refs_1_, ...), custom_call_target="tpu_custom_call" | custom-call | flops 1073741824 | bytes 4194304 | tf_op jit(solution)/shard_map/key_part/pallas_call | solution.py:194
  77.6 1.2 collective-permute-done.7.came_ref
  78.8 0.1 add.38.mine_ref
  78.9 2.2 %collective-permute-start.8 = (bf16[256,1024]{1,0:T(8,128)(2,1)S(1)}, bf16[256,1024]{1,0:T(8,128)(2,1)S(1)}, u32[]{:S(2)}, u32[]{:S(2)}) collective-permute-start(bf16[256,1024]{1,0:T(8,128)(2,1)S(1)} %add.38.mine_ref), channel_id=1, source_target_pairs={{0,6},{1,3},{2,4},{3,1},{4,2},{5,7},{6,0},{7,5},{8,14},{9,11},{10,... | collective-permute-start | bytes 1572872 | tf_op jit(solution)/shard_map/ppermute | solution.py:38
  81.1 3.9 %collective-permute-done.6.came_ref = bf16[256,1024]{1,0:T(8,128)(2,1)S(1)} collective-permute-done((bf16[256,1024]{1,0:T(8,128)(2,1)S(1)}, bf16[256,1024]{1,0:T(8,128)(2,1)S(1)}, u32[]{:S(2)}, u32[]{:S(2)}) %collective-permute-start.6) | collective-permute-done | bytes 524320 | tf_op jit(solution)/shard_map/ppermute | solution.py:38
  84.9 0.1 add.37.mine_ref
  85.0 1.9 %collective-permute-start.9 = (bf16[256,1024]{1,0:T(8,128)(2,1)S(1)}, bf16[256,1024]{1,0:T(8,128)(2,1)S(1)}, u32[]{:S(2)}, u32[]{:S(2)}) collective-permute-start(bf16[256,1024]{1,0:T(8,128)(2,1)S(1)} %add.37.mine_ref), channel_id=1, source_target_pairs={{0,6},{1,3},{2,4},{3,1},{4,2},{5,7},{6,0},{7,5},{8,14},{9,11},{10,... | collective-permute-start | bytes 1572872 | tf_op jit(solution)/shard_map/ppermute | solution.py:38
  87.0 2.7 %collective-permute-done.8.came_ref = bf16[256,1024]{1,0:T(8,128)(2,1)S(1)} collective-permute-done((bf16[256,1024]{1,0:T(8,128)(2,1)S(1)}, bf16[256,1024]{1,0:T(8,128)(2,1)S(1)}, u32[]{:S(2)}, u32[]{:S(2)}) %collective-permute-start.8) | collective-permute-done | bytes 524320 | tf_op jit(solution)/shard_map/ppermute | solution.py:38
  89.7 0.2 square.2.refs_0_
  89.9 4.3 %collective-permute-start.10 = (bf16[256,1024]{1,0:T(8,128)(2,1)S(1)}, bf16[256,1024]{1,0:T(8,128)(2,1)S(1)}, u32[]{:S(2)}, u32[]{:S(2)}) collective-permute-start(bf16[256,1024]{1,0:T(8,128)(2,1)S(1)} %square.2.refs_0_), channel_id=1, source_target_pairs={{0,2},{1,7},{2,0},{3,5},{4,6},{5,3},{6,4},{7,1},{8,10},{9,15},{10,... | collective-permute-start | bytes 1572872 | tf_op jit(solution)/shard_map/ppermute | solution.py:38
  94.2 1.1 collective-permute-done.9.came_ref
  95.4 0.2 square.3.refs_1_
  95.5 4.3 %collective-permute-start.11 = (bf16[256,1024]{1,0:T(8,128)(2,1)S(1)}, bf16[256,1024]{1,0:T(8,128)(2,1)S(1)}, u32[]{:S(2)}, u32[]{:S(2)}) collective-permute-start(bf16[256,1024]{1,0:T(8,128)(2,1)S(1)} %square.3.refs_1_), channel_id=1, source_target_pairs={{0,2},{1,7},{2,0},{3,5},{4,6},{5,3},{6,4},{7,1},{8,10},{9,15},{10,... | collective-permute-start | bytes 1572872 | tf_op jit(solution)/shard_map/ppermute | solution.py:38
  99.8 2.6 %collective-permute-done.10.refs_2_ = bf16[256,1024]{1,0:T(8,128)(2,1)S(1)} collective-permute-done((bf16[256,1024]{1,0:T(8,128)(2,1)S(1)}, bf16[256,1024]{1,0:T(8,128)(2,1)S(1)}, u32[]{:S(2)}, u32[]{:S(2)}) %collective-permute-start.10) | collective-permute-done | bytes 524320 | tf_op jit(solution)/shard_map/ppermute | solution.py:38
  102.5 2.2 %all-gather.7.cloned.1.call-done = bf16[1152,1024]{1,0:T(8,128)(2,1)} async-done(((bf16[144,1024]{1,0:T(8,128)(2,1)}), bf16[1152,1024]{1,0:T(8,128)(2,1)}) %all-gather.7.cloned.1.call-update) | async-done | bytes 2359312 | tf_op jit(solution)/shard_map/all_gather | solution.py:240
  104.7 1.7 %copy-done = bf16[1152,1024]{1,0:T(8,128)(2,1)S(1)} copy-done((bf16[1152,1024]{1,0:T(8,128)(2,1)S(1)}, bf16[1152,1024]{1,0:T(8,128)(2,1)}, u32[]{:S(2)}) %copy-start) | copy-done | bytes 2359320
  106.3 1.8 %out_part.4.refs_4_ = bf16[3,2,128,512]{3,2,1,0:T(8,128)(2,1)S(1)} custom-call(s32[4]{0:T(128)S(1)} %pad_add_fusion.order_ref, s32[16,4]{1,0:T(8,128)S(1)} %slice_convert_fusion.ids_ref, bf16[256,1024]{1,0:T(8,128)(2,1)S(1)} %square.2.refs_0_, bf16[256,1024]{1,0:T(8,128)(2,1)S(1)} %square.3.refs_1_, bf16[256,1024]{1,0:T(8,128)(2,1)S(1)} %collective-permute-done.10.refs_2_, ...), custom_call_target="tpu_custom_call" | custom-call | flops 805306368 | bytes 3407872 | tf_op jit(solution)/shard_map/out_part/pallas_call | solution.py:194
  108.1 0.0 collective-permute-done.11.refs_3_.refs_0_
  108.2 0.0 copy-done.1
  108.2 1.2 out_part.5
  109.3 5.7 %collective-permute-start.13 = (bf16[4,2,128,512]{3,2,1,0:T(8,128)(2,1)S(1)}, bf16[4,2,128,512]{3,2,1,0:T(8,128)(2,1)S(1)}, u32[]{:S(2)}, u32[]{:S(2)}) collective-permute-start(bf16[4,2,128,512]{3,2,1,0:T(8,128)(2,1)S(1)} %out_part.5), channel_id=1, source_target_pairs={{0,1},{1,0},{2,3},{3,2},{4,5},{5,4},{6,7},{7,6},{8,9},{9,8},{10,11... | collective-permute-start | bytes 3145736 | tf_op jit(solution)/shard_map/ppermute | solution.py:29
  115.1 2.1 %out_part.3.mine_ref = f32[4,2,128,512]{3,2,1,0:T(8,128)S(1)} custom-call(s32[4]{0:T(128)S(1)} %pad_add_fusion.order_ref, s32[16,4]{1,0:T(8,128)S(1)} %slice_convert_fusion.ids_ref, bf16[256,1024]{1,0:T(8,128)(2,1)S(1)} %square.2.refs_0_, bf16[256,1024]{1,0:T(8,128)(2,1)S(1)} %square.3.refs_1_, bf16[256,1024]{1,0:T(8,128)(2,1)S(1)} %collective-permute-done.10.refs_2_, ...), custom_call_target="tpu_custom_call" | custom-call | flops 1073741824 | bytes 4194304 | tf_op jit(solution)/shard_map/out_part/pallas_call | solution.py:194
  117.2 0.1 collective-permute-done.13.came_ref
  117.3 1.8 %place.1 = bf16[8,128,512]{2,1,0:T(8,128)(2,1)} custom-call(s32[4]{0:T(128)S(1)} %pad_add_fusion.order_ref, s32[3]{0:T(128)S(1)} %pad_add_fusion.1.at_ref, f32[4,2,128,512]{3,2,1,0:T(8,128)S(1)} %out_part.3.mine_ref, bf16[4,2,128,512]{3,2,1,0:T(8,128)(2,1)S(1)} %collective-permute-done.13.came_ref), custom_call_target="tpu_custom_call" | custom-call | flops 1048576 | bytes 1051648 | tf_op jit(solution)/shard_map/place/pallas_call | solution.py:194
  119.2 6.7 %all-to-all-start.1 = ((bf16[8,128,512]{2,1,0:T(8,128)(2,1)}), bf16[8,128,512]{2,1,0:T(8,128)(2,1)S(1)}, u32[]{:S(2)}, u32[]{:S(2)}) async-start(bf16[8,128,512]{2,1,0:T(8,128)(2,1)} %place.1), calls=%async_computation.1 | async-start | bytes 2097152 | tf_op jit(solution)/shard_map/all_to_all | solution.py:295
  125.9 3.0 %steps.1 = (f32[512,256]{1,0:T(8,128)}, f32[256,512]{1,0:T(8,128)}) custom-call(s32[3]{0:T(128)S(1)} %pad_add_fusion.1.at_ref, bf16[128,128]{1,0:T(8,128)(2,1)S(1)} %bitcast.23, f32[64,512]{1,0:T(8,128)S(1)} %copy-done.3, f32[64,4096]{1,0:T(8,128)S(1)} %copy-done.5), custom_call_target="tpu_custom_call" | custom-call | flops 134217728 | bytes 1048576 | tf_op jit(solution)/shard_map/steps/pallas_call | solution.py:194
  128.9 26.2 %all-to-all-done.1 = bf16[8,128,512]{2,1,0:T(8,128)(2,1)S(1)} async-done(((bf16[8,128,512]{2,1,0:T(8,128)(2,1)}), bf16[8,128,512]{2,1,0:T(8,128)(2,1)S(1)}, u32[]{:S(2)}, u32[]{:S(2)}) %all-to-all-start.1) | async-done | bytes 1048608 | tf_op jit(solution)/shard_map/all_to_all | solution.py:295
  155.1 0.8 reduce_sum.12
  (17 shorter events, 0.1 us)
Async XLA Ops:
  7.2 16.5 %copy-start.6 = (bf16[256,512]{1,0:T(8,128)(2,1)S(1)}, bf16[256,512]{1,0:T(8,128)(2,1)}, u32[]{:S(2)}) copy-start(bf16[256,512]{1,0:T(8,128)(2,1)} %param.11) | copy-start | bytes 786436
  7.2 54.5 %all-gather.5.cloned.1.call-start = ((), (), s32[]{:S(2)}) async-start(), calls=%async_computation.2 | async-start | bytes 2359296 | tf_op jit(solution)/shard_map/all_gather | solution.py:237
  7.2 10.3 %collective-permute-start.3 = (bf16[512,256]{1,0:T(8,128)(2,1)}, bf16[512,256]{1,0:T(8,128)(2,1)S(1)}, u32[]{:S(2)}, u32[]{:S(2)}) collective-permute-start(bf16[512,256]{1,0:T(8,128)(2,1)} %param.10), channel_id=1, source_target_pairs={{0,1},{1,0},{2,3},{3,2},{4,5},{5,4},{6,7},{7,6},{8,9},{9,8},{10,11... | collective-permute-start | bytes 786440 | tf_op jit(solution)/shard_map/ppermute | solution.py:29
  17.5 39.6 %copy-start.3 = (f32[64,512]{1,0:T(8,128)S(1)}, f32[64,512]{1,0:T(8,128)}, u32[]{:S(2)}) copy-start(f32[64,512]{1,0:T(8,128)} %bank_ref.1) | copy-start | bytes 393220
  20.1 19.6 %all-to-all-start = ((bf16[4,144,512]{2,1,0:T(8,128)(2,1)}), bf16[4,144,512]{2,1,0:T(8,128)(2,1)S(1)}, u32[]{:S(2)}, u32[]{:S(2)}) async-start(bf16[4,144,512]{2,1,0:T(8,128)(2,1)} %shift.1), calls=%async_computation | async-start | bytes 1179648 | tf_op jit(solution)/shard_map/all_to_all | solution.py:226
  23.6 81.0 %all-gather.7.cloned.1.call-start = ((), (), s32[]{:S(2)}) async-start(), calls=%async_computation.3 | async-start | bytes 2654208 | tf_op jit(solution)/shard_map/all_gather | solution.py:240
  23.7 18.0 %collective-permute-start.12 = (bf16[256,512]{1,0:T(8,128)(2,1)S(1)}, bf16[256,512]{1,0:T(8,128)(2,1)S(1)}, u32[]{:S(2)}, u32[]{:S(2)}) collective-permute-start(bf16[256,512]{1,0:T(8,128)(2,1)S(1)} %copy-done.6), channel_id=1, source_target_pairs={{0,1},{1,0},{2,3},{3,2},{4,5},{5,4},{6,7},{7,6},{8,9},{9,8},{10,11... | collective-permute-start | bytes 786440 | tf_op jit(solution)/shard_map/ppermute | solution.py:29
  39.7 11.8 %collective-permute-start = (bf16[4,144,512]{2,1,0:T(8,128)(2,1)S(1)}, bf16[4,144,512]{2,1,0:T(8,128)(2,1)S(1)}, u32[]{:S(2)}, u32[]{:S(2)}) collective-permute-start(bf16[4,144,512]{2,1,0:T(8,128)(2,1)S(1)} %all-to-all-done.refs_0_), channel_id=1, source_target_pairs={{0,8},{1,57},{8,0},{9,17},{16,24},{17,9},{24,16},{25,33},{32,40},{... | collective-permute-start | bytes 1769480 | tf_op jit(solution)/shard_map/ppermute | solution.py:47
  52.3 9.3 %collective-permute-start.1 = (bf16[4,144,512]{2,1,0:T(8,128)(2,1)S(1)}, bf16[4,144,512]{2,1,0:T(8,128)(2,1)S(1)}, u32[]{:S(2)}, u32[]{:S(2)}) collective-permute-start(bf16[4,144,512]{2,1,0:T(8,128)(2,1)S(1)} %all-to-all-done.refs_0_), channel_id=1, source_target_pairs={{0,1},{1,0},{2,3},{3,2},{4,5},{5,4},{6,7},{7,6},{8,9},{9,8},{10,11... | collective-permute-start | bytes 1769480 | tf_op jit(solution)/shard_map/ppermute | solution.py:29
  55.1 6.5 %collective-permute-start.2 = (bf16[4,144,512]{2,1,0:T(8,128)(2,1)S(1)}, bf16[4,144,512]{2,1,0:T(8,128)(2,1)S(1)}, u32[]{:S(2)}, u32[]{:S(2)}) collective-permute-start(bf16[4,144,512]{2,1,0:T(8,128)(2,1)S(1)} %collective-permute-done.refs_1_), channel_id=1, source_target_pairs={{0,1},{1,0},{2,3},{3,2},{4,5},{5,4},{6,7},{7,6},{8,9},{9,8},{10,11... | collective-permute-start | bytes 1769480 | tf_op jit(solution)/shard_map/ppermute | solution.py:29
  57.1 4.6 %collective-permute-start.4 = (f32[64,512]{1,0:T(8,128)S(1)}, f32[64,512]{1,0:T(8,128)S(1)}, u32[]{:S(2)}, u32[]{:S(2)}) collective-permute-start(f32[64,512]{1,0:T(8,128)S(1)} %copy-done.3), channel_id=1, source_target_pairs={{0,1},{1,0},{2,3},{3,2},{4,5},{5,4},{6,7},{7,6},{8,9},{9,8},{10,11... | collective-permute-start | bytes 393224 | tf_op jit(solution)/shard_map/ppermute | solution.py:29
  59.6 1.2 copy-start.4
  61.7 1.6 copy-start.2
  64.7 7.3 %collective-permute-start.5 = (f32[64,512]{1,0:T(8,128)S(1)}, f32[64,512]{1,0:T(8,128)S(1)}, u32[]{:S(2)}, u32[]{:S(2)}) collective-permute-start(f32[64,512]{1,0:T(8,128)S(1)} %bank.1), channel_id=1, source_target_pairs={{0,1},{1,0},{2,3},{3,2},{4,5},{5,4},{6,7},{7,6},{8,9},{9,8},{10,11... | collective-permute-start | bytes 393224 | tf_op jit(solution)/shard_map/ppermute | solution.py:29
  67.7 11.1 %collective-permute-start.7 = (bf16[256,1024]{1,0:T(8,128)(2,1)S(1)}, bf16[256,1024]{1,0:T(8,128)(2,1)S(1)}, u32[]{:S(2)}, u32[]{:S(2)}) collective-permute-start(bf16[256,1024]{1,0:T(8,128)(2,1)S(1)} %key_part.3._), channel_id=1, source_target_pairs={{0,2},{1,7},{2,0},{3,5},{4,6},{5,3},{6,4},{7,1},{8,10},{9,15},{10,... | collective-permute-start | bytes 1572872 | tf_op jit(solution)/shard_map/ppermute | solution.py:38
  73.4 11.5 %collective-permute-start.6 = (bf16[256,1024]{1,0:T(8,128)(2,1)S(1)}, bf16[256,1024]{1,0:T(8,128)(2,1)S(1)}, u32[]{:S(2)}, u32[]{:S(2)}) collective-permute-start(bf16[256,1024]{1,0:T(8,128)(2,1)S(1)} %key_part.5), channel_id=1, source_target_pairs={{0,2},{1,7},{2,0},{3,5},{4,6},{5,3},{6,4},{7,1},{8,10},{9,15},{10,... | collective-permute-start | bytes 1572872 | tf_op jit(solution)/shard_map/ppermute | solution.py:38
  78.9 10.8 %collective-permute-start.8 = (bf16[256,1024]{1,0:T(8,128)(2,1)S(1)}, bf16[256,1024]{1,0:T(8,128)(2,1)S(1)}, u32[]{:S(2)}, u32[]{:S(2)}) collective-permute-start(bf16[256,1024]{1,0:T(8,128)(2,1)S(1)} %add.38.mine_ref), channel_id=1, source_target_pairs={{0,6},{1,3},{2,4},{3,1},{4,2},{5,7},{6,0},{7,5},{8,14},{9,11},{10,... | collective-permute-start | bytes 1572872 | tf_op jit(solution)/shard_map/ppermute | solution.py:38
  85.0 10.3 %collective-permute-start.9 = (bf16[256,1024]{1,0:T(8,128)(2,1)S(1)}, bf16[256,1024]{1,0:T(8,128)(2,1)S(1)}, u32[]{:S(2)}, u32[]{:S(2)}) collective-permute-start(bf16[256,1024]{1,0:T(8,128)(2,1)S(1)} %add.37.mine_ref), channel_id=1, source_target_pairs={{0,6},{1,3},{2,4},{3,1},{4,2},{5,7},{6,0},{7,5},{8,14},{9,11},{10,... | collective-permute-start | bytes 1572872 | tf_op jit(solution)/shard_map/ppermute | solution.py:38
  89.9 12.6 %collective-permute-start.10 = (bf16[256,1024]{1,0:T(8,128)(2,1)S(1)}, bf16[256,1024]{1,0:T(8,128)(2,1)S(1)}, u32[]{:S(2)}, u32[]{:S(2)}) collective-permute-start(bf16[256,1024]{1,0:T(8,128)(2,1)S(1)} %square.2.refs_0_), channel_id=1, source_target_pairs={{0,2},{1,7},{2,0},{3,5},{4,6},{5,3},{6,4},{7,1},{8,10},{9,15},{10,... | collective-permute-start | bytes 1572872 | tf_op jit(solution)/shard_map/ppermute | solution.py:38
  95.5 12.6 %collective-permute-start.11 = (bf16[256,1024]{1,0:T(8,128)(2,1)S(1)}, bf16[256,1024]{1,0:T(8,128)(2,1)S(1)}, u32[]{:S(2)}, u32[]{:S(2)}) collective-permute-start(bf16[256,1024]{1,0:T(8,128)(2,1)S(1)} %square.3.refs_1_), channel_id=1, source_target_pairs={{0,2},{1,7},{2,0},{3,5},{4,6},{5,3},{6,4},{7,1},{8,10},{9,15},{10,... | collective-permute-start | bytes 1572872 | tf_op jit(solution)/shard_map/ppermute | solution.py:38
  104.7 1.7 %copy-start = (bf16[1152,1024]{1,0:T(8,128)(2,1)S(1)}, bf16[1152,1024]{1,0:T(8,128)(2,1)}, u32[]{:S(2)}) copy-start(bf16[1152,1024]{1,0:T(8,128)(2,1)} %all-gather.7.cloned.1.call-done) | copy-start | bytes 7077892
  106.3 1.8 %copy-start.1 = (bf16[1152,1024]{1,0:T(8,128)(2,1)S(1)}, bf16[1152,1024]{1,0:T(8,128)(2,1)}, u32[]{:S(2)}) copy-start(bf16[1152,1024]{1,0:T(8,128)(2,1)} %all-gather.7.cloned.1.call-done) | copy-start | bytes 7077892
  109.3 8.0 %collective-permute-start.13 = (bf16[4,2,128,512]{3,2,1,0:T(8,128)(2,1)S(1)}, bf16[4,2,128,512]{3,2,1,0:T(8,128)(2,1)S(1)}, u32[]{:S(2)}, u32[]{:S(2)}) collective-permute-start(bf16[4,2,128,512]{3,2,1,0:T(8,128)(2,1)S(1)} %out_part.5), channel_id=1, source_target_pairs={{0,1},{1,0},{2,3},{3,2},{4,5},{5,4},{6,7},{7,6},{8,9},{9,8},{10,11... | collective-permute-start | bytes 3145736 | tf_op jit(solution)/shard_map/ppermute | solution.py:29
  119.2 6.7 %copy-start.5 = (f32[64,4096]{1,0:T(8,128)S(1)}, f32[64,4096]{1,0:T(8,128)}, u32[]{:S(2)}) copy-start(f32[64,4096]{1,0:T(8,128)} %hid_ref.1) | copy-start | bytes 3145732
  119.2 35.9 %all-to-all-start.1 = ((bf16[8,128,512]{2,1,0:T(8,128)(2,1)}), bf16[8,128,512]{2,1,0:T(8,128)(2,1)S(1)}, u32[]{:S(2)}, u32[]{:S(2)}) async-start(bf16[8,128,512]{2,1,0:T(8,128)(2,1)} %place.1), calls=%async_computation.1 | async-start | bytes 2097152 | tf_op jit(solution)/shard_map/all_to_all | solution.py:295
Sparse Core Ops, SparseCore 0:
  18.4 39.5 all-gather.4
  60.6 43.9 all-gather.6

commit v10 on v9

--- a/solution.py
+++ b/solution.py
@@ -197,7 +197,7 @@
         in_specs=specs,
         out_specs=[VMEM] * len(outs),
         scratch_shapes=scratch,
-        compiler_params=pltpu.CompilerParams(vmem_limit_bytes=16 << 20),
+        compiler_params=pltpu.CompilerParams(vmem_limit_bytes=10 << 20),
         cost_estimate=estimate,
         name=name,
     )(*args)

time: 163 us -> 163 us (level)
  no operation moved by 1% of the time
where the time goes in v10:
time: 163 us
  waiting for transfers between devices  64.2 us (39%)
  starting transfers between devices  58.4 us (36%)
  Pallas kernels  17.8 us (11%)
  between operations  14.4 us (9%)
  local copies, waits for them, and re-layouts  5.48 us (3%)
  other arithmetic  2.45 us (2%)
    ppermute x7, starting transfers between devices, swap(): return lax.ppermute(x, 'core', [(0, 1), (1, 0)])  27 us
    all_to_all x1, waiting for transfers between devices, shards(): pieces = lax.all_to_all(result, YQ + ('y_low',), 0, 0)  26.2 us
    ppermute x6, starting transfers between devices, exchange(): return lax.ppermute(x, ('x', 'core'), pairs)  19.2 us
    pallas_call x15, Pallas kernels, call(): pl.pallas_call(kernel, out_shape=[jax.ShapeDtypeStruct(*out) for out in o...  17.8 us
    all_to_all x1, waiting for transfers between devices, shards(): same = lax.all_to_all(shifted, YQ, 0, 0)  13.7 us
    ppermute x6, waiting for transfers between devices, exchange(): return lax.ppermute(x, ('x', 'core'), pairs)  11.6 us
    ppermute x1, waiting for transfers between devices, beside(): return lax.ppermute(x, YQ + ('y_low', 'core'), pairs)  9.83 us
    all_to_all x1, starting transfers between devices, shards(): pieces = lax.all_to_all(result, YQ + ('y_low',), 0, 0)  6.68 us
  transfers between devices with their start and end apart: 18, of which 11 were waited for; matrix products, arithmetic and copies ran while one was open for 1% of the time, Pallas kernels for 9%

profile of v10, /device:TPU:1, one launch (start us, length us, event | category | flops | bytes accessed | tf_op | source)
XLA Modules:
  0.0 162.7 jit_solution(6802496852196936364)
XLA Ops:
  7.2 0.0 copy-start.6
  7.2 0.0 all-gather.5.cloned.1.call-start
  7.2 8.9 %collective-permute-start.3 = (bf16[512,256]{1,0:T(8,128)(2,1)}, bf16[512,256]{1,0:T(8,128)(2,1)S(1)}, u32[]{:S(2)}, u32[]{:S(2)}) collective-permute-start(bf16[512,256]{1,0:T(8,128)(2,1)} %param.10), channel_id=1, source_target_pairs={{0,1},{1,0},{2,3},{3,2},{4,5},{5,4},{6,7},{7,6},{8,9},{9,8},{10,11... | collective-permute-start | bytes 786440 | tf_op jit(solution)/shard_map/ppermute | solution.py:29
  16.2 0.9 constant_dynamic-slice_fusion.3
  17.1 0.4 collective-permute-done.3
  17.5 0.0 copy-start.3
  17.5 0.7 pad_maximum_fusion
  18.2 0.0 all-gather.5.cloned.1.call-update
  18.3 1.9 %shift.1 = bf16[4,144,512]{2,1,0:T(8,128)(2,1)} custom-call(s32[2,4]{1,0:T(2,128)} %picks_hbm.1, s32[2]{0:T(128)} %ranks_hbm.1, bf16[128,512]{1,0:T(8,128)(2,1)} %x_hbm.1, f32[1,512]{1,0:T(1,128)} %bitcast.26), custom_call_target="tpu_custom_call" | custom-call | flops 2097152 | bytes 151552 | tf_op jit(solution)/shard_map/shift/pallas_call | solution.py:194
  20.1 3.5 %all-to-all-start = ((bf16[4,144,512]{2,1,0:T(8,128)(2,1)}), bf16[4,144,512]{2,1,0:T(8,128)(2,1)S(1)}, u32[]{:S(2)}, u32[]{:S(2)}) async-start(bf16[4,144,512]{2,1,0:T(8,128)(2,1)} %shift.1), calls=%async_computation | async-start | bytes 1179648 | tf_op jit(solution)/shard_map/all_to_all | solution.py:226
  23.6 0.0 all-gather.7.cloned.1.call-start
  23.7 2.3 %collective-permute-start.12 = (bf16[256,512]{1,0:T(8,128)(2,1)S(1)}, bf16[256,512]{1,0:T(8,128)(2,1)S(1)}, u32[]{:S(2)}, u32[]{:S(2)}) collective-permute-start(bf16[256,512]{1,0:T(8,128)(2,1)S(1)} %copy-done.6), channel_id=1, source_target_pairs={{0,1},{1,0},{2,3},{3,2},{4,5},{5,4},{6,7},{7,6},{8,9},{9,8},{10,11... | collective-permute-start | bytes 786440 | tf_op jit(solution)/shard_map/ppermute | solution.py:29
  26.0 13.7 %all-to-all-done.refs_0_ = bf16[4,144,512]{2,1,0:T(8,128)(2,1)S(1)} async-done(((bf16[4,144,512]{2,1,0:T(8,128)(2,1)}), bf16[4,144,512]{2,1,0:T(8,128)(2,1)S(1)}, u32[]{:S(2)}, u32[]{:S(2)}) %all-to-all-start) | async-done | bytes 589856 | tf_op jit(solution)/shard_map/all_to_all | solution.py:226
  39.7 1.9 %collective-permute-start = (bf16[4,144,512]{2,1,0:T(8,128)(2,1)S(1)}, bf16[4,144,512]{2,1,0:T(8,128)(2,1)S(1)}, u32[]{:S(2)}, u32[]{:S(2)}) collective-permute-start(bf16[4,144,512]{2,1,0:T(8,128)(2,1)S(1)} %all-to-all-done.refs_0_), channel_id=1, source_target_pairs={{0,8},{1,57},{8,0},{9,17},{16,24},{17,9},{24,16},{25,33},{32,40},{... | collective-permute-start | bytes 1769480 | tf_op jit(solution)/shard_map/ppermute | solution.py:47
  41.7 0.0 collective-permute-done.12
  41.7 9.8 %collective-permute-done.refs_1_ = bf16[4,144,512]{2,1,0:T(8,128)(2,1)S(1)} collective-permute-done((bf16[4,144,512]{2,1,0:T(8,128)(2,1)S(1)}, bf16[4,144,512]{2,1,0:T(8,128)(2,1)S(1)}, u32[]{:S(2)}, u32[]{:S(2)}) %collective-permute-start) | collective-permute-done | bytes 589856 | tf_op jit(solution)/shard_map/ppermute | solution.py:47
  51.6 0.7 fusion.1
  52.3 0.0 all-gather.7.cloned.1.call-update
  52.3 2.8 %collective-permute-start.1 = (bf16[4,144,512]{2,1,0:T(8,128)(2,1)S(1)}, bf16[4,144,512]{2,1,0:T(8,128)(2,1)S(1)}, u32[]{:S(2)}, u32[]{:S(2)}) collective-permute-start(bf16[4,144,512]{2,1,0:T(8,128)(2,1)S(1)} %all-to-all-done.refs_0_), channel_id=1, source_target_pairs={{0,1},{1,0},{2,3},{3,2},{4,5},{5,4},{6,7},{7,6},{8,9},{9,8},{10,11... | collective-permute-start | bytes 1769480 | tf_op jit(solution)/shard_map/ppermute | solution.py:29
  55.1 1.9 %collective-permute-start.2 = (bf16[4,144,512]{2,1,0:T(8,128)(2,1)S(1)}, bf16[4,144,512]{2,1,0:T(8,128)(2,1)S(1)}, u32[]{:S(2)}, u32[]{:S(2)}) collective-permute-start(bf16[4,144,512]{2,1,0:T(8,128)(2,1)S(1)} %collective-permute-done.refs_1_), channel_id=1, source_target_pairs={{0,1},{1,0},{2,3},{3,2},{4,5},{5,4},{6,7},{7,6},{8,9},{9,8},{10,11... | collective-permute-start | bytes 1769480 | tf_op jit(solution)/shard_map/ppermute | solution.py:29
  57.1 2.4 %collective-permute-start.4 = (f32[64,512]{1,0:T(8,128)S(1)}, f32[64,512]{1,0:T(8,128)S(1)}, u32[]{:S(2)}, u32[]{:S(2)}) collective-permute-start(f32[64,512]{1,0:T(8,128)S(1)} %copy-done.3), channel_id=1, source_target_pairs={{0,1},{1,0},{2,3},{3,2},{4,5},{5,4},{6,7},{7,6},{8,9},{9,8},{10,11... | collective-permute-start | bytes 393224 | tf_op jit(solution)/shard_map/ppermute | solution.py:29
  59.5 0.1 pad_add_fusion.1.at_ref
  59.6 1.2 copy-done.4
  60.8 0.7 hidden.1.refs_7_.refs_6_.refs_5_.refs_3_
  61.5 0.1 pad_add_fusion.order_ref
  61.6 0.0 collective-permute-done.4.refs_6_
  61.6 0.0 collective-permute-done.1.refs_2_
  61.6 0.0 collective-permute-done.2.refs_3_
  61.6 0.0 all-gather.5.cloned.1.call-done
  61.7 0.0 copy-start.2
  61.7 1.6 copy-done.2
  63.3 1.4 key_part.3._
  64.7 3.0 %collective-permute-start.5 = (f32[64,512]{1,0:T(8,128)S(1)}, f32[64,512]{1,0:T(8,128)S(1)}, u32[]{:S(2)}, u32[]{:S(2)}) collective-permute-start(f32[64,512]{1,0:T(8,128)S(1)} %bank.1), channel_id=1, source_target_pairs={{0,1},{1,0},{2,3},{3,2},{4,5},{5,4},{6,7},{7,6},{8,9},{9,8},{10,11... | collective-permute-start | bytes 393224 | tf_op jit(solution)/shard_map/ppermute | solution.py:29
  67.7 4.3 %collective-permute-start.7 = (bf16[256,1024]{1,0:T(8,128)(2,1)S(1)}, bf16[256,1024]{1,0:T(8,128)(2,1)S(1)}, u32[]{:S(2)}, u32[]{:S(2)}) collective-permute-start(bf16[256,1024]{1,0:T(8,128)(2,1)S(1)} %key_part.3._), channel_id=1, source_target_pairs={{0,2},{1,7},{2,0},{3,5},{4,6},{5,3},{6,4},{7,1},{8,10},{9,15},{10,... | collective-permute-start | bytes 1572872 | tf_op jit(solution)/shard_map/ppermute | solution.py:38
  72.0 0.0 collective-permute-done.5.refs_6_.refs_4_.refs_2_
  72.0 1.4 key_part.5
  73.4 2.2 %collective-permute-start.6 = (bf16[256,1024]{1,0:T(8,128)(2,1)S(1)}, bf16[256,1024]{1,0:T(8,128)(2,1)S(1)}, u32[]{:S(2)}, u32[]{:S(2)}) collective-permute-start(bf16[256,1024]{1,0:T(8,128)(2,1)S(1)} %key_part.5), channel_id=1, source_target_pairs={{0,2},{1,7},{2,0},{3,5},{4,6},{5,3},{6,4},{7,1},{8,10},{9,15},{10,... | collective-permute-start | bytes 1572872 | tf_op jit(solution)/shard_map/ppermute | solution.py:38
  75.6 2.0 %key_part.4 = (f32[256,1024]{1,0:T(8,128)S(1)}, f32[256,1024]{1,0:T(8,128)S(1)}) custom-call(s32[4]{0:T(128)S(1)} %pad_add_fusion.order_ref, s32[16,4]{1,0:T(8,128)S(1)} %slice_convert_fusion.ids_ref, bf16[4,144,512]{2,1,0:T(8,128)(2,1)S(1)} %all-to-all-done.refs_0_, bf16[4,144,512]{2,1,0:T(8,128)(2,1)S(1)} %collective-permute-done.refs_1_, ...), custom_call_target="tpu_custom_call" | custom-call | flops 1073741824 | bytes 4194304 | tf_op jit(solution)/shard_map/key_part/pallas_call | solution.py:194
  77.6 1.2 collective-permute-done.7.came_ref
  78.8 0.1 add.38.mine_ref
  78.9 2.2 %collective-permute-start.8 = (bf16[256,1024]{1,0:T(8,128)(2,1)S(1)}, bf16[256,1024]{1,0:T(8,128)(2,1)S(1)}, u32[]{:S(2)}, u32[]{:S(2)}) collective-permute-start(bf16[256,1024]{1,0:T(8,128)(2,1)S(1)} %add.38.mine_ref), channel_id=1, source_target_pairs={{0,6},{1,3},{2,4},{3,1},{4,2},{5,7},{6,0},{7,5},{8,14},{9,11},{10,... | collective-permute-start | bytes 1572872 | tf_op jit(solution)/shard_map/ppermute | solution.py:38
  81.1 3.9 %collective-permute-done.6.came_ref = bf16[256,1024]{1,0:T(8,128)(2,1)S(1)} collective-permute-done((bf16[256,1024]{1,0:T(8,128)(2,1)S(1)}, bf16[256,1024]{1,0:T(8,128)(2,1)S(1)}, u32[]{:S(2)}, u32[]{:S(2)}) %collective-permute-start.6) | collective-permute-done | bytes 524320 | tf_op jit(solution)/shard_map/ppermute | solution.py:38
  84.9 0.1 add.37.mine_ref
  85.0 1.9 %collective-permute-start.9 = (bf16[256,1024]{1,0:T(8,128)(2,1)S(1)}, bf16[256,1024]{1,0:T(8,128)(2,1)S(1)}, u32[]{:S(2)}, u32[]{:S(2)}) collective-permute-start(bf16[256,1024]{1,0:T(8,128)(2,1)S(1)} %add.37.mine_ref), channel_id=1, source_target_pairs={{0,6},{1,3},{2,4},{3,1},{4,2},{5,7},{6,0},{7,5},{8,14},{9,11},{10,... | collective-permute-start | bytes 1572872 | tf_op jit(solution)/shard_map/ppermute | solution.py:38
  87.0 2.7 %collective-permute-done.8.came_ref = bf16[256,1024]{1,0:T(8,128)(2,1)S(1)} collective-permute-done((bf16[256,1024]{1,0:T(8,128)(2,1)S(1)}, bf16[256,1024]{1,0:T(8,128)(2,1)S(1)}, u32[]{:S(2)}, u32[]{:S(2)}) %collective-permute-start.8) | collective-permute-done | bytes 524320 | tf_op jit(solution)/shard_map/ppermute | solution.py:38
  89.7 0.2 square.2.refs_0_
  89.9 4.3 %collective-permute-start.10 = (bf16[256,1024]{1,0:T(8,128)(2,1)S(1)}, bf16[256,1024]{1,0:T(8,128)(2,1)S(1)}, u32[]{:S(2)}, u32[]{:S(2)}) collective-permute-start(bf16[256,1024]{1,0:T(8,128)(2,1)S(1)} %square.2.refs_0_), channel_id=1, source_target_pairs={{0,2},{1,7},{2,0},{3,5},{4,6},{5,3},{6,4},{7,1},{8,10},{9,15},{10,... | collective-permute-start | bytes 1572872 | tf_op jit(solution)/shard_map/ppermute | solution.py:38
  94.2 1.1 collective-permute-done.9.came_ref
  95.4 0.2 square.3.refs_1_
  95.5 4.3 %collective-permute-start.11 = (bf16[256,1024]{1,0:T(8,128)(2,1)S(1)}, bf16[256,1024]{1,0:T(8,128)(2,1)S(1)}, u32[]{:S(2)}, u32[]{:S(2)}) collective-permute-start(bf16[256,1024]{1,0:T(8,128)(2,1)S(1)} %square.3.refs_1_), channel_id=1, source_target_pairs={{0,2},{1,7},{2,0},{3,5},{4,6},{5,3},{6,4},{7,1},{8,10},{9,15},{10,... | collective-permute-start | bytes 1572872 | tf_op jit(solution)/shard_map/ppermute | solution.py:38
  99.8 2.6 %collective-permute-done.10.refs_2_ = bf16[256,1024]{1,0:T(8,128)(2,1)S(1)} collective-permute-done((bf16[256,1024]{1,0:T(8,128)(2,1)S(1)}, bf16[256,1024]{1,0:T(8,128)(2,1)S(1)}, u32[]{:S(2)}, u32[]{:S(2)}) %collective-permute-start.10) | collective-permute-done | bytes 524320 | tf_op jit(solution)/shard_map/ppermute | solution.py:38
  102.5 2.2 %all-gather.7.cloned.1.call-done = bf16[1152,1024]{1,0:T(8,128)(2,1)} async-done(((bf16[144,1024]{1,0:T(8,128)(2,1)}), bf16[1152,1024]{1,0:T(8,128)(2,1)}) %all-gather.7.cloned.1.call-update) | async-done | bytes 2359312 | tf_op jit(solution)/shard_map/all_gather | solution.py:240
  104.7 1.7 %copy-done = bf16[1152,1024]{1,0:T(8,128)(2,1)S(1)} copy-done((bf16[1152,1024]{1,0:T(8,128)(2,1)S(1)}, bf16[1152,1024]{1,0:T(8,128)(2,1)}, u32[]{:S(2)}) %copy-start) | copy-done | bytes 2359320
  106.3 1.8 %out_part.4.refs_4_ = bf16[3,2,128,512]{3,2,1,0:T(8,128)(2,1)S(1)} custom-call(s32[4]{0:T(128)S(1)} %pad_add_fusion.order_ref, s32[16,4]{1,0:T(8,128)S(1)} %slice_convert_fusion.ids_ref, bf16[256,1024]{1,0:T(8,128)(2,1)S(1)} %square.2.refs_0_, bf16[256,1024]{1,0:T(8,128)(2,1)S(1)} %square.3.refs_1_, bf16[256,1024]{1,0:T(8,128)(2,1)S(1)} %collective-permute-done.10.refs_2_, ...), custom_call_target="tpu_custom_call" | custom-call | flops 805306368 | bytes 3407872 | tf_op jit(solution)/shard_map/out_part/pallas_call | solution.py:194
  108.1 0.0 collective-permute-done.11.refs_3_.refs_0_
  108.2 1.2 out_part.5
  109.3 5.7 %collective-permute-start.13 = (bf16[4,2,128,512]{3,2,1,0:T(8,128)(2,1)S(1)}, bf16[4,2,128,512]{3,2,1,0:T(8,128)(2,1)S(1)}, u32[]{:S(2)}, u32[]{:S(2)}) collective-permute-start(bf16[4,2,128,512]{3,2,1,0:T(8,128)(2,1)S(1)} %out_part.5), channel_id=1, source_target_pairs={{0,1},{1,0},{2,3},{3,2},{4,5},{5,4},{6,7},{7,6},{8,9},{9,8},{10,11... | collective-permute-start | bytes 3145736 | tf_op jit(solution)/shard_map/ppermute | solution.py:29
  115.1 2.1 %out_part.3.mine_ref = f32[4,2,128,512]{3,2,1,0:T(8,128)S(1)} custom-call(s32[4]{0:T(128)S(1)} %pad_add_fusion.order_ref, s32[16,4]{1,0:T(8,128)S(1)} %slice_convert_fusion.ids_ref, bf16[256,1024]{1,0:T(8,128)(2,1)S(1)} %square.2.refs_0_, bf16[256,1024]{1,0:T(8,128)(2,1)S(1)} %square.3.refs_1_, bf16[256,1024]{1,0:T(8,128)(2,1)S(1)} %collective-permute-done.10.refs_2_, ...), custom_call_target="tpu_custom_call" | custom-call | flops 1073741824 | bytes 4194304 | tf_op jit(solution)/shard_map/out_part/pallas_call | solution.py:194
  117.2 0.1 collective-permute-done.13.came_ref
  117.3 1.7 %place.1 = bf16[8,128,512]{2,1,0:T(8,128)(2,1)} custom-call(s32[4]{0:T(128)S(1)} %pad_add_fusion.order_ref, s32[3]{0:T(128)S(1)} %pad_add_fusion.1.at_ref, f32[4,2,128,512]{3,2,1,0:T(8,128)S(1)} %out_part.3.mine_ref, bf16[4,2,128,512]{3,2,1,0:T(8,128)(2,1)S(1)} %collective-permute-done.13.came_ref), custom_call_target="tpu_custom_call" | custom-call | flops 1048576 | bytes 1051648 | tf_op jit(solution)/shard_map/place/pallas_call | solution.py:194
  119.1 6.7 %all-to-all-start.1 = ((bf16[8,128,512]{2,1,0:T(8,128)(2,1)}), bf16[8,128,512]{2,1,0:T(8,128)(2,1)S(1)}, u32[]{:S(2)}, u32[]{:S(2)}) async-start(bf16[8,128,512]{2,1,0:T(8,128)(2,1)} %place.1), calls=%async_computation.1 | async-start | bytes 2097152 | tf_op jit(solution)/shard_map/all_to_all | solution.py:295
  125.8 3.0 %steps.1 = (f32[512,256]{1,0:T(8,128)}, f32[256,512]{1,0:T(8,128)}) custom-call(s32[3]{0:T(128)S(1)} %pad_add_fusion.1.at_ref, bf16[128,128]{1,0:T(8,128)(2,1)S(1)} %bitcast.23, f32[64,512]{1,0:T(8,128)S(1)} %copy-done.3, f32[64,4096]{1,0:T(8,128)S(1)} %copy-done.5), custom_call_target="tpu_custom_call" | custom-call | flops 134217728 | bytes 1048576 | tf_op jit(solution)/shard_map/steps/pallas_call | solution.py:194
  128.8 26.2 %all-to-all-done.1 = bf16[8,128,512]{2,1,0:T(8,128)(2,1)S(1)} async-done(((bf16[8,128,512]{2,1,0:T(8,128)(2,1)}), bf16[8,128,512]{2,1,0:T(8,128)(2,1)S(1)}, u32[]{:S(2)}, u32[]{:S(2)}) %all-to-all-start.1) | async-done | bytes 1048608 | tf_op jit(solution)/shard_map/all_to_all | solution.py:295
  155.0 0.8 reduce_sum.12
  (17 shorter events, 0.1 us)
Async XLA Ops:
  7.2 16.5 %copy-start.6 = (bf16[256,512]{1,0:T(8,128)(2,1)S(1)}, bf16[256,512]{1,0:T(8,128)(2,1)}, u32[]{:S(2)}) copy-start(bf16[256,512]{1,0:T(8,128)(2,1)} %param.11) | copy-start | bytes 786436
  7.2 54.5 %all-gather.5.cloned.1.call-start = ((), (), s32[]{:S(2)}) async-start(), calls=%async_computation.2 | async-start | bytes 2359296 | tf_op jit(solution)/shard_map/all_gather | solution.py:237
  7.2 10.3 %collective-permute-start.3 = (bf16[512,256]{1,0:T(8,128)(2,1)}, bf16[512,256]{1,0:T(8,128)(2,1)S(1)}, u32[]{:S(2)}, u32[]{:S(2)}) collective-permute-start(bf16[512,256]{1,0:T(8,128)(2,1)} %param.10), channel_id=1, source_target_pairs={{0,1},{1,0},{2,3},{3,2},{4,5},{5,4},{6,7},{7,6},{8,9},{9,8},{10,11... | collective-permute-start | bytes 786440 | tf_op jit(solution)/shard_map/ppermute | solution.py:29
  17.5 39.6 %copy-start.3 = (f32[64,512]{1,0:T(8,128)S(1)}, f32[64,512]{1,0:T(8,128)}, u32[]{:S(2)}) copy-start(f32[64,512]{1,0:T(8,128)} %bank_ref.1) | copy-start | bytes 393220
  20.1 19.6 %all-to-all-start = ((bf16[4,144,512]{2,1,0:T(8,128)(2,1)}), bf16[4,144,512]{2,1,0:T(8,128)(2,1)S(1)}, u32[]{:S(2)}, u32[]{:S(2)}) async-start(bf16[4,144,512]{2,1,0:T(8,128)(2,1)} %shift.1), calls=%async_computation | async-start | bytes 1179648 | tf_op jit(solution)/shard_map/all_to_all | solution.py:226
  23.6 81.0 %all-gather.7.cloned.1.call-start = ((), (), s32[]{:S(2)}) async-start(), calls=%async_computation.3 | async-start | bytes 2654208 | tf_op jit(solution)/shard_map/all_gather | solution.py:240
  23.7 18.0 %collective-permute-start.12 = (bf16[256,512]{1,0:T(8,128)(2,1)S(1)}, bf16[256,512]{1,0:T(8,128)(2,1)S(1)}, u32[]{:S(2)}, u32[]{:S(2)}) collective-permute-start(bf16[256,512]{1,0:T(8,128)(2,1)S(1)} %copy-done.6), channel_id=1, source_target_pairs={{0,1},{1,0},{2,3},{3,2},{4,5},{5,4},{6,7},{7,6},{8,9},{9,8},{10,11... | collective-permute-start | bytes 786440 | tf_op jit(solution)/shard_map/ppermute | solution.py:29
  39.7 11.8 %collective-permute-start = (bf16[4,144,512]{2,1,0:T(8,128)(2,1)S(1)}, bf16[4,144,512]{2,1,0:T(8,128)(2,1)S(1)}, u32[]{:S(2)}, u32[]{:S(2)}) collective-permute-start(bf16[4,144,512]{2,1,0:T(8,128)(2,1)S(1)} %all-to-all-done.refs_0_), channel_id=1, source_target_pairs={{0,8},{1,57},{8,0},{9,17},{16,24},{17,9},{24,16},{25,33},{32,40},{... | collective-permute-start | bytes 1769480 | tf_op jit(solution)/shard_map/ppermute | solution.py:47
  52.3 9.3 %collective-permute-start.1 = (bf16[4,144,512]{2,1,0:T(8,128)(2,1)S(1)}, bf16[4,144,512]{2,1,0:T(8,128)(2,1)S(1)}, u32[]{:S(2)}, u32[]{:S(2)}) collective-permute-start(bf16[4,144,512]{2,1,0:T(8,128)(2,1)S(1)} %all-to-all-done.refs_0_), channel_id=1, source_target_pairs={{0,1},{1,0},{2,3},{3,2},{4,5},{5,4},{6,7},{7,6},{8,9},{9,8},{10,11... | collective-permute-start | bytes 1769480 | tf_op jit(solution)/shard_map/ppermute | solution.py:29
  55.1 6.5 %collective-permute-start.2 = (bf16[4,144,512]{2,1,0:T(8,128)(2,1)S(1)}, bf16[4,144,512]{2,1,0:T(8,128)(2,1)S(1)}, u32[]{:S(2)}, u32[]{:S(2)}) collective-permute-start(bf16[4,144,512]{2,1,0:T(8,128)(2,1)S(1)} %collective-permute-done.refs_1_), channel_id=1, source_target_pairs={{0,1},{1,0},{2,3},{3,2},{4,5},{5,4},{6,7},{7,6},{8,9},{9,8},{10,11... | collective-permute-start | bytes 1769480 | tf_op jit(solution)/shard_map/ppermute | solution.py:29
  57.1 4.6 %collective-permute-start.4 = (f32[64,512]{1,0:T(8,128)S(1)}, f32[64,512]{1,0:T(8,128)S(1)}, u32[]{:S(2)}, u32[]{:S(2)}) collective-permute-start(f32[64,512]{1,0:T(8,128)S(1)} %copy-done.3), channel_id=1, source_target_pairs={{0,1},{1,0},{2,3},{3,2},{4,5},{5,4},{6,7},{7,6},{8,9},{9,8},{10,11... | collective-permute-start | bytes 393224 | tf_op jit(solution)/shard_map/ppermute | solution.py:29
  59.6 1.2 copy-start.4
  61.7 1.6 copy-start.2
  64.7 7.3 %collective-permute-start.5 = (f32[64,512]{1,0:T(8,128)S(1)}, f32[64,512]{1,0:T(8,128)S(1)}, u32[]{:S(2)}, u32[]{:S(2)}) collective-permute-start(f32[64,512]{1,0:T(8,128)S(1)} %bank.1), channel_id=1, source_target_pairs={{0,1},{1,0},{2,3},{3,2},{4,5},{5,4},{6,7},{7,6},{8,9},{9,8},{10,11... | collective-permute-start | bytes 393224 | tf_op jit(solution)/shard_map/ppermute | solution.py:29
  67.7 11.1 %collective-permute-start.7 = (bf16[256,1024]{1,0:T(8,128)(2,1)S(1)}, bf16[256,1024]{1,0:T(8,128)(2,1)S(1)}, u32[]{:S(2)}, u32[]{:S(2)}) collective-permute-start(bf16[256,1024]{1,0:T(8,128)(2,1)S(1)} %key_part.3._), channel_id=1, source_target_pairs={{0,2},{1,7},{2,0},{3,5},{4,6},{5,3},{6,4},{7,1},{8,10},{9,15},{10,... | collective-permute-start | bytes 1572872 | tf_op jit(solution)/shard_map/ppermute | solution.py:38
  73.4 11.5 %collective-permute-start.6 = (bf16[256,1024]{1,0:T(8,128)(2,1)S(1)}, bf16[256,1024]{1,0:T(8,128)(2,1)S(1)}, u32[]{:S(2)}, u32[]{:S(2)}) collective-permute-start(bf16[256,1024]{1,0:T(8,128)(2,1)S(1)} %key_part.5), channel_id=1, source_target_pairs={{0,2},{1,7},{2,0},{3,5},{4,6},{5,3},{6,4},{7,1},{8,10},{9,15},{10,... | collective-permute-start | bytes 1572872 | tf_op jit(solution)/shard_map/ppermute | solution.py:38
  78.9 10.8 %collective-permute-start.8 = (bf16[256,1024]{1,0:T(8,128)(2,1)S(1)}, bf16[256,1024]{1,0:T(8,128)(2,1)S(1)}, u32[]{:S(2)}, u32[]{:S(2)}) collective-permute-start(bf16[256,1024]{1,0:T(8,128)(2,1)S(1)} %add.38.mine_ref), channel_id=1, source_target_pairs={{0,6},{1,3},{2,4},{3,1},{4,2},{5,7},{6,0},{7,5},{8,14},{9,11},{10,... | collective-permute-start | bytes 1572872 | tf_op jit(solution)/shard_map/ppermute | solution.py:38
  85.0 10.3 %collective-permute-start.9 = (bf16[256,1024]{1,0:T(8,128)(2,1)S(1)}, bf16[256,1024]{1,0:T(8,128)(2,1)S(1)}, u32[]{:S(2)}, u32[]{:S(2)}) collective-permute-start(bf16[256,1024]{1,0:T(8,128)(2,1)S(1)} %add.37.mine_ref), channel_id=1, source_target_pairs={{0,6},{1,3},{2,4},{3,1},{4,2},{5,7},{6,0},{7,5},{8,14},{9,11},{10,... | collective-permute-start | bytes 1572872 | tf_op jit(solution)/shard_map/ppermute | solution.py:38
  89.9 12.6 %collective-permute-start.10 = (bf16[256,1024]{1,0:T(8,128)(2,1)S(1)}, bf16[256,1024]{1,0:T(8,128)(2,1)S(1)}, u32[]{:S(2)}, u32[]{:S(2)}) collective-permute-start(bf16[256,1024]{1,0:T(8,128)(2,1)S(1)} %square.2.refs_0_), channel_id=1, source_target_pairs={{0,2},{1,7},{2,0},{3,5},{4,6},{5,3},{6,4},{7,1},{8,10},{9,15},{10,... | collective-permute-start | bytes 1572872 | tf_op jit(solution)/shard_map/ppermute | solution.py:38
  95.5 12.6 %collective-permute-start.11 = (bf16[256,1024]{1,0:T(8,128)(2,1)S(1)}, bf16[256,1024]{1,0:T(8,128)(2,1)S(1)}, u32[]{:S(2)}, u32[]{:S(2)}) collective-permute-start(bf16[256,1024]{1,0:T(8,128)(2,1)S(1)} %square.3.refs_1_), channel_id=1, source_target_pairs={{0,2},{1,7},{2,0},{3,5},{4,6},{5,3},{6,4},{7,1},{8,10},{9,15},{10,... | collective-permute-start | bytes 1572872 | tf_op jit(solution)/shard_map/ppermute | solution.py:38
  104.7 1.7 %copy-start = (bf16[1152,1024]{1,0:T(8,128)(2,1)S(1)}, bf16[1152,1024]{1,0:T(8,128)(2,1)}, u32[]{:S(2)}) copy-start(bf16[1152,1024]{1,0:T(8,128)(2,1)} %all-gather.7.cloned.1.call-done) | copy-start | bytes 7077892
  106.3 1.8 %copy-start.1 = (bf16[1152,1024]{1,0:T(8,128)(2,1)S(1)}, bf16[1152,1024]{1,0:T(8,128)(2,1)}, u32[]{:S(2)}) copy-start(bf16[1152,1024]{1,0:T(8,128)(2,1)} %all-gather.7.cloned.1.call-done) | copy-start | bytes 7077892
  109.3 8.0 %collective-permute-start.13 = (bf16[4,2,128,512]{3,2,1,0:T(8,128)(2,1)S(1)}, bf16[4,2,128,512]{3,2,1,0:T(8,128)(2,1)S(1)}, u32[]{:S(2)}, u32[]{:S(2)}) collective-permute-start(bf16[4,2,128,512]{3,2,1,0:T(8,128)(2,1)S(1)} %out_part.5), channel_id=1, source_target_pairs={{0,1},{1,0},{2,3},{3,2},{4,5},{5,4},{6,7},{7,6},{8,9},{9,8},{10,11... | collective-permute-start | bytes 3145736 | tf_op jit(solution)/shard_map/ppermute | solution.py:29
  119.1 6.7 %copy-start.5 = (f32[64,4096]{1,0:T(8,128)S(1)}, f32[64,4096]{1,0:T(8,128)}, u32[]{:S(2)}) copy-start(f32[64,4096]{1,0:T(8,128)} %hid_ref.1) | copy-start | bytes 3145732
  119.1 35.9 %all-to-all-start.1 = ((bf16[8,128,512]{2,1,0:T(8,128)(2,1)}), bf16[8,128,512]{2,1,0:T(8,128)(2,1)S(1)}, u32[]{:S(2)}, u32[]{:S(2)}) async-start(bf16[8,128,512]{2,1,0:T(8,128)(2,1)} %place.1), calls=%async_computation.1 | async-start | bytes 2097152 | tf_op jit(solution)/shard_map/all_to_all | solution.py:295
Sparse Core Ops, SparseCore 0:
  18.4 39.5 all-gather.4
  60.6 43.9 all-gather.6
